TPU v7x, 256 devices: a whole 4x4x8 slice. The times are simulated.
256 devices in a mesh: ctx: 32 (over y, z), head: 8 (over x, core).
Axes of the slice: x: 4, y: 4, z: 8, core: 2. Of those that a mesh axis runs over, the one named last changes fastest.
Arguments:
- queries: bfloat16 [16384, 4096], P('ctx', 'head'), may hold values from -48 to 48
- key_rows: bfloat16 [16384, 1024], P('ctx', 'head'), may hold values from -48 to 48
- value_rows: bfloat16 [16384, 1024], P('ctx', 'head'), may hold values from -6 to 6
- kept_positions: int32 [8, 8192], P('head', 'ctx'), may hold values from 0 to 511, as said below
- anchor_length: int32 [8], P('head'), may hold values from 128 to 512
- output_weight: bfloat16 [4096, 4096], P('head'), may hold values from -0.125 to 0.125
Outputs:
- layer_output: bfloat16 [16384, 4096], P('ctx', 'head')
Inputs may be any that keep to these rules, and one draw needn't show every extreme that they name: `kept_positions`: for each key-value head and block, 256 distinct positions of that block.
All inputs are finite; a program needn't handle non-finite values.
Results may differ from a plain program's by a relative error of at most 0.02.
Values may be sent and summed in bfloat16 or wider, within the bound.
No kernel may reach another device: no remote copies, remote signals or barrier semaphores. Data moves between devices by JAX's collectives and lax.ppermute only.
A program may use at most 192 MiB of HBM per device.

v0:
```python
import functools

import jax
import jax.numpy as jnp
from jax import lax
from jax.experimental import pallas as pl
from jax.experimental.pallas import tpu as pltpu
from jax.sharding import PartitionSpec as P

HEAD = 128
WIDE = 8
NEAR = 192
INFO = 16
PER_BLOCK = 256
OWN, BELOW, ABOVE, BELOW2 = range(4)
LOG2E = 1.4426950408889634
FACTOR = HEAD**-0.5 * LOG2E
LIMIT = 2.0**100
NEGATIVE = -1e30
NT = (((1,), (1,)), ((), ()))
VMEM = pl.BlockSpec(memory_space=pltpu.VMEM)
SMEM = pl.BlockSpec(memory_space=pltpu.SMEM)
HBM = pl.BlockSpec(memory_space=pltpu.HBM)
ANY = pl.BlockSpec(memory_space=pl.ANY)
TILE = 512
EACH = 64
PARAMS = pltpu.CompilerParams(vmem_limit_bytes=28 * 2**20)


def dot(a, b):
    return jnp.dot(a, b, preferred_element_type=jnp.float32)


def dot_nt(a, b):
    return lax.dot_general(a, b, NT, preferred_element_type=jnp.float32)


def count_along(shape, dim):
    return lax.broadcasted_iota(jnp.int32, shape, dim)


def ones_where(condition):
    return jnp.where(condition, 1.0, 0.0).astype(jnp.bfloat16)


def select_kernel(used_ref, *refs):
    sources, (near_ref, far_ref), targets, sems = refs[:3], refs[3:5], refs[5:8], refs[8]
    copies = [
        pltpu.make_async_copy(source, target, sems.at[at])
        for at, (source, target) in enumerate(zip(sources, targets))
    ]
    for copy in copies:
        copy.start()
    for copy in copies:
        copy.wait()
    kept_ref, key_ref, value_ref = targets
    length, keep = key_ref.shape[0], kept_ref.shape[1]
    near = near_ref.shape[0]
    hit = ones_where(count_along((length, keep), 0) == kept_ref[...])
    kept = dot_nt(jnp.ones((8, keep), jnp.bfloat16), hit)
    square = (length, length)
    before = ones_where(count_along(square, 0) < count_along(square, 1))
    rank = dot(kept.astype(jnp.bfloat16), before)
    column = count_along((8, length), 1)
    place = jnp.where(kept > 0.5, rank, column.astype(jnp.float32) + keep - rank)
    order = ones_where(count_along(square, 0).astype(jnp.float32) == place[:1])
    for at, ref in enumerate((key_ref, value_ref)):
        columns = slice(at * HEAD, (at + 1) * HEAD)
        rows = dot(order, ref[...]).astype(jnp.bfloat16)
        near_ref[:, columns] = rows[:near]
        far_ref[: length - near, columns] = rows[near:]
    in_both = jnp.where((kept > 0.5) & (column < used_ref[0]), 1.0, 0.0)[:1]
    number = jnp.sum(in_both, axis=1, keepdims=True)
    far_ref[length - near :] = jnp.broadcast_to(number, (INFO, 2 * HEAD)).astype(jnp.bfloat16)


def select(used, kept, keys, values):
    length = keys.shape[0]
    rows = (NEAR, length - NEAR + INFO)
    return pl.pallas_call(
        select_kernel,
        out_shape=[jax.ShapeDtypeStruct((n, 2 * HEAD), jnp.bfloat16) for n in rows],
        in_specs=[SMEM, HBM, HBM, HBM],
        out_specs=[VMEM] * 2,
        scratch_shapes=[
            *[pltpu.VMEM(x.shape, x.dtype) for x in (kept, keys, values)],
            pltpu.SemaphoreType.DMA((3,)),
        ],
        compiler_params=PARAMS,
        name="select_kept",
    )(used, kept, keys, values)


def wide(column, width):
    return jnp.concatenate([column] * (width // HEAD), axis=1)


def widened(values):
    return jnp.concatenate([values, jnp.ones_like(values)], axis=1)


def scores(query, keys):
    return dot_nt(query, keys) * FACTOR


def local(k_ref, v_ref, acc_ref, peak_ref, h, query):
    shape = (query.shape[0], k_ref.shape[0])
    causal = count_along(shape, 1) <= count_along(shape, 0) + pl.program_id(0) * shape[0]
    raw = jnp.where(causal, scores(query, k_ref[...]), NEGATIVE)
    peak = jnp.broadcast_to(jnp.max(raw, axis=1, keepdims=True), (shape[0], HEAD))
    peak_ref[h] = peak
    weights = jnp.exp2(raw - wide(peak, shape[1])).astype(jnp.bfloat16)
    acc_ref[h] = dot(weights, widened(v_ref[...]))


def biased(raw, bias):
    return (raw.reshape(-1, *bias.shape) + bias).reshape(raw.shape)


def fixed(acc_ref, peak_ref, h, query, keys, values, bias):
    raw = biased(scores(query, keys), bias)
    weights = jnp.exp2(raw - wide(peak_ref[h], keys.shape[0])).astype(jnp.bfloat16)
    acc_ref[h] += dot(weights, values)


def moving(acc_ref, peak_ref, h, query, keys, values, bias):
    raw = biased(scores(query, keys), bias)
    old = peak_ref[h]
    peak = jnp.maximum(old, jnp.max(raw, axis=1, keepdims=True))
    weights = jnp.exp2(raw - wide(peak, keys.shape[0])).astype(jnp.bfloat16)
    peak_ref[h] = peak
    acc_ref[h] = acc_ref[h] * wide(jnp.exp2(old - peak), 2 * HEAD) + dot(weights, values)


def absorb(q_ref, acc_ref, peak_ref, start, tiles, read):
    heads = acc_ref.shape[0]

    def each_head(act):
        for h in range(heads):
            act(h, q_ref[:, h * HEAD : (h + 1) * HEAD])

    each_head(start)

    @pl.loop(0, tiles)
    def _(tile):
        keys = read(tile)
        each_head(lambda h, query: fixed(acc_ref, peak_ref, h, query, *keys))

    largest = jnp.max(acc_ref[:, :, HEAD:])

    @pl.when(jnp.logical_not(largest < LIMIT))
    def _():
        @pl.loop(0, heads)
        def _(h):
            query = q_ref[:, pl.ds(pl.multiple_of(h * HEAD, HEAD), HEAD)]
            start(h, query)

            @pl.loop(0, tiles)
            def _(tile):
                moving(acc_ref, peak_ref, h, query, *read(tile))


def tile_of(ref, at):
    rows = pl.ds(pl.multiple_of(at * TILE, TILE), TILE)
    return ref[rows, :HEAD], widened(ref[rows, HEAD:])


def bias_where(allowed):
    return jnp.where(allowed, 0.0, NEGATIVE)


def own_row_kernel(place_ref, q_ref, k_ref, v_ref, row_ref, acc_ref, peak_ref, bias_ref):
    keys = place_ref[0] % WIDE * NEAR
    start = functools.partial(local, k_ref, v_ref, acc_ref, peak_ref)

    def read(tile):
        bias_ref[...] = bias_where(count_along(bias_ref.shape, 1) + tile * TILE < keys)
        return *tile_of(row_ref, tile), bias_ref[...]

    absorb(q_ref, acc_ref, peak_ref, start, (keys + TILE - 1) // TILE, read)


def rest_kernel(
    place_ref, q_ref, row_ref, below_ref, above_ref, below2_ref, above2_ref, far_ref, rest_ref,
    acc_in, peak_in, out_ref, bank_ref, bias_ref, acc_ref, peak_ref, sems,
):
    mine, used = place_ref[0], place_ref[1]
    y, z = mine // WIDE, mine % WIDE
    span, far_rows = WIDE * NEAR, far_ref.shape[0]
    half = TILE // 2
    copies = []

    def copy(source, at, rows, condition=None):
        target = bank_ref.at[pl.ds(at, rows)]
        copies.append((pltpu.make_async_copy(source, target, sems.at[len(copies)]), condition))

    for row, ref in enumerate((row_ref, below_ref, below2_ref, above_ref)):
        copy(ref.at[pl.ds(0, NEAR)], 0, NEAR, y == row)
    at_row = jnp.where(y == 1, BELOW, jnp.where(y == 2, BELOW2, jnp.where(y == 3, ABOVE, OWN)))
    copy(far_ref.at[pl.ds(pl.multiple_of(at_row * EACH, EACH), EACH)], NEAR, EACH)
    copy(far_ref, TILE, far_rows)
    at = TILE + far_rows
    copy(below_ref, at, span, y > 0)
    copy(below2_ref, at + span, span // 2, y > 1)
    copy(above2_ref, at + span + span // 2, span // 2, y > 1)
    copy(above_ref, at + 2 * span, span, y == 3)

    def under(condition, act):
        if condition is None:
            act()
        else:
            pl.when(condition)(act)

    for one, condition in copies:
        under(condition, one.start)
    bank_ref[half:TILE] = rest_ref[:half]
    number = wide(rest_ref[half : half + 1, :HEAD].astype(jnp.int32), TILE)
    at = count_along((1, TILE), 1)
    limit = jnp.where(at < half, number, half + used - number)
    bias_ref[0] = jnp.broadcast_to(bias_where(at < limit), bias_ref.shape[1:])
    piece = count_along(bias_ref.shape[1:], 1) // EACH
    row = piece % 4
    for tile in range(far_rows // TILE):
        column = piece // 4 + tile * (TILE // EACH // 4)
        reach = jnp.where(
            row == OWN, z, jnp.where(row == BELOW, y, jnp.where(row == BELOW2, y - 1, y - 2)) * WIDE
        )
        bias_ref[1 + tile] = bias_where(column < reach)
    bias_ref[1 + far_rows // TILE] = jnp.zeros(bias_ref.shape[1:], jnp.float32)

    def start(h, query):
        acc_ref[h] = acc_in[h]
        peak_ref[h] = peak_in[h]

    for one, condition in copies:
        under(condition, one.wait)

    def read(tile):
        return *tile_of(bank_ref, tile), bias_ref[jnp.minimum(tile, bias_ref.shape[0] - 1)]

    tiles = jnp.where(mine > 0, 1 + far_rows // TILE + span // TILE * y, 0)
    absorb(q_ref, acc_ref, peak_ref, start, tiles, read)
    for h in range(acc_ref.shape[0]):
        out_ref[:, h * HEAD : (h + 1) * HEAD] = (
            acc_ref[h, :, :HEAD] / acc_ref[h, :, HEAD:]
        ).astype(jnp.bfloat16)


def pack_far_kernel(place_ref, own_ref, below_ref, above_ref, below2_ref, far_ref, rest_ref):
    y, z = place_ref[0] // WIDE, place_ref[0] % WIDE
    each = far_ref.shape[1]
    for at, ref in ((OWN, own_ref), (BELOW, below_ref), (ABOVE, above_ref), (BELOW2, below2_ref)):
        far_ref[at] = ref[:each]
    for row, ref in enumerate((own_ref, below_ref, below2_ref, above_ref)):

        @pl.when((y == row) & (z == 0))
        def _():
            rest_ref[...] = ref[each:]

    @pl.when(z > 0)
    def _():
        rest_ref[...] = jnp.zeros_like(rest_ref)


def pack_far(place, *pieces):
    rows, keep = pieces[0].shape[0], PER_BLOCK - NEAR
    return pl.pallas_call(
        pack_far_kernel,
        out_shape=[
            jax.ShapeDtypeStruct((len(pieces), keep, 2 * HEAD), jnp.bfloat16),
            jax.ShapeDtypeStruct((rows - keep, 2 * HEAD), jnp.bfloat16),
        ],
        in_specs=[SMEM] + [VMEM] * len(pieces),
        out_specs=[VMEM] * 2,
        compiler_params=PARAMS,
        name="pack_far",
    )(place, *pieces)


def cost(rows, keys):
    return pl.CostEstimate(
        flops=rows * keys * HEAD * 8, bytes_accessed=8 * 2**20, transcendentals=rows * keys
    )


def state_of(length, heads):
    return [
        jax.ShapeDtypeStruct((heads, length, 2 * HEAD), jnp.float32),
        jax.ShapeDtypeStruct((heads, length, HEAD), jnp.float32),
    ]


def own_row(place, queries, keys, values, row, parts):
    length, width = queries.shape
    rows, heads = length // parts, width // HEAD
    whole = lambda x: pl.BlockSpec(x.shape, lambda i: (0,) * x.ndim)
    slab = lambda columns: pl.BlockSpec((heads, rows, columns), lambda i: (0, i, 0))
    return pl.pallas_call(
        own_row_kernel,
        grid=(parts,),
        out_shape=state_of(length, heads),
        in_specs=[
            SMEM,
            pl.BlockSpec((rows, width), lambda i: (i, 0)),
            *[whole(x) for x in (keys, values, row)],
        ],
        out_specs=[slab(2 * HEAD), slab(HEAD)],
        scratch_shapes=[pltpu.VMEM((8, TILE), jnp.float32)],
        compiler_params=PARAMS,
        cost_estimate=cost(length * heads, length + WIDE * NEAR),
        name="own_row",
    )(place, queries, keys, values, row)


def rest_rows(place, queries, banks, rest, state, part, parts):
    length, width = queries.shape
    rows, heads = length // parts, width // HEAD
    tiles = 14
    slab = lambda columns: pl.BlockSpec((heads, rows, columns), lambda i: (0, part, 0))
    return pl.pallas_call(
        rest_kernel,
        grid=(1,),
        out_shape=jax.ShapeDtypeStruct((rows, width), jnp.bfloat16),
        in_specs=[
            SMEM,
            pl.BlockSpec((rows, width), lambda i: (part, 0)),
            *[HBM, ANY, ANY, ANY, ANY, HBM],
            pl.BlockSpec(rest.shape, lambda i: (0, 0)),
            slab(2 * HEAD),
            slab(HEAD),
        ],
        out_specs=pl.BlockSpec((rows, width), lambda i: (0, 0)),
        scratch_shapes=[
            pltpu.VMEM((tiles * TILE, 2 * HEAD), jnp.bfloat16),
            pltpu.VMEM((6, 8, TILE), jnp.float32),
            pltpu.VMEM((heads, rows, 2 * HEAD), jnp.float32),
            pltpu.VMEM((heads, rows, HEAD), jnp.float32),
            pltpu.SemaphoreType.DMA((10,)),
        ],
        compiler_params=PARAMS,
        cost_estimate=cost(rows * heads, tiles * TILE),
        name=f"rest_rows_{part}",
    )(place, queries, *banks, rest, *state)


def project_kernel(place_ref, own_ref, other_ref, weight_ref, other_w_ref, out_ref):
    chips, _, columns = out_ref.shape
    for step in range(chips):
        at = lax.rem(place_ref[0] + step, chips)
        mine = pl.ds(pl.multiple_of((2 * at + place_ref[1]) * columns, columns), columns)
        total = dot(own_ref[...], weight_ref[:, mine]) + dot(other_ref[...], other_w_ref[at])
        out_ref[step] = total.astype(jnp.bfloat16)


def project(place, own, other, weight, other_w):
    chips, _, columns = other_w.shape
    return pl.pallas_call(
        project_kernel,
        out_shape=jax.ShapeDtypeStruct((chips, own.shape[0], columns), jnp.bfloat16),
        in_specs=[SMEM] + [VMEM] * 4,
        out_specs=VMEM,
        compiler_params=PARAMS,
        cost_estimate=pl.CostEstimate(
            flops=4 * own.size * chips * columns, bytes_accessed=8 * 2**20, transcendentals=0
        ),
        name="project",
    )(place, own, other, weight, other_w)


def weight_kernel(place_ref, weight_ref, out_ref):
    columns = out_ref.shape[2]
    start = pl.multiple_of((1 - place_ref[1]) * columns, columns)
    out_ref[0] = weight_ref[:, pl.ds(start, columns)]


def weight_half(place, weight, chips):
    rows, columns = weight.shape[0], weight.shape[1] // chips // 2
    return pl.pallas_call(
        weight_kernel,
        grid=(chips,),
        out_shape=jax.ShapeDtypeStruct((chips, rows, columns), weight.dtype),
        in_specs=[SMEM, pl.BlockSpec((rows, 2 * columns), lambda i: (0, i))],
        out_specs=pl.BlockSpec((1, rows, columns), lambda i: (i, 0, 0)),
        compiler_params=PARAMS,
        cost_estimate=pl.CostEstimate(flops=0, bytes_accessed=6 * 2**20, transcendentals=0),
        name="weight_half",
    )(place, weight)


def added(*terms):
    return sum(term.astype(jnp.float32) for term in terms).astype(jnp.bfloat16)


def on_device(queries, key_rows, value_rows, kept_positions, anchor_length, output_weight):
    mine, head = lax.axis_index("ctx"), lax.axis_index("head")
    length, devices, blocks = queries.shape[0], lax.axis_size("head"), lax.axis_size("ctx")
    chips, chip, core = devices // 2, head // 2, head % 2
    tall = blocks // WIDE
    swap = [(i, i ^ 1) for i in range(devices)]
    up = [(i, (i + 2) % devices) for i in range(devices)]
    down = [(i, (i - 2) % devices) for i in range(devices)]
    across = lambda hops: [(a * WIDE + c, b * WIDE + c) for a, b in hops for c in range(WIDE)]
    permute = lambda x, pairs: lax.ppermute(x, "ctx", pairs)

    place = jnp.concatenate([mine.astype(jnp.int32)[None], anchor_length])
    spot = jnp.stack([chip, core]).astype(jnp.int32)
    near, far = select(anchor_length, kept_positions, key_rows, value_rows)

    below = permute(far, across([(0, 1), (1, 2), (2, 3)]))
    above = permute(far, across([(0, 3)]))
    below2 = permute(below, across([(1, 2), (2, 3)]))
    far, rest = pack_far(place, far, below, above, below2)
    half_w = weight_half(spot, output_weight, chips)
    rows = [[r * WIDE + c for c in range(WIDE)] for r in range(tall)]

    row = lax.all_gather(near, "ctx", axis_index_groups=rows).reshape(-1, 2 * HEAD)
    row, far, rest, half_w = lax.optimization_barrier((row, far, rest, half_w))
    far = lax.all_gather(far, "ctx", axis_index_groups=rows).reshape(-1, 2 * HEAD)
    below = permute(row, across([(0, 1), (1, 2), (2, 3)]))
    above = permute(row, across([(0, 3), (1, 0)]))
    middle = row.shape[0] // 2
    below2 = permute(below[:middle], across([(1, 2), (2, 3)]))
    above2 = permute(above[middle:], across([(0, 3), (3, 2)]))

    chain = lambda hops: [(r * WIDE + a, r * WIDE + b) for a, b in hops for r in range(tall)]
    for hops in ([(0, 1)], [(0, 7), (1, 2)], [(7, 6), (2, 3)], [(6, 5), (3, 4)]):
        rest = rest + permute(rest, chain(hops))

    other_w = lax.ppermute(half_w, "head", swap)

    parts = 2
    state = own_row(place, queries, key_rows, value_rows, row, parts)
    banks = (row, below, above, below2, above2, far)

    outs = []
    rows_each = length // parts
    half = rows_each // 2
    for part in range(parts):
        own = rest_rows(place, queries, banks, rest, state, part, parts)
        other = lax.ppermute(own, "head", swap)
        terms = project(spot, own, other, output_weight, other_w)
        from_below = lax.ppermute(terms[2, :half], "head", up)
        from_above = lax.ppermute(terms[2, half:], "head", down)
        upward = jnp.concatenate([added(terms[1, :half], from_below), terms[1, half:]])
        downward = jnp.concatenate([terms[3, :half], added(terms[3, half:], from_above)])
        outs.append(
            added(terms[0], lax.ppermute(upward, "head", up), lax.ppermute(downward, "head", down))
        )
    return jnp.concatenate(outs)


def solution(mesh):
    placed = (
        P("ctx", "head"),
        P("ctx", "head"),
        P("ctx", "head"),
        P("head", "ctx"),
        P("head"),
        P("head", None),
    )
    return jax.shard_map(
        on_device, mesh=mesh, in_specs=placed, out_specs=P("ctx", "head"), check_vma=False
    )
```

profile of v0, /device:TPU:30, one launch (start us, length us, event | category | flops | bytes accessed | tf_op | source)
XLA Modules:
  0.0 224.0 jit_solution(4564860196318188570)
XLA Ops:
  13.4 29.8 %all-gather.row_ref = bf16[1536,256]{1,0:T(8,128)(2,1)S(1)} all-gather(bf16[192,256]{1,0:T(8,128)(2,1)S(1)} %get-tuple-element.15), channel_id=2, replica_groups={{0,8,16,24,32,40,48,56},{64,72,80,88,96,104,112,120},{128,136,144,152,1..., dimensions={0}, use_global_device_ids=true | all-gather | bytes 884736 | tf_op jit(solution)/shard_map/all_gather | solution.py:416
  44.5 2.2 copy-done
  47.8 1.3 copy-done.2
  49.2 1.9 collective-permute-done.2.below2_ref
  54.9 3.1 %collective-permute-start.7 = (bf16[272,256]{1,0:T(8,128)(2,1)S(1)}, bf16[272,256]{1,0:T(8,128)(2,1)S(1)}, u32[]{:S(2)}, u32[]{:S(2)}) collective-permute-start(bf16[272,256]{1,0:T(8,128)(2,1)S(1)} %get-tuple-element.21), channel_id=1, source_target_pairs={{0,8},{64,72},{128,136},{192,200},{1,9},{65,73},{129,137},{193,201... | collective-permute-start | bytes 417800 | tf_op jit(solution)/shard_map/ppermute | solution.py:403
  58.1 2.5 %collective-permute-done.7 = bf16[272,256]{1,0:T(8,128)(2,1)S(1)} collective-permute-done((bf16[272,256]{1,0:T(8,128)(2,1)S(1)}, bf16[272,256]{1,0:T(8,128)(2,1)S(1)}, u32[]{:S(2)}, u32[]{:S(2)}) %collective-permute-start.7) | collective-permute-done | bytes 139296 | tf_op jit(solution)/shard_map/ppermute | solution.py:403
  60.6 1.3 collective-permute-start.8
  61.9 3.5 %collective-permute-done.8 = bf16[272,256]{1,0:T(8,128)(2,1)S(1)} collective-permute-done((bf16[272,256]{1,0:T(8,128)(2,1)S(1)}, bf16[272,256]{1,0:T(8,128)(2,1)S(1)}, u32[]{:S(2)}, u32[]{:S(2)}) %collective-permute-start.8) | collective-permute-done | bytes 139296 | tf_op jit(solution)/shard_map/ppermute | solution.py:403
  68.2 3.0 %collective-permute-start.6 = (bf16[768,256]{1,0:T(8,128)(2,1)S(1)}, bf16[768,256]{1,0:T(8,128)(2,1)S(1)}, u32[]{:S(2)}, u32[]{:S(2)}) collective-permute-start(bf16[768,256]{1,0:T(8,128)(2,1)S(1)} %slice.65), channel_id=1, source_target_pairs={{0,192},{8,200},{16,208},{24,216},{32,224},{40,232},{48,240},{56,2... | collective-permute-start | bytes 1179656 | tf_op jit(solution)/shard_map/ppermute | solution.py:403
  74.4 3.5 %own_row.1 = (f32[4,512,256]{2,1,0:T(8,128)S(1)}, f32[4,512,128]{2,1,0:T(8,128)S(1)}) custom-call(s32[2]{0:T(128)S(1)} %pad_add_fusion.1.place_ref, bf16[512,512]{1,0:T(8,128)(2,1)S(1)} %copy-done.16, bf16[512,128]{1,0:T(8,128)(2,1)S(1)} %copy-done.10, bf16[512,128]{1,0:T(8,128)(2,1)S(1)} %copy-done.12, bf16[1536,256]{1,0:T(8,128)(2,1)S(1)} %all-gather.row_ref), custom_call_target="tpu_custom_call" | custom-call | flops 4294967296 | bytes 8388608 | tf_op jit(solution)/shard_map/own_row/pallas_call | solution.py:298
  77.9 1.4 copy-done.22
  82.6 9.0 %all-gather.4.cloned.1.call-done = bf16[32,64,256]{2,1,0:T(8,128)(2,1)} async-done(((bf16[4,64,256]{2,1,0:T(8,128)(2,1)}), bf16[32,64,256]{2,1,0:T(8,128)(2,1)}) %all-gather.4.cloned.1.call-update) | async-done | bytes 1048592 | tf_op jit(solution)/shard_map/all_gather | solution.py:418
  98.2 1.6 copy-done.23
  101.0 44.9 %rest_rows_0.1.own_ref = bf16[256,512]{1,0:T(8,128)(2,1)S(1)} custom-call(s32[2]{0:T(128)S(1)} %pad_add_fusion.1.place_ref, bf16[512,512]{1,0:T(8,128)(2,1)S(1)} %copy-done.17, bf16[1536,256]{1,0:T(8,128)(2,1)S(1)} %all-gather.row_ref, bf16[1536,256]{1,0:T(8,128)(2,1)S(1)} %copy-done.7, bf16[1536,256]{1,0:T(8,128)(2,1)S(1)} %copy-done.4, ...), custom_call_target="tpu_custom_call" | custom-call | flops 7516192768 | bytes 8388608 | tf_op jit(solution)/shard_map/rest_rows_0/pallas_call | solution.py:320
  146.0 44.9 %rest_rows_1.1.own_ref = bf16[256,512]{1,0:T(8,128)(2,1)S(1)} custom-call(s32[2]{0:T(128)S(1)} %pad_add_fusion.1.place_ref, bf16[512,512]{1,0:T(8,128)(2,1)S(1)} %copy-done.17, bf16[1536,256]{1,0:T(8,128)(2,1)S(1)} %all-gather.row_ref, bf16[1536,256]{1,0:T(8,128)(2,1)S(1)} %copy-done.8, bf16[1536,256]{1,0:T(8,128)(2,1)S(1)} %copy-done.5, ...), custom_call_target="tpu_custom_call" | custom-call | flops 7516192768 | bytes 8388608 | tf_op jit(solution)/shard_map/rest_rows_1/pallas_call | solution.py:320
  191.5 1.8 project.2
  194.0 1.5 collective-permute-start.15
  195.4 1.8 project.3
  197.3 1.8 collective-permute-start.18
  200.8 3.1 %collective-permute-start.14 = (bf16[256,512]{1,0:T(8,128)(2,1)S(1)}, bf16[256,512]{1,0:T(8,128)(2,1)S(1)}, u32[]{:S(2)}, u32[]{:S(2)}) collective-permute-start(bf16[256,512]{1,0:T(8,128)(2,1)S(1)} %pad_maximum_fusion.1), channel_id=1, source_target_pairs={{0,2},{1,3},{2,4},{3,5},{4,6},{5,7},{6,0},{7,1},{8,10},{9,11},{10,... | collective-permute-start | bytes 786440 | tf_op jit(solution)/shard_map/ppermute | solution.py:447
  203.8 2.9 %collective-permute-done.20 = bf16[128,512]{1,0:T(8,128)(2,1)S(1)} collective-permute-done((bf16[128,512]{1,0:T(8,128)(2,1)S(1)}, bf16[128,512]{1,0:T(8,128)(2,1)S(1)}, u32[]{:S(2)}, u32[]{:S(2)}) %collective-permute-start.20) | collective-permute-done | bytes 131104 | tf_op jit(solution)/shard_map/ppermute | solution.py:443
  207.0 3.3 %collective-permute-start.19 = (bf16[256,512]{1,0:T(8,128)(2,1)S(1)}, bf16[256,512]{1,0:T(8,128)(2,1)S(1)}, u32[]{:S(2)}, u32[]{:S(2)}) collective-permute-start(bf16[256,512]{1,0:T(8,128)(2,1)S(1)} %pad_maximum_fusion.3), channel_id=1, source_target_pairs={{0,2},{1,3},{2,4},{3,5},{4,6},{5,7},{6,0},{7,1},{8,10},{9,11},{10,... | collective-permute-start | bytes 786440 | tf_op jit(solution)/shard_map/ppermute | solution.py:447
  210.3 2.1 collective-permute-done.16
  212.5 3.7 %collective-permute-done.21 = bf16[256,512]{1,0:T(8,128)(2,1)S(1)} collective-permute-done((bf16[256,512]{1,0:T(8,128)(2,1)S(1)}, bf16[256,512]{1,0:T(8,128)(2,1)S(1)}, u32[]{:S(2)}, u32[]{:S(2)}) %collective-permute-start.21) | collective-permute-done | bytes 262176 | tf_op jit(solution)/shard_map/ppermute | solution.py:447
  (105 shorter events, 33.9 us)
Async XLA Ops:
  6.5 85.1 %all-gather.4.cloned.1.call-start = ((), (), s32[]{:S(2)}) async-start(), calls=%async_computation | async-start | bytes 1179648 | tf_op jit(solution)/shard_map/all_gather | solution.py:418
  10.8 38.4 %collective-permute-start.1 = (bf16[336,256]{1,0:T(8,128)(2,1)S(1)}, bf16[336,256]{1,0:T(8,128)(2,1)S(1)}, u32[]{:S(2)}, u32[]{:S(2)}) collective-permute-start(bf16[336,256]{1,0:T(8,128)(2,1)S(1)} %get-tuple-element.16.own_ref), channel_id=1, source_target_pairs={{0,192},{8,200},{16,208},{24,216},{32,224},{40,232},{48,240},{56,2... | collective-permute-start | bytes 516104 | tf_op jit(solution)/shard_map/ppermute | solution.py:403
  12.1 31.1 %collective-permute-start = (bf16[336,256]{1,0:T(8,128)(2,1)S(1)}, bf16[336,256]{1,0:T(8,128)(2,1)S(1)}, u32[]{:S(2)}, u32[]{:S(2)}) collective-permute-start(bf16[336,256]{1,0:T(8,128)(2,1)S(1)} %get-tuple-element.16.own_ref), channel_id=1, source_target_pairs={{0,64},{8,72},{16,80},{24,88},{32,96},{40,104},{48,112},{56,120},{... | collective-permute-start | bytes 516104 | tf_op jit(solution)/shard_map/ppermute | solution.py:403
  43.2 7.9 %collective-permute-start.2 = (bf16[336,256]{1,0:T(8,128)(2,1)S(1)}, bf16[336,256]{1,0:T(8,128)(2,1)S(1)}, u32[]{:S(2)}, u32[]{:S(2)}) collective-permute-start(bf16[336,256]{1,0:T(8,128)(2,1)S(1)} %collective-permute-done.below_ref), channel_id=1, source_target_pairs={{64,128},{72,136},{80,144},{88,152},{96,160},{104,168},{112,176},{... | collective-permute-start | bytes 516104 | tf_op jit(solution)/shard_map/ppermute | solution.py:403
  52.3 15.9 %collective-permute-start.4 = (bf16[1536,256]{1,0:T(8,128)(2,1)S(1)}, bf16[1536,256]{1,0:T(8,128)(2,1)S(1)}, u32[]{:S(2)}, u32[]{:S(2)}) collective-permute-start(bf16[1536,256]{1,0:T(8,128)(2,1)S(1)} %all-gather.row_ref), channel_id=1, source_target_pairs={{0,192},{8,200},{16,208},{24,216},{32,224},{40,232},{48,240},{56,2... | collective-permute-start | bytes 2359304 | tf_op jit(solution)/shard_map/ppermute | solution.py:403
  53.6 17.6 %collective-permute-start.3 = (bf16[1536,256]{1,0:T(8,128)(2,1)S(1)}, bf16[1536,256]{1,0:T(8,128)(2,1)S(1)}, u32[]{:S(2)}, u32[]{:S(2)}) collective-permute-start(bf16[1536,256]{1,0:T(8,128)(2,1)S(1)} %all-gather.row_ref), channel_id=1, source_target_pairs={{0,64},{8,72},{16,80},{24,88},{32,96},{40,104},{48,112},{56,120},{... | collective-permute-start | bytes 2359304 | tf_op jit(solution)/shard_map/ppermute | solution.py:403
  54.9 5.7 %collective-permute-start.7 = (bf16[272,256]{1,0:T(8,128)(2,1)S(1)}, bf16[272,256]{1,0:T(8,128)(2,1)S(1)}, u32[]{:S(2)}, u32[]{:S(2)}) collective-permute-start(bf16[272,256]{1,0:T(8,128)(2,1)S(1)} %get-tuple-element.21), channel_id=1, source_target_pairs={{0,8},{64,72},{128,136},{192,200},{1,9},{65,73},{129,137},{193,201... | collective-permute-start | bytes 417800 | tf_op jit(solution)/shard_map/ppermute | solution.py:403
  58.0 133.4 %collective-permute-start.12 = (bf16[4,512,512]{2,1,0:T(8,128)(2,1)}, bf16[4,512,512]{2,1,0:T(8,128)(2,1)S(1)}, u32[]{:S(2)}, u32[]{:S(2)}) collective-permute-start(bf16[4,512,512]{2,1,0:T(8,128)(2,1)} %copy-done.2), channel_id=1, source_target_pairs={{0,1},{1,0},{2,3},{3,2},{4,5},{5,4},{6,7},{7,6},{8,9},{9,8},{10,11... | collective-permute-start | bytes 6291464 | tf_op jit(solution)/shard_map/ppermute | solution.py:429
  60.6 4.8 %collective-permute-start.8 = (bf16[272,256]{1,0:T(8,128)(2,1)S(1)}, bf16[272,256]{1,0:T(8,128)(2,1)S(1)}, u32[]{:S(2)}, u32[]{:S(2)}) collective-permute-start(bf16[272,256]{1,0:T(8,128)(2,1)S(1)} %add.42), channel_id=1, source_target_pairs={{0,56},{64,120},{128,184},{192,248},{8,16},{72,80},{136,144},{200,... | collective-permute-start | bytes 417800 | tf_op jit(solution)/shard_map/ppermute | solution.py:403
  65.5 0.7 collective-permute-start.9
  66.2 14.0 %collective-permute-start.10 = (bf16[272,256]{1,0:T(8,128)(2,1)S(1)}, bf16[272,256]{1,0:T(8,128)(2,1)S(1)}, u32[]{:S(2)}, u32[]{:S(2)}) collective-permute-start(bf16[272,256]{1,0:T(8,128)(2,1)S(1)} %add.44), channel_id=1, source_target_pairs={{48,40},{112,104},{176,168},{240,232},{24,32},{88,96},{152,160},{2... | collective-permute-start | bytes 417800 | tf_op jit(solution)/shard_map/ppermute | solution.py:403
  68.2 12.3 %collective-permute-start.6 = (bf16[768,256]{1,0:T(8,128)(2,1)S(1)}, bf16[768,256]{1,0:T(8,128)(2,1)S(1)}, u32[]{:S(2)}, u32[]{:S(2)}) collective-permute-start(bf16[768,256]{1,0:T(8,128)(2,1)S(1)} %slice.65), channel_id=1, source_target_pairs={{0,192},{8,200},{16,208},{24,216},{32,224},{40,232},{48,240},{56,2... | collective-permute-start | bytes 1179656 | tf_op jit(solution)/shard_map/ppermute | solution.py:403
  72.1 9.8 %collective-permute-start.5 = (bf16[768,256]{1,0:T(8,128)(2,1)S(1)}, bf16[768,256]{1,0:T(8,128)(2,1)S(1)}, u32[]{:S(2)}, u32[]{:S(2)}) collective-permute-start(bf16[768,256]{1,0:T(8,128)(2,1)S(1)} %slice.64), channel_id=1, source_target_pairs={{64,128},{72,136},{80,144},{88,152},{96,160},{104,168},{112,176},{... | collective-permute-start | bytes 1179656 | tf_op jit(solution)/shard_map/ppermute | solution.py:403
  145.9 45.6 %collective-permute-start.11 = (bf16[256,512]{1,0:T(8,128)(2,1)S(1)}, bf16[256,512]{1,0:T(8,128)(2,1)S(1)}, u32[]{:S(2)}, u32[]{:S(2)}) collective-permute-start(bf16[256,512]{1,0:T(8,128)(2,1)S(1)} %rest_rows_0.1.own_ref), channel_id=1, source_target_pairs={{0,1},{1,0},{2,3},{3,2},{4,5},{5,4},{6,7},{7,6},{8,9},{9,8},{10,11... | collective-permute-start | bytes 786440 | tf_op jit(solution)/shard_map/ppermute | solution.py:440
  146.0 45.5 %copy-start.1 = (bf16[512,4096]{1,0:T(8,128)(2,1)S(1)}, bf16[512,4096]{1,0:T(8,128)(2,1)}, u32[]{:S(2)}) copy-start(bf16[512,4096]{1,0:T(8,128)(2,1)} %weight_ref.5) | copy-start | bytes 12582916
  190.9 4.5 %collective-permute-start.17 = (bf16[256,512]{1,0:T(8,128)(2,1)S(1)}, bf16[256,512]{1,0:T(8,128)(2,1)S(1)}, u32[]{:S(2)}, u32[]{:S(2)}) collective-permute-start(bf16[256,512]{1,0:T(8,128)(2,1)S(1)} %rest_rows_1.1.own_ref), channel_id=1, source_target_pairs={{0,1},{1,0},{2,3},{3,2},{4,5},{5,4},{6,7},{7,6},{8,9},{9,8},{10,11... | collective-permute-start | bytes 786440 | tf_op jit(solution)/shard_map/ppermute | solution.py:440
  193.3 6.1 %collective-permute-start.13 = (bf16[128,512]{1,0:T(8,128)(2,1)S(1)}, bf16[128,512]{1,0:T(8,128)(2,1)S(1)}, u32[]{:S(2)}, u32[]{:S(2)}) collective-permute-start(bf16[128,512]{1,0:T(8,128)(2,1)S(1)} %get-tuple-element.27), channel_id=1, source_target_pairs={{0,2},{1,3},{2,4},{3,5},{4,6},{5,7},{6,0},{7,1},{8,10},{9,11},{10,... | collective-permute-start | bytes 393224 | tf_op jit(solution)/shard_map/ppermute | solution.py:442
  194.0 6.4 %collective-permute-start.15 = (bf16[128,512]{1,0:T(8,128)(2,1)S(1)}, bf16[128,512]{1,0:T(8,128)(2,1)S(1)}, u32[]{:S(2)}, u32[]{:S(2)}) collective-permute-start(bf16[128,512]{1,0:T(8,128)(2,1)S(1)} %get-tuple-element.28), channel_id=1, source_target_pairs={{0,6},{1,7},{2,0},{3,1},{4,2},{5,3},{6,4},{7,5},{8,14},{9,15},{10,... | collective-permute-start | bytes 393224 | tf_op jit(solution)/shard_map/ppermute | solution.py:443
  197.3 6.6 %collective-permute-start.18 = (bf16[128,512]{1,0:T(8,128)(2,1)S(1)}, bf16[128,512]{1,0:T(8,128)(2,1)S(1)}, u32[]{:S(2)}, u32[]{:S(2)}) collective-permute-start(bf16[128,512]{1,0:T(8,128)(2,1)S(1)} %get-tuple-element.33), channel_id=1, source_target_pairs={{0,2},{1,3},{2,4},{3,5},{4,6},{5,7},{6,0},{7,1},{8,10},{9,11},{10,... | collective-permute-start | bytes 393224 | tf_op jit(solution)/shard_map/ppermute | solution.py:442
  199.1 7.6 %collective-permute-start.20 = (bf16[128,512]{1,0:T(8,128)(2,1)S(1)}, bf16[128,512]{1,0:T(8,128)(2,1)S(1)}, u32[]{:S(2)}, u32[]{:S(2)}) collective-permute-start(bf16[128,512]{1,0:T(8,128)(2,1)S(1)} %get-tuple-element.34), channel_id=1, source_target_pairs={{0,6},{1,7},{2,0},{3,1},{4,2},{5,3},{6,4},{7,5},{8,14},{9,15},{10,... | collective-permute-start | bytes 393224 | tf_op jit(solution)/shard_map/ppermute | solution.py:443
  200.4 12.0 %collective-permute-start.16 = (bf16[256,512]{1,0:T(8,128)(2,1)S(1)}, bf16[256,512]{1,0:T(8,128)(2,1)S(1)}, u32[]{:S(2)}, u32[]{:S(2)}) collective-permute-start(bf16[256,512]{1,0:T(8,128)(2,1)S(1)} %pad_maximum_fusion.2), channel_id=1, source_target_pairs={{0,6},{1,7},{2,0},{3,1},{4,2},{5,3},{6,4},{7,5},{8,14},{9,15},{10,... | collective-permute-start | bytes 786440 | tf_op jit(solution)/shard_map/ppermute | solution.py:447
  200.8 11.6 %collective-permute-start.14 = (bf16[256,512]{1,0:T(8,128)(2,1)S(1)}, bf16[256,512]{1,0:T(8,128)(2,1)S(1)}, u32[]{:S(2)}, u32[]{:S(2)}) collective-permute-start(bf16[256,512]{1,0:T(8,128)(2,1)S(1)} %pad_maximum_fusion.1), channel_id=1, source_target_pairs={{0,2},{1,3},{2,4},{3,5},{4,6},{5,7},{6,0},{7,1},{8,10},{9,11},{10,... | collective-permute-start | bytes 786440 | tf_op jit(solution)/shard_map/ppermute | solution.py:447
  206.9 9.3 %collective-permute-start.21 = (bf16[256,512]{1,0:T(8,128)(2,1)S(1)}, bf16[256,512]{1,0:T(8,128)(2,1)S(1)}, u32[]{:S(2)}, u32[]{:S(2)}) collective-permute-start(bf16[256,512]{1,0:T(8,128)(2,1)S(1)} %pad_maximum_fusion.4), channel_id=1, source_target_pairs={{0,6},{1,7},{2,0},{3,1},{4,2},{5,3},{6,4},{7,5},{8,14},{9,15},{10,... | collective-permute-start | bytes 786440 | tf_op jit(solution)/shard_map/ppermute | solution.py:447
  207.0 9.2 %collective-permute-start.19 = (bf16[256,512]{1,0:T(8,128)(2,1)S(1)}, bf16[256,512]{1,0:T(8,128)(2,1)S(1)}, u32[]{:S(2)}, u32[]{:S(2)}) collective-permute-start(bf16[256,512]{1,0:T(8,128)(2,1)S(1)} %pad_maximum_fusion.3), channel_id=1, source_target_pairs={{0,2},{1,3},{2,4},{3,5},{4,6},{5,7},{6,0},{7,1},{8,10},{9,11},{10,... | collective-permute-start | bytes 786440 | tf_op jit(solution)/shard_map/ppermute | solution.py:447
  (26 other events, 252.8 us)
Sparse Core Ops, SparseCore 0:
  52.4 39.1 all-gather.3
where the time goes:
time: 226 us; the launch traced here: 224 us
  Pallas kernels  100 us (44%)
  blocking collectives  29.8 us (13%)
  waiting for transfers between devices  28.6 us (13%)
  starting transfers between devices  28.2 us (12%)
  local copies, waits for them, and re-layouts  21.3 us (9%)
  between operations  14.5 us (6%)
    pallas_call x2, Pallas kernels, rest_rows(): pl.pallas_call(rest_kernel, grid=(1,), out_shape=jax.ShapeDtypeStruct((ro...  89.7 us
    all_gather x1, blocking collectives, on_device(): lax.all_gather(near, 'ctx', axis_index_groups=rows).reshape(-1, 2 * HEAD)  29.8 us
    unnamed x54, local copies, waits for them, and re-layouts  21.1 us
    ppermute x11, starting transfers between devices, on_device(): permute = lambda x, pairs: lax.ppermute(x, 'ctx', pairs)  16.4 us
    ppermute x11, waiting for transfers between devices, on_device(): permute = lambda x, pairs: lax.ppermute(x, 'ctx', pairs)  9.93 us
    all_gather x1, waiting for transfers between devices, on_device(): lax.all_gather(far, 'ctx', axis_index_groups=rows).reshape(-1, 2 * HEAD)  9.02 us
    ppermute x2, starting transfers between devices, on_device(): lax.ppermute(upward, 'head', up)  6.35 us
    ppermute x2, waiting for transfers between devices, on_device(): lax.ppermute(downward, 'head', down)  5.78 us
  transfers between devices with their start and end apart: 23, of which 11 were waited for; matrix products, arithmetic and copies ran while one was open for 0% of the time, Pallas kernels for 44%

commit v1 on v0

v1 whole, which is shorter than its diff:
```python
import functools

import jax
import jax.numpy as jnp
from jax import lax
from jax.experimental import pallas as pl
from jax.experimental.pallas import tpu as pltpu
from jax.sharding import PartitionSpec as P

HEAD = 128
WIDE = 8
INFO = 16
KEEP = 256
LOG2E = 1.4426950408889634
FACTOR = HEAD**-0.5 * LOG2E
LIMIT = 2.0**100
NEGATIVE = -1e30
NT = (((1,), (1,)), ((), ()))
VMEM = pl.BlockSpec(memory_space=pltpu.VMEM)
SMEM = pl.BlockSpec(memory_space=pltpu.SMEM)
HBM = pl.BlockSpec(memory_space=pltpu.HBM)
ANY = pl.BlockSpec(memory_space=pl.ANY)
TILE = 512
PARAMS = pltpu.CompilerParams(vmem_limit_bytes=60 * 2**20)


def dot(a, b):
    return jnp.dot(a, b, preferred_element_type=jnp.float32)


def dot_nt(a, b):
    return lax.dot_general(a, b, NT, preferred_element_type=jnp.float32)


def count_along(shape, dim):
    return lax.broadcasted_iota(jnp.int32, shape, dim)


def ones_where(condition):
    return jnp.where(condition, 1.0, 0.0).astype(jnp.bfloat16)


def select_kernel(used_ref, *refs):
    sources, (kept_rows_ref, rest_ref), targets, sems = refs[:3], refs[3:5], refs[5:8], refs[8]
    copies = [
        pltpu.make_async_copy(source, target, sems.at[at])
        for at, (source, target) in enumerate(zip(sources, targets))
    ]
    for copy in copies:
        copy.start()
    for copy in copies:
        copy.wait()
    kept_ref, key_ref, value_ref = targets
    length, keep = key_ref.shape[0], kept_ref.shape[1]
    hit = ones_where(count_along((length, keep), 0) == kept_ref[...])
    kept = dot_nt(jnp.ones((8, keep), jnp.bfloat16), hit)
    square = (length, length)
    before = ones_where(count_along(square, 0) < count_along(square, 1))
    rank = dot(kept.astype(jnp.bfloat16), before)
    column = count_along((8, length), 1)
    place = jnp.where(kept > 0.5, rank, column.astype(jnp.float32) + keep - rank)
    order = ones_where(count_along(square, 0).astype(jnp.float32) == place[:1])
    for at, ref in enumerate((key_ref, value_ref)):
        columns = slice(at * HEAD, (at + 1) * HEAD)
        rows = dot(order, ref[...]).astype(jnp.bfloat16)
        kept_rows_ref[:, columns] = rows[:keep]
        rest_ref[: length - keep, columns] = rows[keep:]
    in_both = jnp.where((kept > 0.5) & (column < used_ref[0]), 1.0, 0.0)[:1]
    number = jnp.sum(in_both, axis=1, keepdims=True)
    rest_ref[length - keep :] = jnp.broadcast_to(number, (INFO, 2 * HEAD)).astype(jnp.bfloat16)


def select(used, kept, keys, values):
    length = keys.shape[0]
    rows = (KEEP, length - KEEP + INFO)
    return pl.pallas_call(
        select_kernel,
        out_shape=[jax.ShapeDtypeStruct((n, 2 * HEAD), jnp.bfloat16) for n in rows],
        in_specs=[SMEM, HBM, HBM, HBM],
        out_specs=[VMEM] * 2,
        scratch_shapes=[
            *[pltpu.VMEM(x.shape, x.dtype) for x in (kept, keys, values)],
            pltpu.SemaphoreType.DMA((3,)),
        ],
        compiler_params=PARAMS,
        name="select_kept",
    )(used, kept, keys, values)


def wide(column, width):
    return jnp.concatenate([column] * (width // HEAD), axis=1)


def widened(values):
    return jnp.concatenate([values, jnp.ones_like(values)], axis=1)


def scores(query, keys):
    return dot_nt(query, keys) * FACTOR


def local(k_ref, v_ref, acc_ref, peak_ref, h, query):
    shape = (query.shape[0], k_ref.shape[0])
    causal = count_along(shape, 1) <= count_along(shape, 0) + pl.program_id(0) * shape[0]
    raw = jnp.where(causal, scores(query, k_ref[...]), NEGATIVE)
    peak = jnp.broadcast_to(jnp.max(raw, axis=1, keepdims=True), (shape[0], HEAD))
    peak_ref[h] = peak
    weights = jnp.exp2(raw - wide(peak, shape[1])).astype(jnp.bfloat16)
    acc_ref[h] = dot(weights, widened(v_ref[...]))


def biased(raw, bias):
    if bias is None:
        return raw
    return (raw.reshape(-1, *bias.shape) + bias).reshape(raw.shape)


def moving(acc_ref, peak_ref, h, query, keys, values, bias):
    raw = biased(scores(query, keys), bias)
    old = peak_ref[h]
    peak = jnp.maximum(old, jnp.max(raw, axis=1, keepdims=True))
    weights = jnp.exp2(raw - wide(peak, keys.shape[0])).astype(jnp.bfloat16)
    peak_ref[h] = peak
    acc_ref[h] = acc_ref[h] * wide(jnp.exp2(old - peak), 2 * HEAD) + dot(weights, values)


def absorb(q_ref, acc_ref, peak_ref, start, masked, tiles, read):
    heads = acc_ref.shape[0]

    def query(h):
        return q_ref[:, h * HEAD : (h + 1) * HEAD]

    def fixed(keys, values, bias):
        raw = scores(query(0), keys)
        for h in range(heads):
            ahead = scores(query(h + 1), keys) if h + 1 < heads else None
            weights = jnp.exp2(biased(raw, bias) - wide(peak_ref[h], keys.shape[0]))
            acc_ref[h] += dot(weights.astype(jnp.bfloat16), values)
            raw = ahead

    for h in range(heads):
        start(h, query(h))

    @pl.loop(0, masked)
    def _(tile):
        fixed(*read(tile, True, True))

    if tiles is not None:

        @pl.loop(masked, tiles)
        def _(tile):
            fixed(*read(tile, False, True))

    largest = jnp.max(acc_ref[:, :, HEAD:])

    @pl.when(jnp.logical_not(largest < LIMIT))
    def _():
        @pl.loop(0, heads)
        def _(h):
            query = q_ref[:, pl.ds(pl.multiple_of(h * HEAD, HEAD), HEAD)]
            start(h, query)

            @pl.loop(0, masked if tiles is None else tiles)
            def _(tile):
                moving(acc_ref, peak_ref, h, query, *read(tile, True, False))


def tile_of(ref, at):
    rows = pl.ds(pl.multiple_of(at * TILE, TILE), TILE)
    return ref[rows, :HEAD], widened(ref[rows, HEAD:])


def bias_where(allowed):
    return jnp.where(allowed, 0.0, NEGATIVE)


def own_row_kernel(place_ref, q_ref, k_ref, v_ref, row_ref, acc_ref, peak_ref, bias_ref):
    keys = place_ref[0] % WIDE * KEEP
    start = functools.partial(local, k_ref, v_ref, acc_ref, peak_ref)

    def read(tile, masked, first_time):
        bias_ref[...] = bias_where(count_along(bias_ref.shape, 1) + tile * TILE < keys)
        return *tile_of(row_ref, tile), bias_ref[...]

    absorb(q_ref, acc_ref, peak_ref, start, (keys + TILE - 1) // TILE, None, read)


def rest_kernel(
    place_ref, q_ref, row_ref, below_ref, above_ref, below2_ref, above2_ref, rest_ref,
    acc_in, peak_in, out_ref, bank_ref, bias_ref, acc_ref, peak_ref, sems,
):
    mine, used = place_ref[0], place_ref[1]
    y = mine // WIDE
    span = WIDE * KEEP
    row_tiles = span // TILE
    copies = []

    def copy(source, at, rows, condition, tile):
        target = bank_ref.at[pl.ds(at, rows)]
        one = pltpu.make_async_copy(source, target, sems.at[len(copies)])
        copies.append((one, condition, tile))

    for row, ref in enumerate((row_ref, below_ref, below2_ref, above_ref)):
        copy(ref.at[pl.ds(0, KEEP)], 0, KEEP, (mine > 0) & (y == row), 0)
    copy(below_ref, TILE, span, y > 0, 1)
    copy(below2_ref, TILE + span, span // 2, y > 1, 1 + row_tiles)
    copy(above2_ref, TILE + span + span // 2, span // 2, y > 1, 1 + row_tiles)
    copy(above_ref, TILE + 2 * span, span, y == 3, 1 + 2 * row_tiles)
    for one, condition, _ in copies:
        pl.when(condition)(one.start)
    bank_ref[KEEP:TILE] = rest_ref[: TILE - KEEP]
    number = wide(rest_ref[TILE - KEEP : TILE - KEEP + 1, :HEAD].astype(jnp.int32), TILE)
    at = count_along((1, TILE), 1)
    limit = jnp.where(at < KEEP, number, KEEP + used - number)
    bias_ref[0] = jnp.broadcast_to(bias_where(at < limit), bias_ref.shape[1:])
    bias_ref[1] = jnp.zeros(bias_ref.shape[1:], jnp.float32)

    def start(h, query):
        acc_ref[h] = acc_in[h]
        peak_ref[h] = peak_in[h]

    def read(tile, masked, first_time):
        if first_time:
            for one, condition, when in copies:
                if masked == (when == 0):
                    pl.when(condition & (tile == when))(one.wait)
        bias = bias_ref[jnp.minimum(tile, 1)] if masked else None
        return *tile_of(bank_ref, tile), bias

    masked = jnp.where(mine > 0, 1, 0)
    absorb(q_ref, acc_ref, peak_ref, start, masked, masked + row_tiles * y, read)
    for h in range(acc_ref.shape[0]):
        out_ref[:, h * HEAD : (h + 1) * HEAD] = (
            acc_ref[h, :, :HEAD] / acc_ref[h, :, HEAD:]
        ).astype(jnp.bfloat16)


def pack_row_kernel(place_ref, *refs):
    out_ref = refs[-1]
    z = place_ref[0] % WIDE
    at = KEEP
    for ref in refs[:-1]:
        rows = ref.shape[0]
        start = pl.multiple_of(lax.rem(z * KEEP + at, WIDE * KEEP), KEEP // 2)
        out_ref[pl.ds(start, rows)] = ref[...]
        at += rows


def pack_row(place, pieces):
    return pl.pallas_call(
        pack_row_kernel,
        out_shape=jax.ShapeDtypeStruct((WIDE * KEEP, 2 * HEAD), jnp.bfloat16),
        in_specs=[SMEM] + [VMEM] * len(pieces),
        out_specs=VMEM,
        compiler_params=pltpu.CompilerParams(vmem_limit_bytes=8 * 2**20),
        name="pack_row",
    )(place, *pieces)


def cost(rows, keys):
    return pl.CostEstimate(
        flops=rows * keys * HEAD * 8, bytes_accessed=8 * 2**20, transcendentals=rows * keys
    )


def state_of(length, heads):
    return [
        jax.ShapeDtypeStruct((heads, length, 2 * HEAD), jnp.float32),
        jax.ShapeDtypeStruct((heads, length, HEAD), jnp.float32),
    ]


def own_row(place, queries, keys, values, row, parts):
    length, width = queries.shape
    rows, heads = length // parts, width // HEAD
    whole = lambda x: pl.BlockSpec(x.shape, lambda i: (0,) * x.ndim)
    slab = lambda columns: pl.BlockSpec((heads, rows, columns), lambda i: (0, i, 0))
    return pl.pallas_call(
        own_row_kernel,
        grid=(parts,),
        out_shape=state_of(length, heads),
        in_specs=[
            SMEM,
            pl.BlockSpec((rows, width), lambda i: (i, 0)),
            *[whole(x) for x in (keys, values, row)],
        ],
        out_specs=[slab(2 * HEAD), slab(HEAD)],
        scratch_shapes=[pltpu.VMEM((8, TILE), jnp.float32)],
        compiler_params=PARAMS,
        cost_estimate=cost(length * heads, length + WIDE * KEEP),
        name="own_row",
    )(place, queries, keys, values, row)


def rest_rows(place, queries, banks, rest, state, part, parts):
    length, width = queries.shape
    rows, heads = length // parts, width // HEAD
    tiles = 13
    slab = lambda columns: pl.BlockSpec((heads, rows, columns), lambda i: (0, part, 0))
    return pl.pallas_call(
        rest_kernel,
        grid=(1,),
        out_shape=jax.ShapeDtypeStruct((rows, width), jnp.bfloat16),
        in_specs=[
            SMEM,
            pl.BlockSpec((rows, width), lambda i: (part, 0)),
            *[ANY] * len(banks),
            pl.BlockSpec(rest.shape, lambda i: (0, 0)),
            slab(2 * HEAD),
            slab(HEAD),
        ],
        out_specs=pl.BlockSpec((rows, width), lambda i: (0, 0)),
        scratch_shapes=[
            pltpu.VMEM((tiles * TILE, 2 * HEAD), jnp.bfloat16),
            pltpu.VMEM((2, 8, TILE), jnp.float32),
            pltpu.VMEM((heads, rows, 2 * HEAD), jnp.float32),
            pltpu.VMEM((heads, rows, HEAD), jnp.float32),
            pltpu.SemaphoreType.DMA((8,)),
        ],
        compiler_params=PARAMS,
        cost_estimate=cost(rows * heads, tiles * TILE),
        name=f"rest_rows_{part}",
    )(place, queries, *banks, rest, *state)


def project_kernel(place_ref, own_ref, other_ref, weight_ref, other_w_ref, out_ref):
    total = dot(own_ref[...], weight_ref[...]) + dot(other_ref[...], other_w_ref[...])
    out_ref[...] = total.astype(jnp.bfloat16)


def project(place, own, other, weight, other_w):
    chips, rows, columns = other_w.shape
    chip = lambda i, place: lax.rem(place[0] + i, chips)
    whole = pl.BlockSpec(own.shape, lambda i, place: (0, 0))
    return pl.pallas_call(
        project_kernel,
        grid_spec=pltpu.PrefetchScalarGridSpec(
            num_scalar_prefetch=1,
            grid=(chips,),
            in_specs=[
                whole,
                whole,
                pl.BlockSpec((rows, columns), lambda i, place: (0, 2 * chip(i, place) + place[1])),
                pl.BlockSpec((None, rows, columns), lambda i, place: (chip(i, place), 0, 0)),
            ],
            out_specs=pl.BlockSpec((None, own.shape[0], columns), lambda i, place: (i, 0, 0)),
        ),
        out_shape=jax.ShapeDtypeStruct((chips, own.shape[0], columns), jnp.bfloat16),
        compiler_params=PARAMS,
        cost_estimate=pl.CostEstimate(
            flops=4 * own.size * chips * columns, bytes_accessed=8 * 2**20, transcendentals=0
        ),
        name="project",
    )(place, own, other, weight, other_w)


def weight_kernel(place_ref, weight_ref, out_ref):
    columns = out_ref.shape[2]
    start = pl.multiple_of((1 - place_ref[1]) * columns, columns)
    out_ref[0] = weight_ref[:, pl.ds(start, columns)]


def weight_half(place, weight, chips):
    rows, columns = weight.shape[0], weight.shape[1] // chips // 2
    return pl.pallas_call(
        weight_kernel,
        grid=(chips,),
        out_shape=jax.ShapeDtypeStruct((chips, rows, columns), weight.dtype),
        in_specs=[SMEM, pl.BlockSpec((rows, 2 * columns), lambda i: (0, i))],
        out_specs=pl.BlockSpec((1, rows, columns), lambda i: (i, 0, 0)),
        compiler_params=PARAMS,
        cost_estimate=pl.CostEstimate(flops=0, bytes_accessed=6 * 2**20, transcendentals=0),
        name="weight_half",
    )(place, weight)


def added(*terms):
    return sum(term.astype(jnp.float32) for term in terms).astype(jnp.bfloat16)


def on_device(queries, key_rows, value_rows, kept_positions, anchor_length, output_weight):
    mine, head = lax.axis_index("ctx"), lax.axis_index("head")
    length, devices, blocks = queries.shape[0], lax.axis_size("head"), lax.axis_size("ctx")
    chips, chip, core = devices // 2, head // 2, head % 2
    tall = blocks // WIDE
    swap = [(i, i ^ 1) for i in range(devices)]
    up = [(i, (i + 2) % devices) for i in range(devices)]
    down = [(i, (i - 2) % devices) for i in range(devices)]
    along = lambda step: [
        (r * WIDE + c, r * WIDE + (c + step) % WIDE) for r in range(tall) for c in range(WIDE)
    ]
    across = lambda hops: [(a * WIDE + c, b * WIDE + c) for a, b in hops for c in range(WIDE)]
    permute = lambda x, pairs: lax.ppermute(x, "ctx", pairs)

    place = jnp.concatenate([mine.astype(jnp.int32)[None], anchor_length])
    spot = jnp.stack([chip, core]).astype(jnp.int32)
    kept, rest = select(anchor_length, kept_positions, key_rows, value_rows)

    plus, minus = along(1), along(-1)
    half = KEEP // 2
    left, right = [kept], [kept]
    rest = jnp.where(mine == 0, rest, jnp.zeros_like(rest))
    upward = [[(0, WIDE)], [(0, 3 * WIDE), (WIDE, 2 * WIDE)]]
    for step in range(WIDE // 2 - 1):
        left.append(permute(left[-1], plus))
        right.append(permute(right[-1], minus))
        if step < len(upward):
            rest = rest + permute(rest, upward[step])
            left[-1], right[-1], rest = lax.optimization_barrier((left[-1], right[-1], rest))
    opposite = [permute(left[-1][:half], plus), permute(right[-1][half:], minus)]
    row = pack_row(place, right[1:] + opposite + left[:0:-1] + [kept])

    below = permute(row, across([(0, 1), (1, 2), (2, 3)]))
    above = permute(row, across([(0, 3), (1, 0)]))
    half_w = weight_half(spot, output_weight, chips)
    below, half_w = lax.optimization_barrier((below, half_w))
    middle = row.shape[0] // 2
    below2 = permute(below[:middle], across([(1, 2), (2, 3)]))
    above2 = permute(above[middle:], across([(0, 3), (3, 2)]))

    rest, row = lax.optimization_barrier((rest, row))
    chain = lambda hops: [(r * WIDE + a, r * WIDE + b) for a, b in hops for r in range(tall)]
    for hops in ([(0, 1)], [(0, 7), (1, 2)], [(7, 6), (2, 3)], [(6, 5), (3, 4)]):
        rest = rest + permute(rest, chain(hops))

    other_w = lax.ppermute(half_w, "head", swap)

    parts = 2
    state = own_row(place, queries, key_rows, value_rows, row, parts)
    banks = (row, below, above, below2, above2)

    outs = []
    rows_each = length // parts
    half = rows_each // 2
    for part in range(parts):
        own = rest_rows(place, queries, banks, rest, state, part, parts)
        other = lax.ppermute(own, "head", swap)
        terms = project(spot, own, other, output_weight, other_w)
        from_below = lax.ppermute(terms[2, :half], "head", up)
        from_above = lax.ppermute(terms[2, half:], "head", down)
        upward = jnp.concatenate([added(terms[1, :half], from_below), terms[1, half:]])
        downward = jnp.concatenate([terms[3, :half], added(terms[3, half:], from_above)])
        outs.append(
            added(terms[0], lax.ppermute(upward, "head", up), lax.ppermute(downward, "head", down))
        )
    return jnp.concatenate(outs)


def solution(mesh):
    placed = (
        P("ctx", "head"),
        P("ctx", "head"),
        P("ctx", "head"),
        P("head", "ctx"),
        P("head"),
        P("head", None),
    )
    return jax.shard_map(
        on_device, mesh=mesh, in_specs=placed, out_specs=P("ctx", "head"), check_vma=False
    )
```

time: 226 us -> 215 us (0.951)
  blocking collectives: 29.8 us -> 0 us
  waiting for transfers between devices: 28.6 us -> 51.9 us
  between operations: 14.5 us -> 0.98 us
  local copies, waits for them, and re-layouts: 21.3 us -> 8.21 us
  starting transfers between devices: 28.2 us -> 40.9 us
  Pallas kernels: 100 us -> 108 us
    ppermute x11 -> x18, waiting for transfers between devices: 9.93 us -> 42.4 us  [on_device(): permute = lambda x, pairs: lax.ppermute(x, 'ctx', pairs)]
    all_gather x1 -> x0, blocking collectives: 29.8 us -> none  [on_device(): lax.all_gather(near, 'ctx', axis_index_groups=rows).reshape(-1, 2 * HEAD)]
    unnamed x54 -> x16, local copies, waits for them, and re-layouts: 21.1 us -> 3.7 us
    ppermute x11 -> x18, starting transfers between devices: 16.4 us -> 29.2 us  [on_device(): permute = lambda x, pairs: lax.ppermute(x, 'ctx', pairs)]
    all_gather x1 -> x0, waiting for transfers between devices: 9.02 us -> none  [on_device(): lax.all_gather(far, 'ctx', axis_index_groups=rows).reshape(-1, 2 * HEAD)]
    pallas_call x3, Pallas kernels: 4.82 us -> 11.9 us  [the longest x2 11.2 us: project(): pl.pallas_call(project_kernel, grid_spec=pltpu.PrefetchScalarGridSpec(num...]
    pallas_call x2, Pallas kernels: 89.7 us -> 84.3 us  [rest_rows(): pl.pallas_call(rest_kernel, grid=(1,), out_shape=jax.ShapeDtypeStruct((ro...]
    pallas_call x1, Pallas kernels: 1.01 us -> 4.21 us  [weight_half(): pl.pallas_call(weight_kernel, grid=(chips,), out_shape=jax.ShapeDtypeStru...]
  transfers between devices with their start and end apart: 23 -> 29, of which waited for: 11 -> 14; matrix products, arithmetic and copies ran while one was open for 0% -> 3% of each run, Pallas kernels for 44% -> 49%
where the time goes in v1:
time: 215 us; the launch traced here: 213 us
  Pallas kernels  108 us (50%)
  waiting for transfers between devices  51.9 us (24%)
  starting transfers between devices  40.9 us (19%)
  local copies, waits for them, and re-layouts  8.21 us (4%)
  other arithmetic  2.81 us (1%)
    pallas_call x2, Pallas kernels, rest_rows(): pl.pallas_call(rest_kernel, grid=(1,), out_shape=jax.ShapeDtypeStruct((ro...  84.3 us
    ppermute x18, waiting for transfers between devices, on_device(): permute = lambda x, pairs: lax.ppermute(x, 'ctx', pairs)  42.4 us
    ppermute x18, starting transfers between devices, on_device(): permute = lambda x, pairs: lax.ppermute(x, 'ctx', pairs)  29.2 us
    pallas_call x2, Pallas kernels, project(): pl.pallas_call(project_kernel, grid_spec=pltpu.PrefetchScalarGridSpec(num...  11.2 us
    ppermute x2, starting transfers between devices, on_device(): lax.ppermute(upward, 'head', up)  5.77 us
    ppermute x2, waiting for transfers between devices, on_device(): lax.ppermute(downward, 'head', down)  5.76 us
    pallas_call x1, Pallas kernels, own_row(): pl.pallas_call(own_row_kernel, grid=(parts,), out_shape=state_of(length,...  5.41 us
  transfers between devices with their start and end apart: 29, of which 14 were waited for; matrix products, arithmetic and copies ran while one was open for 3% of the time, Pallas kernels for 49%

profile of v1, /device:TPU:30, one launch (start us, length us, event | category | flops | bytes accessed | tf_op | source)
XLA Modules:
  0.0 213.1 jit_solution(12965375303927657906)
XLA Ops:
  3.8 5.9 %collective-permute-start.1 = (bf16[256,256]{1,0:T(8,128)(2,1)}, bf16[256,256]{1,0:T(8,128)(2,1)S(1)}, u32[]{:S(2)}, u32[]{:S(2)}) collective-permute-start(bf16[256,256]{1,0:T(8,128)(2,1)} %get-tuple-element.19.refs_8_), channel_id=1, source_target_pairs={{0,56},{8,0},{16,8},{24,16},{32,24},{40,32},{48,40},{56,48},{64,12... | collective-permute-start | bytes 393224 | tf_op jit(solution)/shard_map/ppermute | solution.py:393
  9.8 3.0 %collective-permute-done.1.refs_0_ = bf16[256,256]{1,0:T(8,128)(2,1)S(1)} collective-permute-done((bf16[256,256]{1,0:T(8,128)(2,1)}, bf16[256,256]{1,0:T(8,128)(2,1)S(1)}, u32[]{:S(2)}, u32[]{:S(2)}) %collective-permute-start.1) | collective-permute-done | bytes 131104 | tf_op jit(solution)/shard_map/ppermute | solution.py:393
  12.8 3.3 %collective-permute-done.refs_7_ = bf16[256,256]{1,0:T(8,128)(2,1)S(1)} collective-permute-done((bf16[256,256]{1,0:T(8,128)(2,1)}, bf16[256,256]{1,0:T(8,128)(2,1)S(1)}, u32[]{:S(2)}, u32[]{:S(2)}) %collective-permute-start) | collective-permute-done | bytes 131104 | tf_op jit(solution)/shard_map/ppermute | solution.py:393
  17.5 3.2 %collective-permute-start.4 = (bf16[256,256]{1,0:T(8,128)(2,1)S(1)}, bf16[256,256]{1,0:T(8,128)(2,1)S(1)}, u32[]{:S(2)}, u32[]{:S(2)}) collective-permute-start(bf16[256,256]{1,0:T(8,128)(2,1)S(1)} %collective-permute-done.1.refs_0_), channel_id=1, source_target_pairs={{0,56},{8,0},{16,8},{24,16},{32,24},{40,32},{48,40},{56,48},{64,12... | collective-permute-start | bytes 393224 | tf_op jit(solution)/shard_map/ppermute | solution.py:393
  20.7 3.5 %collective-permute-done.5 = bf16[272,256]{1,0:T(8,128)(2,1)S(1)} collective-permute-done((bf16[272,256]{1,0:T(8,128)(2,1)S(1)}, bf16[272,256]{1,0:T(8,128)(2,1)S(1)}, u32[]{:S(2)}, u32[]{:S(2)}) %collective-permute-start.5) | collective-permute-done | bytes 139296 | tf_op jit(solution)/shard_map/ppermute | solution.py:393
  24.3 2.6 %collective-permute-start.6 = (bf16[256,256]{1,0:T(8,128)(2,1)S(1)}, bf16[256,256]{1,0:T(8,128)(2,1)S(1)}, u32[]{:S(2)}, u32[]{:S(2)}) collective-permute-start(bf16[256,256]{1,0:T(8,128)(2,1)S(1)} %collective-permute-done.4.refs_1_), channel_id=1, source_target_pairs={{0,56},{8,0},{16,8},{24,16},{32,24},{40,32},{48,40},{56,48},{64,12... | collective-permute-start | bytes 393224 | tf_op jit(solution)/shard_map/ppermute | solution.py:393
  26.9 3.2 %collective-permute-done.6.refs_2_ = bf16[256,256]{1,0:T(8,128)(2,1)S(1)} collective-permute-done((bf16[256,256]{1,0:T(8,128)(2,1)S(1)}, bf16[256,256]{1,0:T(8,128)(2,1)S(1)}, u32[]{:S(2)}, u32[]{:S(2)}) %collective-permute-start.6) | collective-permute-done | bytes 131104 | tf_op jit(solution)/shard_map/ppermute | solution.py:393
  30.1 3.4 %collective-permute-start.9 = (bf16[128,256]{1,0:T(8,128)(2,1)S(1)}, bf16[128,256]{1,0:T(8,128)(2,1)S(1)}, u32[]{:S(2)}, u32[]{:S(2)}) collective-permute-start(bf16[128,256]{1,0:T(8,128)(2,1)S(1)} %slice.73), channel_id=1, source_target_pairs={{0,56},{8,0},{16,8},{24,16},{32,24},{40,32},{48,40},{56,48},{64,12... | collective-permute-start | bytes 196616 | tf_op jit(solution)/shard_map/ppermute | solution.py:393
  35.3 3.8 %collective-permute-done.8.refs_3_ = bf16[128,256]{1,0:T(8,128)(2,1)S(1)} collective-permute-done((bf16[128,256]{1,0:T(8,128)(2,1)S(1)}, bf16[128,256]{1,0:T(8,128)(2,1)S(1)}, u32[]{:S(2)}, u32[]{:S(2)}) %collective-permute-start.8) | collective-permute-done | bytes 65568 | tf_op jit(solution)/shard_map/ppermute | solution.py:393
  45.2 4.2 %weight_half.1 = bf16[4,512,512]{2,1,0:T(8,128)(2,1)} custom-call(s32[2]{0:T(128)} %pad_add_fusion.place_ref, bf16[512,4096]{1,0:T(8,128)(2,1)} %weight_ref.5), custom_call_target="tpu_custom_call" | custom-call | bytes 6291456 | tf_op jit(solution)/shard_map/weight_half/pallas_call | solution.py:365
  49.4 13.0 %collective-permute-done.10.below_ref = bf16[2048,256]{1,0:T(8,128)(2,1)} collective-permute-done((bf16[2048,256]{1,0:T(8,128)(2,1)S(1)}, bf16[2048,256]{1,0:T(8,128)(2,1)}, u32[]{:S(2)}, u32[]{:S(2)}) %collective-permute-start.10) | collective-permute-done | bytes 1048608 | tf_op jit(solution)/shard_map/ppermute | solution.py:393
  64.2 3.6 %collective-permute-done.15 = bf16[272,256]{1,0:T(8,128)(2,1)S(1)} collective-permute-done((bf16[272,256]{1,0:T(8,128)(2,1)S(1)}, bf16[272,256]{1,0:T(8,128)(2,1)S(1)}, u32[]{:S(2)}, u32[]{:S(2)}) %collective-permute-start.15) | collective-permute-done | bytes 139296 | tf_op jit(solution)/shard_map/ppermute | solution.py:393
  69.6 3.8 %collective-permute-start.13 = (bf16[1024,256]{1,0:T(8,128)(2,1)S(1)}, bf16[1024,256]{1,0:T(8,128)(2,1)}, u32[]{:S(2)}, u32[]{:S(2)}) collective-permute-start(bf16[1024,256]{1,0:T(8,128)(2,1)S(1)} %slice.74), channel_id=1, source_target_pairs={{0,192},{8,200},{16,208},{24,216},{32,224},{40,232},{48,240},{56,2... | collective-permute-start | bytes 1572872 | tf_op jit(solution)/shard_map/ppermute | solution.py:393
  76.5 5.4 %own_row.1 = (f32[4,512,256]{2,1,0:T(8,128)}, f32[4,512,128]{2,1,0:T(8,128)}) custom-call(s32[2]{0:T(128)} %copy-done.2, bf16[512,512]{1,0:T(8,128)(2,1)} %q_ref.5, bf16[512,128]{1,0:T(8,128)(2,1)} %k_ref.1, bf16[512,128]{1,0:T(8,128)(2,1)} %v_ref.1, bf16[2048,256]{1,0:T(8,128)(2,1)} %copy-done), custom_call_target="tpu_custom_call" | custom-call | flops 5368709120 | bytes 8388608 | tf_op jit(solution)/shard_map/own_row/pallas_call | solution.py:278
  82.6 3.7 %collective-permute-done.13.above2_ref = bf16[1024,256]{1,0:T(8,128)(2,1)} collective-permute-done((bf16[1024,256]{1,0:T(8,128)(2,1)S(1)}, bf16[1024,256]{1,0:T(8,128)(2,1)}, u32[]{:S(2)}, u32[]{:S(2)}) %collective-permute-start.13) | collective-permute-done | bytes 524320 | tf_op jit(solution)/shard_map/ppermute | solution.py:393
  86.4 3.4 %collective-permute-done.12.below2_ref = bf16[1024,256]{1,0:T(8,128)(2,1)} collective-permute-done((bf16[1024,256]{1,0:T(8,128)(2,1)S(1)}, bf16[1024,256]{1,0:T(8,128)(2,1)}, u32[]{:S(2)}, u32[]{:S(2)}) %collective-permute-start.12) | collective-permute-done | bytes 524320 | tf_op jit(solution)/shard_map/ppermute | solution.py:393
  89.8 42.3 %rest_rows_0.1.own_ref = bf16[256,512]{1,0:T(8,128)(2,1)} custom-call(s32[2]{0:T(128)} %copy-done.2, bf16[512,512]{1,0:T(8,128)(2,1)} %q_ref.5, bf16[2048,256]{1,0:T(8,128)(2,1)} %copy-done, bf16[2048,256]{1,0:T(8,128)(2,1)} %collective-permute-done.10.below_ref, bf16[2048,256]{1,0:T(8,128)(2,1)} %collective-permute-done.11.above_ref, ...), custom_call_target="tpu_custom_call" | custom-call | flops 6979321856 | bytes 8388608 | tf_op jit(solution)/shard_map/rest_rows_0/pallas_call | solution.py:300
  132.2 42.1 %rest_rows_1.1.own_ref = bf16[256,512]{1,0:T(8,128)(2,1)} custom-call(s32[2]{0:T(128)} %copy-done.2, bf16[512,512]{1,0:T(8,128)(2,1)} %q_ref.5, bf16[2048,256]{1,0:T(8,128)(2,1)} %copy-done, bf16[2048,256]{1,0:T(8,128)(2,1)} %collective-permute-done.10.below_ref, bf16[2048,256]{1,0:T(8,128)(2,1)} %collective-permute-done.11.above_ref, ...), custom_call_target="tpu_custom_call" | custom-call | flops 6979321856 | bytes 8388608 | tf_op jit(solution)/shard_map/rest_rows_1/pallas_call | solution.py:300
  176.9 5.6 %project.2 = bf16[4,256,512]{2,1,0:T(8,128)(2,1)} custom-call(s32[2]{0:T(128)} %pad_add_fusion.place_ref, bf16[256,512]{1,0:T(8,128)(2,1)} %rest_rows_0.1.own_ref, bf16[256,512]{1,0:T(8,128)(2,1)} %copy-done.7, bf16[512,4096]{1,0:T(8,128)(2,1)} %weight_ref.5, bf16[4,512,512]{2,1,0:T(8,128)(2,1)} %copy-done.3), custom_call_target="tpu_custom_call" | custom-call | flops 1073741824 | bytes 8388608 | tf_op jit(solution)/shard_map/project/pallas_call | solution.py:335
  186.5 5.6 %project.3 = bf16[4,256,512]{2,1,0:T(8,128)(2,1)} custom-call(s32[2]{0:T(128)} %pad_add_fusion.place_ref, bf16[256,512]{1,0:T(8,128)(2,1)} %rest_rows_1.1.own_ref, bf16[256,512]{1,0:T(8,128)(2,1)} %copy-done.6, bf16[512,4096]{1,0:T(8,128)(2,1)} %weight_ref.5, bf16[4,512,512]{2,1,0:T(8,128)(2,1)} %copy-done.3), custom_call_target="tpu_custom_call" | custom-call | flops 1073741824 | bytes 8388608 | tf_op jit(solution)/shard_map/project/pallas_call | solution.py:335
  196.5 2.5 %collective-permute-start.21 = (bf16[256,512]{1,0:T(8,128)(2,1)S(1)}, bf16[256,512]{1,0:T(8,128)(2,1)S(1)}, u32[]{:S(2)}, u32[]{:S(2)}) collective-permute-start(bf16[256,512]{1,0:T(8,128)(2,1)S(1)} %pad_maximum_fusion.1), channel_id=1, source_target_pairs={{0,2},{1,3},{2,4},{3,5},{4,6},{5,7},{6,0},{7,1},{8,10},{9,11},{10,... | collective-permute-start | bytes 786440 | tf_op jit(solution)/shard_map/ppermute | solution.py:444
  199.0 3.7 %collective-permute-done.27 = bf16[128,512]{1,0:T(8,128)(2,1)S(1)} collective-permute-done((bf16[128,512]{1,0:T(8,128)(2,1)S(1)}, bf16[128,512]{1,0:T(8,128)(2,1)S(1)}, u32[]{:S(2)}, u32[]{:S(2)}) %collective-permute-start.27) | collective-permute-done | bytes 131104 | tf_op jit(solution)/shard_map/ppermute | solution.py:440
  203.0 3.3 %collective-permute-start.26 = (bf16[256,512]{1,0:T(8,128)(2,1)S(1)}, bf16[256,512]{1,0:T(8,128)(2,1)S(1)}, u32[]{:S(2)}, u32[]{:S(2)}) collective-permute-start(bf16[256,512]{1,0:T(8,128)(2,1)S(1)} %pad_maximum_fusion.3), channel_id=1, source_target_pairs={{0,2},{1,3},{2,4},{3,5},{4,6},{5,7},{6,0},{7,1},{8,10},{9,11},{10,... | collective-permute-start | bytes 786440 | tf_op jit(solution)/shard_map/ppermute | solution.py:444
  208.5 3.7 %collective-permute-done.28 = bf16[256,512]{1,0:T(8,128)(2,1)S(1)} collective-permute-done((bf16[256,512]{1,0:T(8,128)(2,1)S(1)}, bf16[256,512]{1,0:T(8,128)(2,1)S(1)}, u32[]{:S(2)}, u32[]{:S(2)}) %collective-permute-start.28) | collective-permute-done | bytes 262176 | tf_op jit(solution)/shard_map/ppermute | solution.py:444
  (82 shorter events, 34.3 us)
Async XLA Ops:
  3.1 6.6 %collective-permute-start.2 = (bf16[272,256]{1,0:T(8,128)(2,1)S(1)}, bf16[272,256]{1,0:T(8,128)(2,1)S(1)}, u32[]{:S(2)}, u32[]{:S(2)}) collective-permute-start(bf16[272,256]{1,0:T(8,128)(2,1)S(1)} %broadcast_select_fusion), channel_id=1, source_target_pairs={{0,64},{1,65},{2,66},{3,67},{4,68},{5,69},{6,70},{7,71}} | collective-permute-start | bytes 417800 | tf_op jit(solution)/shard_map/ppermute | solution.py:393
  3.8 9.0 %collective-permute-start.1 = (bf16[256,256]{1,0:T(8,128)(2,1)}, bf16[256,256]{1,0:T(8,128)(2,1)S(1)}, u32[]{:S(2)}, u32[]{:S(2)}) collective-permute-start(bf16[256,256]{1,0:T(8,128)(2,1)} %get-tuple-element.19.refs_8_), channel_id=1, source_target_pairs={{0,56},{8,0},{16,8},{24,16},{32,24},{40,32},{48,40},{56,48},{64,12... | collective-permute-start | bytes 393224 | tf_op jit(solution)/shard_map/ppermute | solution.py:393
  9.7 6.4 %collective-permute-start = (bf16[256,256]{1,0:T(8,128)(2,1)}, bf16[256,256]{1,0:T(8,128)(2,1)S(1)}, u32[]{:S(2)}, u32[]{:S(2)}) collective-permute-start(bf16[256,256]{1,0:T(8,128)(2,1)} %get-tuple-element.19.refs_8_), channel_id=1, source_target_pairs={{0,8},{8,16},{16,24},{24,32},{32,40},{40,48},{48,56},{56,0},{64,72... | collective-permute-start | bytes 393224 | tf_op jit(solution)/shard_map/ppermute | solution.py:393
  16.1 8.1 %collective-permute-start.5 = (bf16[272,256]{1,0:T(8,128)(2,1)S(1)}, bf16[272,256]{1,0:T(8,128)(2,1)S(1)}, u32[]{:S(2)}, u32[]{:S(2)}) collective-permute-start(bf16[272,256]{1,0:T(8,128)(2,1)S(1)} %fusion.8), channel_id=1, source_target_pairs={{0,192},{64,128},{1,193},{65,129},{2,194},{66,130},{3,195},{67,131... | collective-permute-start | bytes 417800 | tf_op jit(solution)/shard_map/ppermute | solution.py:393
  17.4 6.9 %collective-permute-start.3 = (bf16[256,256]{1,0:T(8,128)(2,1)S(1)}, bf16[256,256]{1,0:T(8,128)(2,1)S(1)}, u32[]{:S(2)}, u32[]{:S(2)}) collective-permute-start(bf16[256,256]{1,0:T(8,128)(2,1)S(1)} %collective-permute-done.refs_7_), channel_id=1, source_target_pairs={{0,8},{8,16},{16,24},{24,32},{32,40},{40,48},{48,56},{56,0},{64,72... | collective-permute-start | bytes 393224 | tf_op jit(solution)/shard_map/ppermute | solution.py:393
  17.5 6.8 %collective-permute-start.4 = (bf16[256,256]{1,0:T(8,128)(2,1)S(1)}, bf16[256,256]{1,0:T(8,128)(2,1)S(1)}, u32[]{:S(2)}, u32[]{:S(2)}) collective-permute-start(bf16[256,256]{1,0:T(8,128)(2,1)S(1)} %collective-permute-done.1.refs_0_), channel_id=1, source_target_pairs={{0,56},{8,0},{16,8},{24,16},{32,24},{40,32},{48,40},{56,48},{64,12... | collective-permute-start | bytes 393224 | tf_op jit(solution)/shard_map/ppermute | solution.py:393
  26.9 6.8 %collective-permute-start.7 = (bf16[256,256]{1,0:T(8,128)(2,1)S(1)}, bf16[256,256]{1,0:T(8,128)(2,1)S(1)}, u32[]{:S(2)}, u32[]{:S(2)}) collective-permute-start(bf16[256,256]{1,0:T(8,128)(2,1)S(1)} %collective-permute-done.3.refs_6_), channel_id=1, source_target_pairs={{0,8},{8,16},{16,24},{24,32},{32,40},{40,48},{48,56},{56,0},{64,72... | collective-permute-start | bytes 393224 | tf_op jit(solution)/shard_map/ppermute | solution.py:393
  40.7 21.7 %collective-permute-start.10 = (bf16[2048,256]{1,0:T(8,128)(2,1)S(1)}, bf16[2048,256]{1,0:T(8,128)(2,1)}, u32[]{:S(2)}, u32[]{:S(2)}) collective-permute-start(bf16[2048,256]{1,0:T(8,128)(2,1)S(1)} %pack_row.1.row_ref), channel_id=1, source_target_pairs={{0,64},{8,72},{16,80},{24,88},{32,96},{40,104},{48,112},{56,120},{... | collective-permute-start | bytes 3145736 | tf_op jit(solution)/shard_map/ppermute | solution.py:393
  42.0 26.5 %collective-permute-start.11 = (bf16[2048,256]{1,0:T(8,128)(2,1)S(1)}, bf16[2048,256]{1,0:T(8,128)(2,1)}, u32[]{:S(2)}, u32[]{:S(2)}) collective-permute-start(bf16[2048,256]{1,0:T(8,128)(2,1)S(1)} %pack_row.1.row_ref), channel_id=1, source_target_pairs={{0,192},{8,200},{16,208},{24,216},{32,224},{40,232},{48,240},{56,2... | collective-permute-start | bytes 3145736 | tf_op jit(solution)/shard_map/ppermute | solution.py:393
  43.3 19.1 %collective-permute-start.14 = (bf16[272,256]{1,0:T(8,128)(2,1)S(1)}, bf16[272,256]{1,0:T(8,128)(2,1)S(1)}, u32[]{:S(2)}, u32[]{:S(2)}) collective-permute-start(bf16[272,256]{1,0:T(8,128)(2,1)S(1)} %add.49), channel_id=1, source_target_pairs={{0,8},{64,72},{128,136},{192,200},{1,9},{65,73},{129,137},{193,201... | collective-permute-start | bytes 417800 | tf_op jit(solution)/shard_map/ppermute | solution.py:393
  62.4 112.4 %collective-permute-start.19 = (bf16[4,512,512]{2,1,0:T(8,128)(2,1)}, bf16[4,512,512]{2,1,0:T(8,128)(2,1)S(1)}, u32[]{:S(2)}, u32[]{:S(2)}) collective-permute-start(bf16[4,512,512]{2,1,0:T(8,128)(2,1)} %weight_half.1), channel_id=1, source_target_pairs={{0,1},{1,0},{2,3},{3,2},{4,5},{5,4},{6,7},{7,6},{8,9},{9,8},{10,11... | collective-permute-start | bytes 6291464 | tf_op jit(solution)/shard_map/ppermute | solution.py:426
  67.8 8.0 %collective-permute-start.16 = (bf16[272,256]{1,0:T(8,128)(2,1)S(1)}, bf16[272,256]{1,0:T(8,128)(2,1)S(1)}, u32[]{:S(2)}, u32[]{:S(2)}) collective-permute-start(bf16[272,256]{1,0:T(8,128)(2,1)S(1)} %add.51), channel_id=1, source_target_pairs={{56,48},{120,112},{184,176},{248,240},{16,24},{80,88},{144,152},{2... | collective-permute-start | bytes 417800 | tf_op jit(solution)/shard_map/ppermute | solution.py:393
  69.6 16.8 %collective-permute-start.13 = (bf16[1024,256]{1,0:T(8,128)(2,1)S(1)}, bf16[1024,256]{1,0:T(8,128)(2,1)}, u32[]{:S(2)}, u32[]{:S(2)}) collective-permute-start(bf16[1024,256]{1,0:T(8,128)(2,1)S(1)} %slice.74), channel_id=1, source_target_pairs={{0,192},{8,200},{16,208},{24,216},{32,224},{40,232},{48,240},{56,2... | collective-permute-start | bytes 1572872 | tf_op jit(solution)/shard_map/ppermute | solution.py:393
  74.5 15.3 %collective-permute-start.12 = (bf16[1024,256]{1,0:T(8,128)(2,1)S(1)}, bf16[1024,256]{1,0:T(8,128)(2,1)}, u32[]{:S(2)}, u32[]{:S(2)}) collective-permute-start(bf16[1024,256]{1,0:T(8,128)(2,1)S(1)} %slice.56), channel_id=1, source_target_pairs={{64,128},{72,136},{80,144},{88,152},{96,160},{104,168},{112,176},{... | collective-permute-start | bytes 1572872 | tf_op jit(solution)/shard_map/ppermute | solution.py:393
  75.9 6.1 %collective-permute-start.17 = (bf16[272,256]{1,0:T(8,128)(2,1)S(1)}, bf16[272,256]{1,0:T(8,128)(2,1)S(1)}, u32[]{:S(2)}, u32[]{:S(2)}) collective-permute-start(bf16[272,256]{1,0:T(8,128)(2,1)S(1)} %add.52), channel_id=1, source_target_pairs={{48,40},{112,104},{176,168},{240,232},{24,32},{88,96},{152,160},{2... | collective-permute-start | bytes 417800 | tf_op jit(solution)/shard_map/ppermute | solution.py:393
  132.1 42.8 %collective-permute-start.18 = (bf16[256,512]{1,0:T(8,128)(2,1)}, bf16[256,512]{1,0:T(8,128)(2,1)S(1)}, u32[]{:S(2)}, u32[]{:S(2)}) collective-permute-start(bf16[256,512]{1,0:T(8,128)(2,1)} %rest_rows_0.1.own_ref), channel_id=1, source_target_pairs={{0,1},{1,0},{2,3},{3,2},{4,5},{5,4},{6,7},{7,6},{8,9},{9,8},{10,11... | collective-permute-start | bytes 786440 | tf_op jit(solution)/shard_map/ppermute | solution.py:437
  174.2 11.5 %collective-permute-start.24 = (bf16[256,512]{1,0:T(8,128)(2,1)}, bf16[256,512]{1,0:T(8,128)(2,1)S(1)}, u32[]{:S(2)}, u32[]{:S(2)}) collective-permute-start(bf16[256,512]{1,0:T(8,128)(2,1)} %rest_rows_1.1.own_ref), channel_id=1, source_target_pairs={{0,1},{1,0},{2,3},{3,2},{4,5},{5,4},{6,7},{7,6},{8,9},{9,8},{10,11... | collective-permute-start | bytes 786440 | tf_op jit(solution)/shard_map/ppermute | solution.py:437
  183.6 11.8 %collective-permute-start.20 = (bf16[128,512]{1,0:T(8,128)(2,1)S(1)}, bf16[128,512]{1,0:T(8,128)(2,1)S(1)}, u32[]{:S(2)}, u32[]{:S(2)}) collective-permute-start(bf16[128,512]{1,0:T(8,128)(2,1)S(1)} %get-tuple-element.35), channel_id=1, source_target_pairs={{0,2},{1,3},{2,4},{3,5},{4,6},{5,7},{6,0},{7,1},{8,10},{9,11},{10,... | collective-permute-start | bytes 393224 | tf_op jit(solution)/shard_map/ppermute | solution.py:439
  184.2 11.2 %collective-permute-start.22 = (bf16[128,512]{1,0:T(8,128)(2,1)S(1)}, bf16[128,512]{1,0:T(8,128)(2,1)S(1)}, u32[]{:S(2)}, u32[]{:S(2)}) collective-permute-start(bf16[128,512]{1,0:T(8,128)(2,1)S(1)} %get-tuple-element.36), channel_id=1, source_target_pairs={{0,6},{1,7},{2,0},{3,1},{4,2},{5,3},{6,4},{7,5},{8,14},{9,15},{10,... | collective-permute-start | bytes 393224 | tf_op jit(solution)/shard_map/ppermute | solution.py:440
  195.1 7.6 %collective-permute-start.27 = (bf16[128,512]{1,0:T(8,128)(2,1)S(1)}, bf16[128,512]{1,0:T(8,128)(2,1)S(1)}, u32[]{:S(2)}, u32[]{:S(2)}) collective-permute-start(bf16[128,512]{1,0:T(8,128)(2,1)S(1)} %get-tuple-element.42), channel_id=1, source_target_pairs={{0,6},{1,7},{2,0},{3,1},{4,2},{5,3},{6,4},{7,5},{8,14},{9,15},{10,... | collective-permute-start | bytes 393224 | tf_op jit(solution)/shard_map/ppermute | solution.py:440
  195.5 12.8 %collective-permute-start.23 = (bf16[256,512]{1,0:T(8,128)(2,1)S(1)}, bf16[256,512]{1,0:T(8,128)(2,1)S(1)}, u32[]{:S(2)}, u32[]{:S(2)}) collective-permute-start(bf16[256,512]{1,0:T(8,128)(2,1)S(1)} %pad_maximum_fusion.2), channel_id=1, source_target_pairs={{0,6},{1,7},{2,0},{3,1},{4,2},{5,3},{6,4},{7,5},{8,14},{9,15},{10,... | collective-permute-start | bytes 786440 | tf_op jit(solution)/shard_map/ppermute | solution.py:444
  196.5 11.9 %collective-permute-start.21 = (bf16[256,512]{1,0:T(8,128)(2,1)S(1)}, bf16[256,512]{1,0:T(8,128)(2,1)S(1)}, u32[]{:S(2)}, u32[]{:S(2)}) collective-permute-start(bf16[256,512]{1,0:T(8,128)(2,1)S(1)} %pad_maximum_fusion.1), channel_id=1, source_target_pairs={{0,2},{1,3},{2,4},{3,5},{4,6},{5,7},{6,0},{7,1},{8,10},{9,11},{10,... | collective-permute-start | bytes 786440 | tf_op jit(solution)/shard_map/ppermute | solution.py:444
  202.8 9.3 %collective-permute-start.28 = (bf16[256,512]{1,0:T(8,128)(2,1)S(1)}, bf16[256,512]{1,0:T(8,128)(2,1)S(1)}, u32[]{:S(2)}, u32[]{:S(2)}) collective-permute-start(bf16[256,512]{1,0:T(8,128)(2,1)S(1)} %pad_maximum_fusion.4), channel_id=1, source_target_pairs={{0,6},{1,7},{2,0},{3,1},{4,2},{5,3},{6,4},{7,5},{8,14},{9,15},{10,... | collective-permute-start | bytes 786440 | tf_op jit(solution)/shard_map/ppermute | solution.py:444
  203.0 9.2 %collective-permute-start.26 = (bf16[256,512]{1,0:T(8,128)(2,1)S(1)}, bf16[256,512]{1,0:T(8,128)(2,1)S(1)}, u32[]{:S(2)}, u32[]{:S(2)}) collective-permute-start(bf16[256,512]{1,0:T(8,128)(2,1)S(1)} %pad_maximum_fusion.3), channel_id=1, source_target_pairs={{0,2},{1,3},{2,4},{3,5},{4,6},{5,7},{6,0},{7,1},{8,10},{9,11},{10,... | collective-permute-start | bytes 786440 | tf_op jit(solution)/shard_map/ppermute | solution.py:444
  (13 other events, 77.5 us)

commit v2 on v1

v2 whole, which is shorter than its diff:
```python
import functools

import jax
import jax.numpy as jnp
from jax import lax
from jax.experimental import pallas as pl
from jax.experimental.pallas import tpu as pltpu
from jax.sharding import PartitionSpec as P

HEAD = 128
WIDE = 8
INFO = 16
KEEP = 256
LOG2E = 1.4426950408889634
FACTOR = HEAD**-0.5 * LOG2E
LIMIT = 2.0**100
NEGATIVE = -1e30
NT = (((1,), (1,)), ((), ()))
VMEM = pl.BlockSpec(memory_space=pltpu.VMEM)
SMEM = pl.BlockSpec(memory_space=pltpu.SMEM)
HBM = pl.BlockSpec(memory_space=pltpu.HBM)
ANY = pl.BlockSpec(memory_space=pl.ANY)
TILE = 512
CHUNK = 512
PARAMS = pltpu.CompilerParams(vmem_limit_bytes=60 * 2**20)


def dot(a, b):
    return jnp.dot(a, b, preferred_element_type=jnp.float32)


def dot_nt(a, b):
    return lax.dot_general(a, b, NT, preferred_element_type=jnp.float32)


def count_along(shape, dim):
    return lax.broadcasted_iota(jnp.int32, shape, dim)


def ones_where(condition):
    return jnp.where(condition, 1.0, 0.0).astype(jnp.bfloat16)


def select_kernel(used_ref, *refs):
    sources, (kept_rows_ref, rest_ref), targets, sems = refs[:3], refs[3:5], refs[5:8], refs[8]
    copies = [
        pltpu.make_async_copy(source, target, sems.at[at])
        for at, (source, target) in enumerate(zip(sources, targets))
    ]
    for copy in copies:
        copy.start()
    for copy in copies:
        copy.wait()
    kept_ref, key_ref, value_ref = targets
    length, keep = key_ref.shape[0], kept_ref.shape[1]
    hit = ones_where(count_along((length, keep), 0) == kept_ref[...])
    kept = dot_nt(jnp.ones((8, keep), jnp.bfloat16), hit)
    square = (length, length)
    before = ones_where(count_along(square, 0) < count_along(square, 1))
    rank = dot(kept.astype(jnp.bfloat16), before)
    column = count_along((8, length), 1)
    place = jnp.where(kept > 0.5, rank, column.astype(jnp.float32) + keep - rank)
    order = ones_where(count_along(square, 0).astype(jnp.float32) == place[:1])
    for at, ref in enumerate((key_ref, value_ref)):
        columns = slice(at * HEAD, (at + 1) * HEAD)
        rows = dot(order, ref[...]).astype(jnp.bfloat16)
        kept_rows_ref[:, columns] = rows[:keep]
        rest_ref[: length - keep, columns] = rows[keep:]
    in_both = jnp.where((kept > 0.5) & (column < used_ref[0]), 1.0, 0.0)[:1]
    number = jnp.sum(in_both, axis=1, keepdims=True)
    rest_ref[length - keep :] = jnp.broadcast_to(number, (INFO, 2 * HEAD)).astype(jnp.bfloat16)


def select(used, kept, keys, values):
    length = keys.shape[0]
    rows = (KEEP, length - KEEP + INFO)
    return pl.pallas_call(
        select_kernel,
        out_shape=[jax.ShapeDtypeStruct((n, 2 * HEAD), jnp.bfloat16) for n in rows],
        in_specs=[SMEM, HBM, HBM, HBM],
        out_specs=[VMEM] * 2,
        scratch_shapes=[
            *[pltpu.VMEM(x.shape, x.dtype) for x in (kept, keys, values)],
            pltpu.SemaphoreType.DMA((3,)),
        ],
        compiler_params=PARAMS,
        name="select_kept",
    )(used, kept, keys, values)


def wide(column, width):
    return jnp.concatenate([column] * (width // HEAD), axis=1)


def widened(values):
    return jnp.concatenate([values, jnp.ones_like(values)], axis=1)


def scores(query, keys):
    return dot_nt(query, keys) * FACTOR


def local(query, keys, values, acc_ref, peak_ref):
    length = query.shape[0]
    causal = count_along((length, length), 1) <= count_along((length, length), 0)
    raw = jnp.where(causal, scores(query, keys), NEGATIVE)
    peak = jnp.broadcast_to(jnp.max(raw, axis=1, keepdims=True), (length, HEAD))
    peak_ref[...] = peak
    weights = jnp.exp2(raw - wide(peak, length)).astype(jnp.bfloat16)
    acc_ref[...] = dot(weights, widened(values))


def biased(raw, bias):
    if bias is None:
        return raw
    return (raw.reshape(-1, *bias.shape) + bias).reshape(raw.shape)


def fixed(query, acc_ref, peak_ref, keys, values, bias):
    raw = biased(scores(query, keys), bias)
    weights = jnp.exp2(raw - wide(peak_ref[...], keys.shape[0]))
    acc_ref[...] += dot(weights.astype(jnp.bfloat16), values)


def moving(query, acc_ref, peak_ref, keys, values, bias):
    raw = biased(scores(query, keys), bias)
    old = peak_ref[...]
    peak = jnp.maximum(old, jnp.max(raw, axis=1, keepdims=True))
    weights = jnp.exp2(raw - wide(peak, keys.shape[0])).astype(jnp.bfloat16)
    peak_ref[...] = peak
    acc_ref[...] = acc_ref[...] * wide(jnp.exp2(old - peak), 2 * HEAD) + dot(weights, values)


def absorb(acc_ref, chunks, view, start, masked, tiles, read):
    for c in range(chunks):
        start(c)

    @pl.loop(0, masked)
    def _(tile):
        keys = read(tile, True, True)
        for c in range(chunks):
            fixed(*view(c), *keys)

    @pl.loop(masked, tiles)
    def _(tile):
        keys = read(tile, False, True)
        for c in range(chunks):
            fixed(*view(c), *keys)

    largest = jnp.max(acc_ref[..., HEAD:])

    @pl.when(jnp.logical_not(largest < LIMIT))
    def _():
        @pl.loop(0, chunks)
        def _(c):
            start(c)

            @pl.loop(0, tiles)
            def _(tile):
                moving(*view(c), *read(tile, True, False))


def tile_of(ref, at):
    rows = pl.ds(pl.multiple_of(at * TILE, TILE), TILE)
    return ref[rows, :HEAD], widened(ref[rows, HEAD:])


def bias_where(allowed):
    return jnp.where(allowed, 0.0, NEGATIVE)


def own_row_kernel(
    place_ref, q_ref, k_ref, v_ref, row_a, row_b, acc_ref, peak_ref, row_ref, bias_ref, sems
):
    keys = place_ref[0] % WIDE * KEEP
    masked = jnp.where(keys % TILE > 0, 1, 0)
    tiles = (keys + TILE - 1) // TILE
    half = row_a.shape[0]
    copies = [
        pltpu.make_async_copy(ref, row_ref.at[pl.ds(at * half, half)], sems.at[at])
        for at, ref in enumerate((row_a, row_b))
    ]

    @pl.when(tiles > 0)
    def _():
        for copy in copies:
            copy.start()

    def view(c):
        columns = pl.ds(pl.multiple_of(c * HEAD, HEAD), HEAD)
        return q_ref[:, columns], acc_ref.at[c], peak_ref.at[c]

    def start(c):
        query, acc, peak = view(c)
        local(query, k_ref[...], v_ref[...], acc, peak)

    def read(tile, with_bias, first_time):
        if first_time:

            @pl.when(tile == 0)
            def _():
                for copy in copies:
                    copy.wait()

        at = jnp.where(tile < masked, tiles - 1, tile - masked)
        if not with_bias:
            return *tile_of(row_ref, at), None
        bias_ref[...] = bias_where(count_along(bias_ref.shape, 1) + at * TILE < keys)
        return *tile_of(row_ref, at), bias_ref[...]

    absorb(acc_ref, acc_ref.shape[0], view, start, masked, tiles, read)


def rest_kernel(
    place_ref, q_ref, rest_ref, row_ref, below_a, below_b, above_a, above_b, below2_ref,
    above2_ref, weight_ref, acc_in, peak_in, keep_ref, send_ref, bank_ref, w_ref, bias_ref,
    stack_ref, acc_ref, peak_ref, att_ref, sems,
):
    mine, used = place_ref[0], place_ref[1]
    y, tokens, heads = mine // WIDE, q_ref.shape[0], acc_in.shape[0]
    span = WIDE * KEEP
    part, row_tiles = span // 2, span // TILE
    copies = []

    def copy(source, at, rows, condition, tile):
        target = bank_ref.at[pl.ds(at, rows)]
        one = pltpu.make_async_copy(source, target, sems.at[len(copies)])
        copies.append((one, condition, tile))

    for row, ref in enumerate((row_ref, below_a, below2_ref, above_a)):
        copy(ref.at[pl.ds(0, KEEP)], 0, KEEP, (mine > 0) & (y == row), 0)
    at, tile = TILE, 1
    for condition, first, second in (
        (y > 0, below_a, below_b),
        (y > 1, below2_ref, above2_ref),
        (y == 3, above_a, above_b),
    ):
        copy(first, at, part, condition, tile)
        copy(second, at + part, part, condition, tile)
        at, tile = at + span, tile + row_tiles
    for one, condition, _ in copies:
        pl.when(condition)(one.start)
    weight_copy = pltpu.make_async_copy(weight_ref, w_ref, sems.at[len(copies)])
    weight_copy.start()
    bank_ref[KEEP:TILE] = rest_ref[: TILE - KEEP]
    number = wide(rest_ref[TILE - KEEP : TILE - KEEP + 1, :HEAD].astype(jnp.int32), TILE)
    at = count_along((1, TILE), 1)
    limit = jnp.where(at < KEEP, number, KEEP + used - number)
    bias_ref[0] = jnp.broadcast_to(bias_where(at < limit), bias_ref.shape[1:])
    bias_ref[1] = jnp.zeros(bias_ref.shape[1:], jnp.float32)
    for h in range(heads):
        stack_ref[h * tokens : (h + 1) * tokens] = q_ref[:, h * HEAD : (h + 1) * HEAD]
    together = CHUNK // tokens

    def view(c):
        rows = pl.ds(pl.multiple_of(c * CHUNK, CHUNK), CHUNK)
        return stack_ref[rows], acc_ref.at[rows], peak_ref.at[rows]

    def start(c):
        for h in range(together):
            rows = pl.ds(pl.multiple_of((c * together + h) * tokens, tokens), tokens)
            acc_ref[rows] = acc_in[c * together + h]
            peak_ref[rows] = peak_in[c * together + h]

    def read(tile, masked, first_time):
        if first_time:
            for one, condition, when in copies:
                if masked == (when == 0):
                    pl.when(condition & (tile == when))(one.wait)
        bias = bias_ref[jnp.minimum(tile, 1)] if masked else None
        return *tile_of(bank_ref, tile), bias

    masked = jnp.where(mine > 0, 1, 0)
    chunks = heads // together
    absorb(acc_ref, chunks, view, start, masked, masked + row_tiles * y, read)
    for h in range(heads):
        rows = slice(h * tokens, (h + 1) * tokens)
        att_ref[:, h * HEAD : (h + 1) * HEAD] = (
            acc_ref[rows, :HEAD] / acc_ref[rows, HEAD:]
        ).astype(jnp.bfloat16)
    weight_copy.wait()
    chips, _, columns = keep_ref.shape
    chip, core = place_ref[2], place_ref[3]

    @pl.loop(0, chips)
    def _(step):
        at = lax.rem(chip + step, chips) * 2
        for ref, side in ((keep_ref, core), (send_ref, 1 - core)):
            start = pl.multiple_of((at + side) * columns, columns)
            ref[step] = dot(att_ref[...], w_ref[:, pl.ds(start, columns)]).astype(jnp.bfloat16)


def pack_row_kernel(place_ref, *refs):
    z = place_ref[0] % WIDE
    at, middle = KEEP, WIDE * KEEP // 2
    for ref in refs[:-2]:
        rows = ref.shape[0]
        start = pl.multiple_of(lax.rem(z * KEEP + at, WIDE * KEEP), KEEP // 2)
        at += rows
        for out_ref, first in zip(refs[-2:], (0, middle)):

            @pl.when((start >= first) & (start < first + middle))
            def _():
                out_ref[pl.ds(pl.multiple_of(start - first, KEEP // 2), rows)] = ref[...]


def pack_row(place, pieces):
    return pl.pallas_call(
        pack_row_kernel,
        out_shape=[jax.ShapeDtypeStruct((WIDE * KEEP // 2, 2 * HEAD), jnp.bfloat16)] * 2,
        in_specs=[SMEM] + [VMEM] * len(pieces),
        out_specs=[VMEM] * 2,
        compiler_params=pltpu.CompilerParams(vmem_limit_bytes=8 * 2**20),
        name="pack_row",
    )(place, *pieces)


def cost(rows, keys):
    return pl.CostEstimate(
        flops=rows * keys * HEAD * 8, bytes_accessed=8 * 2**20, transcendentals=rows * keys
    )


def state_of(length, heads):
    return [
        jax.ShapeDtypeStruct((heads, length, 2 * HEAD), jnp.float32),
        jax.ShapeDtypeStruct((heads, length, HEAD), jnp.float32),
    ]


def own_row(place, queries, keys, values, row_a, row_b):
    length, width = queries.shape
    whole = lambda x: pl.BlockSpec(x.shape, lambda i: (0,) * x.ndim)
    state = state_of(length, width // HEAD)
    return pl.pallas_call(
        own_row_kernel,
        grid=(1,),
        out_shape=state,
        in_specs=[SMEM, *[whole(x) for x in (queries, keys, values)], ANY, ANY],
        out_specs=[whole(x) for x in state],
        scratch_shapes=[
            pltpu.VMEM((WIDE * KEEP, 2 * HEAD), jnp.bfloat16),
            pltpu.VMEM((8, TILE), jnp.float32),
            pltpu.SemaphoreType.DMA((2,)),
        ],
        compiler_params=PARAMS,
        cost_estimate=cost(length * width // HEAD, length + WIDE * KEEP),
        name="own_row",
    )(place, queries, keys, values, row_a, row_b)


def rest_rows(place, queries, rest, banks, weight, state, part, parts, chips):
    length, width = queries.shape
    rows, heads = length // parts, width // HEAD
    tiles = 13
    slab = lambda columns: pl.BlockSpec((heads, rows, columns), lambda i: (0, part, 0))
    out = jax.ShapeDtypeStruct((chips, rows, weight.shape[1] // chips // 2), jnp.bfloat16)
    return pl.pallas_call(
        rest_kernel,
        grid=(1,),
        out_shape=[out, out],
        in_specs=[
            SMEM,
            pl.BlockSpec((rows, width), lambda i: (part, 0)),
            pl.BlockSpec(rest.shape, lambda i: (0, 0)),
            *[ANY] * (len(banks) + 1),
            slab(2 * HEAD),
            slab(HEAD),
        ],
        out_specs=[pl.BlockSpec(out.shape, lambda i: (0, 0, 0))] * 2,
        scratch_shapes=[
            pltpu.VMEM((tiles * TILE, 2 * HEAD), jnp.bfloat16),
            pltpu.VMEM(weight.shape, weight.dtype),
            pltpu.VMEM((2, 8, TILE), jnp.float32),
            pltpu.VMEM((heads * rows, HEAD), jnp.bfloat16),
            pltpu.VMEM((heads * rows, 2 * HEAD), jnp.float32),
            pltpu.VMEM((heads * rows, HEAD), jnp.float32),
            pltpu.VMEM((rows, width), jnp.bfloat16),
            pltpu.SemaphoreType.DMA((11,)),
        ],
        compiler_params=PARAMS,
        cost_estimate=cost(rows * heads, tiles * TILE),
        name=f"rest_rows_{part}",
    )(place, queries, rest, *banks, weight, *state)


def added(*terms):
    return sum(term.astype(jnp.float32) for term in terms).astype(jnp.bfloat16)


def on_device(queries, key_rows, value_rows, kept_positions, anchor_length, output_weight):
    mine, head = lax.axis_index("ctx"), lax.axis_index("head")
    length, devices, blocks = queries.shape[0], lax.axis_size("head"), lax.axis_size("ctx")
    chips, chip, core = devices // 2, head // 2, head % 2
    tall = blocks // WIDE
    swap = [(i, i ^ 1) for i in range(devices)]
    up = [(i, (i + 2) % devices) for i in range(devices)]
    down = [(i, (i - 2) % devices) for i in range(devices)]
    along = lambda step: [
        (r * WIDE + c, r * WIDE + (c + step) % WIDE) for r in range(tall) for c in range(WIDE)
    ]
    across = lambda hops: [(a * WIDE + c, b * WIDE + c) for a, b in hops for c in range(WIDE)]
    permute = lambda x, pairs: lax.ppermute(x, "ctx", pairs)

    spots = jnp.stack([chip, core]).astype(jnp.int32)
    place = jnp.concatenate([mine.astype(jnp.int32)[None], anchor_length, spots])
    kept, rest = select(anchor_length, kept_positions, key_rows, value_rows)

    plus, minus = along(1), along(-1)
    half = KEEP // 2
    left, right = [kept], [kept]
    rest = jnp.where(mine == 0, rest, jnp.zeros_like(rest))
    upward = [[(0, WIDE)], [(0, 3 * WIDE), (WIDE, 2 * WIDE)]]
    for step in range(WIDE // 2 - 1):
        left.append(permute(left[-1], plus))
        right.append(permute(right[-1], minus))
        if step < len(upward):
            rest = rest + permute(rest, upward[step])
            left[-1], right[-1], rest = lax.optimization_barrier((left[-1], right[-1], rest))
    opposite = [permute(left[-1][:half], plus), permute(right[-1][half:], minus)]
    ends = pack_row(place, right[1:] + opposite + left[:0:-1] + [kept])

    below_a = permute(ends[0], across([(0, 1), (1, 2), (2, 3)]))
    above_b = permute(ends[1], across([(0, 3), (1, 0)]))
    below_b = permute(ends[1], across([(0, 1), (1, 2), (2, 3)]))
    above_a = permute(ends[0], across([(0, 3)]))

    rest, ends = lax.optimization_barrier((rest, ends))
    spread = lambda hops: [(r * WIDE + a, r * WIDE + b) for a, b in hops for r in range(tall)]
    rest = rest + permute(rest, spread([(0, 4)]))
    rest, below_a, above_b = lax.optimization_barrier((rest, below_a, above_b))
    below2 = permute(below_a, across([(1, 2), (2, 3)]))
    above2 = permute(above_b, across([(0, 3), (3, 2)]))
    rest = rest + permute(rest, spread([(0, 2), (4, 6)]))
    rest = rest + permute(rest, spread([(0, 1), (2, 3), (4, 5), (6, 7)]))

    parts = 2
    state = own_row(place, queries, key_rows, value_rows, *ends)
    banks = (ends[0], below_a, below_b, above_a, above_b, below2, above2)

    outs = []
    half = length // parts // 2
    for part in range(parts):
        own, send = rest_rows(
            place, queries, rest, banks, output_weight, state, part, parts, chips
        )
        other = lax.ppermute(send, "head", swap)
        across_x = added(own[2], other[2])
        from_below = lax.ppermute(across_x[:half], "head", up)
        from_above = lax.ppermute(across_x[half:], "head", down)
        upward = jnp.concatenate(
            [added(own[1, :half], other[1, :half], from_below), added(own[1, half:], other[1, half:])]
        )
        downward = jnp.concatenate(
            [added(own[3, :half], other[3, :half]), added(own[3, half:], other[3, half:], from_above)]
        )
        upward, downward = lax.ppermute(upward, "head", up), lax.ppermute(downward, "head", down)
        outs.append(added(own[0], other[0], upward, downward))
    return jnp.concatenate(outs)


def solution(mesh):
    placed = (
        P("ctx", "head"),
        P("ctx", "head"),
        P("ctx", "head"),
        P("head", "ctx"),
        P("head"),
        P("head", None),
    )
    return jax.shard_map(
        on_device, mesh=mesh, in_specs=placed, out_specs=P("ctx", "head"), check_vma=False
    )
```

time: 215 us -> 175 us (0.81)
  Pallas kernels: 108 us -> 81.4 us
  waiting for transfers between devices: 51.9 us -> 37.8 us
  starting transfers between devices: 40.9 us -> 49.2 us
  local copies, waits for them, and re-layouts: 8.21 us -> 0.99 us
    pallas_call x7 -> x4, Pallas kernels: 106 us -> 78.9 us  [the longest x2 73.3 us: rest_rows(): pl.pallas_call(rest_kernel, grid=(1,), out_shape=[out, out], in_specs=[SM...]
    ppermute x18 -> x19, waiting for transfers between devices: 42.4 us -> 26.2 us  [on_device(): permute = lambda x, pairs: lax.ppermute(x, 'ctx', pairs)]
    ppermute x18 -> x19, starting transfers between devices: 29.2 us -> 39.3 us  [on_device(): permute = lambda x, pairs: lax.ppermute(x, 'ctx', pairs)]
    ppermute x2, waiting for transfers between devices: 0.01 us -> 3.16 us  [on_device(): lax.ppermute(upward, 'head', up)]
    unnamed x16 -> x18, local copies, waits for them, and re-layouts: 3.7 us -> 0.94 us
    squeeze x2 -> x0, local copies, waits for them, and re-layouts: 2.34 us -> none  [on_device(): from_below = lax.ppermute(terms[2, :half], 'head', up)]
    convert_element_type x4 -> x8, other arithmetic: 0.34 us -> 2.66 us  [added(): sum((term.astype(jnp.float32) for term in terms)).astype(jnp.bfloat16)]
    ppermute x7 -> x6, starting transfers between devices: 4.88 us -> 5.05 us  [the longest x2 2.27 us: on_device(): from_below = lax.ppermute(across_x[:half], 'head', up)]
  transfers between devices with their start and end apart: 29 -> 29, of which waited for: 14 -> 17; matrix products, arithmetic and copies ran while one was open for 3% -> 2% of each run, Pallas kernels for 49% -> 24%
where the time goes in v2:
time: 175 us
  Pallas kernels  81.4 us (47%)
  starting transfers between devices  49.2 us (28%)
  waiting for transfers between devices  37.8 us (22%)
  other arithmetic  4.47 us (3%)
    pallas_call x2, Pallas kernels, rest_rows(): pl.pallas_call(rest_kernel, grid=(1,), out_shape=[out, out], in_specs=[SM...  73.3 us
    ppermute x19, starting transfers between devices, on_device(): permute = lambda x, pairs: lax.ppermute(x, 'ctx', pairs)  39.3 us
    ppermute x19, waiting for transfers between devices, on_device(): permute = lambda x, pairs: lax.ppermute(x, 'ctx', pairs)  26.2 us
    ppermute x2, waiting for transfers between devices, on_device(): lax.ppermute(downward, 'head', down)  6.59 us
    pallas_call x1, Pallas kernels, own_row(): pl.pallas_call(own_row_kernel, grid=(1,), out_shape=state, in_specs=[SMEM...  4.96 us
    ppermute x2, starting transfers between devices, on_device(): lax.ppermute(upward, 'head', up)  4.45 us
  transfers between devices with their start and end apart: 29, of which 17 were waited for; matrix products, arithmetic and copies ran while one was open for 2% of the time, Pallas kernels for 24%

profile of v2, /device:TPU:30, one launch (start us, length us, event | category | flops | bytes accessed | tf_op | source)
XLA Modules:
  0.0 174.9 jit_solution(3141418437911203273)
XLA Ops:
  0.7 2.4 %select_kept.1 = (bf16[256,256]{1,0:T(8,128)(2,1)}, bf16[272,256]{1,0:T(8,128)(2,1)}) custom-call(s32[1]{0:T(128)S(6)} %copy.7.used_ref, s32[1,256]{1,0:T(1,128)} %refs_0_.1, bf16[512,128]{1,0:T(8,128)(2,1)} %k_ref.1, bf16[512,128]{1,0:T(8,128)(2,1)} %v_ref.1), custom_call_target="tpu_custom_call" | custom-call | tf_op jit(solution)/shard_map/select_kept/pallas_call | solution.py:77
  3.8 2.0 %collective-permute-start = (bf16[256,256]{1,0:T(8,128)(2,1)}, bf16[256,256]{1,0:T(8,128)(2,1)S(1)}, u32[]{:S(2)}, u32[]{:S(2)}) collective-permute-start(bf16[256,256]{1,0:T(8,128)(2,1)} %get-tuple-element.27.refs_8_), channel_id=1, source_target_pairs={{0,8},{8,16},{16,24},{24,32},{32,40},{40,48},{48,56},{56,0},{64,72... | collective-permute-start | bytes 393224 | tf_op jit(solution)/shard_map/ppermute | solution.py:403
  5.8 4.0 %collective-permute-start.1 = (bf16[256,256]{1,0:T(8,128)(2,1)}, bf16[256,256]{1,0:T(8,128)(2,1)S(1)}, u32[]{:S(2)}, u32[]{:S(2)}) collective-permute-start(bf16[256,256]{1,0:T(8,128)(2,1)} %get-tuple-element.27.refs_8_), channel_id=1, source_target_pairs={{0,56},{8,0},{16,8},{24,16},{32,24},{40,32},{48,40},{56,48},{64,12... | collective-permute-start | bytes 393224 | tf_op jit(solution)/shard_map/ppermute | solution.py:403
  9.9 3.6 %collective-permute-done.refs_7_ = bf16[256,256]{1,0:T(8,128)(2,1)S(1)} collective-permute-done((bf16[256,256]{1,0:T(8,128)(2,1)}, bf16[256,256]{1,0:T(8,128)(2,1)S(1)}, u32[]{:S(2)}, u32[]{:S(2)}) %collective-permute-start) | collective-permute-done | bytes 131104 | tf_op jit(solution)/shard_map/ppermute | solution.py:403
  14.8 3.2 %collective-permute-start.4 = (bf16[256,256]{1,0:T(8,128)(2,1)S(1)}, bf16[256,256]{1,0:T(8,128)(2,1)S(1)}, u32[]{:S(2)}, u32[]{:S(2)}) collective-permute-start(bf16[256,256]{1,0:T(8,128)(2,1)S(1)} %collective-permute-done.1.refs_0_), channel_id=1, source_target_pairs={{0,56},{8,0},{16,8},{24,16},{32,24},{40,32},{48,40},{56,48},{64,12... | collective-permute-start | bytes 393224 | tf_op jit(solution)/shard_map/ppermute | solution.py:403
  18.1 3.5 %collective-permute-done.5 = bf16[272,256]{1,0:T(8,128)(2,1)S(1)} collective-permute-done((bf16[272,256]{1,0:T(8,128)(2,1)S(1)}, bf16[272,256]{1,0:T(8,128)(2,1)S(1)}, u32[]{:S(2)}, u32[]{:S(2)}) %collective-permute-start.5) | collective-permute-done | bytes 139296 | tf_op jit(solution)/shard_map/ppermute | solution.py:403
  22.9 2.1 %collective-permute-start.6 = (bf16[256,256]{1,0:T(8,128)(2,1)S(1)}, bf16[256,256]{1,0:T(8,128)(2,1)S(1)}, u32[]{:S(2)}, u32[]{:S(2)}) collective-permute-start(bf16[256,256]{1,0:T(8,128)(2,1)S(1)} %collective-permute-done.4.refs_1_), channel_id=1, source_target_pairs={{0,56},{8,0},{16,8},{24,16},{32,24},{40,32},{48,40},{56,48},{64,12... | collective-permute-start | bytes 393224 | tf_op jit(solution)/shard_map/ppermute | solution.py:403
  25.0 2.9 %collective-permute-done.7.refs_5_ = bf16[256,256]{1,0:T(8,128)(2,1)S(1)} collective-permute-done((bf16[256,256]{1,0:T(8,128)(2,1)S(1)}, bf16[256,256]{1,0:T(8,128)(2,1)S(1)}, u32[]{:S(2)}, u32[]{:S(2)}) %collective-permute-start.7) | collective-permute-done | bytes 131104 | tf_op jit(solution)/shard_map/ppermute | solution.py:403
  28.1 3.2 %collective-permute-start.9 = (bf16[128,256]{1,0:T(8,128)(2,1)S(1)}, bf16[128,256]{1,0:T(8,128)(2,1)S(1)}, u32[]{:S(2)}, u32[]{:S(2)}) collective-permute-start(bf16[128,256]{1,0:T(8,128)(2,1)S(1)} %slice.137), channel_id=1, source_target_pairs={{0,56},{8,0},{16,8},{24,16},{32,24},{40,32},{48,40},{56,48},{64,12... | collective-permute-start | bytes 196616 | tf_op jit(solution)/shard_map/ppermute | solution.py:403
  31.3 2.1 %collective-permute-done.8.refs_3_ = bf16[128,256]{1,0:T(8,128)(2,1)S(1)} collective-permute-done((bf16[128,256]{1,0:T(8,128)(2,1)S(1)}, bf16[128,256]{1,0:T(8,128)(2,1)S(1)}, u32[]{:S(2)}, u32[]{:S(2)}) %collective-permute-start.8) | collective-permute-done | bytes 65568 | tf_op jit(solution)/shard_map/ppermute | solution.py:403
  37.7 4.8 %collective-permute-start.10 = (bf16[272,256]{1,0:T(8,128)(2,1)S(1)}, bf16[272,256]{1,0:T(8,128)(2,1)S(1)}, u32[]{:S(2)}, u32[]{:S(2)}) collective-permute-start(bf16[272,256]{1,0:T(8,128)(2,1)S(1)} %add.106), channel_id=1, source_target_pairs={{0,32},{64,96},{128,160},{192,224},{1,33},{65,97},{129,161},{193,2... | collective-permute-start | bytes 417800 | tf_op jit(solution)/shard_map/ppermute | solution.py:403
  42.5 2.6 %collective-permute-done.10 = bf16[272,256]{1,0:T(8,128)(2,1)S(1)} collective-permute-done((bf16[272,256]{1,0:T(8,128)(2,1)S(1)}, bf16[272,256]{1,0:T(8,128)(2,1)S(1)}, u32[]{:S(2)}, u32[]{:S(2)}) %collective-permute-start.10) | collective-permute-done | bytes 139296 | tf_op jit(solution)/shard_map/ppermute | solution.py:403
  46.9 2.6 %collective-permute-done.12.above_b = bf16[1024,256]{1,0:T(8,128)(2,1)S(1)} collective-permute-done((bf16[1024,256]{1,0:T(8,128)(2,1)S(1)}, bf16[1024,256]{1,0:T(8,128)(2,1)S(1)}, u32[]{:S(2)}, u32[]{:S(2)}) %collective-permute-start.12) | collective-permute-done | bytes 524320 | tf_op jit(solution)/shard_map/ppermute | solution.py:403
  49.5 3.4 %collective-permute-start.13 = (bf16[272,256]{1,0:T(8,128)(2,1)S(1)}, bf16[272,256]{1,0:T(8,128)(2,1)S(1)}, u32[]{:S(2)}, u32[]{:S(2)}) collective-permute-start(bf16[272,256]{1,0:T(8,128)(2,1)S(1)} %add.107), channel_id=1, source_target_pairs={{0,16},{64,80},{128,144},{192,208},{32,48},{96,112},{160,176},{224... | collective-permute-start | bytes 417800 | tf_op jit(solution)/shard_map/ppermute | solution.py:403
  56.9 5.4 %collective-permute-start.18 = (bf16[1024,256]{1,0:T(8,128)(2,1)S(1)}, bf16[1024,256]{1,0:T(8,128)(2,1)}, u32[]{:S(2)}, u32[]{:S(2)}) collective-permute-start(bf16[1024,256]{1,0:T(8,128)(2,1)S(1)} %collective-permute-done.12.above_b), channel_id=1, source_target_pairs={{0,192},{8,200},{16,208},{24,216},{32,224},{40,232},{48,240},{56,2... | collective-permute-start | bytes 1572872 | tf_op jit(solution)/shard_map/ppermute | solution.py:403
  63.7 5.0 %own_row.1 = (f32[4,512,256]{2,1,0:T(8,128)}, f32[4,512,128]{2,1,0:T(8,128)}) custom-call(s32[4]{0:T(128)} %copy-done.1, bf16[512,512]{1,0:T(8,128)(2,1)} %q_ref.5, bf16[512,128]{1,0:T(8,128)(2,1)} %k_ref.1, bf16[512,128]{1,0:T(8,128)(2,1)} %v_ref.1, bf16[1024,256]{1,0:T(8,128)(2,1)} %copy-done.2, bf16[1024,256]{1,0:T(8,128)(2,1)} %copy-done.3), custom_call_target="tpu_custom_call" | custom-call | flops 5368709120 | bytes 8388608 | tf_op jit(solution)/shard_map/own_row/pallas_call | solution.py:335
  70.8 3.1 %collective-permute-done.17.below2_ref = bf16[1024,256]{1,0:T(8,128)(2,1)} collective-permute-done((bf16[1024,256]{1,0:T(8,128)(2,1)S(1)}, bf16[1024,256]{1,0:T(8,128)(2,1)}, u32[]{:S(2)}, u32[]{:S(2)}) %collective-permute-start.17) | collective-permute-done | bytes 524320 | tf_op jit(solution)/shard_map/ppermute | solution.py:403
  73.9 2.5 %collective-permute-done.18.above2_ref = bf16[1024,256]{1,0:T(8,128)(2,1)} collective-permute-done((bf16[1024,256]{1,0:T(8,128)(2,1)S(1)}, bf16[1024,256]{1,0:T(8,128)(2,1)}, u32[]{:S(2)}, u32[]{:S(2)}) %collective-permute-start.18) | collective-permute-done | bytes 524320 | tf_op jit(solution)/shard_map/ppermute | solution.py:403
  76.4 36.6 %rest_rows_0.1 = (bf16[4,256,512]{2,1,0:T(8,128)(2,1)}, bf16[4,256,512]{2,1,0:T(8,128)(2,1)}) custom-call(s32[4]{0:T(128)} %copy-done.1, bf16[512,512]{1,0:T(8,128)(2,1)} %q_ref.5, bf16[272,256]{1,0:T(8,128)(2,1)} %add.109.rest_ref, bf16[1024,256]{1,0:T(8,128)(2,1)} %copy-done.2, bf16[1024,256]{1,0:T(8,128)(2,1)} %copy-done.6, bf16[1024,256]{1,0:T(8,128)(2,1)} %copy-done.8, ...), custom_call_target="tpu_custom_call" | custom-call | flops 6979321856 | bytes 8388608 | tf_op jit(solution)/shard_map/rest_rows_0/pallas_call | solution.py:358
  113.1 36.7 %rest_rows_1.1 = (bf16[4,256,512]{2,1,0:T(8,128)(2,1)}, bf16[4,256,512]{2,1,0:T(8,128)(2,1)}) custom-call(s32[4]{0:T(128)} %copy-done.1, bf16[512,512]{1,0:T(8,128)(2,1)} %q_ref.5, bf16[272,256]{1,0:T(8,128)(2,1)} %add.109.rest_ref, bf16[1024,256]{1,0:T(8,128)(2,1)} %copy-done.2, bf16[1024,256]{1,0:T(8,128)(2,1)} %copy-done.6, bf16[1024,256]{1,0:T(8,128)(2,1)} %copy-done.8, ...), custom_call_target="tpu_custom_call" | custom-call | flops 6979321856 | bytes 8388608 | tf_op jit(solution)/shard_map/rest_rows_1/pallas_call | solution.py:358
  157.5 2.6 %collective-permute-start.21 = (bf16[256,512]{1,0:T(8,128)(2,1)S(1)}, bf16[256,512]{1,0:T(8,128)(2,1)S(1)}, u32[]{:S(2)}, u32[]{:S(2)}) collective-permute-start(bf16[256,512]{1,0:T(8,128)(2,1)S(1)} %pad_maximum_fusion.1), channel_id=1, source_target_pairs={{0,2},{1,3},{2,4},{3,5},{4,6},{5,7},{6,0},{7,1},{8,10},{9,11},{10,... | collective-permute-start | bytes 786440 | tf_op jit(solution)/shard_map/ppermute | solution.py:457
  164.0 2.8 %collective-permute-done.21 = bf16[256,512]{1,0:T(8,128)(2,1)S(1)} collective-permute-done((bf16[256,512]{1,0:T(8,128)(2,1)S(1)}, bf16[256,512]{1,0:T(8,128)(2,1)S(1)}, u32[]{:S(2)}, u32[]{:S(2)}) %collective-permute-start.21) | collective-permute-done | bytes 262176 | tf_op jit(solution)/shard_map/ppermute | solution.py:457
  166.9 3.8 %collective-permute-done.23 = bf16[256,512]{1,0:T(8,128)(2,1)S(1)} collective-permute-done((bf16[256,512]{1,0:T(8,128)(2,1)S(1)}, bf16[256,512]{1,0:T(8,128)(2,1)S(1)}, u32[]{:S(2)}, u32[]{:S(2)}) %collective-permute-start.23) | collective-permute-done | bytes 262176 | tf_op jit(solution)/shard_map/ppermute | solution.py:457
  171.1 2.8 %collective-permute-done.28 = bf16[256,512]{1,0:T(8,128)(2,1)S(1)} collective-permute-done((bf16[256,512]{1,0:T(8,128)(2,1)S(1)}, bf16[256,512]{1,0:T(8,128)(2,1)S(1)}, u32[]{:S(2)}, u32[]{:S(2)}) %collective-permute-start.28) | collective-permute-done | bytes 262176 | tf_op jit(solution)/shard_map/ppermute | solution.py:457
  (81 shorter events, 30.0 us)
Async XLA Ops:
  3.1 6.7 %collective-permute-start.2 = (bf16[272,256]{1,0:T(8,128)(2,1)S(1)}, bf16[272,256]{1,0:T(8,128)(2,1)S(1)}, u32[]{:S(2)}, u32[]{:S(2)}) collective-permute-start(bf16[272,256]{1,0:T(8,128)(2,1)S(1)} %broadcast_select_fusion), channel_id=1, source_target_pairs={{0,64},{1,65},{2,66},{3,67},{4,68},{5,69},{6,70},{7,71}} | collective-permute-start | bytes 417800 | tf_op jit(solution)/shard_map/ppermute | solution.py:403
  3.8 9.6 %collective-permute-start = (bf16[256,256]{1,0:T(8,128)(2,1)}, bf16[256,256]{1,0:T(8,128)(2,1)S(1)}, u32[]{:S(2)}, u32[]{:S(2)}) collective-permute-start(bf16[256,256]{1,0:T(8,128)(2,1)} %get-tuple-element.27.refs_8_), channel_id=1, source_target_pairs={{0,8},{8,16},{16,24},{24,32},{32,40},{40,48},{48,56},{56,0},{64,72... | collective-permute-start | bytes 393224 | tf_op jit(solution)/shard_map/ppermute | solution.py:403
  5.8 7.6 %collective-permute-start.1 = (bf16[256,256]{1,0:T(8,128)(2,1)}, bf16[256,256]{1,0:T(8,128)(2,1)S(1)}, u32[]{:S(2)}, u32[]{:S(2)}) collective-permute-start(bf16[256,256]{1,0:T(8,128)(2,1)} %get-tuple-element.27.refs_8_), channel_id=1, source_target_pairs={{0,56},{8,0},{16,8},{24,16},{32,24},{40,32},{48,40},{56,48},{64,12... | collective-permute-start | bytes 393224 | tf_op jit(solution)/shard_map/ppermute | solution.py:403
  13.5 8.1 %collective-permute-start.5 = (bf16[272,256]{1,0:T(8,128)(2,1)S(1)}, bf16[272,256]{1,0:T(8,128)(2,1)S(1)}, u32[]{:S(2)}, u32[]{:S(2)}) collective-permute-start(bf16[272,256]{1,0:T(8,128)(2,1)S(1)} %fusion.12), channel_id=1, source_target_pairs={{0,192},{64,128},{1,193},{65,129},{2,194},{66,130},{3,195},{67,131... | collective-permute-start | bytes 417800 | tf_op jit(solution)/shard_map/ppermute | solution.py:403
  14.8 6.9 %collective-permute-start.3 = (bf16[256,256]{1,0:T(8,128)(2,1)S(1)}, bf16[256,256]{1,0:T(8,128)(2,1)S(1)}, u32[]{:S(2)}, u32[]{:S(2)}) collective-permute-start(bf16[256,256]{1,0:T(8,128)(2,1)S(1)} %collective-permute-done.refs_7_), channel_id=1, source_target_pairs={{0,8},{8,16},{16,24},{24,32},{32,40},{40,48},{48,56},{56,0},{64,72... | collective-permute-start | bytes 393224 | tf_op jit(solution)/shard_map/ppermute | solution.py:403
  14.8 6.8 %collective-permute-start.4 = (bf16[256,256]{1,0:T(8,128)(2,1)S(1)}, bf16[256,256]{1,0:T(8,128)(2,1)S(1)}, u32[]{:S(2)}, u32[]{:S(2)}) collective-permute-start(bf16[256,256]{1,0:T(8,128)(2,1)S(1)} %collective-permute-done.1.refs_0_), channel_id=1, source_target_pairs={{0,56},{8,0},{16,8},{24,16},{32,24},{40,32},{48,40},{56,48},{64,12... | collective-permute-start | bytes 393224 | tf_op jit(solution)/shard_map/ppermute | solution.py:403
  21.7 6.3 %collective-permute-start.7 = (bf16[256,256]{1,0:T(8,128)(2,1)S(1)}, bf16[256,256]{1,0:T(8,128)(2,1)S(1)}, u32[]{:S(2)}, u32[]{:S(2)}) collective-permute-start(bf16[256,256]{1,0:T(8,128)(2,1)S(1)} %collective-permute-done.3.refs_6_), channel_id=1, source_target_pairs={{0,8},{8,16},{16,24},{24,32},{32,40},{40,48},{48,56},{56,0},{64,72... | collective-permute-start | bytes 393224 | tf_op jit(solution)/shard_map/ppermute | solution.py:403
  35.1 11.9 %collective-permute-start.11 = (bf16[1024,256]{1,0:T(8,128)(2,1)S(1)}, bf16[1024,256]{1,0:T(8,128)(2,1)S(1)}, u32[]{:S(2)}, u32[]{:S(2)}) collective-permute-start(bf16[1024,256]{1,0:T(8,128)(2,1)S(1)} %get-tuple-element.39.row_a.row_ref), channel_id=1, source_target_pairs={{0,64},{8,72},{16,80},{24,88},{32,96},{40,104},{48,112},{56,120},{... | collective-permute-start | bytes 1572872 | tf_op jit(solution)/shard_map/ppermute | solution.py:403
  36.4 13.2 %collective-permute-start.12 = (bf16[1024,256]{1,0:T(8,128)(2,1)S(1)}, bf16[1024,256]{1,0:T(8,128)(2,1)S(1)}, u32[]{:S(2)}, u32[]{:S(2)}) collective-permute-start(bf16[1024,256]{1,0:T(8,128)(2,1)S(1)} %get-tuple-element.42.row_b), channel_id=1, source_target_pairs={{0,192},{8,200},{16,208},{24,216},{32,224},{40,232},{48,240},{56,2... | collective-permute-start | bytes 1572872 | tf_op jit(solution)/shard_map/ppermute | solution.py:403
  37.7 7.4 %collective-permute-start.10 = (bf16[272,256]{1,0:T(8,128)(2,1)S(1)}, bf16[272,256]{1,0:T(8,128)(2,1)S(1)}, u32[]{:S(2)}, u32[]{:S(2)}) collective-permute-start(bf16[272,256]{1,0:T(8,128)(2,1)S(1)} %add.106), channel_id=1, source_target_pairs={{0,32},{64,96},{128,160},{192,224},{1,33},{65,97},{129,161},{193,2... | collective-permute-start | bytes 417800 | tf_op jit(solution)/shard_map/ppermute | solution.py:403
  49.5 12.7 %collective-permute-start.13 = (bf16[272,256]{1,0:T(8,128)(2,1)S(1)}, bf16[272,256]{1,0:T(8,128)(2,1)S(1)}, u32[]{:S(2)}, u32[]{:S(2)}) collective-permute-start(bf16[272,256]{1,0:T(8,128)(2,1)S(1)} %add.107), channel_id=1, source_target_pairs={{0,16},{64,80},{128,144},{192,208},{32,48},{96,112},{160,176},{224... | collective-permute-start | bytes 417800 | tf_op jit(solution)/shard_map/ppermute | solution.py:403
  53.0 16.3 %collective-permute-start.15 = (bf16[1024,256]{1,0:T(8,128)(2,1)S(1)}, bf16[1024,256]{1,0:T(8,128)(2,1)S(1)}, u32[]{:S(2)}, u32[]{:S(2)}) collective-permute-start(bf16[1024,256]{1,0:T(8,128)(2,1)S(1)} %get-tuple-element.42.row_b), channel_id=1, source_target_pairs={{0,64},{8,72},{16,80},{24,88},{32,96},{40,104},{48,112},{56,120},{... | collective-permute-start | bytes 1572872 | tf_op jit(solution)/shard_map/ppermute | solution.py:403
  54.3 16.5 %collective-permute-start.16 = (bf16[1024,256]{1,0:T(8,128)(2,1)S(1)}, bf16[1024,256]{1,0:T(8,128)(2,1)}, u32[]{:S(2)}, u32[]{:S(2)}) collective-permute-start(bf16[1024,256]{1,0:T(8,128)(2,1)S(1)} %get-tuple-element.39.row_a.row_ref), channel_id=1, source_target_pairs={{0,192},{8,200},{16,208},{24,216},{32,224},{40,232},{48,240},{56,2... | collective-permute-start | bytes 1572872 | tf_op jit(solution)/shard_map/ppermute | solution.py:403
  55.6 18.3 %collective-permute-start.17 = (bf16[1024,256]{1,0:T(8,128)(2,1)S(1)}, bf16[1024,256]{1,0:T(8,128)(2,1)}, u32[]{:S(2)}, u32[]{:S(2)}) collective-permute-start(bf16[1024,256]{1,0:T(8,128)(2,1)S(1)} %collective-permute-done.11.below_a), channel_id=1, source_target_pairs={{64,128},{72,136},{80,144},{88,152},{96,160},{104,168},{112,176},{... | collective-permute-start | bytes 1572872 | tf_op jit(solution)/shard_map/ppermute | solution.py:403
  56.9 19.5 %collective-permute-start.18 = (bf16[1024,256]{1,0:T(8,128)(2,1)S(1)}, bf16[1024,256]{1,0:T(8,128)(2,1)}, u32[]{:S(2)}, u32[]{:S(2)}) collective-permute-start(bf16[1024,256]{1,0:T(8,128)(2,1)S(1)} %collective-permute-done.12.above_b), channel_id=1, source_target_pairs={{0,192},{8,200},{16,208},{24,216},{32,224},{40,232},{48,240},{56,2... | collective-permute-start | bytes 1572872 | tf_op jit(solution)/shard_map/ppermute | solution.py:403
  62.3 6.3 %collective-permute-start.14 = (bf16[272,256]{1,0:T(8,128)(2,1)S(1)}, bf16[272,256]{1,0:T(8,128)(2,1)S(1)}, u32[]{:S(2)}, u32[]{:S(2)}) collective-permute-start(bf16[272,256]{1,0:T(8,128)(2,1)S(1)} %add.108), channel_id=1, source_target_pairs={{0,8},{64,72},{128,136},{192,200},{16,24},{80,88},{144,152},{208,2... | collective-permute-start | bytes 417800 | tf_op jit(solution)/shard_map/ppermute | solution.py:403
  113.0 37.3 %collective-permute-start.19 = (bf16[4,256,512]{2,1,0:T(8,128)(2,1)}, bf16[4,256,512]{2,1,0:T(8,128)(2,1)S(1)}, u32[]{:S(2)}, u32[]{:S(2)}) collective-permute-start(bf16[4,256,512]{2,1,0:T(8,128)(2,1)} %get-tuple-element.46), channel_id=1, source_target_pairs={{0,1},{1,0},{2,3},{3,2},{4,5},{5,4},{6,7},{7,6},{8,9},{9,8},{10,11... | collective-permute-start | bytes 3145736 | tf_op jit(solution)/shard_map/ppermute | solution.py:447
  150.4 6.9 %collective-permute-start.20 = (bf16[128,512]{1,0:T(8,128)(2,1)S(1)}, bf16[128,512]{1,0:T(8,128)(2,1)S(1)}, u32[]{:S(2)}, u32[]{:S(2)}) collective-permute-start(bf16[128,512]{1,0:T(8,128)(2,1)S(1)} %get-tuple-element.57), channel_id=1, source_target_pairs={{0,2},{1,3},{2,4},{3,5},{4,6},{5,7},{6,0},{7,1},{8,10},{9,11},{10,... | collective-permute-start | bytes 393224 | tf_op jit(solution)/shard_map/ppermute | solution.py:449
  150.9 6.4 %collective-permute-start.22 = (bf16[128,512]{1,0:T(8,128)(2,1)S(1)}, bf16[128,512]{1,0:T(8,128)(2,1)S(1)}, u32[]{:S(2)}, u32[]{:S(2)}) collective-permute-start(bf16[128,512]{1,0:T(8,128)(2,1)S(1)} %get-tuple-element.58), channel_id=1, source_target_pairs={{0,6},{1,7},{2,0},{3,1},{4,2},{5,3},{6,4},{7,5},{8,14},{9,15},{10,... | collective-permute-start | bytes 393224 | tf_op jit(solution)/shard_map/ppermute | solution.py:450
  153.8 6.4 %collective-permute-start.25 = (bf16[128,512]{1,0:T(8,128)(2,1)S(1)}, bf16[128,512]{1,0:T(8,128)(2,1)S(1)}, u32[]{:S(2)}, u32[]{:S(2)}) collective-permute-start(bf16[128,512]{1,0:T(8,128)(2,1)S(1)} %get-tuple-element.59), channel_id=1, source_target_pairs={{0,2},{1,3},{2,4},{3,5},{4,6},{5,7},{6,0},{7,1},{8,10},{9,11},{10,... | collective-permute-start | bytes 393224 | tf_op jit(solution)/shard_map/ppermute | solution.py:449
  157.5 9.4 %collective-permute-start.21 = (bf16[256,512]{1,0:T(8,128)(2,1)S(1)}, bf16[256,512]{1,0:T(8,128)(2,1)S(1)}, u32[]{:S(2)}, u32[]{:S(2)}) collective-permute-start(bf16[256,512]{1,0:T(8,128)(2,1)S(1)} %pad_maximum_fusion.1), channel_id=1, source_target_pairs={{0,2},{1,3},{2,4},{3,5},{4,6},{5,7},{6,0},{7,1},{8,10},{9,11},{10,... | collective-permute-start | bytes 786440 | tf_op jit(solution)/shard_map/ppermute | solution.py:457
  160.1 10.5 %collective-permute-start.23 = (bf16[256,512]{1,0:T(8,128)(2,1)S(1)}, bf16[256,512]{1,0:T(8,128)(2,1)S(1)}, u32[]{:S(2)}, u32[]{:S(2)}) collective-permute-start(bf16[256,512]{1,0:T(8,128)(2,1)S(1)} %pad_maximum_fusion.2), channel_id=1, source_target_pairs={{0,6},{1,7},{2,0},{3,1},{4,2},{5,3},{6,4},{7,5},{8,14},{9,15},{10,... | collective-permute-start | bytes 786440 | tf_op jit(solution)/shard_map/ppermute | solution.py:457
  161.8 9.3 %collective-permute-start.26 = (bf16[256,512]{1,0:T(8,128)(2,1)S(1)}, bf16[256,512]{1,0:T(8,128)(2,1)S(1)}, u32[]{:S(2)}, u32[]{:S(2)}) collective-permute-start(bf16[256,512]{1,0:T(8,128)(2,1)S(1)} %pad_maximum_fusion.3), channel_id=1, source_target_pairs={{0,2},{1,3},{2,4},{3,5},{4,6},{5,7},{6,0},{7,1},{8,10},{9,11},{10,... | collective-permute-start | bytes 786440 | tf_op jit(solution)/shard_map/ppermute | solution.py:457
  163.7 10.2 %collective-permute-start.28 = (bf16[256,512]{1,0:T(8,128)(2,1)S(1)}, bf16[256,512]{1,0:T(8,128)(2,1)S(1)}, u32[]{:S(2)}, u32[]{:S(2)}) collective-permute-start(bf16[256,512]{1,0:T(8,128)(2,1)S(1)} %pad_maximum_fusion.4), channel_id=1, source_target_pairs={{0,6},{1,7},{2,0},{3,1},{4,2},{5,3},{6,4},{7,5},{8,14},{9,15},{10,... | collective-permute-start | bytes 786440 | tf_op jit(solution)/shard_map/ppermute | solution.py:457
  (14 other events, 212.7 us)

commit v3 on v2

--- a/solution.py
+++ b/solution.py
@@ -21,7 +21,7 @@
 HBM = pl.BlockSpec(memory_space=pltpu.HBM)
 ANY = pl.BlockSpec(memory_space=pl.ANY)
 TILE = 512
-CHUNK = 512
+STEP = 1024
 PARAMS = pltpu.CompilerParams(vmem_limit_bytes=60 * 2**20)
 
 
@@ -116,10 +116,14 @@
     return (raw.reshape(-1, *bias.shape) + bias).reshape(raw.shape)
 
 
-def fixed(query, acc_ref, peak_ref, keys, values, bias):
-    raw = biased(scores(query, keys), bias)
-    weights = jnp.exp2(raw - wide(peak_ref[...], keys.shape[0]))
-    acc_ref[...] += dot(weights.astype(jnp.bfloat16), values)
+def fixed(heads, view, keys, values, bias):
+    raw = scores(view(0)[0], keys)
+    for h in range(heads):
+        _, acc_ref, peak_ref = view(h)
+        ahead = scores(view(h + 1)[0], keys) if h + 1 < heads else None
+        weights = jnp.exp2(biased(raw, bias) - wide(peak_ref[...], keys.shape[0]))
+        acc_ref[...] += dot(weights.astype(jnp.bfloat16), values)
+        raw = ahead
 
 
 def moving(query, acc_ref, peak_ref, keys, values, bias):
@@ -131,38 +135,41 @@
     acc_ref[...] = acc_ref[...] * wide(jnp.exp2(old - peak), 2 * HEAD) + dot(weights, values)
 
 
-def absorb(acc_ref, chunks, view, start, masked, tiles, read):
-    for c in range(chunks):
-        start(c)
-
+def absorb(heads, view, masked, steps, read):
     @pl.loop(0, masked)
-    def _(tile):
-        keys = read(tile, True, True)
-        for c in range(chunks):
-            fixed(*view(c), *keys)
-
-    @pl.loop(masked, tiles)
-    def _(tile):
-        keys = read(tile, False, True)
-        for c in range(chunks):
-            fixed(*view(c), *keys)
-
-    largest = jnp.max(acc_ref[..., HEAD:])
+    def _(step):
+        fixed(heads, view, *read(step, True))
+
+    @pl.loop(0, steps)
+    def _(step):
+        fixed(heads, view, *read(step, False))
+
+
+def absorb_again(acc_ref, view, start, tiles, read):
+    largest = jnp.max(acc_ref[:, :, HEAD:])
 
     @pl.when(jnp.logical_not(largest < LIMIT))
     def _():
-        @pl.loop(0, chunks)
-        def _(c):
-            start(c)
+        @pl.loop(0, acc_ref.shape[0])
+        def _(h):
+            start(h)
 
             @pl.loop(0, tiles)
             def _(tile):
-                moving(*view(c), *read(tile, True, False))
-
-
-def tile_of(ref, at):
-    rows = pl.ds(pl.multiple_of(at * TILE, TILE), TILE)
+                moving(*view(h), *read(tile))
+
+
+def tile_of(ref, start, size):
+    rows = pl.ds(pl.multiple_of(start, TILE), size)
     return ref[rows, :HEAD], widened(ref[rows, HEAD:])
+
+
+def head_view(q_ref, acc_ref, peak_ref):
+    def view(h):
+        columns = pl.ds(pl.multiple_of(h * HEAD, HEAD), HEAD)
+        return q_ref[:, columns], acc_ref.at[h], peak_ref.at[h]
+
+    return view
 
 
 def bias_where(allowed):
@@ -173,121 +180,122 @@
     place_ref, q_ref, k_ref, v_ref, row_a, row_b, acc_ref, peak_ref, row_ref, bias_ref, sems
 ):
     keys = place_ref[0] % WIDE * KEEP
-    masked = jnp.where(keys % TILE > 0, 1, 0)
-    tiles = (keys + TILE - 1) // TILE
+    tiles, part = keys // TILE, jnp.where(keys % TILE > 0, 1, 0)
     half = row_a.shape[0]
     copies = [
         pltpu.make_async_copy(ref, row_ref.at[pl.ds(at * half, half)], sems.at[at])
         for at, ref in enumerate((row_a, row_b))
     ]
-
-    @pl.when(tiles > 0)
-    def _():
-        for copy in copies:
-            copy.start()
-
-    def view(c):
-        columns = pl.ds(pl.multiple_of(c * HEAD, HEAD), HEAD)
-        return q_ref[:, columns], acc_ref.at[c], peak_ref.at[c]
-
-    def start(c):
-        query, acc, peak = view(c)
+    for copy in copies:
+        copy.start()
+    view, heads = head_view(q_ref, acc_ref, peak_ref), acc_ref.shape[0]
+
+    def start(h):
+        query, acc, peak = view(h)
         local(query, k_ref[...], v_ref[...], acc, peak)
 
-    def read(tile, with_bias, first_time):
-        if first_time:
-
-            @pl.when(tile == 0)
-            def _():
-                for copy in copies:
-                    copy.wait()
-
-        at = jnp.where(tile < masked, tiles - 1, tile - masked)
-        if not with_bias:
-            return *tile_of(row_ref, at), None
-        bias_ref[...] = bias_where(count_along(bias_ref.shape, 1) + at * TILE < keys)
-        return *tile_of(row_ref, at), bias_ref[...]
-
-    absorb(acc_ref, acc_ref.shape[0], view, start, masked, tiles, read)
+    def read(tile):
+        bias_ref[...] = bias_where(count_along(bias_ref.shape, 1) + tile * TILE < keys)
+        return *tile_of(row_ref, tile * TILE, TILE), bias_ref[...]
+
+    def read_fast(step, masked):
+        return read(tiles) if masked else (*tile_of(row_ref, step * TILE, TILE), None)
+
+    for h in range(heads):
+        start(h)
+    for copy in copies:
+        copy.wait()
+    absorb(heads, view, part, tiles, read_fast)
+    absorb_again(acc_ref, view, start, tiles + part, read)
 
 
 def rest_kernel(
     place_ref, q_ref, rest_ref, row_ref, below_a, below_b, above_a, above_b, below2_ref,
-    above2_ref, weight_ref, acc_in, peak_in, keep_ref, send_ref, bank_ref, w_ref, bias_ref,
-    stack_ref, acc_ref, peak_ref, att_ref, sems,
+    above2_ref, weight_ref, acc_in, peak_in, *refs,
 ):
+    outs, (bank_ref, w_ref, bias_ref, acc_ref, carried_ref, peak_ref, att_ref, sems) = (
+        refs[:-8],
+        refs[-8:],
+    )
     mine, used = place_ref[0], place_ref[1]
-    y, tokens, heads = mine // WIDE, q_ref.shape[0], acc_in.shape[0]
+    y, heads = mine // WIDE, acc_ref.shape[0]
     span = WIDE * KEEP
-    part, row_tiles = span // 2, span // TILE
+    part, row_steps = span // 2, span // STEP
     copies = []
 
-    def copy(source, at, rows, condition, tile):
+    def copy(source, at, rows, condition, step):
         target = bank_ref.at[pl.ds(at, rows)]
         one = pltpu.make_async_copy(source, target, sems.at[len(copies)])
-        copies.append((one, condition, tile))
+        copies.append((one, condition, step))
 
     for row, ref in enumerate((row_ref, below_a, below2_ref, above_a)):
-        copy(ref.at[pl.ds(0, KEEP)], 0, KEEP, (mine > 0) & (y == row), 0)
-    at, tile = TILE, 1
+        copy(ref.at[pl.ds(0, KEEP)], 0, KEEP, (mine > 0) & (y == row), None)
+    at, step = TILE, 0
     for condition, first, second in (
         (y > 0, below_a, below_b),
         (y > 1, below2_ref, above2_ref),
         (y == 3, above_a, above_b),
     ):
-        copy(first, at, part, condition, tile)
-        copy(second, at + part, part, condition, tile)
-        at, tile = at + span, tile + row_tiles
+        copy(first, at, part, condition, step)
+        copy(second, at + part, part, condition, step)
+        at, step = at + span, step + row_steps
     for one, condition, _ in copies:
         pl.when(condition)(one.start)
-    weight_copy = pltpu.make_async_copy(weight_ref, w_ref, sems.at[len(copies)])
-    weight_copy.start()
+    whole = [
+        pltpu.make_async_copy(source, target, sems.at[len(copies) + at])
+        for at, (source, target) in enumerate(
+            ((peak_in, peak_ref), (acc_in, carried_ref), (weight_ref, w_ref))
+        )
+    ]
+    for one in whole:
+        one.start()
+    acc_ref[...] = jnp.zeros_like(acc_ref)
     bank_ref[KEEP:TILE] = rest_ref[: TILE - KEEP]
     number = wide(rest_ref[TILE - KEEP : TILE - KEEP + 1, :HEAD].astype(jnp.int32), TILE)
     at = count_along((1, TILE), 1)
     limit = jnp.where(at < KEEP, number, KEEP + used - number)
     bias_ref[0] = jnp.broadcast_to(bias_where(at < limit), bias_ref.shape[1:])
     bias_ref[1] = jnp.zeros(bias_ref.shape[1:], jnp.float32)
+    view = head_view(q_ref, acc_ref, peak_ref)
+
+    def start(h):
+        acc_ref[h] = carried_ref[h]
+
+    def read_fast(step, masked):
+        for one, condition, when in copies:
+            if masked and when is None:
+                pl.when(condition)(one.wait)
+            elif when is not None and not masked:
+                pl.when(condition & (step == when))(one.wait)
+        if masked:
+            return read(0)
+        return *tile_of(bank_ref, TILE + step * STEP, STEP), None
+
+    def read(tile):
+        return *tile_of(bank_ref, tile * TILE, TILE), bias_ref[jnp.minimum(tile, 1)]
+
+    masked = jnp.where(mine > 0, 1, 0)
+    whole[0].wait()
+    absorb(heads, view, masked, row_steps * y, read_fast)
+    whole[1].wait()
+    acc_ref[...] += carried_ref[...]
+    absorb_again(acc_ref, view, start, masked + span // TILE * y, read)
     for h in range(heads):
-        stack_ref[h * tokens : (h + 1) * tokens] = q_ref[:, h * HEAD : (h + 1) * HEAD]
-    together = CHUNK // tokens
-
-    def view(c):
-        rows = pl.ds(pl.multiple_of(c * CHUNK, CHUNK), CHUNK)
-        return stack_ref[rows], acc_ref.at[rows], peak_ref.at[rows]
-
-    def start(c):
-        for h in range(together):
-            rows = pl.ds(pl.multiple_of((c * together + h) * tokens, tokens), tokens)
-            acc_ref[rows] = acc_in[c * together + h]
-            peak_ref[rows] = peak_in[c * together + h]
-
-    def read(tile, masked, first_time):
-        if first_time:
-            for one, condition, when in copies:
-                if masked == (when == 0):
-                    pl.when(condition & (tile == when))(one.wait)
-        bias = bias_ref[jnp.minimum(tile, 1)] if masked else None
-        return *tile_of(bank_ref, tile), bias
-
-    masked = jnp.where(mine > 0, 1, 0)
-    chunks = heads // together
-    absorb(acc_ref, chunks, view, start, masked, masked + row_tiles * y, read)
-    for h in range(heads):
-        rows = slice(h * tokens, (h + 1) * tokens)
         att_ref[:, h * HEAD : (h + 1) * HEAD] = (
-            acc_ref[rows, :HEAD] / acc_ref[rows, HEAD:]
+            acc_ref[h, :, :HEAD] / acc_ref[h, :, HEAD:]
         ).astype(jnp.bfloat16)
-    weight_copy.wait()
-    chips, _, columns = keep_ref.shape
+    whole[2].wait()
+    chips, rows, columns = outs[0].shape
     chip, core = place_ref[2], place_ref[3]
 
     @pl.loop(0, chips)
     def _(step):
         at = lax.rem(chip + step, chips) * 2
-        for ref, side in ((keep_ref, core), (send_ref, 1 - core)):
+        for first, side in enumerate((core, 1 - core)):
             start = pl.multiple_of((at + side) * columns, columns)
-            ref[step] = dot(att_ref[...], w_ref[:, pl.ds(start, columns)]).astype(jnp.bfloat16)
+            product = dot(att_ref[...], w_ref[:, pl.ds(start, columns)]).astype(jnp.bfloat16)
+            for part, ref in enumerate(outs[first::2]):
+                ref[step] = product[part * rows : (part + 1) * rows]
 
 
 def pack_row_kernel(place_ref, *refs):
@@ -349,38 +357,31 @@
     )(place, queries, keys, values, row_a, row_b)
 
 
-def rest_rows(place, queries, rest, banks, weight, state, part, parts, chips):
+def rest_rows(place, queries, rest, banks, weight, state, parts, chips):
     length, width = queries.shape
-    rows, heads = length // parts, width // HEAD
-    tiles = 13
-    slab = lambda columns: pl.BlockSpec((heads, rows, columns), lambda i: (0, part, 0))
-    out = jax.ShapeDtypeStruct((chips, rows, weight.shape[1] // chips // 2), jnp.bfloat16)
+    heads = width // HEAD
+    keys = TILE + 3 * WIDE * KEEP
+    whole = lambda x: pl.BlockSpec(x.shape, lambda i: (0,) * len(x.shape))
+    out = jax.ShapeDtypeStruct((chips, length // parts, weight.shape[1] // chips // 2), jnp.bfloat16)
     return pl.pallas_call(
         rest_kernel,
         grid=(1,),
-        out_shape=[out, out],
-        in_specs=[
-            SMEM,
-            pl.BlockSpec((rows, width), lambda i: (part, 0)),
-            pl.BlockSpec(rest.shape, lambda i: (0, 0)),
-            *[ANY] * (len(banks) + 1),
-            slab(2 * HEAD),
-            slab(HEAD),
-        ],
-        out_specs=[pl.BlockSpec(out.shape, lambda i: (0, 0, 0))] * 2,
+        out_shape=[out] * (2 * parts),
+        in_specs=[SMEM, whole(queries), whole(rest), *[ANY] * (len(banks) + 3)],
+        out_specs=[whole(out)] * (2 * parts),
         scratch_shapes=[
-            pltpu.VMEM((tiles * TILE, 2 * HEAD), jnp.bfloat16),
+            pltpu.VMEM((keys, 2 * HEAD), jnp.bfloat16),
             pltpu.VMEM(weight.shape, weight.dtype),
             pltpu.VMEM((2, 8, TILE), jnp.float32),
-            pltpu.VMEM((heads * rows, HEAD), jnp.bfloat16),
-            pltpu.VMEM((heads * rows, 2 * HEAD), jnp.float32),
-            pltpu.VMEM((heads * rows, HEAD), jnp.float32),
-            pltpu.VMEM((rows, width), jnp.bfloat16),
-            pltpu.SemaphoreType.DMA((11,)),
+            pltpu.VMEM((heads, length, 2 * HEAD), jnp.float32),
+            pltpu.VMEM((heads, length, 2 * HEAD), jnp.float32),
+            pltpu.VMEM((heads, length, HEAD), jnp.float32),
+            pltpu.VMEM((length, width), jnp.bfloat16),
+            pltpu.SemaphoreType.DMA((13,)),
         ],
         compiler_params=PARAMS,
-        cost_estimate=cost(rows * heads, tiles * TILE),
-        name=f"rest_rows_{part}",
+        cost_estimate=cost(length * heads, keys),
+        name="rest_rows",
     )(place, queries, rest, *banks, weight, *state)
 
 
@@ -440,11 +441,9 @@
 
     outs = []
     half = length // parts // 2
-    for part in range(parts):
-        own, send = rest_rows(
-            place, queries, rest, banks, output_weight, state, part, parts, chips
-        )
-        other = lax.ppermute(send, "head", swap)
+    terms = rest_rows(place, queries, rest, banks, output_weight, state, parts, chips)
+    others = [lax.ppermute(send, "head", swap) for send in terms[1::2]]
+    for own, other in zip(terms[::2], others):
         across_x = added(own[2], other[2])
         from_below = lax.ppermute(across_x[:half], "head", up)
         from_above = lax.ppermute(across_x[half:], "head", down)

time: 175 us -> 173 us (0.989); the launches traced: 175 us -> 170 us
  Pallas kernels: 81.4 us -> 72.1 us
  waiting for transfers between devices: 37.8 us -> 44 us
  starting transfers between devices: 49.2 us -> 45.6 us
  other arithmetic: 4.47 us -> 6.39 us
    pallas_call x2 -> x1, Pallas kernels: 73.3 us -> 63.9 us  [rest_rows(): pl.pallas_call(rest_kernel, grid=(1,), out_shape=[out] * (2 * parts), in_...]
    ppermute x19, waiting for transfers between devices: 26.2 us -> 34.1 us  [on_device(): permute = lambda x, pairs: lax.ppermute(x, 'ctx', pairs)]
    ppermute x19, starting transfers between devices: 39.3 us -> 33.8 us  [on_device(): permute = lambda x, pairs: lax.ppermute(x, 'ctx', pairs)]
    ppermute x2, waiting for transfers between devices: 3.16 us -> 0.01 us  [on_device(): lax.ppermute(upward, 'head', up)]
    ppermute x2, waiting for transfers between devices: 0.29 us -> 2.36 us  [on_device(): others = [lax.ppermute(send, 'head', swap) for send in terms[1::2]]]
    convert_element_type x8, other arithmetic: 2.66 us -> 4.57 us  [added(): sum((term.astype(jnp.float32) for term in terms)).astype(jnp.bfloat16)]
  transfers between devices with their start and end apart: 29 -> 29, of which waited for: 17 -> 15; matrix products, arithmetic and copies ran while one was open for 2% -> 3% of each run, Pallas kernels for 24% -> 3%
where the time goes in v3:
time: 173 us; the launch traced here: 170 us
  Pallas kernels  72.1 us (42%)
  starting transfers between devices  45.6 us (26%)
  waiting for transfers between devices  44 us (25%)
  other arithmetic  6.39 us (4%)
    pallas_call x1, Pallas kernels, rest_rows(): pl.pallas_call(rest_kernel, grid=(1,), out_shape=[out] * (2 * parts), in_...  63.9 us
    ppermute x19, waiting for transfers between devices, on_device(): permute = lambda x, pairs: lax.ppermute(x, 'ctx', pairs)  34.1 us
    ppermute x19, starting transfers between devices, on_device(): permute = lambda x, pairs: lax.ppermute(x, 'ctx', pairs)  33.8 us
    ppermute x2, waiting for transfers between devices, on_device(): lax.ppermute(downward, 'head', down)  7.06 us
    ppermute x2, starting transfers between devices, on_device(): lax.ppermute(upward, 'head', up)  5.78 us
    pallas_call x1, Pallas kernels, own_row(): pl.pallas_call(own_row_kernel, grid=(1,), out_shape=state, in_specs=[SMEM...  4.97 us
    convert_element_type x8, other arithmetic, added(): sum((term.astype(jnp.float32) for term in terms)).astype(jnp.bfloat16)  4.57 us
  transfers between devices with their start and end apart: 29, of which 15 were waited for; matrix products, arithmetic and copies ran while one was open for 3% of the time, Pallas kernels for 3%

profile of v3, /device:TPU:30, one launch (start us, length us, event | category | flops | bytes accessed | tf_op | source)
XLA Modules:
  0.0 170.2 jit_solution(242466649049855545)
XLA Ops:
  0.7 2.4 %select_kept.1 = (bf16[256,256]{1,0:T(8,128)(2,1)}, bf16[272,256]{1,0:T(8,128)(2,1)}) custom-call(s32[1]{0:T(128)S(6)} %copy.7.used_ref, s32[1,256]{1,0:T(1,128)} %refs_0_.1, bf16[512,128]{1,0:T(8,128)(2,1)} %k_ref.1, bf16[512,128]{1,0:T(8,128)(2,1)} %v_ref.1), custom_call_target="tpu_custom_call" | custom-call | tf_op jit(solution)/shard_map/select_kept/pallas_call | solution.py:77
  3.8 5.9 %collective-permute-start.1 = (bf16[256,256]{1,0:T(8,128)(2,1)}, bf16[256,256]{1,0:T(8,128)(2,1)S(1)}, u32[]{:S(2)}, u32[]{:S(2)}) collective-permute-start(bf16[256,256]{1,0:T(8,128)(2,1)} %get-tuple-element.27.refs_8_), channel_id=1, source_target_pairs={{0,56},{8,0},{16,8},{24,16},{32,24},{40,32},{48,40},{56,48},{64,12... | collective-permute-start | bytes 393224 | tf_op jit(solution)/shard_map/ppermute | solution.py:404
  9.8 3.0 %collective-permute-done.1.refs_0_ = bf16[256,256]{1,0:T(8,128)(2,1)S(1)} collective-permute-done((bf16[256,256]{1,0:T(8,128)(2,1)}, bf16[256,256]{1,0:T(8,128)(2,1)S(1)}, u32[]{:S(2)}, u32[]{:S(2)}) %collective-permute-start.1) | collective-permute-done | bytes 131104 | tf_op jit(solution)/shard_map/ppermute | solution.py:404
  12.8 3.3 %collective-permute-done.refs_7_ = bf16[256,256]{1,0:T(8,128)(2,1)S(1)} collective-permute-done((bf16[256,256]{1,0:T(8,128)(2,1)}, bf16[256,256]{1,0:T(8,128)(2,1)S(1)}, u32[]{:S(2)}, u32[]{:S(2)}) %collective-permute-start) | collective-permute-done | bytes 131104 | tf_op jit(solution)/shard_map/ppermute | solution.py:404
  17.5 3.2 %collective-permute-start.4 = (bf16[256,256]{1,0:T(8,128)(2,1)S(1)}, bf16[256,256]{1,0:T(8,128)(2,1)S(1)}, u32[]{:S(2)}, u32[]{:S(2)}) collective-permute-start(bf16[256,256]{1,0:T(8,128)(2,1)S(1)} %collective-permute-done.1.refs_0_), channel_id=1, source_target_pairs={{0,56},{8,0},{16,8},{24,16},{32,24},{40,32},{48,40},{56,48},{64,12... | collective-permute-start | bytes 393224 | tf_op jit(solution)/shard_map/ppermute | solution.py:404
  20.7 3.5 %collective-permute-done.5 = bf16[272,256]{1,0:T(8,128)(2,1)S(1)} collective-permute-done((bf16[272,256]{1,0:T(8,128)(2,1)S(1)}, bf16[272,256]{1,0:T(8,128)(2,1)S(1)}, u32[]{:S(2)}, u32[]{:S(2)}) %collective-permute-start.5) | collective-permute-done | bytes 139296 | tf_op jit(solution)/shard_map/ppermute | solution.py:404
  24.4 2.6 %collective-permute-start.6 = (bf16[256,256]{1,0:T(8,128)(2,1)S(1)}, bf16[256,256]{1,0:T(8,128)(2,1)S(1)}, u32[]{:S(2)}, u32[]{:S(2)}) collective-permute-start(bf16[256,256]{1,0:T(8,128)(2,1)S(1)} %collective-permute-done.4.refs_1_), channel_id=1, source_target_pairs={{0,56},{8,0},{16,8},{24,16},{32,24},{40,32},{48,40},{56,48},{64,12... | collective-permute-start | bytes 393224 | tf_op jit(solution)/shard_map/ppermute | solution.py:404
  26.9 3.2 %collective-permute-done.6.refs_2_ = bf16[256,256]{1,0:T(8,128)(2,1)S(1)} collective-permute-done((bf16[256,256]{1,0:T(8,128)(2,1)S(1)}, bf16[256,256]{1,0:T(8,128)(2,1)S(1)}, u32[]{:S(2)}, u32[]{:S(2)}) %collective-permute-start.6) | collective-permute-done | bytes 131104 | tf_op jit(solution)/shard_map/ppermute | solution.py:404
  30.1 3.4 %collective-permute-start.9 = (bf16[128,256]{1,0:T(8,128)(2,1)S(1)}, bf16[128,256]{1,0:T(8,128)(2,1)S(1)}, u32[]{:S(2)}, u32[]{:S(2)}) collective-permute-start(bf16[128,256]{1,0:T(8,128)(2,1)S(1)} %slice.137), channel_id=1, source_target_pairs={{0,56},{8,0},{16,8},{24,16},{32,24},{40,32},{48,40},{56,48},{64,12... | collective-permute-start | bytes 196616 | tf_op jit(solution)/shard_map/ppermute | solution.py:404
  35.4 3.8 %collective-permute-done.8.refs_3_ = bf16[128,256]{1,0:T(8,128)(2,1)S(1)} collective-permute-done((bf16[128,256]{1,0:T(8,128)(2,1)S(1)}, bf16[128,256]{1,0:T(8,128)(2,1)S(1)}, u32[]{:S(2)}, u32[]{:S(2)}) %collective-permute-start.8) | collective-permute-done | bytes 65568 | tf_op jit(solution)/shard_map/ppermute | solution.py:404
  43.4 2.5 %collective-permute-start.10 = (bf16[272,256]{1,0:T(8,128)(2,1)S(1)}, bf16[272,256]{1,0:T(8,128)(2,1)S(1)}, u32[]{:S(2)}, u32[]{:S(2)}) collective-permute-start(bf16[272,256]{1,0:T(8,128)(2,1)S(1)} %add.106), channel_id=1, source_target_pairs={{0,32},{64,96},{128,160},{192,224},{1,33},{65,97},{129,161},{193,2... | collective-permute-start | bytes 417800 | tf_op jit(solution)/shard_map/ppermute | solution.py:404
  45.9 2.6 %collective-permute-done.10 = bf16[272,256]{1,0:T(8,128)(2,1)S(1)} collective-permute-done((bf16[272,256]{1,0:T(8,128)(2,1)S(1)}, bf16[272,256]{1,0:T(8,128)(2,1)S(1)}, u32[]{:S(2)}, u32[]{:S(2)}) %collective-permute-start.10) | collective-permute-done | bytes 139296 | tf_op jit(solution)/shard_map/ppermute | solution.py:404
  48.5 3.4 %collective-permute-done.11.below_a = bf16[1024,256]{1,0:T(8,128)(2,1)S(1)} collective-permute-done((bf16[1024,256]{1,0:T(8,128)(2,1)S(1)}, bf16[1024,256]{1,0:T(8,128)(2,1)S(1)}, u32[]{:S(2)}, u32[]{:S(2)}) %collective-permute-start.11) | collective-permute-done | bytes 524320 | tf_op jit(solution)/shard_map/ppermute | solution.py:404
  51.9 4.1 %collective-permute-done.12.above_b = bf16[1024,256]{1,0:T(8,128)(2,1)S(1)} collective-permute-done((bf16[1024,256]{1,0:T(8,128)(2,1)S(1)}, bf16[1024,256]{1,0:T(8,128)(2,1)S(1)}, u32[]{:S(2)}, u32[]{:S(2)}) %collective-permute-start.12) | collective-permute-done | bytes 524320 | tf_op jit(solution)/shard_map/ppermute | solution.py:404
  61.2 5.2 %collective-permute-start.18 = (bf16[1024,256]{1,0:T(8,128)(2,1)S(1)}, bf16[1024,256]{1,0:T(8,128)(2,1)}, u32[]{:S(2)}, u32[]{:S(2)}) collective-permute-start(bf16[1024,256]{1,0:T(8,128)(2,1)S(1)} %collective-permute-done.12.above_b), channel_id=1, source_target_pairs={{0,192},{8,200},{16,208},{24,216},{32,224},{40,232},{48,240},{56,2... | collective-permute-start | bytes 1572872 | tf_op jit(solution)/shard_map/ppermute | solution.py:404
  67.8 5.0 %own_row.1 = (f32[4,512,256]{2,1,0:T(8,128)}, f32[4,512,128]{2,1,0:T(8,128)}) custom-call(s32[4]{0:T(128)} %copy-done.1, bf16[512,512]{1,0:T(8,128)(2,1)} %q_ref.3, bf16[512,128]{1,0:T(8,128)(2,1)} %k_ref.1, bf16[512,128]{1,0:T(8,128)(2,1)} %v_ref.1, bf16[1024,256]{1,0:T(8,128)(2,1)} %copy-done.2, bf16[1024,256]{1,0:T(8,128)(2,1)} %copy-done.3), custom_call_target="tpu_custom_call" | custom-call | flops 5368709120 | bytes 8388608 | tf_op jit(solution)/shard_map/own_row/pallas_call | solution.py:343
  73.5 5.4 %collective-permute-done.17.below2_ref = bf16[1024,256]{1,0:T(8,128)(2,1)} collective-permute-done((bf16[1024,256]{1,0:T(8,128)(2,1)S(1)}, bf16[1024,256]{1,0:T(8,128)(2,1)}, u32[]{:S(2)}, u32[]{:S(2)}) %collective-permute-start.17) | collective-permute-done | bytes 524320 | tf_op jit(solution)/shard_map/ppermute | solution.py:404
  78.9 63.9 %rest_rows.1 = (bf16[4,256,512]{2,1,0:T(8,128)(2,1)}, bf16[4,256,512]{2,1,0:T(8,128)(2,1)}, bf16[4,256,512]{2,1,0:T(8,128)(2,1)}, bf16[4,256,512]{2,1,0:T(8,128)(2,1)}) custom-call(s32[4]{0:T(128)} %copy-done.1, bf16[512,512]{1,0:T(8,128)(2,1)} %q_ref.3, bf16[272,256]{1,0:T(8,128)(2,1)} %add.109.rest_ref, bf16[1024,256]{1,0:T(8,128)(2,1)} %copy-done.2, ...), custom_call_target="tpu_custom_call" | custom-call | flops 13958643712 | bytes 8388608 | tf_op jit(solution)/shard_map/rest_rows/pallas_call | solution.py:366
  143.5 2.4 %collective-permute-done.19 = bf16[4,256,512]{2,1,0:T(8,128)(2,1)S(1)} collective-permute-done((bf16[4,256,512]{2,1,0:T(8,128)(2,1)}, bf16[4,256,512]{2,1,0:T(8,128)(2,1)S(1)}, u32[]{:S(2)}, u32[]{:S(2)}) %collective-permute-start.19) | collective-permute-done | bytes 1048608 | tf_op jit(solution)/shard_map/ppermute | solution.py:445
  150.0 1.8 %collective-permute-start.25 = (bf16[128,512]{1,0:T(8,128)(2,1)S(1)}, bf16[128,512]{1,0:T(8,128)(2,1)S(1)}, u32[]{:S(2)}, u32[]{:S(2)}) collective-permute-start(bf16[128,512]{1,0:T(8,128)(2,1)S(1)} %get-tuple-element.59), channel_id=1, source_target_pairs={{0,2},{1,3},{2,4},{3,5},{4,6},{5,7},{6,0},{7,1},{8,10},{9,11},{10,... | collective-permute-start | bytes 393224 | tf_op jit(solution)/shard_map/ppermute | solution.py:448
  155.5 2.5 %collective-permute-start.21 = (bf16[256,512]{1,0:T(8,128)(2,1)S(1)}, bf16[256,512]{1,0:T(8,128)(2,1)S(1)}, u32[]{:S(2)}, u32[]{:S(2)}) collective-permute-start(bf16[256,512]{1,0:T(8,128)(2,1)S(1)} %pad_maximum_fusion.1), channel_id=1, source_target_pairs={{0,2},{1,3},{2,4},{3,5},{4,6},{5,7},{6,0},{7,1},{8,10},{9,11},{10,... | collective-permute-start | bytes 786440 | tf_op jit(solution)/shard_map/ppermute | solution.py:456
  158.7 3.3 %collective-permute-start.26 = (bf16[256,512]{1,0:T(8,128)(2,1)S(1)}, bf16[256,512]{1,0:T(8,128)(2,1)S(1)}, u32[]{:S(2)}, u32[]{:S(2)}) collective-permute-start(bf16[256,512]{1,0:T(8,128)(2,1)S(1)} %pad_maximum_fusion.3), channel_id=1, source_target_pairs={{0,2},{1,3},{2,4},{3,5},{4,6},{5,7},{6,0},{7,1},{8,10},{9,11},{10,... | collective-permute-start | bytes 786440 | tf_op jit(solution)/shard_map/ppermute | solution.py:456
  162.0 3.1 %collective-permute-done.23 = bf16[256,512]{1,0:T(8,128)(2,1)S(1)} collective-permute-done((bf16[256,512]{1,0:T(8,128)(2,1)S(1)}, bf16[256,512]{1,0:T(8,128)(2,1)S(1)}, u32[]{:S(2)}, u32[]{:S(2)}) %collective-permute-start.23) | collective-permute-done | bytes 262176 | tf_op jit(solution)/shard_map/ppermute | solution.py:456
  165.3 3.9 %collective-permute-done.28 = bf16[256,512]{1,0:T(8,128)(2,1)S(1)} collective-permute-done((bf16[256,512]{1,0:T(8,128)(2,1)S(1)}, bf16[256,512]{1,0:T(8,128)(2,1)S(1)}, u32[]{:S(2)}, u32[]{:S(2)}) %collective-permute-start.28) | collective-permute-done | bytes 262176 | tf_op jit(solution)/shard_map/ppermute | solution.py:456
  (82 shorter events, 25.7 us)
Async XLA Ops:
  3.1 6.6 %collective-permute-start.2 = (bf16[272,256]{1,0:T(8,128)(2,1)S(1)}, bf16[272,256]{1,0:T(8,128)(2,1)S(1)}, u32[]{:S(2)}, u32[]{:S(2)}) collective-permute-start(bf16[272,256]{1,0:T(8,128)(2,1)S(1)} %broadcast_select_fusion), channel_id=1, source_target_pairs={{0,64},{1,65},{2,66},{3,67},{4,68},{5,69},{6,70},{7,71}} | collective-permute-start | bytes 417800 | tf_op jit(solution)/shard_map/ppermute | solution.py:404
  3.8 9.0 %collective-permute-start.1 = (bf16[256,256]{1,0:T(8,128)(2,1)}, bf16[256,256]{1,0:T(8,128)(2,1)S(1)}, u32[]{:S(2)}, u32[]{:S(2)}) collective-permute-start(bf16[256,256]{1,0:T(8,128)(2,1)} %get-tuple-element.27.refs_8_), channel_id=1, source_target_pairs={{0,56},{8,0},{16,8},{24,16},{32,24},{40,32},{48,40},{56,48},{64,12... | collective-permute-start | bytes 393224 | tf_op jit(solution)/shard_map/ppermute | solution.py:404
  9.8 6.4 %collective-permute-start = (bf16[256,256]{1,0:T(8,128)(2,1)}, bf16[256,256]{1,0:T(8,128)(2,1)S(1)}, u32[]{:S(2)}, u32[]{:S(2)}) collective-permute-start(bf16[256,256]{1,0:T(8,128)(2,1)} %get-tuple-element.27.refs_8_), channel_id=1, source_target_pairs={{0,8},{8,16},{16,24},{24,32},{32,40},{40,48},{48,56},{56,0},{64,72... | collective-permute-start | bytes 393224 | tf_op jit(solution)/shard_map/ppermute | solution.py:404
  16.1 8.1 %collective-permute-start.5 = (bf16[272,256]{1,0:T(8,128)(2,1)S(1)}, bf16[272,256]{1,0:T(8,128)(2,1)S(1)}, u32[]{:S(2)}, u32[]{:S(2)}) collective-permute-start(bf16[272,256]{1,0:T(8,128)(2,1)S(1)} %fusion.12), channel_id=1, source_target_pairs={{0,192},{64,128},{1,193},{65,129},{2,194},{66,130},{3,195},{67,131... | collective-permute-start | bytes 417800 | tf_op jit(solution)/shard_map/ppermute | solution.py:404
  17.4 6.9 %collective-permute-start.3 = (bf16[256,256]{1,0:T(8,128)(2,1)S(1)}, bf16[256,256]{1,0:T(8,128)(2,1)S(1)}, u32[]{:S(2)}, u32[]{:S(2)}) collective-permute-start(bf16[256,256]{1,0:T(8,128)(2,1)S(1)} %collective-permute-done.refs_7_), channel_id=1, source_target_pairs={{0,8},{8,16},{16,24},{24,32},{32,40},{40,48},{48,56},{56,0},{64,72... | collective-permute-start | bytes 393224 | tf_op jit(solution)/shard_map/ppermute | solution.py:404
  17.5 6.8 %collective-permute-start.4 = (bf16[256,256]{1,0:T(8,128)(2,1)S(1)}, bf16[256,256]{1,0:T(8,128)(2,1)S(1)}, u32[]{:S(2)}, u32[]{:S(2)}) collective-permute-start(bf16[256,256]{1,0:T(8,128)(2,1)S(1)} %collective-permute-done.1.refs_0_), channel_id=1, source_target_pairs={{0,56},{8,0},{16,8},{24,16},{32,24},{40,32},{48,40},{56,48},{64,12... | collective-permute-start | bytes 393224 | tf_op jit(solution)/shard_map/ppermute | solution.py:404
  26.9 6.8 %collective-permute-start.7 = (bf16[256,256]{1,0:T(8,128)(2,1)S(1)}, bf16[256,256]{1,0:T(8,128)(2,1)S(1)}, u32[]{:S(2)}, u32[]{:S(2)}) collective-permute-start(bf16[256,256]{1,0:T(8,128)(2,1)S(1)} %collective-permute-done.3.refs_6_), channel_id=1, source_target_pairs={{0,8},{8,16},{16,24},{24,32},{32,40},{40,48},{48,56},{56,0},{64,72... | collective-permute-start | bytes 393224 | tf_op jit(solution)/shard_map/ppermute | solution.py:404
  40.8 11.1 %collective-permute-start.11 = (bf16[1024,256]{1,0:T(8,128)(2,1)S(1)}, bf16[1024,256]{1,0:T(8,128)(2,1)S(1)}, u32[]{:S(2)}, u32[]{:S(2)}) collective-permute-start(bf16[1024,256]{1,0:T(8,128)(2,1)S(1)} %get-tuple-element.39.row_a.row_ref), channel_id=1, source_target_pairs={{0,64},{8,72},{16,80},{24,88},{32,96},{40,104},{48,112},{56,120},{... | collective-permute-start | bytes 1572872 | tf_op jit(solution)/shard_map/ppermute | solution.py:404
  42.1 13.9 %collective-permute-start.12 = (bf16[1024,256]{1,0:T(8,128)(2,1)S(1)}, bf16[1024,256]{1,0:T(8,128)(2,1)S(1)}, u32[]{:S(2)}, u32[]{:S(2)}) collective-permute-start(bf16[1024,256]{1,0:T(8,128)(2,1)S(1)} %get-tuple-element.42.row_b), channel_id=1, source_target_pairs={{0,192},{8,200},{16,208},{24,216},{32,224},{40,232},{48,240},{56,2... | collective-permute-start | bytes 1572872 | tf_op jit(solution)/shard_map/ppermute | solution.py:404
  56.0 10.4 %collective-permute-start.13 = (bf16[272,256]{1,0:T(8,128)(2,1)S(1)}, bf16[272,256]{1,0:T(8,128)(2,1)S(1)}, u32[]{:S(2)}, u32[]{:S(2)}) collective-permute-start(bf16[272,256]{1,0:T(8,128)(2,1)S(1)} %add.107), channel_id=1, source_target_pairs={{0,16},{64,80},{128,144},{192,208},{32,48},{96,112},{160,176},{224... | collective-permute-start | bytes 417800 | tf_op jit(solution)/shard_map/ppermute | solution.py:404
  57.3 16.2 %collective-permute-start.16 = (bf16[1024,256]{1,0:T(8,128)(2,1)S(1)}, bf16[1024,256]{1,0:T(8,128)(2,1)S(1)}, u32[]{:S(2)}, u32[]{:S(2)}) collective-permute-start(bf16[1024,256]{1,0:T(8,128)(2,1)S(1)} %get-tuple-element.39.row_a.row_ref), channel_id=1, source_target_pairs={{0,192},{8,200},{16,208},{24,216},{32,224},{40,232},{48,240},{56,2... | collective-permute-start | bytes 1572872 | tf_op jit(solution)/shard_map/ppermute | solution.py:404
  58.6 14.9 %collective-permute-start.15 = (bf16[1024,256]{1,0:T(8,128)(2,1)S(1)}, bf16[1024,256]{1,0:T(8,128)(2,1)S(1)}, u32[]{:S(2)}, u32[]{:S(2)}) collective-permute-start(bf16[1024,256]{1,0:T(8,128)(2,1)S(1)} %get-tuple-element.42.row_b), channel_id=1, source_target_pairs={{0,64},{8,72},{16,80},{24,88},{32,96},{40,104},{48,112},{56,120},{... | collective-permute-start | bytes 1572872 | tf_op jit(solution)/shard_map/ppermute | solution.py:404
  59.9 19.0 %collective-permute-start.17 = (bf16[1024,256]{1,0:T(8,128)(2,1)S(1)}, bf16[1024,256]{1,0:T(8,128)(2,1)}, u32[]{:S(2)}, u32[]{:S(2)}) collective-permute-start(bf16[1024,256]{1,0:T(8,128)(2,1)S(1)} %collective-permute-done.11.below_a), channel_id=1, source_target_pairs={{64,128},{72,136},{80,144},{88,152},{96,160},{104,168},{112,176},{... | collective-permute-start | bytes 1572872 | tf_op jit(solution)/shard_map/ppermute | solution.py:404
  61.2 17.7 %collective-permute-start.18 = (bf16[1024,256]{1,0:T(8,128)(2,1)S(1)}, bf16[1024,256]{1,0:T(8,128)(2,1)}, u32[]{:S(2)}, u32[]{:S(2)}) collective-permute-start(bf16[1024,256]{1,0:T(8,128)(2,1)S(1)} %collective-permute-done.12.above_b), channel_id=1, source_target_pairs={{0,192},{8,200},{16,208},{24,216},{32,224},{40,232},{48,240},{56,2... | collective-permute-start | bytes 1572872 | tf_op jit(solution)/shard_map/ppermute | solution.py:404
  66.5 6.3 %collective-permute-start.14 = (bf16[272,256]{1,0:T(8,128)(2,1)S(1)}, bf16[272,256]{1,0:T(8,128)(2,1)S(1)}, u32[]{:S(2)}, u32[]{:S(2)}) collective-permute-start(bf16[272,256]{1,0:T(8,128)(2,1)S(1)} %add.108), channel_id=1, source_target_pairs={{0,8},{64,72},{128,136},{192,200},{16,24},{80,88},{144,152},{208,2... | collective-permute-start | bytes 417800 | tf_op jit(solution)/shard_map/ppermute | solution.py:404
  143.0 6.0 %collective-permute-start.24 = (bf16[4,256,512]{2,1,0:T(8,128)(2,1)}, bf16[4,256,512]{2,1,0:T(8,128)(2,1)S(1)}, u32[]{:S(2)}, u32[]{:S(2)}) collective-permute-start(bf16[4,256,512]{2,1,0:T(8,128)(2,1)} %get-tuple-element.48), channel_id=1, source_target_pairs={{0,1},{1,0},{2,3},{3,2},{4,5},{5,4},{6,7},{7,6},{8,9},{9,8},{10,11... | collective-permute-start | bytes 3145736 | tf_op jit(solution)/shard_map/ppermute | solution.py:445
  146.9 7.3 %collective-permute-start.20 = (bf16[128,512]{1,0:T(8,128)(2,1)S(1)}, bf16[128,512]{1,0:T(8,128)(2,1)S(1)}, u32[]{:S(2)}, u32[]{:S(2)}) collective-permute-start(bf16[128,512]{1,0:T(8,128)(2,1)S(1)} %get-tuple-element.57), channel_id=1, source_target_pairs={{0,2},{1,3},{2,4},{3,5},{4,6},{5,7},{6,0},{7,1},{8,10},{9,11},{10,... | collective-permute-start | bytes 393224 | tf_op jit(solution)/shard_map/ppermute | solution.py:448
  147.4 6.8 %collective-permute-start.22 = (bf16[128,512]{1,0:T(8,128)(2,1)S(1)}, bf16[128,512]{1,0:T(8,128)(2,1)S(1)}, u32[]{:S(2)}, u32[]{:S(2)}) collective-permute-start(bf16[128,512]{1,0:T(8,128)(2,1)S(1)} %get-tuple-element.58), channel_id=1, source_target_pairs={{0,6},{1,7},{2,0},{3,1},{4,2},{5,3},{6,4},{7,5},{8,14},{9,15},{10,... | collective-permute-start | bytes 393224 | tf_op jit(solution)/shard_map/ppermute | solution.py:449
  150.0 8.0 %collective-permute-start.25 = (bf16[128,512]{1,0:T(8,128)(2,1)S(1)}, bf16[128,512]{1,0:T(8,128)(2,1)S(1)}, u32[]{:S(2)}, u32[]{:S(2)}) collective-permute-start(bf16[128,512]{1,0:T(8,128)(2,1)S(1)} %get-tuple-element.59), channel_id=1, source_target_pairs={{0,2},{1,3},{2,4},{3,5},{4,6},{5,7},{6,0},{7,1},{8,10},{9,11},{10,... | collective-permute-start | bytes 393224 | tf_op jit(solution)/shard_map/ppermute | solution.py:448
  151.8 6.7 %collective-permute-start.27 = (bf16[128,512]{1,0:T(8,128)(2,1)S(1)}, bf16[128,512]{1,0:T(8,128)(2,1)S(1)}, u32[]{:S(2)}, u32[]{:S(2)}) collective-permute-start(bf16[128,512]{1,0:T(8,128)(2,1)S(1)} %get-tuple-element.60), channel_id=1, source_target_pairs={{0,6},{1,7},{2,0},{3,1},{4,2},{5,3},{6,4},{7,5},{8,14},{9,15},{10,... | collective-permute-start | bytes 393224 | tf_op jit(solution)/shard_map/ppermute | solution.py:449
  154.4 10.8 %collective-permute-start.23 = (bf16[256,512]{1,0:T(8,128)(2,1)S(1)}, bf16[256,512]{1,0:T(8,128)(2,1)S(1)}, u32[]{:S(2)}, u32[]{:S(2)}) collective-permute-start(bf16[256,512]{1,0:T(8,128)(2,1)S(1)} %pad_maximum_fusion.2), channel_id=1, source_target_pairs={{0,6},{1,7},{2,0},{3,1},{4,2},{5,3},{6,4},{7,5},{8,14},{9,15},{10,... | collective-permute-start | bytes 786440 | tf_op jit(solution)/shard_map/ppermute | solution.py:456
  155.5 9.6 %collective-permute-start.21 = (bf16[256,512]{1,0:T(8,128)(2,1)S(1)}, bf16[256,512]{1,0:T(8,128)(2,1)S(1)}, u32[]{:S(2)}, u32[]{:S(2)}) collective-permute-start(bf16[256,512]{1,0:T(8,128)(2,1)S(1)} %pad_maximum_fusion.1), channel_id=1, source_target_pairs={{0,2},{1,3},{2,4},{3,5},{4,6},{5,7},{6,0},{7,1},{8,10},{9,11},{10,... | collective-permute-start | bytes 786440 | tf_op jit(solution)/shard_map/ppermute | solution.py:456
  158.6 10.6 %collective-permute-start.28 = (bf16[256,512]{1,0:T(8,128)(2,1)S(1)}, bf16[256,512]{1,0:T(8,128)(2,1)S(1)}, u32[]{:S(2)}, u32[]{:S(2)}) collective-permute-start(bf16[256,512]{1,0:T(8,128)(2,1)S(1)} %pad_maximum_fusion.4), channel_id=1, source_target_pairs={{0,6},{1,7},{2,0},{3,1},{4,2},{5,3},{6,4},{7,5},{8,14},{9,15},{10,... | collective-permute-start | bytes 786440 | tf_op jit(solution)/shard_map/ppermute | solution.py:456
  158.7 10.5 %collective-permute-start.26 = (bf16[256,512]{1,0:T(8,128)(2,1)S(1)}, bf16[256,512]{1,0:T(8,128)(2,1)S(1)}, u32[]{:S(2)}, u32[]{:S(2)}) collective-permute-start(bf16[256,512]{1,0:T(8,128)(2,1)S(1)} %pad_maximum_fusion.3), channel_id=1, source_target_pairs={{0,2},{1,3},{2,4},{3,5},{4,6},{5,7},{6,0},{7,1},{8,10},{9,11},{10,... | collective-permute-start | bytes 786440 | tf_op jit(solution)/shard_map/ppermute | solution.py:456
  (15 other events, 188.8 us)

commit v4 on v3

--- a/solution.py
+++ b/solution.py
@@ -136,9 +136,11 @@
 
 
 def absorb(heads, view, masked, steps, read):
-    @pl.loop(0, masked)
-    def _(step):
-        fixed(heads, view, *read(step, True))
+    if masked is not None:
+
+        @pl.loop(0, masked)
+        def _(step):
+            fixed(heads, view, *read(step, True))
 
     @pl.loop(0, steps)
     def _(step):
@@ -209,18 +211,47 @@
     absorb_again(acc_ref, view, start, tiles + part, read)
 
 
+def early_kernel(
+    place_ref, q_ref, below_a, above_b, acc_in, peak_in, acc_ref, peak_ref, bank_ref, carried_ref,
+    sems,
+):
+    y, heads = place_ref[0] // WIDE, acc_ref.shape[0]
+    steps = jnp.where(y == 3, 2, jnp.minimum(y, 1))
+    sources = (peak_in, peak_ref), (below_a, bank_ref.at[pl.ds(0, STEP)]), (
+        above_b,
+        bank_ref.at[pl.ds(STEP, STEP)],
+    )
+    copies = [
+        pltpu.make_async_copy(source, target, sems.at[at])
+        for at, (source, target) in enumerate((*sources, (acc_in, carried_ref)))
+    ]
+    for copy in copies:
+        copy.start()
+    acc_ref[...] = jnp.zeros_like(acc_ref)
+    view = head_view(q_ref, acc_ref, peak_ref)
+
+    def start(h):
+        acc_ref[h] = carried_ref[h]
+
+    def read(tile):
+        return *tile_of(bank_ref, tile * TILE, TILE), None
+
+    for copy in copies[:3]:
+        copy.wait()
+    absorb(heads, view, None, steps, lambda at, _: (*tile_of(bank_ref, at * STEP, STEP), None))
+    copies[3].wait()
+    acc_ref[...] += carried_ref[...]
+    absorb_again(acc_ref, view, start, steps * (STEP // TILE), read)
+
+
 def rest_kernel(
-    place_ref, q_ref, rest_ref, row_ref, below_a, below_b, above_a, above_b, below2_ref,
-    above2_ref, weight_ref, acc_in, peak_in, *refs,
+    place_ref, q_ref, rest_ref, row_a, below_a, below_b, above_a, below2_ref, above2_ref,
+    weight_ref, acc_in, peak_in, *refs,
 ):
-    outs, (bank_ref, w_ref, bias_ref, acc_ref, carried_ref, peak_ref, att_ref, sems) = (
-        refs[:-8],
-        refs[-8:],
-    )
+    outs, made = refs[:4], refs[4:8]
+    bank_ref, w_ref, bias_ref, acc_ref, carried_ref, peak_ref, att_ref, sems, out_sems = refs[8:]
     mine, used = place_ref[0], place_ref[1]
     y, heads = mine // WIDE, acc_ref.shape[0]
-    span = WIDE * KEEP
-    part, row_steps = span // 2, span // STEP
     copies = []
 
     def copy(source, at, rows, condition, step):
@@ -228,17 +259,12 @@
         one = pltpu.make_async_copy(source, target, sems.at[len(copies)])
         copies.append((one, condition, step))
 
-    for row, ref in enumerate((row_ref, below_a, below2_ref, above_a)):
+    for row, ref in enumerate((row_a, below_a, below2_ref, above_a)):
         copy(ref.at[pl.ds(0, KEEP)], 0, KEEP, (mine > 0) & (y == row), None)
-    at, step = TILE, 0
-    for condition, first, second in (
-        (y > 0, below_a, below_b),
-        (y > 1, below2_ref, above2_ref),
-        (y == 3, above_a, above_b),
+    for step, (ref, condition) in enumerate(
+        ((below_b, y > 0), (below2_ref, y > 1), (above2_ref, y > 1), (above_a, y == 3))
     ):
-        copy(first, at, part, condition, step)
-        copy(second, at + part, part, condition, step)
-        at, step = at + span, step + row_steps
+        copy(ref, TILE + step * STEP, STEP, condition, step)
     for one, condition, _ in copies:
         pl.when(condition)(one.start)
     whole = [
@@ -276,10 +302,11 @@
 
     masked = jnp.where(mine > 0, 1, 0)
     whole[0].wait()
-    absorb(heads, view, masked, row_steps * y, read_fast)
+    steps = jnp.where(y == 3, 4, jnp.where(y == 2, 3, y))
+    absorb(heads, view, masked, steps, read_fast)
     whole[1].wait()
     acc_ref[...] += carried_ref[...]
-    absorb_again(acc_ref, view, start, masked + span // TILE * y, read)
+    absorb_again(acc_ref, view, start, masked + STEP // TILE * steps, read)
     for h in range(heads):
         att_ref[:, h * HEAD : (h + 1) * HEAD] = (
             acc_ref[h, :, :HEAD] / acc_ref[h, :, HEAD:]
@@ -288,14 +315,22 @@
     chips, rows, columns = outs[0].shape
     chip, core = place_ref[2], place_ref[3]
 
+    def written(at, step):
+        return pltpu.make_async_copy(made[at].at[step], outs[at].at[step], out_sems.at[at])
+
     @pl.loop(0, chips)
     def _(step):
-        at = lax.rem(chip + step, chips) * 2
+        column = lax.rem(chip + step, chips) * 2
         for first, side in enumerate((core, 1 - core)):
-            start = pl.multiple_of((at + side) * columns, columns)
+            start = pl.multiple_of((column + side) * columns, columns)
             product = dot(att_ref[...], w_ref[:, pl.ds(start, columns)]).astype(jnp.bfloat16)
-            for part, ref in enumerate(outs[first::2]):
-                ref[step] = product[part * rows : (part + 1) * rows]
+            for part in range(2):
+                made[2 * part + first][step] = product[part * rows : (part + 1) * rows]
+        for at in range(4):
+            written(at, step).start()
+
+    for at in range(4):
+        pltpu.make_async_copy(made[at], outs[at], out_sems.at[at]).wait()
 
 
 def pack_row_kernel(place_ref, *refs):
@@ -357,19 +392,39 @@
     )(place, queries, keys, values, row_a, row_b)
 
 
-def rest_rows(place, queries, rest, banks, weight, state, parts, chips):
+def early_rows(place, queries, below_a, above_b, state):
     length, width = queries.shape
-    heads = width // HEAD
-    keys = TILE + 3 * WIDE * KEEP
     whole = lambda x: pl.BlockSpec(x.shape, lambda i: (0,) * len(x.shape))
-    out = jax.ShapeDtypeStruct((chips, length // parts, weight.shape[1] // chips // 2), jnp.bfloat16)
+    return pl.pallas_call(
+        early_kernel,
+        grid=(1,),
+        out_shape=state_of(length, width // HEAD),
+        in_specs=[SMEM, whole(queries), *[ANY] * 4],
+        out_specs=[whole(x) for x in state],
+        scratch_shapes=[
+            pltpu.VMEM((2 * STEP, 2 * HEAD), jnp.bfloat16),
+            pltpu.VMEM(state[0].shape, jnp.float32),
+            pltpu.SemaphoreType.DMA((4,)),
+        ],
+        compiler_params=PARAMS,
+        cost_estimate=cost(length * width // HEAD, 2 * STEP),
+        name="early_rows",
+    )(place, queries, below_a, above_b, *state)
+
+
+def rest_rows(place, queries, rest, banks, weight, state, chips):
+    length, width = queries.shape
+    heads, keys = width // HEAD, TILE + 4 * STEP
+    whole = lambda x: pl.BlockSpec(x.shape, lambda i: (0,) * len(x.shape))
+    out = jax.ShapeDtypeStruct((chips, length // 2, weight.shape[1] // chips // 2), jnp.bfloat16)
     return pl.pallas_call(
         rest_kernel,
         grid=(1,),
-        out_shape=[out] * (2 * parts),
+        out_shape=[out] * 4,
         in_specs=[SMEM, whole(queries), whole(rest), *[ANY] * (len(banks) + 3)],
-        out_specs=[whole(out)] * (2 * parts),
+        out_specs=[ANY] * 4,
         scratch_shapes=[
+            *[pltpu.VMEM(out.shape, out.dtype)] * 4,
             pltpu.VMEM((keys, 2 * HEAD), jnp.bfloat16),
             pltpu.VMEM(weight.shape, weight.dtype),
             pltpu.VMEM((2, 8, TILE), jnp.float32),
@@ -377,16 +432,58 @@
             pltpu.VMEM((heads, length, 2 * HEAD), jnp.float32),
             pltpu.VMEM((heads, length, HEAD), jnp.float32),
             pltpu.VMEM((length, width), jnp.bfloat16),
-            pltpu.SemaphoreType.DMA((13,)),
+            pltpu.SemaphoreType.DMA((11,)),
+            pltpu.SemaphoreType.DMA((4,)),
         ],
-        compiler_params=PARAMS,
+        compiler_params=pltpu.CompilerParams(vmem_limit_bytes=44 * 2**20),
         cost_estimate=cost(length * heads, keys),
         name="rest_rows",
     )(place, queries, rest, *banks, weight, *state)
 
 
-def added(*terms):
-    return sum(term.astype(jnp.float32) for term in terms).astype(jnp.bfloat16)
+def summed(*refs):
+    return sum(ref[...].astype(jnp.float32) for ref in refs)
+
+
+def cross_kernel(own_ref, other_ref, upper_ref, lower_ref):
+    total = summed(own_ref, other_ref).astype(jnp.bfloat16)
+    half = upper_ref.shape[0]
+    upper_ref[...] = total[:half]
+    lower_ref[...] = total[half:]
+
+
+def turn_kernel(own1, other1, own3, other3, below_ref, above_ref, up_ref, down_ref):
+    half = below_ref.shape[0]
+    up, down = summed(own1, other1), summed(own3, other3)
+    up_ref[:half] = (up[:half] + summed(below_ref)).astype(jnp.bfloat16)
+    up_ref[half:] = up[half:].astype(jnp.bfloat16)
+    down_ref[:half] = down[:half].astype(jnp.bfloat16)
+    down_ref[half:] = (down[half:] + summed(above_ref)).astype(jnp.bfloat16)
+
+
+def finish_kernel(own_ref, other_ref, up_ref, down_ref, *refs):
+    refs[-1][...] = summed(own_ref, other_ref, up_ref, down_ref).astype(jnp.bfloat16)
+
+
+def small_call(kernel, name, args, chunks, shapes, out_specs=None, **more):
+    specs = [
+        pl.BlockSpec(x.shape, lambda i: (0, 0))
+        if chunk is None
+        else pl.BlockSpec((None, *x.shape[1:]), lambda i, chunk=chunk: (chunk, 0, 0))
+        for x, chunk in zip(args, chunks)
+    ]
+    if out_specs is None:
+        out_specs = [pl.BlockSpec(shape, lambda i: (0, 0)) for shape in shapes]
+    return pl.pallas_call(
+        kernel,
+        grid=(1,),
+        out_shape=[jax.ShapeDtypeStruct(shape, jnp.bfloat16) for shape in shapes],
+        in_specs=specs + more.pop("extra", []),
+        out_specs=out_specs,
+        compiler_params=pltpu.CompilerParams(vmem_limit_bytes=8 * 2**20),
+        name=name,
+        **more,
+    )
 
 
 def on_device(queries, key_rows, value_rows, kept_positions, anchor_length, output_weight):
@@ -429,33 +526,37 @@
     rest, ends = lax.optimization_barrier((rest, ends))
     spread = lambda hops: [(r * WIDE + a, r * WIDE + b) for a, b in hops for r in range(tall)]
     rest = rest + permute(rest, spread([(0, 4)]))
-    rest, below_a, above_b = lax.optimization_barrier((rest, below_a, above_b))
+    state = own_row(place, queries, key_rows, value_rows, *ends)
+    rest, below_a, above_b, state = lax.optimization_barrier((rest, below_a, above_b, state))
     below2 = permute(below_a, across([(1, 2), (2, 3)]))
     above2 = permute(above_b, across([(0, 3), (3, 2)]))
     rest = rest + permute(rest, spread([(0, 2), (4, 6)]))
     rest = rest + permute(rest, spread([(0, 1), (2, 3), (4, 5), (6, 7)]))
 
-    parts = 2
-    state = own_row(place, queries, key_rows, value_rows, *ends)
-    banks = (ends[0], below_a, below_b, above_a, above_b, below2, above2)
-
-    outs = []
-    half = length // parts // 2
-    terms = rest_rows(place, queries, rest, banks, output_weight, state, parts, chips)
+    state = early_rows(place, queries, below_a, above_b, state)
+    banks = (ends[0], below_a, below_b, above_a, below2, above2)
+    terms = rest_rows(place, queries, rest, banks, output_weight, state, chips)
     others = [lax.ppermute(send, "head", swap) for send in terms[1::2]]
-    for own, other in zip(terms[::2], others):
-        across_x = added(own[2], other[2])
-        from_below = lax.ppermute(across_x[:half], "head", up)
-        from_above = lax.ppermute(across_x[half:], "head", down)
-        upward = jnp.concatenate(
-            [added(own[1, :half], other[1, :half], from_below), added(own[1, half:], other[1, half:])]
-        )
-        downward = jnp.concatenate(
-            [added(own[3, :half], other[3, :half]), added(own[3, half:], other[3, half:], from_above)]
-        )
+
+    rows, columns = terms[0].shape[1:]
+    shape, half = (rows, columns), (rows // 2, columns)
+    out = None
+    for part, (own, other) in enumerate(zip(terms[::2], others)):
+        pair = (own, other)
+        upper, lower = small_call(cross_kernel, "cross", pair, (2, 2), [half, half])(*pair)
+        below, above = lax.ppermute(upper, "head", up), lax.ppermute(lower, "head", down)
+        args = (own, other, own, other, below, above)
+        upward, downward = small_call(
+            turn_kernel, "turn", args, (1, 1, 3, 3, None, None), [shape, shape]
+        )(*args)
         upward, downward = lax.ppermute(upward, "head", up), lax.ppermute(downward, "head", down)
-        outs.append(added(own[0], other[0], upward, downward))
-    return jnp.concatenate(outs)
+        args = (own, other, upward, downward)
+        extra = {} if out is None else dict(extra=[ANY], input_output_aliases={4: 0})
+        (out,) = small_call(
+            finish_kernel, f"finish_{part}", args, (0, 0, None, None), [(length, columns)],
+            [pl.BlockSpec(shape, lambda i, part=part: (part, 0))], **extra,
+        )(*args, *([] if out is None else [out]))
+    return out
 
 
 def solution(mesh):

time: 173 us -> 161 us (0.931)
  the two profiles are of different devices: /device:TPU:30 before, /device:TPU:254 now
where the time goes in v4:
time: 161 us; the launch traced here: 160 us
  Pallas kernels  68.5 us (43%)
  waiting for transfers between devices  49.7 us (31%)
  starting transfers between devices  37.7 us (23%)
  local copies, waits for them, and re-layouts  3.21 us (2%)
    pallas_call x1, Pallas kernels, rest_rows(): pl.pallas_call(rest_kernel, grid=(1,), out_shape=[out] * 4, in_specs=[SME...  43.7 us
    ppermute x19, waiting for transfers between devices, on_device(): permute = lambda x, pairs: lax.ppermute(x, 'ctx', pairs)  35.5 us
    ppermute x19, starting transfers between devices, on_device(): permute = lambda x, pairs: lax.ppermute(x, 'ctx', pairs)  28.7 us
    pallas_call x1, Pallas kernels, own_row(): pl.pallas_call(own_row_kernel, grid=(1,), out_shape=state, in_specs=[SMEM...  10.1 us
    pallas_call x1, Pallas kernels, early_rows(): pl.pallas_call(early_kernel, grid=(1,), out_shape=state_of(length, width...  9.39 us
    ppermute x2, waiting for transfers between devices, on_device(): lax.ppermute(upward, 'head', up)  4.4 us
    ppermute x2, waiting for transfers between devices, on_device(): lax.ppermute(downward, 'head', down)  4.1 us
    ppermute x2, starting transfers between devices, on_device(): lax.ppermute(upward, 'head', up)  3.3 us
  transfers between devices with their start and end apart: 29, of which 16 were waited for; matrix products, arithmetic and copies ran while one was open for 0% of the time, Pallas kernels for 13%

profile of v4, /device:TPU:254, one launch (start us, length us, event | category | flops | bytes accessed | tf_op | source)
XLA Modules:
  0.0 160.4 jit_solution(14531591456188103537)
XLA Ops:
  0.7 2.4 %select_kept.1 = (bf16[256,256]{1,0:T(8,128)(2,1)}, bf16[272,256]{1,0:T(8,128)(2,1)}) custom-call(s32[1]{0:T(128)S(6)} %copy.9.used_ref, s32[1,256]{1,0:T(1,128)} %refs_0_.1, bf16[512,128]{1,0:T(8,128)(2,1)} %k_ref.1, bf16[512,128]{1,0:T(8,128)(2,1)} %v_ref.1), custom_call_target="tpu_custom_call" | custom-call | tf_op jit(solution)/shard_map/select_kept/pallas_call | solution.py:77
  4.9 2.2 %collective-permute-start = (bf16[256,256]{1,0:T(8,128)(2,1)}, bf16[256,256]{1,0:T(8,128)(2,1)S(1)}, u32[]{:S(2)}, u32[]{:S(2)}) collective-permute-start(bf16[256,256]{1,0:T(8,128)(2,1)} %get-tuple-element.39.refs_8_), channel_id=1, source_target_pairs={{0,8},{8,16},{16,24},{24,32},{32,40},{40,48},{48,56},{56,0},{64,72... | collective-permute-start | bytes 393224 | tf_op jit(solution)/shard_map/ppermute | solution.py:501
  7.1 3.4 %collective-permute-done.1.refs_0_ = bf16[256,256]{1,0:T(8,128)(2,1)S(1)} collective-permute-done((bf16[256,256]{1,0:T(8,128)(2,1)}, bf16[256,256]{1,0:T(8,128)(2,1)S(1)}, u32[]{:S(2)}, u32[]{:S(2)}) %collective-permute-start.1) | collective-permute-done | bytes 131104 | tf_op jit(solution)/shard_map/ppermute | solution.py:501
  11.2 3.7 %collective-permute-start.3 = (bf16[256,256]{1,0:T(8,128)(2,1)S(1)}, bf16[256,256]{1,0:T(8,128)(2,1)S(1)}, u32[]{:S(2)}, u32[]{:S(2)}) collective-permute-start(bf16[256,256]{1,0:T(8,128)(2,1)S(1)} %collective-permute-done.refs_7_), channel_id=1, source_target_pairs={{0,8},{8,16},{16,24},{24,32},{32,40},{40,48},{48,56},{56,0},{64,72... | collective-permute-start | bytes 393224 | tf_op jit(solution)/shard_map/ppermute | solution.py:501
  14.9 2.5 %collective-permute-done.3.refs_6_ = bf16[256,256]{1,0:T(8,128)(2,1)S(1)} collective-permute-done((bf16[256,256]{1,0:T(8,128)(2,1)S(1)}, bf16[256,256]{1,0:T(8,128)(2,1)S(1)}, u32[]{:S(2)}, u32[]{:S(2)}) %collective-permute-start.3) | collective-permute-done | bytes 131104 | tf_op jit(solution)/shard_map/ppermute | solution.py:501
  17.4 3.7 %collective-permute-done.4.refs_1_ = bf16[256,256]{1,0:T(8,128)(2,1)S(1)} collective-permute-done((bf16[256,256]{1,0:T(8,128)(2,1)S(1)}, bf16[256,256]{1,0:T(8,128)(2,1)S(1)}, u32[]{:S(2)}, u32[]{:S(2)}) %collective-permute-start.4) | collective-permute-done | bytes 131104 | tf_op jit(solution)/shard_map/ppermute | solution.py:501
  21.1 3.2 %collective-permute-start.7 = (bf16[256,256]{1,0:T(8,128)(2,1)S(1)}, bf16[256,256]{1,0:T(8,128)(2,1)S(1)}, u32[]{:S(2)}, u32[]{:S(2)}) collective-permute-start(bf16[256,256]{1,0:T(8,128)(2,1)S(1)} %collective-permute-done.3.refs_6_), channel_id=1, source_target_pairs={{0,8},{8,16},{16,24},{24,32},{32,40},{40,48},{48,56},{56,0},{64,72... | collective-permute-start | bytes 393224 | tf_op jit(solution)/shard_map/ppermute | solution.py:501
  24.3 3.3 %collective-permute-done.6.refs_2_ = bf16[256,256]{1,0:T(8,128)(2,1)S(1)} collective-permute-done((bf16[256,256]{1,0:T(8,128)(2,1)S(1)}, bf16[256,256]{1,0:T(8,128)(2,1)S(1)}, u32[]{:S(2)}, u32[]{:S(2)}) %collective-permute-start.6) | collective-permute-done | bytes 131104 | tf_op jit(solution)/shard_map/ppermute | solution.py:501
  27.6 3.4 %collective-permute-start.8 = (bf16[128,256]{1,0:T(8,128)(2,1)S(1)}, bf16[128,256]{1,0:T(8,128)(2,1)S(1)}, u32[]{:S(2)}, u32[]{:S(2)}) collective-permute-start(bf16[128,256]{1,0:T(8,128)(2,1)S(1)} %slice.8), channel_id=1, source_target_pairs={{0,8},{8,16},{16,24},{24,32},{32,40},{40,48},{48,56},{56,0},{64,72... | collective-permute-start | bytes 196616 | tf_op jit(solution)/shard_map/ppermute | solution.py:501
  31.1 1.9 %collective-permute-done.9.refs_4_ = bf16[128,256]{1,0:T(8,128)(2,1)S(1)} collective-permute-done((bf16[128,256]{1,0:T(8,128)(2,1)S(1)}, bf16[128,256]{1,0:T(8,128)(2,1)S(1)}, u32[]{:S(2)}, u32[]{:S(2)}) %collective-permute-start.9) | collective-permute-done | bytes 65568 | tf_op jit(solution)/shard_map/ppermute | solution.py:501
  38.0 10.1 %own_row.1 = (f32[4,512,256]{2,1,0:T(8,128)}, f32[4,512,128]{2,1,0:T(8,128)}) custom-call(s32[4]{0:T(128)} %copy-done.1, bf16[512,512]{1,0:T(8,128)(2,1)} %q_ref.5, bf16[512,128]{1,0:T(8,128)(2,1)} %k_ref.1, bf16[512,128]{1,0:T(8,128)(2,1)} %v_ref.1, bf16[1024,256]{1,0:T(8,128)(2,1)} %copy-done.4, bf16[1024,256]{1,0:T(8,128)(2,1)} %copy-done.8), custom_call_target="tpu_custom_call" | custom-call | flops 5368709120 | bytes 8388608 | tf_op jit(solution)/shard_map/own_row/pallas_call | solution.py:378
  48.2 1.9 %collective-permute-done.12.above_b = bf16[1024,256]{1,0:T(8,128)(2,1)} collective-permute-done((bf16[1024,256]{1,0:T(8,128)(2,1)S(1)}, bf16[1024,256]{1,0:T(8,128)(2,1)}, u32[]{:S(2)}, u32[]{:S(2)}) %collective-permute-start.12) | collective-permute-done | bytes 524320 | tf_op jit(solution)/shard_map/ppermute | solution.py:501
  53.4 4.5 %collective-permute-start.18 = (bf16[1024,256]{1,0:T(8,128)(2,1)}, bf16[1024,256]{1,0:T(8,128)(2,1)S(1)}, u32[]{:S(2)}, u32[]{:S(2)}) collective-permute-start(bf16[1024,256]{1,0:T(8,128)(2,1)} %collective-permute-done.12.above_b), channel_id=1, source_target_pairs={{0,192},{8,200},{16,208},{24,216},{32,224},{40,232},{48,240},{56,2... | collective-permute-start | bytes 1572872 | tf_op jit(solution)/shard_map/ppermute | solution.py:501
  60.8 9.4 %early_rows.1 = (f32[4,512,256]{2,1,0:T(8,128)}, f32[4,512,128]{2,1,0:T(8,128)}) custom-call(s32[4]{0:T(128)} %copy-done.1, bf16[512,512]{1,0:T(8,128)(2,1)} %q_ref.5, bf16[1024,256]{1,0:T(8,128)(2,1)} %copy-done.6, bf16[1024,256]{1,0:T(8,128)(2,1)} %collective-permute-done.12.above_b, f32[4,512,256]{2,1,0:T(8,128)} %get-tuple-element.57.acc_in, ...), custom_call_target="tpu_custom_call" | custom-call | flops 4294967296 | bytes 8388608 | tf_op jit(solution)/shard_map/early_rows/pallas_call | solution.py:398
  70.3 13.2 %collective-permute-done.16.above_a = bf16[1024,256]{1,0:T(8,128)(2,1)S(1)} collective-permute-done((bf16[1024,256]{1,0:T(8,128)(2,1)}, bf16[1024,256]{1,0:T(8,128)(2,1)S(1)}, u32[]{:S(2)}, u32[]{:S(2)}) %collective-permute-start.16) | collective-permute-done | bytes 524320 | tf_op jit(solution)/shard_map/ppermute | solution.py:501
  83.5 5.6 %collective-permute-done.18.above2_ref = bf16[1024,256]{1,0:T(8,128)(2,1)S(1)} collective-permute-done((bf16[1024,256]{1,0:T(8,128)(2,1)}, bf16[1024,256]{1,0:T(8,128)(2,1)S(1)}, u32[]{:S(2)}, u32[]{:S(2)}) %collective-permute-start.18) | collective-permute-done | bytes 524320 | tf_op jit(solution)/shard_map/ppermute | solution.py:501
  91.4 43.7 %rest_rows.1 = (bf16[4,256,512]{2,1,0:T(8,128)(2,1)S(1)}, bf16[4,256,512]{2,1,0:T(8,128)(2,1)S(1)}, bf16[4,256,512]{2,1,0:T(8,128)(2,1)S(1)}, bf16[4,256,512]{2,1,0:T(8,128)(2,1)S(1)}) custom-call(s32[4]{0:T(128)S(1)} %copy-done.2, bf16[512,512]{1,0:T(8,128)(2,1)S(1)} %copy-done.3, bf16[272,256]{1,0:T(8,128)(2,1)S(1)} %add.25.rest_ref, ...), custom_call_target="tpu_custom_call" | custom-call | flops 9663676416 | bytes 8388608 | tf_op jit(solution)/shard_map/rest_rows/pallas_call | solution.py:420
  135.6 2.1 %collective-permute-done.24.other_ref.other1.other3 = bf16[4,256,512]{2,1,0:T(8,128)(2,1)S(1)} collective-permute-done((bf16[4,256,512]{2,1,0:T(8,128)(2,1)S(1)}, bf16[4,256,512]{2,1,0:T(8,128)(2,1)S(1)}, u32[]{:S(2)}, u32[]{:S(2)}) %collective-permute-start.24) | collective-permute-done | bytes 1048608 | tf_op jit(solution)/shard_map/ppermute | solution.py:539
  140.0 1.8 %collective-permute-start.20 = (bf16[128,512]{1,0:T(8,128)(2,1)S(1)}, bf16[128,512]{1,0:T(8,128)(2,1)S(1)}, u32[]{:S(2)}, u32[]{:S(2)}) collective-permute-start(bf16[128,512]{1,0:T(8,128)(2,1)S(1)} %get-tuple-element.63), channel_id=1, source_target_pairs={{0,2},{1,3},{2,4},{3,5},{4,6},{5,7},{6,0},{7,1},{8,10},{9,11},{10,... | collective-permute-start | bytes 393224 | tf_op jit(solution)/shard_map/ppermute | solution.py:547
  142.1 2.1 %collective-permute-done.25.below_ref = bf16[128,512]{1,0:T(8,128)(2,1)S(1)} collective-permute-done((bf16[128,512]{1,0:T(8,128)(2,1)S(1)}, bf16[128,512]{1,0:T(8,128)(2,1)S(1)}, u32[]{:S(2)}, u32[]{:S(2)}) %collective-permute-start.25) | collective-permute-done | bytes 131104 | tf_op jit(solution)/shard_map/ppermute | solution.py:547
  148.1 1.8 %collective-permute-start.22 = (bf16[256,512]{1,0:T(8,128)(2,1)S(1)}, bf16[256,512]{1,0:T(8,128)(2,1)S(1)}, u32[]{:S(2)}, u32[]{:S(2)}) collective-permute-start(bf16[256,512]{1,0:T(8,128)(2,1)S(1)} %get-tuple-element.65), channel_id=1, source_target_pairs={{0,2},{1,3},{2,4},{3,5},{4,6},{5,7},{6,0},{7,1},{8,10},{9,11},{10,... | collective-permute-start | bytes 786440 | tf_op jit(solution)/shard_map/ppermute | solution.py:552
  150.2 4.1 %collective-permute-done.27.up_ref = bf16[256,512]{1,0:T(8,128)(2,1)S(1)} collective-permute-done((bf16[256,512]{1,0:T(8,128)(2,1)S(1)}, bf16[256,512]{1,0:T(8,128)(2,1)S(1)}, u32[]{:S(2)}, u32[]{:S(2)}) %collective-permute-start.27) | collective-permute-done | bytes 262176 | tf_op jit(solution)/shard_map/ppermute | solution.py:552
  154.3 2.4 %collective-permute-done.28.down_ref = bf16[256,512]{1,0:T(8,128)(2,1)S(1)} collective-permute-done((bf16[256,512]{1,0:T(8,128)(2,1)S(1)}, bf16[256,512]{1,0:T(8,128)(2,1)S(1)}, u32[]{:S(2)}, u32[]{:S(2)}) %collective-permute-start.28) | collective-permute-done | bytes 262176 | tf_op jit(solution)/shard_map/ppermute | solution.py:552
  157.9 1.7 %collective-permute-done.23.down_ref = bf16[256,512]{1,0:T(8,128)(2,1)S(1)} collective-permute-done((bf16[256,512]{1,0:T(8,128)(2,1)S(1)}, bf16[256,512]{1,0:T(8,128)(2,1)S(1)}, u32[]{:S(2)}, u32[]{:S(2)}) %collective-permute-start.23) | collective-permute-done | bytes 262176 | tf_op jit(solution)/shard_map/ppermute | solution.py:552
  (74 shorter events, 25.1 us)
Async XLA Ops:
  3.8 6.7 %collective-permute-start.1 = (bf16[256,256]{1,0:T(8,128)(2,1)}, bf16[256,256]{1,0:T(8,128)(2,1)S(1)}, u32[]{:S(2)}, u32[]{:S(2)}) collective-permute-start(bf16[256,256]{1,0:T(8,128)(2,1)} %get-tuple-element.39.refs_8_), channel_id=1, source_target_pairs={{0,56},{8,0},{16,8},{24,16},{32,24},{40,32},{48,40},{56,48},{64,12... | collective-permute-start | bytes 393224 | tf_op jit(solution)/shard_map/ppermute | solution.py:501
  4.9 5.7 %collective-permute-start = (bf16[256,256]{1,0:T(8,128)(2,1)}, bf16[256,256]{1,0:T(8,128)(2,1)S(1)}, u32[]{:S(2)}, u32[]{:S(2)}) collective-permute-start(bf16[256,256]{1,0:T(8,128)(2,1)} %get-tuple-element.39.refs_8_), channel_id=1, source_target_pairs={{0,8},{8,16},{16,24},{24,32},{32,40},{40,48},{48,56},{56,0},{64,72... | collective-permute-start | bytes 393224 | tf_op jit(solution)/shard_map/ppermute | solution.py:501
  11.2 6.2 %collective-permute-start.3 = (bf16[256,256]{1,0:T(8,128)(2,1)S(1)}, bf16[256,256]{1,0:T(8,128)(2,1)S(1)}, u32[]{:S(2)}, u32[]{:S(2)}) collective-permute-start(bf16[256,256]{1,0:T(8,128)(2,1)S(1)} %collective-permute-done.refs_7_), channel_id=1, source_target_pairs={{0,8},{8,16},{16,24},{24,32},{32,40},{40,48},{48,56},{56,0},{64,72... | collective-permute-start | bytes 393224 | tf_op jit(solution)/shard_map/ppermute | solution.py:501
  14.9 6.2 %collective-permute-start.4 = (bf16[256,256]{1,0:T(8,128)(2,1)S(1)}, bf16[256,256]{1,0:T(8,128)(2,1)S(1)}, u32[]{:S(2)}, u32[]{:S(2)}) collective-permute-start(bf16[256,256]{1,0:T(8,128)(2,1)S(1)} %collective-permute-done.1.refs_0_), channel_id=1, source_target_pairs={{0,56},{8,0},{16,8},{24,16},{32,24},{40,32},{48,40},{56,48},{64,12... | collective-permute-start | bytes 393224 | tf_op jit(solution)/shard_map/ppermute | solution.py:501
  21.1 6.5 %collective-permute-start.6 = (bf16[256,256]{1,0:T(8,128)(2,1)S(1)}, bf16[256,256]{1,0:T(8,128)(2,1)S(1)}, u32[]{:S(2)}, u32[]{:S(2)}) collective-permute-start(bf16[256,256]{1,0:T(8,128)(2,1)S(1)} %collective-permute-done.4.refs_1_), channel_id=1, source_target_pairs={{0,56},{8,0},{16,8},{24,16},{32,24},{40,32},{48,40},{56,48},{64,12... | collective-permute-start | bytes 393224 | tf_op jit(solution)/shard_map/ppermute | solution.py:501
  21.1 6.5 %collective-permute-start.7 = (bf16[256,256]{1,0:T(8,128)(2,1)S(1)}, bf16[256,256]{1,0:T(8,128)(2,1)S(1)}, u32[]{:S(2)}, u32[]{:S(2)}) collective-permute-start(bf16[256,256]{1,0:T(8,128)(2,1)S(1)} %collective-permute-done.3.refs_6_), channel_id=1, source_target_pairs={{0,8},{8,16},{16,24},{24,32},{32,40},{40,48},{48,56},{56,0},{64,72... | collective-permute-start | bytes 393224 | tf_op jit(solution)/shard_map/ppermute | solution.py:501
  27.6 5.5 %collective-permute-start.9 = (bf16[128,256]{1,0:T(8,128)(2,1)S(1)}, bf16[128,256]{1,0:T(8,128)(2,1)S(1)}, u32[]{:S(2)}, u32[]{:S(2)}) collective-permute-start(bf16[128,256]{1,0:T(8,128)(2,1)S(1)} %slice.9), channel_id=1, source_target_pairs={{0,56},{8,0},{16,8},{24,16},{32,24},{40,32},{48,40},{56,48},{64,12... | collective-permute-start | bytes 196616 | tf_op jit(solution)/shard_map/ppermute | solution.py:501
  34.7 13.5 %collective-permute-start.11 = (bf16[1024,256]{1,0:T(8,128)(2,1)S(1)}, bf16[1024,256]{1,0:T(8,128)(2,1)S(1)}, u32[]{:S(2)}, u32[]{:S(2)}) collective-permute-start(bf16[1024,256]{1,0:T(8,128)(2,1)S(1)} %get-tuple-element.50.row_a), channel_id=1, source_target_pairs={{0,64},{8,72},{16,80},{24,88},{32,96},{40,104},{48,112},{56,120},{... | collective-permute-start | bytes 1572872 | tf_op jit(solution)/shard_map/ppermute | solution.py:501
  36.0 14.1 %collective-permute-start.12 = (bf16[1024,256]{1,0:T(8,128)(2,1)S(1)}, bf16[1024,256]{1,0:T(8,128)(2,1)}, u32[]{:S(2)}, u32[]{:S(2)}) collective-permute-start(bf16[1024,256]{1,0:T(8,128)(2,1)S(1)} %get-tuple-element.51.row_b), channel_id=1, source_target_pairs={{0,192},{8,200},{16,208},{24,216},{32,224},{40,232},{48,240},{56,2... | collective-permute-start | bytes 1572872 | tf_op jit(solution)/shard_map/ppermute | solution.py:501
  37.3 10.8 %collective-permute-start.10 = (bf16[272,256]{1,0:T(8,128)(2,1)S(1)}, bf16[272,256]{1,0:T(8,128)(2,1)S(1)}, u32[]{:S(2)}, u32[]{:S(2)}) collective-permute-start(bf16[272,256]{1,0:T(8,128)(2,1)S(1)} %add.22), channel_id=1, source_target_pairs={{0,32},{64,96},{128,160},{192,224},{1,33},{65,97},{129,161},{193,2... | collective-permute-start | bytes 417800 | tf_op jit(solution)/shard_map/ppermute | solution.py:501
  50.2 9.1 %collective-permute-start.13 = (bf16[272,256]{1,0:T(8,128)(2,1)S(1)}, bf16[272,256]{1,0:T(8,128)(2,1)S(1)}, u32[]{:S(2)}, u32[]{:S(2)}) collective-permute-start(bf16[272,256]{1,0:T(8,128)(2,1)S(1)} %add.23), channel_id=1, source_target_pairs={{0,16},{64,80},{128,144},{192,208},{32,48},{96,112},{160,176},{224... | collective-permute-start | bytes 417800 | tf_op jit(solution)/shard_map/ppermute | solution.py:501
  50.8 32.6 %collective-permute-start.16 = (bf16[1024,256]{1,0:T(8,128)(2,1)}, bf16[1024,256]{1,0:T(8,128)(2,1)S(1)}, u32[]{:S(2)}, u32[]{:S(2)}) collective-permute-start(bf16[1024,256]{1,0:T(8,128)(2,1)} %copy-done.4), channel_id=1, source_target_pairs={{0,192},{8,200},{16,208},{24,216},{32,224},{40,232},{48,240},{56,2... | collective-permute-start | bytes 1572872 | tf_op jit(solution)/shard_map/ppermute | solution.py:501
  52.1 31.3 %collective-permute-start.15 = (bf16[1024,256]{1,0:T(8,128)(2,1)}, bf16[1024,256]{1,0:T(8,128)(2,1)S(1)}, u32[]{:S(2)}, u32[]{:S(2)}) collective-permute-start(bf16[1024,256]{1,0:T(8,128)(2,1)} %copy-done.8), channel_id=1, source_target_pairs={{0,64},{8,72},{16,80},{24,88},{32,96},{40,104},{48,112},{56,120},{... | collective-permute-start | bytes 1572872 | tf_op jit(solution)/shard_map/ppermute | solution.py:501
  53.4 35.6 %collective-permute-start.18 = (bf16[1024,256]{1,0:T(8,128)(2,1)}, bf16[1024,256]{1,0:T(8,128)(2,1)S(1)}, u32[]{:S(2)}, u32[]{:S(2)}) collective-permute-start(bf16[1024,256]{1,0:T(8,128)(2,1)} %collective-permute-done.12.above_b), channel_id=1, source_target_pairs={{0,192},{8,200},{16,208},{24,216},{32,224},{40,232},{48,240},{56,2... | collective-permute-start | bytes 1572872 | tf_op jit(solution)/shard_map/ppermute | solution.py:501
  58.0 31.1 %collective-permute-start.17 = (bf16[1024,256]{1,0:T(8,128)(2,1)S(1)}, bf16[1024,256]{1,0:T(8,128)(2,1)S(1)}, u32[]{:S(2)}, u32[]{:S(2)}) collective-permute-start(bf16[1024,256]{1,0:T(8,128)(2,1)S(1)} %collective-permute-done.11.below_a), channel_id=1, source_target_pairs={{64,128},{72,136},{80,144},{88,152},{96,160},{104,168},{112,176},{... | collective-permute-start | bytes 1572872 | tf_op jit(solution)/shard_map/ppermute | solution.py:501
  59.4 10.8 %collective-permute-start.14 = (bf16[272,256]{1,0:T(8,128)(2,1)S(1)}, bf16[272,256]{1,0:T(8,128)(2,1)S(1)}, u32[]{:S(2)}, u32[]{:S(2)}) collective-permute-start(bf16[272,256]{1,0:T(8,128)(2,1)S(1)} %add.24), channel_id=1, source_target_pairs={{0,8},{64,72},{128,136},{192,200},{16,24},{80,88},{144,152},{208,2... | collective-permute-start | bytes 417800 | tf_op jit(solution)/shard_map/ppermute | solution.py:501
  137.8 6.4 %collective-permute-start.25 = (bf16[128,512]{1,0:T(8,128)(2,1)S(1)}, bf16[128,512]{1,0:T(8,128)(2,1)S(1)}, u32[]{:S(2)}, u32[]{:S(2)}) collective-permute-start(bf16[128,512]{1,0:T(8,128)(2,1)S(1)} %get-tuple-element.69), channel_id=1, source_target_pairs={{0,2},{1,3},{2,4},{3,5},{4,6},{5,7},{6,0},{7,1},{8,10},{9,11},{10,... | collective-permute-start | bytes 393224 | tf_op jit(solution)/shard_map/ppermute | solution.py:547
  138.4 6.5 %collective-permute-start.26 = (bf16[128,512]{1,0:T(8,128)(2,1)S(1)}, bf16[128,512]{1,0:T(8,128)(2,1)S(1)}, u32[]{:S(2)}, u32[]{:S(2)}) collective-permute-start(bf16[128,512]{1,0:T(8,128)(2,1)S(1)} %get-tuple-element.70), channel_id=1, source_target_pairs={{0,6},{1,7},{2,0},{3,1},{4,2},{5,3},{6,4},{7,5},{8,14},{9,15},{10,... | collective-permute-start | bytes 393224 | tf_op jit(solution)/shard_map/ppermute | solution.py:547
  140.0 7.1 %collective-permute-start.20 = (bf16[128,512]{1,0:T(8,128)(2,1)S(1)}, bf16[128,512]{1,0:T(8,128)(2,1)S(1)}, u32[]{:S(2)}, u32[]{:S(2)}) collective-permute-start(bf16[128,512]{1,0:T(8,128)(2,1)S(1)} %get-tuple-element.63), channel_id=1, source_target_pairs={{0,2},{1,3},{2,4},{3,5},{4,6},{5,7},{6,0},{7,1},{8,10},{9,11},{10,... | collective-permute-start | bytes 393224 | tf_op jit(solution)/shard_map/ppermute | solution.py:547
  141.8 6.2 %collective-permute-start.21 = (bf16[128,512]{1,0:T(8,128)(2,1)S(1)}, bf16[128,512]{1,0:T(8,128)(2,1)S(1)}, u32[]{:S(2)}, u32[]{:S(2)}) collective-permute-start(bf16[128,512]{1,0:T(8,128)(2,1)S(1)} %get-tuple-element.64), channel_id=1, source_target_pairs={{0,6},{1,7},{2,0},{3,1},{4,2},{5,3},{6,4},{7,5},{8,14},{9,15},{10,... | collective-permute-start | bytes 393224 | tf_op jit(solution)/shard_map/ppermute | solution.py:547
  145.0 9.3 %collective-permute-start.27 = (bf16[256,512]{1,0:T(8,128)(2,1)S(1)}, bf16[256,512]{1,0:T(8,128)(2,1)S(1)}, u32[]{:S(2)}, u32[]{:S(2)}) collective-permute-start(bf16[256,512]{1,0:T(8,128)(2,1)S(1)} %get-tuple-element.71), channel_id=1, source_target_pairs={{0,2},{1,3},{2,4},{3,5},{4,6},{5,7},{6,0},{7,1},{8,10},{9,11},{10,... | collective-permute-start | bytes 786440 | tf_op jit(solution)/shard_map/ppermute | solution.py:552
  146.5 10.3 %collective-permute-start.28 = (bf16[256,512]{1,0:T(8,128)(2,1)S(1)}, bf16[256,512]{1,0:T(8,128)(2,1)S(1)}, u32[]{:S(2)}, u32[]{:S(2)}) collective-permute-start(bf16[256,512]{1,0:T(8,128)(2,1)S(1)} %get-tuple-element.72), channel_id=1, source_target_pairs={{0,6},{1,7},{2,0},{3,1},{4,2},{5,3},{6,4},{7,5},{8,14},{9,15},{10,... | collective-permute-start | bytes 786440 | tf_op jit(solution)/shard_map/ppermute | solution.py:552
  148.1 9.8 %collective-permute-start.22 = (bf16[256,512]{1,0:T(8,128)(2,1)S(1)}, bf16[256,512]{1,0:T(8,128)(2,1)S(1)}, u32[]{:S(2)}, u32[]{:S(2)}) collective-permute-start(bf16[256,512]{1,0:T(8,128)(2,1)S(1)} %get-tuple-element.65), channel_id=1, source_target_pairs={{0,2},{1,3},{2,4},{3,5},{4,6},{5,7},{6,0},{7,1},{8,10},{9,11},{10,... | collective-permute-start | bytes 786440 | tf_op jit(solution)/shard_map/ppermute | solution.py:552
  150.0 9.6 %collective-permute-start.23 = (bf16[256,512]{1,0:T(8,128)(2,1)S(1)}, bf16[256,512]{1,0:T(8,128)(2,1)S(1)}, u32[]{:S(2)}, u32[]{:S(2)}) collective-permute-start(bf16[256,512]{1,0:T(8,128)(2,1)S(1)} %get-tuple-element.66), channel_id=1, source_target_pairs={{0,6},{1,7},{2,0},{3,1},{4,2},{5,3},{6,4},{7,5},{8,14},{9,15},{10,... | collective-permute-start | bytes 786440 | tf_op jit(solution)/shard_map/ppermute | solution.py:552
  (15 other events, 139.8 us)

commit v5 on v3

--- a/solution.py
+++ b/solution.py
@@ -136,9 +136,11 @@
 
 
 def absorb(heads, view, masked, steps, read):
-    @pl.loop(0, masked)
-    def _(step):
-        fixed(heads, view, *read(step, True))
+    if masked is not None:
+
+        @pl.loop(0, masked)
+        def _(step):
+            fixed(heads, view, *read(step, True))
 
     @pl.loop(0, steps)
     def _(step):
@@ -176,9 +178,14 @@
     return jnp.where(allowed, 0.0, NEGATIVE)
 
 
+def sums(state_ref):
+    return state_ref.at[:, :, pl.ds(0, 2 * HEAD)], state_ref.at[:, :, pl.ds(2 * HEAD, HEAD)]
+
+
 def own_row_kernel(
-    place_ref, q_ref, k_ref, v_ref, row_a, row_b, acc_ref, peak_ref, row_ref, bias_ref, sems
+    place_ref, q_ref, k_ref, v_ref, row_a, row_b, state_ref, row_ref, bias_ref, sems
 ):
+    acc_ref, peak_ref = sums(state_ref)
     keys = place_ref[0] % WIDE * KEEP
     tiles, part = keys // TILE, jnp.where(keys % TILE > 0, 1, 0)
     half = row_a.shape[0]
@@ -209,47 +216,27 @@
     absorb_again(acc_ref, view, start, tiles + part, read)
 
 
-def rest_kernel(
-    place_ref, q_ref, rest_ref, row_ref, below_a, below_b, above_a, above_b, below2_ref,
-    above2_ref, weight_ref, acc_in, peak_in, *refs,
-):
-    outs, (bank_ref, w_ref, bias_ref, acc_ref, carried_ref, peak_ref, att_ref, sems) = (
-        refs[:-8],
-        refs[-8:],
-    )
-    mine, used = place_ref[0], place_ref[1]
-    y, heads = mine // WIDE, acc_ref.shape[0]
-    span = WIDE * KEEP
-    part, row_steps = span // 2, span // STEP
-    copies = []
-
-    def copy(source, at, rows, condition, step):
-        target = bank_ref.at[pl.ds(at, rows)]
-        one = pltpu.make_async_copy(source, target, sems.at[len(copies)])
-        copies.append((one, condition, step))
-
-    for row, ref in enumerate((row_ref, below_a, below2_ref, above_a)):
-        copy(ref.at[pl.ds(0, KEEP)], 0, KEEP, (mine > 0) & (y == row), None)
-    at, step = TILE, 0
-    for condition, first, second in (
-        (y > 0, below_a, below_b),
-        (y > 1, below2_ref, above2_ref),
-        (y == 3, above_a, above_b),
-    ):
-        copy(first, at, part, condition, step)
-        copy(second, at + part, part, condition, step)
-        at, step = at + span, step + row_steps
-    for one, condition, _ in copies:
-        pl.when(condition)(one.start)
-    whole = [
-        pltpu.make_async_copy(source, target, sems.at[len(copies) + at])
-        for at, (source, target) in enumerate(
-            ((peak_in, peak_ref), (acc_in, carried_ref), (weight_ref, w_ref))
-        )
+def more_keys(q_ref, rest_ref, state_in, refs, used, firsts, pieces, steps):
+    acc_ref, peak_ref, bank_ref, carried_ref, bias_ref, sems = refs
+    acc_in, peak_in = sums(state_in)
+    copies = [(peak_in, peak_ref, True), (acc_in, carried_ref, True)]
+    copies += [(ref.at[pl.ds(0, KEEP)], bank_ref.at[pl.ds(0, KEEP)], on) for ref, on in firsts]
+    for at, (ref, on) in enumerate(pieces):
+        copies.append((ref, bank_ref.at[pl.ds(TILE + at * STEP, STEP)], on))
+    copies = [
+        (pltpu.make_async_copy(source, target, sems.at[at]), on)
+        for at, (source, target, on) in enumerate(copies)
     ]
-    for one in whole:
-        one.start()
-    acc_ref[...] = jnp.zeros_like(acc_ref)
+
+    def under(condition, act):
+        if condition is True:
+            act()
+        else:
+            pl.when(condition)(act)
+
+    for one, on in copies:
+        under(on, one.start)
+    acc_ref[...] = jnp.zeros(acc_ref.shape, jnp.float32)
     bank_ref[KEEP:TILE] = rest_ref[: TILE - KEEP]
     number = wide(rest_ref[TILE - KEEP : TILE - KEEP + 1, :HEAD].astype(jnp.int32), TILE)
     at = count_along((1, TILE), 1)
@@ -257,45 +244,81 @@
     bias_ref[0] = jnp.broadcast_to(bias_where(at < limit), bias_ref.shape[1:])
     bias_ref[1] = jnp.zeros(bias_ref.shape[1:], jnp.float32)
     view = head_view(q_ref, acc_ref, peak_ref)
+    masked = sum(jnp.where(on, 1, 0) for _, on in firsts)
 
     def start(h):
         acc_ref[h] = carried_ref[h]
 
-    def read_fast(step, masked):
-        for one, condition, when in copies:
-            if masked and when is None:
-                pl.when(condition)(one.wait)
-            elif when is not None and not masked:
-                pl.when(condition & (step == when))(one.wait)
-        if masked:
-            return read(0)
+    def read(step):
+        tile = jnp.where(masked > 0, step, step + 1)
+        return *tile_of(bank_ref, tile * TILE, TILE), bias_ref[jnp.minimum(tile, 1)]
+
+    def read_fast(step, with_bias):
+        if with_bias:
+            return *tile_of(bank_ref, 0, TILE), bias_ref[0]
         return *tile_of(bank_ref, TILE + step * STEP, STEP), None
 
-    def read(tile):
-        return *tile_of(bank_ref, tile * TILE, TILE), bias_ref[jnp.minimum(tile, 1)]
-
-    masked = jnp.where(mine > 0, 1, 0)
-    whole[0].wait()
-    absorb(heads, view, masked, row_steps * y, read_fast)
-    whole[1].wait()
+    for one, on in copies[:1] + copies[2:]:
+        under(on, one.wait)
+    absorb(acc_ref.shape[0], view, masked, steps, read_fast)
+    copies[1][0].wait()
     acc_ref[...] += carried_ref[...]
-    absorb_again(acc_ref, view, start, masked + span // TILE * y, read)
-    for h in range(heads):
+    absorb_again(acc_ref, view, start, masked + STEP // TILE * steps, read)
+
+
+def early_kernel(
+    place_ref, q_ref, rest_ref, row_a, below_a, below_b, above_a, above_b, state_in, state_ref,
+    *refs,
+):
+    mine, used = place_ref[0], place_ref[1]
+    y = mine // WIDE
+    firsts = (row_a, (mine > 0) & (y == 0)), (below_a, y == 1), (above_a, y == 3)
+    pieces = (below_a, y > 0), (below_b, y > 0), (above_a, y == 3), (above_b, y == 3)
+    steps = jnp.where(y == 3, 4, jnp.where(y > 0, 2, 0))
+    refs = *sums(state_ref), *refs
+    more_keys(q_ref, rest_ref, state_in, refs, used, firsts, pieces, steps)
+
+
+def rest_kernel(
+    place_ref, q_ref, rest_ref, below2_ref, above2_ref, weight_ref, state_in,
+    own_out, far_out, near_out, own_ref, send_ref, w_ref, att_ref, out_sems, *refs,
+):
+    y, used = place_ref[0] // WIDE, place_ref[1]
+    weight_copy = pltpu.make_async_copy(weight_ref, w_ref, out_sems.at[3])
+    weight_copy.start()
+    pieces = (below2_ref, y > 1), (above2_ref, y > 1)
+    firsts = ((below2_ref, y == 2),)
+    more_keys(q_ref, rest_ref, state_in, refs, used, firsts, pieces, jnp.where(y > 1, 2, 0))
+    acc_ref = refs[0]
+    for h in range(acc_ref.shape[0]):
         att_ref[:, h * HEAD : (h + 1) * HEAD] = (
             acc_ref[h, :, :HEAD] / acc_ref[h, :, HEAD:]
         ).astype(jnp.bfloat16)
-    whole[2].wait()
-    chips, rows, columns = outs[0].shape
+    weight_copy.wait()
+    chips, _, columns = own_out.shape
     chip, core = place_ref[2], place_ref[3]
 
     @pl.loop(0, chips)
     def _(step):
-        at = lax.rem(chip + step, chips) * 2
-        for first, side in enumerate((core, 1 - core)):
-            start = pl.multiple_of((at + side) * columns, columns)
-            product = dot(att_ref[...], w_ref[:, pl.ds(start, columns)]).astype(jnp.bfloat16)
-            for part, ref in enumerate(outs[first::2]):
-                ref[step] = product[part * rows : (part + 1) * rows]
+        ahead = jnp.where(step == 0, 2, jnp.where(step == 1, 1, jnp.where(step == 2, 3, 0)))
+        column = lax.rem(chip + ahead, chips) * 2
+        for ref, side in ((own_ref, core), (send_ref, 1 - core)):
+            start = pl.multiple_of((column + side) * columns, columns)
+            ref[step] = dot(att_ref[...], w_ref[:, pl.ds(start, columns)]).astype(jnp.bfloat16)
+        pltpu.make_async_copy(own_ref.at[step], own_out.at[step], out_sems.at[0]).start()
+
+        @pl.when(step == 0)
+        def _():
+            pltpu.make_async_copy(send_ref.at[0], far_out, out_sems.at[1]).start()
+
+        @pl.when(step > 0)
+        def _():
+            target = near_out.at[step - 1]
+            pltpu.make_async_copy(send_ref.at[step], target, out_sems.at[2]).start()
+
+    pltpu.make_async_copy(own_ref, own_out, out_sems.at[0]).wait()
+    pltpu.make_async_copy(send_ref.at[0], far_out, out_sems.at[1]).wait()
+    pltpu.make_async_copy(send_ref.at[pl.ds(1, chips - 1)], near_out, out_sems.at[2]).wait()
 
 
 def pack_row_kernel(place_ref, *refs):
@@ -330,9 +353,15 @@
 
 
 def state_of(length, heads):
+    return jax.ShapeDtypeStruct((heads, length, 3 * HEAD), jnp.float32)
+
+
+def work_of(length, heads, steps):
     return [
-        jax.ShapeDtypeStruct((heads, length, 2 * HEAD), jnp.float32),
-        jax.ShapeDtypeStruct((heads, length, HEAD), jnp.float32),
+        pltpu.VMEM((TILE + steps * STEP, 2 * HEAD), jnp.bfloat16),
+        pltpu.VMEM((heads, length, 2 * HEAD), jnp.float32),
+        pltpu.VMEM((2, 8, TILE), jnp.float32),
+        pltpu.SemaphoreType.DMA((9,)),
     ]
 
 
@@ -345,7 +374,7 @@
         grid=(1,),
         out_shape=state,
         in_specs=[SMEM, *[whole(x) for x in (queries, keys, values)], ANY, ANY],
-        out_specs=[whole(x) for x in state],
+        out_specs=whole(state),
         scratch_shapes=[
             pltpu.VMEM((WIDE * KEEP, 2 * HEAD), jnp.bfloat16),
             pltpu.VMEM((8, TILE), jnp.float32),
@@ -357,36 +386,92 @@
     )(place, queries, keys, values, row_a, row_b)
 
 
-def rest_rows(place, queries, rest, banks, weight, state, parts, chips):
+def early_rows(place, queries, rest, banks, state):
     length, width = queries.shape
     heads = width // HEAD
-    keys = TILE + 3 * WIDE * KEEP
     whole = lambda x: pl.BlockSpec(x.shape, lambda i: (0,) * len(x.shape))
-    out = jax.ShapeDtypeStruct((chips, length // parts, weight.shape[1] // chips // 2), jnp.bfloat16)
+    return pl.pallas_call(
+        early_kernel,
+        grid=(1,),
+        out_shape=state_of(length, heads),
+        in_specs=[SMEM, whole(queries), whole(rest), *[ANY] * (len(banks) + 1)],
+        out_specs=whole(state),
+        scratch_shapes=work_of(length, heads, 4),
+        compiler_params=PARAMS,
+        cost_estimate=cost(length * heads, TILE + 4 * STEP),
+        name="early_rows",
+    )(place, queries, rest, *banks, state)
+
+
+def rest_rows(place, queries, rest, banks, weight, state, chips):
+    length, width = queries.shape
+    heads, keys = width // HEAD, TILE + 2 * STEP
+    whole = lambda x: pl.BlockSpec(x.shape, lambda i: (0,) * len(x.shape))
+    one = (length, weight.shape[1] // chips // 2)
+    shapes = (chips, *one), one, (chips - 1, *one)
     return pl.pallas_call(
         rest_kernel,
         grid=(1,),
-        out_shape=[out] * (2 * parts),
-        in_specs=[SMEM, whole(queries), whole(rest), *[ANY] * (len(banks) + 3)],
-        out_specs=[whole(out)] * (2 * parts),
+        out_shape=[jax.ShapeDtypeStruct(shape, jnp.bfloat16) for shape in shapes],
+        in_specs=[SMEM, whole(queries), whole(rest), *[ANY] * (len(banks) + 2)],
+        out_specs=[ANY] * 3,
         scratch_shapes=[
-            pltpu.VMEM((keys, 2 * HEAD), jnp.bfloat16),
+            *[pltpu.VMEM((chips, *one), jnp.bfloat16)] * 2,
             pltpu.VMEM(weight.shape, weight.dtype),
-            pltpu.VMEM((2, 8, TILE), jnp.float32),
-            pltpu.VMEM((heads, length, 2 * HEAD), jnp.float32),
+            pltpu.VMEM((length, width), jnp.bfloat16),
+            pltpu.SemaphoreType.DMA((4,)),
             pltpu.VMEM((heads, length, 2 * HEAD), jnp.float32),
             pltpu.VMEM((heads, length, HEAD), jnp.float32),
-            pltpu.VMEM((length, width), jnp.bfloat16),
-            pltpu.SemaphoreType.DMA((13,)),
+            *work_of(length, heads, 2),
         ],
-        compiler_params=PARAMS,
+        compiler_params=pltpu.CompilerParams(vmem_limit_bytes=47 * 2**20),
         cost_estimate=cost(length * heads, keys),
         name="rest_rows",
-    )(place, queries, rest, *banks, weight, *state)
-
-
-def added(*terms):
-    return sum(term.astype(jnp.float32) for term in terms).astype(jnp.bfloat16)
+    )(place, queries, rest, *banks, weight, state)
+
+
+def summed(*refs):
+    return sum(ref[...].astype(jnp.float32) for ref in refs)
+
+
+def cross_kernel(own_ref, other_ref, upper_ref, lower_ref):
+    total = summed(own_ref, other_ref).astype(jnp.bfloat16)
+    half = upper_ref.shape[0]
+    upper_ref[...] = total[:half]
+    lower_ref[...] = total[half:]
+
+
+def add_kernel(*refs):
+    terms = refs[:-2]
+    middle = len(terms) // 2
+    refs[-2][...] = summed(*terms[:middle]).astype(jnp.bfloat16)
+    refs[-1][...] = summed(*terms[middle:]).astype(jnp.bfloat16)
+
+
+def halves_kernel(*refs):
+    (*terms, upper_ref, lower_ref), out_ref = refs[:-1], refs[-1]
+    half, total = upper_ref.shape[0], summed(*terms)
+    out_ref[:half] = (total[:half] + summed(upper_ref)).astype(out_ref.dtype)
+    out_ref[half:] = (total[half:] + summed(lower_ref)).astype(out_ref.dtype)
+
+
+def small_call(kernel, name, terms, shapes, dtype=jnp.bfloat16):
+    def spec(term):
+        if not isinstance(term, tuple):
+            return pl.BlockSpec(term.shape, lambda i: (0, 0))
+        x, chunk, half = term
+        rows = x.shape[1] // (1 if half is None else 2)
+        return pl.BlockSpec((None, rows, x.shape[2]), lambda i: (chunk, half or 0, 0))
+
+    return pl.pallas_call(
+        kernel,
+        grid=(1,),
+        out_shape=[jax.ShapeDtypeStruct(shape, dtype) for shape in shapes],
+        in_specs=[spec(term) for term in terms],
+        out_specs=[pl.BlockSpec(shape, lambda i: (0, 0)) for shape in shapes],
+        compiler_params=pltpu.CompilerParams(vmem_limit_bytes=8 * 2**20),
+        name=name,
+    )(*[term[0] if isinstance(term, tuple) else term for term in terms])
 
 
 def on_device(queries, key_rows, value_rows, kept_positions, anchor_length, output_weight):
@@ -411,13 +496,13 @@
     half = KEEP // 2
     left, right = [kept], [kept]
     rest = jnp.where(mine == 0, rest, jnp.zeros_like(rest))
-    upward = [[(0, WIDE)], [(0, 3 * WIDE), (WIDE, 2 * WIDE)]]
+    spread = lambda hops: [(r * WIDE + a, r * WIDE + b) for a, b in hops for r in range(tall)]
+    upward = [(0, WIDE)], [(0, 3 * WIDE), (WIDE, 2 * WIDE)], spread([(0, 4)])
     for step in range(WIDE // 2 - 1):
         left.append(permute(left[-1], plus))
         right.append(permute(right[-1], minus))
-        if step < len(upward):
-            rest = rest + permute(rest, upward[step])
-            left[-1], right[-1], rest = lax.optimization_barrier((left[-1], right[-1], rest))
+        rest = rest + permute(rest, upward[step])
+        left[-1], right[-1], rest = lax.optimization_barrier((left[-1], right[-1], rest))
     opposite = [permute(left[-1][:half], plus), permute(right[-1][half:], minus)]
     ends = pack_row(place, right[1:] + opposite + left[:0:-1] + [kept])
 
@@ -427,35 +512,34 @@
     above_a = permute(ends[0], across([(0, 3)]))
 
     rest, ends = lax.optimization_barrier((rest, ends))
-    spread = lambda hops: [(r * WIDE + a, r * WIDE + b) for a, b in hops for r in range(tall)]
-    rest = rest + permute(rest, spread([(0, 4)]))
-    rest, below_a, above_b = lax.optimization_barrier((rest, below_a, above_b))
+    rest = rest + permute(rest, spread([(0, 2), (4, 6)]))
+    state = own_row(place, queries, key_rows, value_rows, *ends)
+    rest, below_a, above_b, state = lax.optimization_barrier((rest, below_a, above_b, state))
     below2 = permute(below_a, across([(1, 2), (2, 3)]))
     above2 = permute(above_b, across([(0, 3), (3, 2)]))
-    rest = rest + permute(rest, spread([(0, 2), (4, 6)]))
     rest = rest + permute(rest, spread([(0, 1), (2, 3), (4, 5), (6, 7)]))
 
-    parts = 2
-    state = own_row(place, queries, key_rows, value_rows, *ends)
-    banks = (ends[0], below_a, below_b, above_a, above_b, below2, above2)
-
-    outs = []
-    half = length // parts // 2
-    terms = rest_rows(place, queries, rest, banks, output_weight, state, parts, chips)
-    others = [lax.ppermute(send, "head", swap) for send in terms[1::2]]
-    for own, other in zip(terms[::2], others):
-        across_x = added(own[2], other[2])
-        from_below = lax.ppermute(across_x[:half], "head", up)
-        from_above = lax.ppermute(across_x[half:], "head", down)
-        upward = jnp.concatenate(
-            [added(own[1, :half], other[1, :half], from_below), added(own[1, half:], other[1, half:])]
-        )
-        downward = jnp.concatenate(
-            [added(own[3, :half], other[3, :half]), added(own[3, half:], other[3, half:], from_above)]
-        )
-        upward, downward = lax.ppermute(upward, "head", up), lax.ppermute(downward, "head", down)
-        outs.append(added(own[0], other[0], upward, downward))
-    return jnp.concatenate(outs)
+    state = early_rows(place, queries, rest, (ends[0], below_a, below_b, above_a, above_b), state)
+    own, far, near = rest_rows(
+        place, queries, rest, (below2, above2), output_weight, state, chips
+    )
+
+    far, near = lax.optimization_barrier((lax.ppermute(far, "head", swap), near))
+    near = lax.ppermute(near, "head", swap)
+    columns = own.shape[2]
+    whole, half = (length, columns), (length // 2, columns)
+    upper, lower = small_call(cross_kernel, "cross", [(own, 0, None), far], [half, half])
+    upper, lower = lax.ppermute(upper, "head", up), lax.ppermute(lower, "head", down)
+    terms = [(own, 1, 1), (near, 0, 1), (own, 2, 0), (near, 1, 0)]
+    lower_up, upper_down = small_call(add_kernel, "direct", terms, [half, half])
+    upper, lower, _, _ = lax.optimization_barrier((upper, lower, lower_up, upper_down))
+    lower_up, upper_down = lax.ppermute(lower_up, "head", up), lax.ppermute(upper_down, "head", down)
+    terms = [(own, 1, 0), (near, 0, 0), upper, (own, 2, 1), (near, 1, 1), lower]
+    upper_up, lower_down = small_call(add_kernel, "turn", terms, [half, half])
+    upper_up, lower_down = lax.ppermute(upper_up, "head", up), lax.ppermute(lower_down, "head", down)
+    terms = [(own, 3, None), (near, 2, None), upper_down, lower_up]
+    (total,) = small_call(halves_kernel, "collect", terms, [whole], jnp.float32)
+    return small_call(halves_kernel, "finish", [total, upper_up, lower_down], [whole])[0]
 
 
 def solution(mesh):

time: 173 us -> 149 us (0.86); the launches traced: 170 us -> 148 us
  waiting for transfers between devices: 44 us -> 36.8 us
  Pallas kernels: 72.1 us -> 64.9 us
  other arithmetic: 6.39 us -> 0.93 us
  starting transfers between devices: 45.6 us -> 43.4 us
    ppermute x19, waiting for transfers between devices: 34.1 us -> 21.7 us  [on_device(): permute = lambda x, pairs: lax.ppermute(x, 'ctx', pairs)]
    pallas_call x1 -> x7, Pallas kernels: 63.9 us -> 56.8 us  [the longest x1 44.7 us: early_rows(): pl.pallas_call(early_kernel, grid=(1,), out_shape=state_of(length, heads)...]
    ppermute x10 -> x8, waiting for transfers between devices: 9.88 us -> 15.1 us  [the longest x1 3.3 us: on_device(): lax.ppermute(upper_down, 'head', down)]
    convert_element_type x8 -> x0, other arithmetic: 4.57 us -> none  [added(): sum((term.astype(jnp.float32) for term in terms)).astype(jnp.bfloat16)]
    ppermute x10 -> x8, starting transfers between devices: 11.8 us -> 7.98 us  [the longest x1 2.41 us: on_device(): lax.ppermute(lower_up, 'head', up)]
  transfers between devices with their start and end apart: 29 -> 27, of which waited for: 15 -> 15; matrix products, arithmetic and copies ran while one was open for 3% -> 1% of each run, Pallas kernels for 3% -> 34%
where the time goes in v5:
time: 149 us; the launch traced here: 148 us
  Pallas kernels  64.9 us (44%)
  starting transfers between devices  43.4 us (29%)
  waiting for transfers between devices  36.8 us (25%)
    pallas_call x1, Pallas kernels, early_rows(): pl.pallas_call(early_kernel, grid=(1,), out_shape=state_of(length, heads)...  44.7 us
    ppermute x19, starting transfers between devices, on_device(): permute = lambda x, pairs: lax.ppermute(x, 'ctx', pairs)  35.4 us
    ppermute x19, waiting for transfers between devices, on_device(): permute = lambda x, pairs: lax.ppermute(x, 'ctx', pairs)  21.7 us
    pallas_call x1, Pallas kernels, rest_rows(): pl.pallas_call(rest_kernel, grid=(1,), out_shape=[jax.ShapeDtypeStruct(sh...  10.4 us
    pallas_call x1, Pallas kernels, own_row(): pl.pallas_call(own_row_kernel, grid=(1,), out_shape=state, in_specs=[SMEM...  4.97 us
    ppermute x1, waiting for transfers between devices, on_device(): lax.ppermute(upper_down, 'head', down)  3.3 us
    ppermute x1, waiting for transfers between devices, on_device(): lax.ppermute(upper_up, 'head', up)  3.09 us
  transfers between devices with their start and end apart: 27, of which 15 were waited for; matrix products, arithmetic and copies ran while one was open for 1% of the time, Pallas kernels for 34%

profile of v5, /device:TPU:30, one launch (start us, length us, event | category | flops | bytes accessed | tf_op | source)
XLA Modules:
  0.0 148.0 jit_solution(14219783936139579407)
XLA Ops:
  0.7 2.4 %select_kept.1 = (bf16[256,256]{1,0:T(8,128)(2,1)}, bf16[272,256]{1,0:T(8,128)(2,1)}) custom-call(s32[1]{0:T(128)S(6)} %copy.7.used_ref, s32[1,256]{1,0:T(1,128)} %refs_0_.1, bf16[512,128]{1,0:T(8,128)(2,1)} %k_ref.1, bf16[512,128]{1,0:T(8,128)(2,1)} %v_ref.1), custom_call_target="tpu_custom_call" | custom-call | tf_op jit(solution)/shard_map/select_kept/pallas_call | solution.py:77
  3.8 5.9 %collective-permute-start.1 = (bf16[256,256]{1,0:T(8,128)(2,1)}, bf16[256,256]{1,0:T(8,128)(2,1)S(1)}, u32[]{:S(2)}, u32[]{:S(2)}) collective-permute-start(bf16[256,256]{1,0:T(8,128)(2,1)} %get-tuple-element.38.refs_8_), channel_id=1, source_target_pairs={{0,56},{8,0},{16,8},{24,16},{32,24},{40,32},{48,40},{56,48},{64,12... | collective-permute-start | bytes 393224 | tf_op jit(solution)/shard_map/ppermute | solution.py:489
  9.8 3.0 %collective-permute-done.1.refs_0_ = bf16[256,256]{1,0:T(8,128)(2,1)S(1)} collective-permute-done((bf16[256,256]{1,0:T(8,128)(2,1)}, bf16[256,256]{1,0:T(8,128)(2,1)S(1)}, u32[]{:S(2)}, u32[]{:S(2)}) %collective-permute-start.1) | collective-permute-done | bytes 131104 | tf_op jit(solution)/shard_map/ppermute | solution.py:489
  12.8 3.3 %collective-permute-done.refs_7_ = bf16[256,256]{1,0:T(8,128)(2,1)S(1)} collective-permute-done((bf16[256,256]{1,0:T(8,128)(2,1)}, bf16[256,256]{1,0:T(8,128)(2,1)S(1)}, u32[]{:S(2)}, u32[]{:S(2)}) %collective-permute-start) | collective-permute-done | bytes 131104 | tf_op jit(solution)/shard_map/ppermute | solution.py:489
  17.5 3.2 %collective-permute-start.4 = (bf16[256,256]{1,0:T(8,128)(2,1)S(1)}, bf16[256,256]{1,0:T(8,128)(2,1)S(1)}, u32[]{:S(2)}, u32[]{:S(2)}) collective-permute-start(bf16[256,256]{1,0:T(8,128)(2,1)S(1)} %collective-permute-done.1.refs_0_), channel_id=1, source_target_pairs={{0,56},{8,0},{16,8},{24,16},{32,24},{40,32},{48,40},{56,48},{64,12... | collective-permute-start | bytes 393224 | tf_op jit(solution)/shard_map/ppermute | solution.py:489
  20.7 3.5 %collective-permute-done.5 = bf16[272,256]{1,0:T(8,128)(2,1)S(1)} collective-permute-done((bf16[272,256]{1,0:T(8,128)(2,1)S(1)}, bf16[272,256]{1,0:T(8,128)(2,1)S(1)}, u32[]{:S(2)}, u32[]{:S(2)}) %collective-permute-start.5) | collective-permute-done | bytes 139296 | tf_op jit(solution)/shard_map/ppermute | solution.py:489
  24.3 2.3 %collective-permute-start.8 = (bf16[272,256]{1,0:T(8,128)(2,1)S(1)}, bf16[272,256]{1,0:T(8,128)(2,1)S(1)}, u32[]{:S(2)}, u32[]{:S(2)}) collective-permute-start(bf16[272,256]{1,0:T(8,128)(2,1)S(1)} %add.22), channel_id=1, source_target_pairs={{0,32},{64,96},{128,160},{192,224},{1,33},{65,97},{129,161},{193,2... | collective-permute-start | bytes 417800 | tf_op jit(solution)/shard_map/ppermute | solution.py:489
  26.7 3.2 %collective-permute-start.7 = (bf16[256,256]{1,0:T(8,128)(2,1)S(1)}, bf16[256,256]{1,0:T(8,128)(2,1)S(1)}, u32[]{:S(2)}, u32[]{:S(2)}) collective-permute-start(bf16[256,256]{1,0:T(8,128)(2,1)S(1)} %collective-permute-done.4.refs_1_), channel_id=1, source_target_pairs={{0,56},{8,0},{16,8},{24,16},{32,24},{40,32},{48,40},{56,48},{64,12... | collective-permute-start | bytes 393224 | tf_op jit(solution)/shard_map/ppermute | solution.py:489
  30.0 2.9 %collective-permute-done.6.refs_5_ = bf16[256,256]{1,0:T(8,128)(2,1)S(1)} collective-permute-done((bf16[256,256]{1,0:T(8,128)(2,1)S(1)}, bf16[256,256]{1,0:T(8,128)(2,1)S(1)}, u32[]{:S(2)}, u32[]{:S(2)}) %collective-permute-start.6) | collective-permute-done | bytes 131104 | tf_op jit(solution)/shard_map/ppermute | solution.py:489
  33.4 2.9 %collective-permute-start.10 = (bf16[128,256]{1,0:T(8,128)(2,1)S(1)}, bf16[128,256]{1,0:T(8,128)(2,1)S(1)}, u32[]{:S(2)}, u32[]{:S(2)}) collective-permute-start(bf16[128,256]{1,0:T(8,128)(2,1)S(1)} %slice.7), channel_id=1, source_target_pairs={{0,56},{8,0},{16,8},{24,16},{32,24},{40,32},{48,40},{56,48},{64,12... | collective-permute-start | bytes 196616 | tf_op jit(solution)/shard_map/ppermute | solution.py:489
  36.4 2.1 %collective-permute-done.9.refs_3_ = bf16[128,256]{1,0:T(8,128)(2,1)S(1)} collective-permute-done((bf16[128,256]{1,0:T(8,128)(2,1)S(1)}, bf16[128,256]{1,0:T(8,128)(2,1)S(1)}, u32[]{:S(2)}, u32[]{:S(2)}) %collective-permute-start.9) | collective-permute-done | bytes 65568 | tf_op jit(solution)/shard_map/ppermute | solution.py:489
  45.3 2.7 %collective-permute-start.11 = (bf16[272,256]{1,0:T(8,128)(2,1)S(1)}, bf16[272,256]{1,0:T(8,128)(2,1)S(1)}, u32[]{:S(2)}, u32[]{:S(2)}) collective-permute-start(bf16[272,256]{1,0:T(8,128)(2,1)S(1)} %add.23), channel_id=1, source_target_pairs={{0,16},{64,80},{128,144},{192,208},{32,48},{96,112},{160,176},{224... | collective-permute-start | bytes 417800 | tf_op jit(solution)/shard_map/ppermute | solution.py:489
  48.0 5.0 %own_row.1.state_in = f32[4,512,384]{2,1,0:T(8,128)} custom-call(s32[4]{0:T(128)} %copy-done.2, bf16[512,512]{1,0:T(8,128)(2,1)} %q_ref.5, bf16[512,128]{1,0:T(8,128)(2,1)} %k_ref.1, bf16[512,128]{1,0:T(8,128)(2,1)} %v_ref.1, bf16[1024,256]{1,0:T(8,128)(2,1)} %copy-done.5, bf16[1024,256]{1,0:T(8,128)(2,1)} %copy-done.6), custom_call_target="tpu_custom_call" | custom-call | flops 5368709120 | bytes 8388608 | tf_op jit(solution)/shard_map/own_row/pallas_call | solution.py:372
  53.1 3.8 %collective-permute-done.12.below_a = bf16[1024,256]{1,0:T(8,128)(2,1)S(1)} collective-permute-done((bf16[1024,256]{1,0:T(8,128)(2,1)S(1)}, bf16[1024,256]{1,0:T(8,128)(2,1)S(1)}, u32[]{:S(2)}, u32[]{:S(2)}) %collective-permute-start.12) | collective-permute-done | bytes 524320 | tf_op jit(solution)/shard_map/ppermute | solution.py:489
  56.9 2.3 %collective-permute-done.13.above_b = bf16[1024,256]{1,0:T(8,128)(2,1)S(1)} collective-permute-done((bf16[1024,256]{1,0:T(8,128)(2,1)S(1)}, bf16[1024,256]{1,0:T(8,128)(2,1)S(1)}, u32[]{:S(2)}, u32[]{:S(2)}) %collective-permute-start.13) | collective-permute-done | bytes 524320 | tf_op jit(solution)/shard_map/ppermute | solution.py:489
  62.1 4.6 %collective-permute-start.16 = (bf16[1024,256]{1,0:T(8,128)(2,1)S(1)}, bf16[1024,256]{1,0:T(8,128)(2,1)S(1)}, u32[]{:S(2)}, u32[]{:S(2)}) collective-permute-start(bf16[1024,256]{1,0:T(8,128)(2,1)S(1)} %collective-permute-done.13.above_b), channel_id=1, source_target_pairs={{0,192},{8,200},{16,208},{24,216},{32,224},{40,232},{48,240},{56,2... | collective-permute-start | bytes 1572872 | tf_op jit(solution)/shard_map/ppermute | solution.py:489
  68.0 44.7 %early_rows.1.state_in = f32[4,512,384]{2,1,0:T(8,128)} custom-call(s32[4]{0:T(128)} %copy-done.2, bf16[512,512]{1,0:T(8,128)(2,1)} %q_ref.5, bf16[272,256]{1,0:T(8,128)(2,1)} %add.25.rest_ref, bf16[1024,256]{1,0:T(8,128)(2,1)} %copy-done.5, bf16[1024,256]{1,0:T(8,128)(2,1)} %copy-done.7, bf16[1024,256]{1,0:T(8,128)(2,1)} %collective-permute-done.17.below_b, ...), custom_call_target="tpu_custom_call" | custom-call | flops 9663676416 | bytes 8388608 | tf_op jit(solution)/shard_map/early_rows/pallas_call | solution.py:393
  112.8 10.4 %rest_rows.1 = (bf16[4,512,512]{2,1,0:T(8,128)(2,1)S(1)}, bf16[512,512]{1,0:T(8,128)(2,1)S(1)}, bf16[3,512,512]{2,1,0:T(8,128)(2,1)S(1)}) custom-call(s32[4]{0:T(128)S(1)} %copy-done.3, bf16[512,512]{1,0:T(8,128)(2,1)S(1)} %copy-done.4, bf16[272,256]{1,0:T(8,128)(2,1)S(1)} %copy-done, bf16[1024,256]{1,0:T(8,128)(2,1)S(1)} %collective-permute-done.15.below2_ref, ...), custom_call_target="tpu_custom_call" | custom-call | flops 5368709120 | bytes 8388608 | tf_op jit(solution)/shard_map/rest_rows/pallas_call | solution.py:412
  123.6 1.9 %collective-permute-done.19.other_ref = bf16[512,512]{1,0:T(8,128)(2,1)S(1)} collective-permute-done((bf16[512,512]{1,0:T(8,128)(2,1)S(1)}, bf16[512,512]{1,0:T(8,128)(2,1)S(1)}, u32[]{:S(2)}, u32[]{:S(2)}) %collective-permute-start.19) | collective-permute-done | bytes 524320 | tf_op jit(solution)/shard_map/ppermute | solution.py:527
  130.0 2.4 %collective-permute-start.22 = (bf16[256,512]{1,0:T(8,128)(2,1)S(1)}, bf16[256,512]{1,0:T(8,128)(2,1)S(1)}, u32[]{:S(2)}, u32[]{:S(2)}) collective-permute-start(bf16[256,512]{1,0:T(8,128)(2,1)S(1)} %get-tuple-element.63), channel_id=1, source_target_pairs={{0,2},{1,3},{2,4},{3,5},{4,6},{5,7},{6,0},{7,1},{8,10},{9,11},{10,... | collective-permute-start | bytes 786440 | tf_op jit(solution)/shard_map/ppermute | solution.py:536
  132.4 2.6 %collective-permute-done.23.refs_2_ = bf16[256,512]{1,0:T(8,128)(2,1)S(1)} collective-permute-done((bf16[256,512]{1,0:T(8,128)(2,1)S(1)}, bf16[256,512]{1,0:T(8,128)(2,1)S(1)}, u32[]{:S(2)}, u32[]{:S(2)}) %collective-permute-start.23) | collective-permute-done | bytes 262176 | tf_op jit(solution)/shard_map/ppermute | solution.py:532
  137.3 1.7 %collective-permute-start.26 = (bf16[256,512]{1,0:T(8,128)(2,1)S(1)}, bf16[256,512]{1,0:T(8,128)(2,1)S(1)}, u32[]{:S(2)}, u32[]{:S(2)}) collective-permute-start(bf16[256,512]{1,0:T(8,128)(2,1)S(1)} %get-tuple-element.70), channel_id=1, source_target_pairs={{0,6},{1,7},{2,0},{3,1},{4,2},{5,3},{6,4},{7,5},{8,14},{9,15},{10,... | collective-permute-start | bytes 786440 | tf_op jit(solution)/shard_map/ppermute | solution.py:539
  139.0 3.3 %collective-permute-done.21.refs_2_ = bf16[256,512]{1,0:T(8,128)(2,1)S(1)} collective-permute-done((bf16[256,512]{1,0:T(8,128)(2,1)S(1)}, bf16[256,512]{1,0:T(8,128)(2,1)S(1)}, u32[]{:S(2)}, u32[]{:S(2)}) %collective-permute-start.21) | collective-permute-done | bytes 262176 | tf_op jit(solution)/shard_map/ppermute | solution.py:536
  142.6 3.1 %collective-permute-done.25.refs_1_ = bf16[256,512]{1,0:T(8,128)(2,1)S(1)} collective-permute-done((bf16[256,512]{1,0:T(8,128)(2,1)S(1)}, bf16[256,512]{1,0:T(8,128)(2,1)S(1)}, u32[]{:S(2)}, u32[]{:S(2)}) %collective-permute-start.25) | collective-permute-done | bytes 262176 | tf_op jit(solution)/shard_map/ppermute | solution.py:539
  (67 shorter events, 23.5 us)
Async XLA Ops:
  3.1 6.6 %collective-permute-start.2 = (bf16[272,256]{1,0:T(8,128)(2,1)S(1)}, bf16[272,256]{1,0:T(8,128)(2,1)S(1)}, u32[]{:S(2)}, u32[]{:S(2)}) collective-permute-start(bf16[272,256]{1,0:T(8,128)(2,1)S(1)} %broadcast_select_fusion), channel_id=1, source_target_pairs={{0,64},{1,65},{2,66},{3,67},{4,68},{5,69},{6,70},{7,71}} | collective-permute-start | bytes 417800 | tf_op jit(solution)/shard_map/ppermute | solution.py:489
  3.8 9.0 %collective-permute-start.1 = (bf16[256,256]{1,0:T(8,128)(2,1)}, bf16[256,256]{1,0:T(8,128)(2,1)S(1)}, u32[]{:S(2)}, u32[]{:S(2)}) collective-permute-start(bf16[256,256]{1,0:T(8,128)(2,1)} %get-tuple-element.38.refs_8_), channel_id=1, source_target_pairs={{0,56},{8,0},{16,8},{24,16},{32,24},{40,32},{48,40},{56,48},{64,12... | collective-permute-start | bytes 393224 | tf_op jit(solution)/shard_map/ppermute | solution.py:489
  9.7 6.4 %collective-permute-start = (bf16[256,256]{1,0:T(8,128)(2,1)}, bf16[256,256]{1,0:T(8,128)(2,1)S(1)}, u32[]{:S(2)}, u32[]{:S(2)}) collective-permute-start(bf16[256,256]{1,0:T(8,128)(2,1)} %get-tuple-element.38.refs_8_), channel_id=1, source_target_pairs={{0,8},{8,16},{16,24},{24,32},{32,40},{40,48},{48,56},{56,0},{64,72... | collective-permute-start | bytes 393224 | tf_op jit(solution)/shard_map/ppermute | solution.py:489
  16.1 8.1 %collective-permute-start.5 = (bf16[272,256]{1,0:T(8,128)(2,1)S(1)}, bf16[272,256]{1,0:T(8,128)(2,1)S(1)}, u32[]{:S(2)}, u32[]{:S(2)}) collective-permute-start(bf16[272,256]{1,0:T(8,128)(2,1)S(1)} %fusion), channel_id=1, source_target_pairs={{0,192},{64,128},{1,193},{65,129},{2,194},{66,130},{3,195},{67,131... | collective-permute-start | bytes 417800 | tf_op jit(solution)/shard_map/ppermute | solution.py:489
  17.4 6.9 %collective-permute-start.3 = (bf16[256,256]{1,0:T(8,128)(2,1)S(1)}, bf16[256,256]{1,0:T(8,128)(2,1)S(1)}, u32[]{:S(2)}, u32[]{:S(2)}) collective-permute-start(bf16[256,256]{1,0:T(8,128)(2,1)S(1)} %collective-permute-done.refs_7_), channel_id=1, source_target_pairs={{0,8},{8,16},{16,24},{24,32},{32,40},{40,48},{48,56},{56,0},{64,72... | collective-permute-start | bytes 393224 | tf_op jit(solution)/shard_map/ppermute | solution.py:489
  17.5 6.8 %collective-permute-start.4 = (bf16[256,256]{1,0:T(8,128)(2,1)S(1)}, bf16[256,256]{1,0:T(8,128)(2,1)S(1)}, u32[]{:S(2)}, u32[]{:S(2)}) collective-permute-start(bf16[256,256]{1,0:T(8,128)(2,1)S(1)} %collective-permute-done.1.refs_0_), channel_id=1, source_target_pairs={{0,56},{8,0},{16,8},{24,16},{32,24},{40,32},{48,40},{56,48},{64,12... | collective-permute-start | bytes 393224 | tf_op jit(solution)/shard_map/ppermute | solution.py:489
  24.3 5.6 %collective-permute-start.8 = (bf16[272,256]{1,0:T(8,128)(2,1)S(1)}, bf16[272,256]{1,0:T(8,128)(2,1)S(1)}, u32[]{:S(2)}, u32[]{:S(2)}) collective-permute-start(bf16[272,256]{1,0:T(8,128)(2,1)S(1)} %add.22), channel_id=1, source_target_pairs={{0,32},{64,96},{128,160},{192,224},{1,33},{65,97},{129,161},{193,2... | collective-permute-start | bytes 417800 | tf_op jit(solution)/shard_map/ppermute | solution.py:489
  26.6 6.3 %collective-permute-start.6 = (bf16[256,256]{1,0:T(8,128)(2,1)S(1)}, bf16[256,256]{1,0:T(8,128)(2,1)S(1)}, u32[]{:S(2)}, u32[]{:S(2)}) collective-permute-start(bf16[256,256]{1,0:T(8,128)(2,1)S(1)} %collective-permute-done.3.refs_6_), channel_id=1, source_target_pairs={{0,8},{8,16},{16,24},{24,32},{32,40},{40,48},{48,56},{56,0},{64,72... | collective-permute-start | bytes 393224 | tf_op jit(solution)/shard_map/ppermute | solution.py:489
  26.7 6.2 %collective-permute-start.7 = (bf16[256,256]{1,0:T(8,128)(2,1)S(1)}, bf16[256,256]{1,0:T(8,128)(2,1)S(1)}, u32[]{:S(2)}, u32[]{:S(2)}) collective-permute-start(bf16[256,256]{1,0:T(8,128)(2,1)S(1)} %collective-permute-done.4.refs_1_), channel_id=1, source_target_pairs={{0,56},{8,0},{16,8},{24,16},{32,24},{40,32},{48,40},{56,48},{64,12... | collective-permute-start | bytes 393224 | tf_op jit(solution)/shard_map/ppermute | solution.py:489
  32.9 5.6 %collective-permute-start.9 = (bf16[128,256]{1,0:T(8,128)(2,1)S(1)}, bf16[128,256]{1,0:T(8,128)(2,1)S(1)}, u32[]{:S(2)}, u32[]{:S(2)}) collective-permute-start(bf16[128,256]{1,0:T(8,128)(2,1)S(1)} %slice.6), channel_id=1, source_target_pairs={{0,8},{8,16},{16,24},{24,32},{32,40},{40,48},{48,56},{56,0},{64,72... | collective-permute-start | bytes 196616 | tf_op jit(solution)/shard_map/ppermute | solution.py:489
  40.1 16.8 %collective-permute-start.12 = (bf16[1024,256]{1,0:T(8,128)(2,1)S(1)}, bf16[1024,256]{1,0:T(8,128)(2,1)S(1)}, u32[]{:S(2)}, u32[]{:S(2)}) collective-permute-start(bf16[1024,256]{1,0:T(8,128)(2,1)S(1)} %get-tuple-element.52.row_a), channel_id=1, source_target_pairs={{0,64},{8,72},{16,80},{24,88},{32,96},{40,104},{48,112},{56,120},{... | collective-permute-start | bytes 1572872 | tf_op jit(solution)/shard_map/ppermute | solution.py:489
  41.4 17.8 %collective-permute-start.13 = (bf16[1024,256]{1,0:T(8,128)(2,1)S(1)}, bf16[1024,256]{1,0:T(8,128)(2,1)S(1)}, u32[]{:S(2)}, u32[]{:S(2)}) collective-permute-start(bf16[1024,256]{1,0:T(8,128)(2,1)S(1)} %get-tuple-element.53.row_b), channel_id=1, source_target_pairs={{0,192},{8,200},{16,208},{24,216},{32,224},{40,232},{48,240},{56,2... | collective-permute-start | bytes 1572872 | tf_op jit(solution)/shard_map/ppermute | solution.py:489
  42.7 24.6 %collective-permute-start.18 = (bf16[1024,256]{1,0:T(8,128)(2,1)S(1)}, bf16[1024,256]{1,0:T(8,128)(2,1)}, u32[]{:S(2)}, u32[]{:S(2)}) collective-permute-start(bf16[1024,256]{1,0:T(8,128)(2,1)S(1)} %get-tuple-element.52.row_a), channel_id=1, source_target_pairs={{0,192},{8,200},{16,208},{24,216},{32,224},{40,232},{48,240},{56,2... | collective-permute-start | bytes 1572872 | tf_op jit(solution)/shard_map/ppermute | solution.py:489
  44.0 24.0 %collective-permute-start.17 = (bf16[1024,256]{1,0:T(8,128)(2,1)S(1)}, bf16[1024,256]{1,0:T(8,128)(2,1)}, u32[]{:S(2)}, u32[]{:S(2)}) collective-permute-start(bf16[1024,256]{1,0:T(8,128)(2,1)S(1)} %get-tuple-element.53.row_b), channel_id=1, source_target_pairs={{0,64},{8,72},{16,80},{24,88},{32,96},{40,104},{48,112},{56,120},{... | collective-permute-start | bytes 1572872 | tf_op jit(solution)/shard_map/ppermute | solution.py:489
  45.3 7.7 %collective-permute-start.11 = (bf16[272,256]{1,0:T(8,128)(2,1)S(1)}, bf16[272,256]{1,0:T(8,128)(2,1)S(1)}, u32[]{:S(2)}, u32[]{:S(2)}) collective-permute-start(bf16[272,256]{1,0:T(8,128)(2,1)S(1)} %add.23), channel_id=1, source_target_pairs={{0,16},{64,80},{128,144},{192,208},{32,48},{96,112},{160,176},{224... | collective-permute-start | bytes 417800 | tf_op jit(solution)/shard_map/ppermute | solution.py:489
  59.2 7.5 %collective-permute-start.14 = (bf16[272,256]{1,0:T(8,128)(2,1)S(1)}, bf16[272,256]{1,0:T(8,128)(2,1)S(1)}, u32[]{:S(2)}, u32[]{:S(2)}) collective-permute-start(bf16[272,256]{1,0:T(8,128)(2,1)S(1)} %add.24), channel_id=1, source_target_pairs={{0,8},{64,72},{128,136},{192,200},{16,24},{80,88},{144,152},{208,2... | collective-permute-start | bytes 417800 | tf_op jit(solution)/shard_map/ppermute | solution.py:489
  60.8 52.0 %collective-permute-start.15 = (bf16[1024,256]{1,0:T(8,128)(2,1)S(1)}, bf16[1024,256]{1,0:T(8,128)(2,1)S(1)}, u32[]{:S(2)}, u32[]{:S(2)}) collective-permute-start(bf16[1024,256]{1,0:T(8,128)(2,1)S(1)} %collective-permute-done.12.below_a), channel_id=1, source_target_pairs={{64,128},{72,136},{80,144},{88,152},{96,160},{104,168},{112,176},{... | collective-permute-start | bytes 1572872 | tf_op jit(solution)/shard_map/ppermute | solution.py:489
  62.1 50.7 %collective-permute-start.16 = (bf16[1024,256]{1,0:T(8,128)(2,1)S(1)}, bf16[1024,256]{1,0:T(8,128)(2,1)S(1)}, u32[]{:S(2)}, u32[]{:S(2)}) collective-permute-start(bf16[1024,256]{1,0:T(8,128)(2,1)S(1)} %collective-permute-done.13.above_b), channel_id=1, source_target_pairs={{0,192},{8,200},{16,208},{24,216},{32,224},{40,232},{48,240},{56,2... | collective-permute-start | bytes 1572872 | tf_op jit(solution)/shard_map/ppermute | solution.py:489
  125.8 9.2 %collective-permute-start.23 = (bf16[256,512]{1,0:T(8,128)(2,1)S(1)}, bf16[256,512]{1,0:T(8,128)(2,1)S(1)}, u32[]{:S(2)}, u32[]{:S(2)}) collective-permute-start(bf16[256,512]{1,0:T(8,128)(2,1)S(1)} %get-tuple-element.65), channel_id=1, source_target_pairs={{0,2},{1,3},{2,4},{3,5},{4,6},{5,7},{6,0},{7,1},{8,10},{9,11},{10,... | collective-permute-start | bytes 786440 | tf_op jit(solution)/shard_map/ppermute | solution.py:532
  126.4 10.4 %collective-permute-start.24 = (bf16[256,512]{1,0:T(8,128)(2,1)S(1)}, bf16[256,512]{1,0:T(8,128)(2,1)S(1)}, u32[]{:S(2)}, u32[]{:S(2)}) collective-permute-start(bf16[256,512]{1,0:T(8,128)(2,1)S(1)} %get-tuple-element.66), channel_id=1, source_target_pairs={{0,6},{1,7},{2,0},{3,1},{4,2},{5,3},{6,4},{7,5},{8,14},{9,15},{10,... | collective-permute-start | bytes 786440 | tf_op jit(solution)/shard_map/ppermute | solution.py:532
  129.1 13.3 %collective-permute-start.21 = (bf16[256,512]{1,0:T(8,128)(2,1)S(1)}, bf16[256,512]{1,0:T(8,128)(2,1)S(1)}, u32[]{:S(2)}, u32[]{:S(2)}) collective-permute-start(bf16[256,512]{1,0:T(8,128)(2,1)S(1)} %get-tuple-element.62), channel_id=1, source_target_pairs={{0,6},{1,7},{2,0},{3,1},{4,2},{5,3},{6,4},{7,5},{8,14},{9,15},{10,... | collective-permute-start | bytes 786440 | tf_op jit(solution)/shard_map/ppermute | solution.py:536
  130.0 12.4 %collective-permute-start.22 = (bf16[256,512]{1,0:T(8,128)(2,1)S(1)}, bf16[256,512]{1,0:T(8,128)(2,1)S(1)}, u32[]{:S(2)}, u32[]{:S(2)}) collective-permute-start(bf16[256,512]{1,0:T(8,128)(2,1)S(1)} %get-tuple-element.63), channel_id=1, source_target_pairs={{0,2},{1,3},{2,4},{3,5},{4,6},{5,7},{6,0},{7,1},{8,10},{9,11},{10,... | collective-permute-start | bytes 786440 | tf_op jit(solution)/shard_map/ppermute | solution.py:536
  136.9 8.7 %collective-permute-start.25 = (bf16[256,512]{1,0:T(8,128)(2,1)S(1)}, bf16[256,512]{1,0:T(8,128)(2,1)S(1)}, u32[]{:S(2)}, u32[]{:S(2)}) collective-permute-start(bf16[256,512]{1,0:T(8,128)(2,1)S(1)} %get-tuple-element.69), channel_id=1, source_target_pairs={{0,2},{1,3},{2,4},{3,5},{4,6},{5,7},{6,0},{7,1},{8,10},{9,11},{10,... | collective-permute-start | bytes 786440 | tf_op jit(solution)/shard_map/ppermute | solution.py:539
  137.3 9.8 %collective-permute-start.26 = (bf16[256,512]{1,0:T(8,128)(2,1)S(1)}, bf16[256,512]{1,0:T(8,128)(2,1)S(1)}, u32[]{:S(2)}, u32[]{:S(2)}) collective-permute-start(bf16[256,512]{1,0:T(8,128)(2,1)S(1)} %get-tuple-element.70), channel_id=1, source_target_pairs={{0,6},{1,7},{2,0},{3,1},{4,2},{5,3},{6,4},{7,5},{8,14},{9,15},{10,... | collective-permute-start | bytes 786440 | tf_op jit(solution)/shard_map/ppermute | solution.py:539
  (12 other events, 195.3 us)

commit v6 on v5

--- a/solution.py
+++ b/solution.py
@@ -253,13 +253,18 @@
         tile = jnp.where(masked > 0, step, step + 1)
         return *tile_of(bank_ref, tile * TILE, TILE), bias_ref[jnp.minimum(tile, 1)]
 
+    here, later = copies[2 : 2 + len(firsts)], copies[2 + len(firsts) :]
+
     def read_fast(step, with_bias):
         if with_bias:
+            for one, on in here:
+                under(on, one.wait)
             return *tile_of(bank_ref, 0, TILE), bias_ref[0]
+        for at, (one, on) in enumerate(later):
+            pl.when(on & (step == at))(one.wait)
         return *tile_of(bank_ref, TILE + step * STEP, STEP), None
 
-    for one, on in copies[:1] + copies[2:]:
-        under(on, one.wait)
+    copies[0][0].wait()
     absorb(acc_ref.shape[0], view, masked, steps, read_fast)
     copies[1][0].wait()
     acc_ref[...] += carried_ref[...]
@@ -497,24 +502,26 @@
     left, right = [kept], [kept]
     rest = jnp.where(mine == 0, rest, jnp.zeros_like(rest))
     spread = lambda hops: [(r * WIDE + a, r * WIDE + b) for a, b in hops for r in range(tall)]
-    upward = [(0, WIDE)], [(0, 3 * WIDE), (WIDE, 2 * WIDE)], spread([(0, 4)])
+    upward = [(0, WIDE)], [(0, 3 * WIDE), (WIDE, 2 * WIDE)]
     for step in range(WIDE // 2 - 1):
         left.append(permute(left[-1], plus))
         right.append(permute(right[-1], minus))
-        rest = rest + permute(rest, upward[step])
-        left[-1], right[-1], rest = lax.optimization_barrier((left[-1], right[-1], rest))
+        if step < len(upward):
+            rest = rest + permute(rest, upward[step])
+            left[-1], right[-1], rest = lax.optimization_barrier((left[-1], right[-1], rest))
     opposite = [permute(left[-1][:half], plus), permute(right[-1][half:], minus)]
     ends = pack_row(place, right[1:] + opposite + left[:0:-1] + [kept])
 
     below_a = permute(ends[0], across([(0, 1), (1, 2), (2, 3)]))
     above_b = permute(ends[1], across([(0, 3), (1, 0)]))
+    rest, ends = lax.optimization_barrier((rest, ends))
+    rest = rest + permute(rest, spread([(0, 4)]))
+    rest, ends = lax.optimization_barrier((rest, ends))
     below_b = permute(ends[1], across([(0, 1), (1, 2), (2, 3)]))
     above_a = permute(ends[0], across([(0, 3)]))
-
-    rest, ends = lax.optimization_barrier((rest, ends))
-    rest = rest + permute(rest, spread([(0, 2), (4, 6)]))
     state = own_row(place, queries, key_rows, value_rows, *ends)
     rest, below_a, above_b, state = lax.optimization_barrier((rest, below_a, above_b, state))
+    rest = rest + permute(rest, spread([(0, 2), (4, 6)]))
     below2 = permute(below_a, across([(1, 2), (2, 3)]))
     above2 = permute(above_b, across([(0, 3), (3, 2)]))
     rest = rest + permute(rest, spread([(0, 1), (2, 3), (4, 5), (6, 7)]))

time: 149 us -> 154 us (1.034)
  waiting for transfers between devices: 36.8 us -> 44.7 us
  starting transfers between devices: 43.4 us -> 41.2 us
    ppermute x19, waiting for transfers between devices: 21.7 us -> 29.6 us  [on_device(): permute = lambda x, pairs: lax.ppermute(x, 'ctx', pairs)]
    ppermute x19, starting transfers between devices: 35.4 us -> 33.2 us  [on_device(): permute = lambda x, pairs: lax.ppermute(x, 'ctx', pairs)]
  transfers between devices with their start and end apart: 27 -> 27, of which waited for: 15 -> 17; matrix products, arithmetic and copies ran while one was open for 1% -> 1% of each run, Pallas kernels for 34% -> 33%
where the time goes in v6:
time: 154 us; the launch traced here: 153 us
  Pallas kernels  64.3 us (42%)
  waiting for transfers between devices  44.7 us (29%)
  starting transfers between devices  41.2 us (27%)
    pallas_call x1, Pallas kernels, early_rows(): pl.pallas_call(early_kernel, grid=(1,), out_shape=state_of(length, heads)...  44.2 us
    ppermute x19, starting transfers between devices, on_device(): permute = lambda x, pairs: lax.ppermute(x, 'ctx', pairs)  33.2 us
    ppermute x19, waiting for transfers between devices, on_device(): permute = lambda x, pairs: lax.ppermute(x, 'ctx', pairs)  29.6 us
    pallas_call x1, Pallas kernels, rest_rows(): pl.pallas_call(rest_kernel, grid=(1,), out_shape=[jax.ShapeDtypeStruct(sh...  10.4 us
    pallas_call x1, Pallas kernels, own_row(): pl.pallas_call(own_row_kernel, grid=(1,), out_shape=state, in_specs=[SMEM...  4.97 us
    ppermute x1, waiting for transfers between devices, on_device(): lax.ppermute(upper_down, 'head', down)  3.3 us
    ppermute x1, waiting for transfers between devices, on_device(): lax.ppermute(upper_up, 'head', up)  3.09 us
  transfers between devices with their start and end apart: 27, of which 17 were waited for; matrix products, arithmetic and copies ran while one was open for 1% of the time, Pallas kernels for 33%

profile of v6, /device:TPU:30, one launch (start us, length us, event | category | flops | bytes accessed | tf_op | source)
XLA Modules:
  0.0 153.1 jit_solution(3794658372981697465)
XLA Ops:
  0.7 2.4 %select_kept.1 = (bf16[256,256]{1,0:T(8,128)(2,1)}, bf16[272,256]{1,0:T(8,128)(2,1)}) custom-call(s32[1]{0:T(128)S(6)} %copy.7.used_ref, s32[1,256]{1,0:T(1,128)} %refs_0_.1, bf16[512,128]{1,0:T(8,128)(2,1)} %k_ref.1, bf16[512,128]{1,0:T(8,128)(2,1)} %v_ref.1), custom_call_target="tpu_custom_call" | custom-call | tf_op jit(solution)/shard_map/select_kept/pallas_call | solution.py:77
  3.8 5.9 %collective-permute-start.1 = (bf16[256,256]{1,0:T(8,128)(2,1)}, bf16[256,256]{1,0:T(8,128)(2,1)S(1)}, u32[]{:S(2)}, u32[]{:S(2)}) collective-permute-start(bf16[256,256]{1,0:T(8,128)(2,1)} %get-tuple-element.38.refs_8_), channel_id=1, source_target_pairs={{0,56},{8,0},{16,8},{24,16},{32,24},{40,32},{48,40},{56,48},{64,12... | collective-permute-start | bytes 393224 | tf_op jit(solution)/shard_map/ppermute | solution.py:494
  9.8 3.0 %collective-permute-done.1.refs_0_ = bf16[256,256]{1,0:T(8,128)(2,1)S(1)} collective-permute-done((bf16[256,256]{1,0:T(8,128)(2,1)}, bf16[256,256]{1,0:T(8,128)(2,1)S(1)}, u32[]{:S(2)}, u32[]{:S(2)}) %collective-permute-start.1) | collective-permute-done | bytes 131104 | tf_op jit(solution)/shard_map/ppermute | solution.py:494
  12.8 3.3 %collective-permute-done.refs_7_ = bf16[256,256]{1,0:T(8,128)(2,1)S(1)} collective-permute-done((bf16[256,256]{1,0:T(8,128)(2,1)}, bf16[256,256]{1,0:T(8,128)(2,1)S(1)}, u32[]{:S(2)}, u32[]{:S(2)}) %collective-permute-start) | collective-permute-done | bytes 131104 | tf_op jit(solution)/shard_map/ppermute | solution.py:494
  17.5 3.2 %collective-permute-start.4 = (bf16[256,256]{1,0:T(8,128)(2,1)S(1)}, bf16[256,256]{1,0:T(8,128)(2,1)S(1)}, u32[]{:S(2)}, u32[]{:S(2)}) collective-permute-start(bf16[256,256]{1,0:T(8,128)(2,1)S(1)} %collective-permute-done.1.refs_0_), channel_id=1, source_target_pairs={{0,56},{8,0},{16,8},{24,16},{32,24},{40,32},{48,40},{56,48},{64,12... | collective-permute-start | bytes 393224 | tf_op jit(solution)/shard_map/ppermute | solution.py:494
  20.7 3.5 %collective-permute-done.5 = bf16[272,256]{1,0:T(8,128)(2,1)S(1)} collective-permute-done((bf16[272,256]{1,0:T(8,128)(2,1)S(1)}, bf16[272,256]{1,0:T(8,128)(2,1)S(1)}, u32[]{:S(2)}, u32[]{:S(2)}) %collective-permute-start.5) | collective-permute-done | bytes 139296 | tf_op jit(solution)/shard_map/ppermute | solution.py:494
  24.3 2.6 %collective-permute-start.6 = (bf16[256,256]{1,0:T(8,128)(2,1)S(1)}, bf16[256,256]{1,0:T(8,128)(2,1)S(1)}, u32[]{:S(2)}, u32[]{:S(2)}) collective-permute-start(bf16[256,256]{1,0:T(8,128)(2,1)S(1)} %collective-permute-done.4.refs_1_), channel_id=1, source_target_pairs={{0,56},{8,0},{16,8},{24,16},{32,24},{40,32},{48,40},{56,48},{64,12... | collective-permute-start | bytes 393224 | tf_op jit(solution)/shard_map/ppermute | solution.py:494
  26.9 3.2 %collective-permute-done.6.refs_2_ = bf16[256,256]{1,0:T(8,128)(2,1)S(1)} collective-permute-done((bf16[256,256]{1,0:T(8,128)(2,1)S(1)}, bf16[256,256]{1,0:T(8,128)(2,1)S(1)}, u32[]{:S(2)}, u32[]{:S(2)}) %collective-permute-start.6) | collective-permute-done | bytes 131104 | tf_op jit(solution)/shard_map/ppermute | solution.py:494
  30.1 3.4 %collective-permute-start.9 = (bf16[128,256]{1,0:T(8,128)(2,1)S(1)}, bf16[128,256]{1,0:T(8,128)(2,1)S(1)}, u32[]{:S(2)}, u32[]{:S(2)}) collective-permute-start(bf16[128,256]{1,0:T(8,128)(2,1)S(1)} %slice.9), channel_id=1, source_target_pairs={{0,56},{8,0},{16,8},{24,16},{32,24},{40,32},{48,40},{56,48},{64,12... | collective-permute-start | bytes 196616 | tf_op jit(solution)/shard_map/ppermute | solution.py:494
  35.4 3.8 %collective-permute-done.8.refs_3_ = bf16[128,256]{1,0:T(8,128)(2,1)S(1)} collective-permute-done((bf16[128,256]{1,0:T(8,128)(2,1)S(1)}, bf16[128,256]{1,0:T(8,128)(2,1)S(1)}, u32[]{:S(2)}, u32[]{:S(2)}) %collective-permute-start.8) | collective-permute-done | bytes 65568 | tf_op jit(solution)/shard_map/ppermute | solution.py:494
  40.8 2.5 %collective-permute-start.10 = (bf16[272,256]{1,0:T(8,128)(2,1)S(1)}, bf16[272,256]{1,0:T(8,128)(2,1)S(1)}, u32[]{:S(2)}, u32[]{:S(2)}) collective-permute-start(bf16[272,256]{1,0:T(8,128)(2,1)S(1)} %add.22), channel_id=1, source_target_pairs={{0,32},{64,96},{128,160},{192,224},{1,33},{65,97},{129,161},{193,2... | collective-permute-start | bytes 417800 | tf_op jit(solution)/shard_map/ppermute | solution.py:494
  48.6 5.0 %own_row.1.state_in = f32[4,512,384]{2,1,0:T(8,128)} custom-call(s32[4]{0:T(128)} %copy-done.2, bf16[512,512]{1,0:T(8,128)(2,1)} %q_ref.5, bf16[512,128]{1,0:T(8,128)(2,1)} %k_ref.1, bf16[512,128]{1,0:T(8,128)(2,1)} %v_ref.1, bf16[1024,256]{1,0:T(8,128)(2,1)} %copy-done.5, bf16[1024,256]{1,0:T(8,128)(2,1)} %copy-done.6), custom_call_target="tpu_custom_call" | custom-call | flops 5368709120 | bytes 8388608 | tf_op jit(solution)/shard_map/own_row/pallas_call | solution.py:377
  53.6 5.8 %collective-permute-done.11.below_a = bf16[1024,256]{1,0:T(8,128)(2,1)S(1)} collective-permute-done((bf16[1024,256]{1,0:T(8,128)(2,1)S(1)}, bf16[1024,256]{1,0:T(8,128)(2,1)S(1)}, u32[]{:S(2)}, u32[]{:S(2)}) %collective-permute-start.11) | collective-permute-done | bytes 524320 | tf_op jit(solution)/shard_map/ppermute | solution.py:494
  59.3 2.6 %collective-permute-done.12.above_b = bf16[1024,256]{1,0:T(8,128)(2,1)S(1)} collective-permute-done((bf16[1024,256]{1,0:T(8,128)(2,1)S(1)}, bf16[1024,256]{1,0:T(8,128)(2,1)S(1)}, u32[]{:S(2)}, u32[]{:S(2)}) %collective-permute-start.12) | collective-permute-done | bytes 524320 | tf_op jit(solution)/shard_map/ppermute | solution.py:494
  63.2 2.6 %collective-permute-done.13 = bf16[272,256]{1,0:T(8,128)(2,1)S(1)} collective-permute-done((bf16[272,256]{1,0:T(8,128)(2,1)S(1)}, bf16[272,256]{1,0:T(8,128)(2,1)S(1)}, u32[]{:S(2)}, u32[]{:S(2)}) %collective-permute-start.13) | collective-permute-done | bytes 139296 | tf_op jit(solution)/shard_map/ppermute | solution.py:494
  68.4 4.6 %collective-permute-start.16 = (bf16[1024,256]{1,0:T(8,128)(2,1)S(1)}, bf16[1024,256]{1,0:T(8,128)(2,1)S(1)}, u32[]{:S(2)}, u32[]{:S(2)}) collective-permute-start(bf16[1024,256]{1,0:T(8,128)(2,1)S(1)} %collective-permute-done.12.above_b), channel_id=1, source_target_pairs={{0,192},{8,200},{16,208},{24,216},{32,224},{40,232},{48,240},{56,2... | collective-permute-start | bytes 1572872 | tf_op jit(solution)/shard_map/ppermute | solution.py:494
  73.8 44.2 %early_rows.1.state_in = f32[4,512,384]{2,1,0:T(8,128)} custom-call(s32[4]{0:T(128)} %copy-done.2, bf16[512,512]{1,0:T(8,128)(2,1)} %q_ref.5, bf16[272,256]{1,0:T(8,128)(2,1)} %add.25.rest_ref, bf16[1024,256]{1,0:T(8,128)(2,1)} %copy-done.5, bf16[1024,256]{1,0:T(8,128)(2,1)} %copy-done.7, bf16[1024,256]{1,0:T(8,128)(2,1)} %collective-permute-done.17.below_b, ...), custom_call_target="tpu_custom_call" | custom-call | flops 9663676416 | bytes 8388608 | tf_op jit(solution)/shard_map/early_rows/pallas_call | solution.py:398
  118.0 10.4 %rest_rows.1 = (bf16[4,512,512]{2,1,0:T(8,128)(2,1)S(1)}, bf16[512,512]{1,0:T(8,128)(2,1)S(1)}, bf16[3,512,512]{2,1,0:T(8,128)(2,1)S(1)}) custom-call(s32[4]{0:T(128)S(1)} %copy-done.3, bf16[512,512]{1,0:T(8,128)(2,1)S(1)} %copy-done.4, bf16[272,256]{1,0:T(8,128)(2,1)S(1)} %copy-done, bf16[1024,256]{1,0:T(8,128)(2,1)S(1)} %collective-permute-done.15.below2_ref, ...), custom_call_target="tpu_custom_call" | custom-call | flops 5368709120 | bytes 8388608 | tf_op jit(solution)/shard_map/rest_rows/pallas_call | solution.py:417
  128.7 1.9 %collective-permute-done.19.other_ref = bf16[512,512]{1,0:T(8,128)(2,1)S(1)} collective-permute-done((bf16[512,512]{1,0:T(8,128)(2,1)S(1)}, bf16[512,512]{1,0:T(8,128)(2,1)S(1)}, u32[]{:S(2)}, u32[]{:S(2)}) %collective-permute-start.19) | collective-permute-done | bytes 524320 | tf_op jit(solution)/shard_map/ppermute | solution.py:534
  135.1 2.4 %collective-permute-start.22 = (bf16[256,512]{1,0:T(8,128)(2,1)S(1)}, bf16[256,512]{1,0:T(8,128)(2,1)S(1)}, u32[]{:S(2)}, u32[]{:S(2)}) collective-permute-start(bf16[256,512]{1,0:T(8,128)(2,1)S(1)} %get-tuple-element.63), channel_id=1, source_target_pairs={{0,2},{1,3},{2,4},{3,5},{4,6},{5,7},{6,0},{7,1},{8,10},{9,11},{10,... | collective-permute-start | bytes 786440 | tf_op jit(solution)/shard_map/ppermute | solution.py:543
  137.5 2.6 %collective-permute-done.23.refs_2_ = bf16[256,512]{1,0:T(8,128)(2,1)S(1)} collective-permute-done((bf16[256,512]{1,0:T(8,128)(2,1)S(1)}, bf16[256,512]{1,0:T(8,128)(2,1)S(1)}, u32[]{:S(2)}, u32[]{:S(2)}) %collective-permute-start.23) | collective-permute-done | bytes 262176 | tf_op jit(solution)/shard_map/ppermute | solution.py:539
  142.4 1.7 %collective-permute-start.26 = (bf16[256,512]{1,0:T(8,128)(2,1)S(1)}, bf16[256,512]{1,0:T(8,128)(2,1)S(1)}, u32[]{:S(2)}, u32[]{:S(2)}) collective-permute-start(bf16[256,512]{1,0:T(8,128)(2,1)S(1)} %get-tuple-element.70), channel_id=1, source_target_pairs={{0,6},{1,7},{2,0},{3,1},{4,2},{5,3},{6,4},{7,5},{8,14},{9,15},{10,... | collective-permute-start | bytes 786440 | tf_op jit(solution)/shard_map/ppermute | solution.py:546
  144.2 3.3 %collective-permute-done.21.refs_2_ = bf16[256,512]{1,0:T(8,128)(2,1)S(1)} collective-permute-done((bf16[256,512]{1,0:T(8,128)(2,1)S(1)}, bf16[256,512]{1,0:T(8,128)(2,1)S(1)}, u32[]{:S(2)}, u32[]{:S(2)}) %collective-permute-start.21) | collective-permute-done | bytes 262176 | tf_op jit(solution)/shard_map/ppermute | solution.py:543
  147.7 3.1 %collective-permute-done.25.refs_1_ = bf16[256,512]{1,0:T(8,128)(2,1)S(1)} collective-permute-done((bf16[256,512]{1,0:T(8,128)(2,1)S(1)}, bf16[256,512]{1,0:T(8,128)(2,1)S(1)}, u32[]{:S(2)}, u32[]{:S(2)}) %collective-permute-start.25) | collective-permute-done | bytes 262176 | tf_op jit(solution)/shard_map/ppermute | solution.py:546
  (67 shorter events, 25.1 us)
Async XLA Ops:
  3.1 6.6 %collective-permute-start.2 = (bf16[272,256]{1,0:T(8,128)(2,1)S(1)}, bf16[272,256]{1,0:T(8,128)(2,1)S(1)}, u32[]{:S(2)}, u32[]{:S(2)}) collective-permute-start(bf16[272,256]{1,0:T(8,128)(2,1)S(1)} %broadcast_select_fusion), channel_id=1, source_target_pairs={{0,64},{1,65},{2,66},{3,67},{4,68},{5,69},{6,70},{7,71}} | collective-permute-start | bytes 417800 | tf_op jit(solution)/shard_map/ppermute | solution.py:494
  3.8 9.0 %collective-permute-start.1 = (bf16[256,256]{1,0:T(8,128)(2,1)}, bf16[256,256]{1,0:T(8,128)(2,1)S(1)}, u32[]{:S(2)}, u32[]{:S(2)}) collective-permute-start(bf16[256,256]{1,0:T(8,128)(2,1)} %get-tuple-element.38.refs_8_), channel_id=1, source_target_pairs={{0,56},{8,0},{16,8},{24,16},{32,24},{40,32},{48,40},{56,48},{64,12... | collective-permute-start | bytes 393224 | tf_op jit(solution)/shard_map/ppermute | solution.py:494
  9.7 6.4 %collective-permute-start = (bf16[256,256]{1,0:T(8,128)(2,1)}, bf16[256,256]{1,0:T(8,128)(2,1)S(1)}, u32[]{:S(2)}, u32[]{:S(2)}) collective-permute-start(bf16[256,256]{1,0:T(8,128)(2,1)} %get-tuple-element.38.refs_8_), channel_id=1, source_target_pairs={{0,8},{8,16},{16,24},{24,32},{32,40},{40,48},{48,56},{56,0},{64,72... | collective-permute-start | bytes 393224 | tf_op jit(solution)/shard_map/ppermute | solution.py:494
  16.1 8.1 %collective-permute-start.5 = (bf16[272,256]{1,0:T(8,128)(2,1)S(1)}, bf16[272,256]{1,0:T(8,128)(2,1)S(1)}, u32[]{:S(2)}, u32[]{:S(2)}) collective-permute-start(bf16[272,256]{1,0:T(8,128)(2,1)S(1)} %fusion), channel_id=1, source_target_pairs={{0,192},{64,128},{1,193},{65,129},{2,194},{66,130},{3,195},{67,131... | collective-permute-start | bytes 417800 | tf_op jit(solution)/shard_map/ppermute | solution.py:494
  17.4 6.9 %collective-permute-start.3 = (bf16[256,256]{1,0:T(8,128)(2,1)S(1)}, bf16[256,256]{1,0:T(8,128)(2,1)S(1)}, u32[]{:S(2)}, u32[]{:S(2)}) collective-permute-start(bf16[256,256]{1,0:T(8,128)(2,1)S(1)} %collective-permute-done.refs_7_), channel_id=1, source_target_pairs={{0,8},{8,16},{16,24},{24,32},{32,40},{40,48},{48,56},{56,0},{64,72... | collective-permute-start | bytes 393224 | tf_op jit(solution)/shard_map/ppermute | solution.py:494
  17.5 6.8 %collective-permute-start.4 = (bf16[256,256]{1,0:T(8,128)(2,1)S(1)}, bf16[256,256]{1,0:T(8,128)(2,1)S(1)}, u32[]{:S(2)}, u32[]{:S(2)}) collective-permute-start(bf16[256,256]{1,0:T(8,128)(2,1)S(1)} %collective-permute-done.1.refs_0_), channel_id=1, source_target_pairs={{0,56},{8,0},{16,8},{24,16},{32,24},{40,32},{48,40},{56,48},{64,12... | collective-permute-start | bytes 393224 | tf_op jit(solution)/shard_map/ppermute | solution.py:494
  24.3 5.7 %collective-permute-start.6 = (bf16[256,256]{1,0:T(8,128)(2,1)S(1)}, bf16[256,256]{1,0:T(8,128)(2,1)S(1)}, u32[]{:S(2)}, u32[]{:S(2)}) collective-permute-start(bf16[256,256]{1,0:T(8,128)(2,1)S(1)} %collective-permute-done.4.refs_1_), channel_id=1, source_target_pairs={{0,56},{8,0},{16,8},{24,16},{32,24},{40,32},{48,40},{56,48},{64,12... | collective-permute-start | bytes 393224 | tf_op jit(solution)/shard_map/ppermute | solution.py:494
  26.9 6.8 %collective-permute-start.7 = (bf16[256,256]{1,0:T(8,128)(2,1)S(1)}, bf16[256,256]{1,0:T(8,128)(2,1)S(1)}, u32[]{:S(2)}, u32[]{:S(2)}) collective-permute-start(bf16[256,256]{1,0:T(8,128)(2,1)S(1)} %collective-permute-done.3.refs_6_), channel_id=1, source_target_pairs={{0,8},{8,16},{16,24},{24,32},{32,40},{40,48},{48,56},{56,0},{64,72... | collective-permute-start | bytes 393224 | tf_op jit(solution)/shard_map/ppermute | solution.py:494
  30.1 5.3 %collective-permute-start.9 = (bf16[128,256]{1,0:T(8,128)(2,1)S(1)}, bf16[128,256]{1,0:T(8,128)(2,1)S(1)}, u32[]{:S(2)}, u32[]{:S(2)}) collective-permute-start(bf16[128,256]{1,0:T(8,128)(2,1)S(1)} %slice.9), channel_id=1, source_target_pairs={{0,56},{8,0},{16,8},{24,16},{32,24},{40,32},{48,40},{56,48},{64,12... | collective-permute-start | bytes 196616 | tf_op jit(solution)/shard_map/ppermute | solution.py:494
  33.7 5.5 %collective-permute-start.8 = (bf16[128,256]{1,0:T(8,128)(2,1)S(1)}, bf16[128,256]{1,0:T(8,128)(2,1)S(1)}, u32[]{:S(2)}, u32[]{:S(2)}) collective-permute-start(bf16[128,256]{1,0:T(8,128)(2,1)S(1)} %slice.8), channel_id=1, source_target_pairs={{0,8},{8,16},{16,24},{24,32},{32,40},{40,48},{48,56},{56,0},{64,72... | collective-permute-start | bytes 196616 | tf_op jit(solution)/shard_map/ppermute | solution.py:494
  40.8 5.1 %collective-permute-start.10 = (bf16[272,256]{1,0:T(8,128)(2,1)S(1)}, bf16[272,256]{1,0:T(8,128)(2,1)S(1)}, u32[]{:S(2)}, u32[]{:S(2)}) collective-permute-start(bf16[272,256]{1,0:T(8,128)(2,1)S(1)} %add.22), channel_id=1, source_target_pairs={{0,32},{64,96},{128,160},{192,224},{1,33},{65,97},{129,161},{193,2... | collective-permute-start | bytes 417800 | tf_op jit(solution)/shard_map/ppermute | solution.py:494
  43.3 16.0 %collective-permute-start.11 = (bf16[1024,256]{1,0:T(8,128)(2,1)S(1)}, bf16[1024,256]{1,0:T(8,128)(2,1)S(1)}, u32[]{:S(2)}, u32[]{:S(2)}) collective-permute-start(bf16[1024,256]{1,0:T(8,128)(2,1)S(1)} %get-tuple-element.52.row_a), channel_id=1, source_target_pairs={{0,64},{8,72},{16,80},{24,88},{32,96},{40,104},{48,112},{56,120},{... | collective-permute-start | bytes 1572872 | tf_op jit(solution)/shard_map/ppermute | solution.py:494
  44.6 17.3 %collective-permute-start.12 = (bf16[1024,256]{1,0:T(8,128)(2,1)S(1)}, bf16[1024,256]{1,0:T(8,128)(2,1)S(1)}, u32[]{:S(2)}, u32[]{:S(2)}) collective-permute-start(bf16[1024,256]{1,0:T(8,128)(2,1)S(1)} %get-tuple-element.53.row_b), channel_id=1, source_target_pairs={{0,192},{8,200},{16,208},{24,216},{32,224},{40,232},{48,240},{56,2... | collective-permute-start | bytes 1572872 | tf_op jit(solution)/shard_map/ppermute | solution.py:494
  46.0 27.8 %collective-permute-start.17 = (bf16[1024,256]{1,0:T(8,128)(2,1)S(1)}, bf16[1024,256]{1,0:T(8,128)(2,1)}, u32[]{:S(2)}, u32[]{:S(2)}) collective-permute-start(bf16[1024,256]{1,0:T(8,128)(2,1)S(1)} %get-tuple-element.53.row_b), channel_id=1, source_target_pairs={{0,64},{8,72},{16,80},{24,88},{32,96},{40,104},{48,112},{56,120},{... | collective-permute-start | bytes 1572872 | tf_op jit(solution)/shard_map/ppermute | solution.py:494
  47.3 26.5 %collective-permute-start.18 = (bf16[1024,256]{1,0:T(8,128)(2,1)S(1)}, bf16[1024,256]{1,0:T(8,128)(2,1)}, u32[]{:S(2)}, u32[]{:S(2)}) collective-permute-start(bf16[1024,256]{1,0:T(8,128)(2,1)S(1)} %get-tuple-element.52.row_a), channel_id=1, source_target_pairs={{0,192},{8,200},{16,208},{24,216},{32,224},{40,232},{48,240},{56,2... | collective-permute-start | bytes 1572872 | tf_op jit(solution)/shard_map/ppermute | solution.py:494
  65.8 7.2 %collective-permute-start.14 = (bf16[272,256]{1,0:T(8,128)(2,1)S(1)}, bf16[272,256]{1,0:T(8,128)(2,1)S(1)}, u32[]{:S(2)}, u32[]{:S(2)}) collective-permute-start(bf16[272,256]{1,0:T(8,128)(2,1)S(1)} %add.24), channel_id=1, source_target_pairs={{0,8},{64,72},{128,136},{192,200},{16,24},{80,88},{144,152},{208,2... | collective-permute-start | bytes 417800 | tf_op jit(solution)/shard_map/ppermute | solution.py:494
  67.1 50.8 %collective-permute-start.15 = (bf16[1024,256]{1,0:T(8,128)(2,1)S(1)}, bf16[1024,256]{1,0:T(8,128)(2,1)S(1)}, u32[]{:S(2)}, u32[]{:S(2)}) collective-permute-start(bf16[1024,256]{1,0:T(8,128)(2,1)S(1)} %collective-permute-done.11.below_a), channel_id=1, source_target_pairs={{64,128},{72,136},{80,144},{88,152},{96,160},{104,168},{112,176},{... | collective-permute-start | bytes 1572872 | tf_op jit(solution)/shard_map/ppermute | solution.py:494
  68.4 49.5 %collective-permute-start.16 = (bf16[1024,256]{1,0:T(8,128)(2,1)S(1)}, bf16[1024,256]{1,0:T(8,128)(2,1)S(1)}, u32[]{:S(2)}, u32[]{:S(2)}) collective-permute-start(bf16[1024,256]{1,0:T(8,128)(2,1)S(1)} %collective-permute-done.12.above_b), channel_id=1, source_target_pairs={{0,192},{8,200},{16,208},{24,216},{32,224},{40,232},{48,240},{56,2... | collective-permute-start | bytes 1572872 | tf_op jit(solution)/shard_map/ppermute | solution.py:494
  130.9 9.2 %collective-permute-start.23 = (bf16[256,512]{1,0:T(8,128)(2,1)S(1)}, bf16[256,512]{1,0:T(8,128)(2,1)S(1)}, u32[]{:S(2)}, u32[]{:S(2)}) collective-permute-start(bf16[256,512]{1,0:T(8,128)(2,1)S(1)} %get-tuple-element.65), channel_id=1, source_target_pairs={{0,2},{1,3},{2,4},{3,5},{4,6},{5,7},{6,0},{7,1},{8,10},{9,11},{10,... | collective-permute-start | bytes 786440 | tf_op jit(solution)/shard_map/ppermute | solution.py:539
  131.5 10.4 %collective-permute-start.24 = (bf16[256,512]{1,0:T(8,128)(2,1)S(1)}, bf16[256,512]{1,0:T(8,128)(2,1)S(1)}, u32[]{:S(2)}, u32[]{:S(2)}) collective-permute-start(bf16[256,512]{1,0:T(8,128)(2,1)S(1)} %get-tuple-element.66), channel_id=1, source_target_pairs={{0,6},{1,7},{2,0},{3,1},{4,2},{5,3},{6,4},{7,5},{8,14},{9,15},{10,... | collective-permute-start | bytes 786440 | tf_op jit(solution)/shard_map/ppermute | solution.py:539
  134.2 13.3 %collective-permute-start.21 = (bf16[256,512]{1,0:T(8,128)(2,1)S(1)}, bf16[256,512]{1,0:T(8,128)(2,1)S(1)}, u32[]{:S(2)}, u32[]{:S(2)}) collective-permute-start(bf16[256,512]{1,0:T(8,128)(2,1)S(1)} %get-tuple-element.62), channel_id=1, source_target_pairs={{0,6},{1,7},{2,0},{3,1},{4,2},{5,3},{6,4},{7,5},{8,14},{9,15},{10,... | collective-permute-start | bytes 786440 | tf_op jit(solution)/shard_map/ppermute | solution.py:543
  135.1 12.4 %collective-permute-start.22 = (bf16[256,512]{1,0:T(8,128)(2,1)S(1)}, bf16[256,512]{1,0:T(8,128)(2,1)S(1)}, u32[]{:S(2)}, u32[]{:S(2)}) collective-permute-start(bf16[256,512]{1,0:T(8,128)(2,1)S(1)} %get-tuple-element.63), channel_id=1, source_target_pairs={{0,2},{1,3},{2,4},{3,5},{4,6},{5,7},{6,0},{7,1},{8,10},{9,11},{10,... | collective-permute-start | bytes 786440 | tf_op jit(solution)/shard_map/ppermute | solution.py:543
  142.1 8.7 %collective-permute-start.25 = (bf16[256,512]{1,0:T(8,128)(2,1)S(1)}, bf16[256,512]{1,0:T(8,128)(2,1)S(1)}, u32[]{:S(2)}, u32[]{:S(2)}) collective-permute-start(bf16[256,512]{1,0:T(8,128)(2,1)S(1)} %get-tuple-element.69), channel_id=1, source_target_pairs={{0,2},{1,3},{2,4},{3,5},{4,6},{5,7},{6,0},{7,1},{8,10},{9,11},{10,... | collective-permute-start | bytes 786440 | tf_op jit(solution)/shard_map/ppermute | solution.py:546
  142.4 9.8 %collective-permute-start.26 = (bf16[256,512]{1,0:T(8,128)(2,1)S(1)}, bf16[256,512]{1,0:T(8,128)(2,1)S(1)}, u32[]{:S(2)}, u32[]{:S(2)}) collective-permute-start(bf16[256,512]{1,0:T(8,128)(2,1)S(1)} %get-tuple-element.70), channel_id=1, source_target_pairs={{0,6},{1,7},{2,0},{3,1},{4,2},{5,3},{6,4},{7,5},{8,14},{9,15},{10,... | collective-permute-start | bytes 786440 | tf_op jit(solution)/shard_map/ppermute | solution.py:546
  (12 other events, 199.8 us)

commit v7 on v6

--- a/solution.py
+++ b/solution.py
@@ -237,19 +237,22 @@
     for one, on in copies:
         under(on, one.start)
     acc_ref[...] = jnp.zeros(acc_ref.shape, jnp.float32)
-    bank_ref[KEEP:TILE] = rest_ref[: TILE - KEEP]
-    number = wide(rest_ref[TILE - KEEP : TILE - KEEP + 1, :HEAD].astype(jnp.int32), TILE)
-    at = count_along((1, TILE), 1)
-    limit = jnp.where(at < KEEP, number, KEEP + used - number)
-    bias_ref[0] = jnp.broadcast_to(bias_where(at < limit), bias_ref.shape[1:])
-    bias_ref[1] = jnp.zeros(bias_ref.shape[1:], jnp.float32)
-    view = head_view(q_ref, acc_ref, peak_ref)
-    masked = sum(jnp.where(on, 1, 0) for _, on in firsts)
+    view, masked = head_view(q_ref, acc_ref, peak_ref), None
+    if firsts:
+        bank_ref[KEEP:TILE] = rest_ref[: TILE - KEEP]
+        number = wide(rest_ref[TILE - KEEP : TILE - KEEP + 1, :HEAD].astype(jnp.int32), TILE)
+        at = count_along((1, TILE), 1)
+        limit = jnp.where(at < KEEP, number, KEEP + used - number)
+        bias_ref[0] = jnp.broadcast_to(bias_where(at < limit), bias_ref.shape[1:])
+        bias_ref[1] = jnp.zeros(bias_ref.shape[1:], jnp.float32)
+        masked = sum(jnp.where(on, 1, 0) for _, on in firsts)
 
     def start(h):
         acc_ref[h] = carried_ref[h]
 
     def read(step):
+        if masked is None:
+            return *tile_of(bank_ref, TILE + step * TILE, TILE), None
         tile = jnp.where(masked > 0, step, step + 1)
         return *tile_of(bank_ref, tile * TILE, TILE), bias_ref[jnp.minimum(tile, 1)]
 
@@ -268,31 +271,42 @@
     absorb(acc_ref.shape[0], view, masked, steps, read_fast)
     copies[1][0].wait()
     acc_ref[...] += carried_ref[...]
-    absorb_again(acc_ref, view, start, masked + STEP // TILE * steps, read)
-
-
-def early_kernel(
-    place_ref, q_ref, rest_ref, row_a, below_a, below_b, above_a, above_b, state_in, state_ref,
-    *refs,
+    tiles = STEP // TILE * steps + (0 if masked is None else masked)
+    absorb_again(acc_ref, view, start, tiles, read)
+
+
+def early_kernel(place_ref, q_ref, below_ref, above_ref, state_in, state_ref, *refs):
+    y = place_ref[0] // WIDE
+    pieces = (below_ref, y > 0), (above_ref, y == 3)
+    steps = jnp.where(y == 3, 2, jnp.minimum(y, 1))
+    refs = *sums(state_ref), *refs
+    more_keys(q_ref, None, state_in, refs, None, (), pieces, steps)
+
+
+def hand_on_kernel(place_ref, q_ref, below_ref, above_ref, row_a, below_a, state_in, *refs):
+    y = place_ref[0] // WIDE
+    state_ref, first_ref, *refs, first_sem = refs
+    copies = [
+        (y == row, pltpu.make_async_copy(ref.at[pl.ds(0, KEEP)], first_ref, first_sem))
+        for row, ref in ((0, row_a), (1, below_a), (3, above_ref))
+    ]
+    for on, copy in copies:
+        pl.when(on)(copy.start)
+    early_kernel(place_ref, q_ref, below_ref, above_ref, state_in, state_ref, *refs)
+    for on, copy in copies:
+        pl.when(on)(copy.wait)
+
+
+def rest_kernel(
+    place_ref, q_ref, rest_ref, first_ref, below2_ref, above2_ref, weight_ref, state_in,
+    own_out, far_out, near_out, own_ref, send_ref, w_ref, att_ref, out_sems, *refs,
 ):
     mine, used = place_ref[0], place_ref[1]
     y = mine // WIDE
-    firsts = (row_a, (mine > 0) & (y == 0)), (below_a, y == 1), (above_a, y == 3)
-    pieces = (below_a, y > 0), (below_b, y > 0), (above_a, y == 3), (above_b, y == 3)
-    steps = jnp.where(y == 3, 4, jnp.where(y > 0, 2, 0))
-    refs = *sums(state_ref), *refs
-    more_keys(q_ref, rest_ref, state_in, refs, used, firsts, pieces, steps)
-
-
-def rest_kernel(
-    place_ref, q_ref, rest_ref, below2_ref, above2_ref, weight_ref, state_in,
-    own_out, far_out, near_out, own_ref, send_ref, w_ref, att_ref, out_sems, *refs,
-):
-    y, used = place_ref[0] // WIDE, place_ref[1]
     weight_copy = pltpu.make_async_copy(weight_ref, w_ref, out_sems.at[3])
     weight_copy.start()
     pieces = (below2_ref, y > 1), (above2_ref, y > 1)
-    firsts = ((below2_ref, y == 2),)
+    firsts = (first_ref, (mine > 0) & (y != 2)), (below2_ref, y == 2)
     more_keys(q_ref, rest_ref, state_in, refs, used, firsts, pieces, jnp.where(y > 1, 2, 0))
     acc_ref = refs[0]
     for h in range(acc_ref.shape[0]):
@@ -391,21 +405,23 @@
     )(place, queries, keys, values, row_a, row_b)
 
 
-def early_rows(place, queries, rest, banks, state):
+def early_rows(place, queries, pieces, state, hand_on):
     length, width = queries.shape
     heads = width // HEAD
     whole = lambda x: pl.BlockSpec(x.shape, lambda i: (0,) * len(x.shape))
+    sources = hand_on or ()
+    first = jax.ShapeDtypeStruct((KEEP, 2 * HEAD), jnp.bfloat16)
     return pl.pallas_call(
-        early_kernel,
+        hand_on_kernel if hand_on else early_kernel,
         grid=(1,),
-        out_shape=state_of(length, heads),
-        in_specs=[SMEM, whole(queries), whole(rest), *[ANY] * (len(banks) + 1)],
-        out_specs=whole(state),
-        scratch_shapes=work_of(length, heads, 4),
+        out_shape=[state_of(length, heads)] + [first] * bool(hand_on),
+        in_specs=[SMEM, whole(queries), *[ANY] * (len(pieces) + len(sources) + 1)],
+        out_specs=[whole(state)] + [ANY] * bool(hand_on),
+        scratch_shapes=work_of(length, heads, 2) + [pltpu.SemaphoreType.DMA] * bool(hand_on),
         compiler_params=PARAMS,
-        cost_estimate=cost(length * heads, TILE + 4 * STEP),
+        cost_estimate=cost(length * heads, 2 * STEP),
         name="early_rows",
-    )(place, queries, rest, *banks, state)
+    )(place, queries, *pieces, *sources, state)
 
 
 def rest_rows(place, queries, rest, banks, weight, state, chips):
@@ -516,19 +532,23 @@
     above_b = permute(ends[1], across([(0, 3), (1, 0)]))
     rest, ends = lax.optimization_barrier((rest, ends))
     rest = rest + permute(rest, spread([(0, 4)]))
-    rest, ends = lax.optimization_barrier((rest, ends))
+    state = own_row(place, queries, key_rows, value_rows, *ends)
+    rest, below_a, above_b, state, ends = lax.optimization_barrier(
+        (rest, below_a, above_b, state, ends)
+    )
     below_b = permute(ends[1], across([(0, 1), (1, 2), (2, 3)]))
     above_a = permute(ends[0], across([(0, 3)]))
-    state = own_row(place, queries, key_rows, value_rows, *ends)
-    rest, below_a, above_b, state = lax.optimization_barrier((rest, below_a, above_b, state))
     rest = rest + permute(rest, spread([(0, 2), (4, 6)]))
+    (state,) = early_rows(place, queries, (below_a, above_b), state, None)
+    rest, below_a, above_b, below_b, above_a, state = lax.optimization_barrier(
+        (rest, below_a, above_b, below_b, above_a, state)
+    )
     below2 = permute(below_a, across([(1, 2), (2, 3)]))
     above2 = permute(above_b, across([(0, 3), (3, 2)]))
     rest = rest + permute(rest, spread([(0, 1), (2, 3), (4, 5), (6, 7)]))
-
-    state = early_rows(place, queries, rest, (ends[0], below_a, below_b, above_a, above_b), state)
+    state, first = early_rows(place, queries, (below_b, above_a), state, (ends[0], below_a))
     own, far, near = rest_rows(
-        place, queries, rest, (below2, above2), output_weight, state, chips
+        place, queries, rest, (first, below2, above2), output_weight, state, chips
     )
 
     far, near = lax.optimization_barrier((lax.ppermute(far, "head", swap), near))

time: 154 us -> 162 us (1.052)
  the two profiles are of different devices: /device:TPU:30 before, /device:TPU:222 now
where the time goes in v7:
time: 162 us; the launch traced here: 161 us
  Pallas kernels  73.4 us (45%)
  waiting for transfers between devices  45 us (28%)
  starting transfers between devices  39.8 us (25%)
  local copies, waits for them, and re-layouts  1.86 us (1%)
    pallas_call x2, Pallas kernels, early_rows(): pl.pallas_call(hand_on_kernel if hand_on else early_kernel, grid=(1,), ou...  32.4 us
    ppermute x19, starting transfers between devices, on_device(): permute = lambda x, pairs: lax.ppermute(x, 'ctx', pairs)  32 us
    ppermute x19, waiting for transfers between devices, on_device(): permute = lambda x, pairs: lax.ppermute(x, 'ctx', pairs)  29.9 us
    pallas_call x1, Pallas kernels, rest_rows(): pl.pallas_call(rest_kernel, grid=(1,), out_shape=[jax.ShapeDtypeStruct(sh...  27.5 us
    pallas_call x1, Pallas kernels, own_row(): pl.pallas_call(own_row_kernel, grid=(1,), out_shape=state, in_specs=[SMEM...  8.73 us
    ppermute x1, waiting for transfers between devices, on_device(): lax.ppermute(upper_down, 'head', down)  3.3 us
  transfers between devices with their start and end apart: 27, of which 15 were waited for; matrix products, arithmetic and copies ran while one was open for 0% of the time, Pallas kernels for 26%

profile of v7, /device:TPU:222, one launch (start us, length us, event | category | flops | bytes accessed | tf_op | source)
XLA Modules:
  0.0 161.4 jit_solution(5372520077937583694)
XLA Ops:
  0.7 2.4 %select_kept.1 = (bf16[256,256]{1,0:T(8,128)(2,1)}, bf16[272,256]{1,0:T(8,128)(2,1)}) custom-call(s32[1]{0:T(128)S(6)} %copy.7.used_ref, s32[1,256]{1,0:T(1,128)} %refs_0_.1, bf16[512,128]{1,0:T(8,128)(2,1)} %k_ref.1, bf16[512,128]{1,0:T(8,128)(2,1)} %v_ref.1), custom_call_target="tpu_custom_call" | custom-call | tf_op jit(solution)/shard_map/select_kept/pallas_call | solution.py:77
  5.9 3.4 %collective-permute-done.1.refs_0_ = bf16[256,256]{1,0:T(8,128)(2,1)S(1)} collective-permute-done((bf16[256,256]{1,0:T(8,128)(2,1)}, bf16[256,256]{1,0:T(8,128)(2,1)S(1)}, u32[]{:S(2)}, u32[]{:S(2)}) %collective-permute-start.1) | collective-permute-done | bytes 131104 | tf_op jit(solution)/shard_map/ppermute | solution.py:510
  10.7 1.6 collective-permute-start.3
  12.9 2.9 %collective-permute-done.3.refs_6_ = bf16[256,256]{1,0:T(8,128)(2,1)S(1)} collective-permute-done((bf16[256,256]{1,0:T(8,128)(2,1)S(1)}, bf16[256,256]{1,0:T(8,128)(2,1)S(1)}, u32[]{:S(2)}, u32[]{:S(2)}) %collective-permute-start.3) | collective-permute-done | bytes 131104 | tf_op jit(solution)/shard_map/ppermute | solution.py:510
  15.8 3.1 %collective-permute-done.4.refs_1_ = bf16[256,256]{1,0:T(8,128)(2,1)S(1)} collective-permute-done((bf16[256,256]{1,0:T(8,128)(2,1)S(1)}, bf16[256,256]{1,0:T(8,128)(2,1)S(1)}, u32[]{:S(2)}, u32[]{:S(2)}) %collective-permute-start.4) | collective-permute-done | bytes 131104 | tf_op jit(solution)/shard_map/ppermute | solution.py:510
  18.8 3.2 %collective-permute-start.7 = (bf16[256,256]{1,0:T(8,128)(2,1)S(1)}, bf16[256,256]{1,0:T(8,128)(2,1)S(1)}, u32[]{:S(2)}, u32[]{:S(2)}) collective-permute-start(bf16[256,256]{1,0:T(8,128)(2,1)S(1)} %collective-permute-done.3.refs_6_), channel_id=1, source_target_pairs={{0,8},{8,16},{16,24},{24,32},{32,40},{40,48},{48,56},{56,0},{64,72... | collective-permute-start | bytes 393224 | tf_op jit(solution)/shard_map/ppermute | solution.py:510
  22.1 3.0 %collective-permute-done.6.refs_2_ = bf16[256,256]{1,0:T(8,128)(2,1)S(1)} collective-permute-done((bf16[256,256]{1,0:T(8,128)(2,1)S(1)}, bf16[256,256]{1,0:T(8,128)(2,1)S(1)}, u32[]{:S(2)}, u32[]{:S(2)}) %collective-permute-start.6) | collective-permute-done | bytes 131104 | tf_op jit(solution)/shard_map/ppermute | solution.py:510
  25.1 3.6 %collective-permute-start.8 = (bf16[128,256]{1,0:T(8,128)(2,1)S(1)}, bf16[128,256]{1,0:T(8,128)(2,1)S(1)}, u32[]{:S(2)}, u32[]{:S(2)}) collective-permute-start(bf16[128,256]{1,0:T(8,128)(2,1)S(1)} %slice.8), channel_id=1, source_target_pairs={{0,8},{8,16},{16,24},{24,32},{32,40},{40,48},{48,56},{56,0},{64,72... | collective-permute-start | bytes 196616 | tf_op jit(solution)/shard_map/ppermute | solution.py:510
  28.8 2.1 %collective-permute-done.9.refs_4_ = bf16[128,256]{1,0:T(8,128)(2,1)S(1)} collective-permute-done((bf16[128,256]{1,0:T(8,128)(2,1)S(1)}, bf16[128,256]{1,0:T(8,128)(2,1)S(1)}, u32[]{:S(2)}, u32[]{:S(2)}) %collective-permute-start.9) | collective-permute-done | bytes 65568 | tf_op jit(solution)/shard_map/ppermute | solution.py:510
  35.8 8.7 %own_row.1.state_in = f32[4,512,384]{2,1,0:T(8,128)} custom-call(s32[4]{0:T(128)} %copy-done.1, bf16[512,512]{1,0:T(8,128)(2,1)} %q_ref.7, bf16[512,128]{1,0:T(8,128)(2,1)} %k_ref.1, bf16[512,128]{1,0:T(8,128)(2,1)} %v_ref.1, bf16[1024,256]{1,0:T(8,128)(2,1)} %copy-done.4, bf16[1024,256]{1,0:T(8,128)(2,1)} %copy-done.5), custom_call_target="tpu_custom_call" | custom-call | flops 5368709120 | bytes 8388608 | tf_op jit(solution)/shard_map/own_row/pallas_call | solution.py:391
  44.6 3.2 %collective-permute-done.12.above_ref = bf16[1024,256]{1,0:T(8,128)(2,1)S(1)} collective-permute-done((bf16[1024,256]{1,0:T(8,128)(2,1)S(1)}, bf16[1024,256]{1,0:T(8,128)(2,1)S(1)}, u32[]{:S(2)}, u32[]{:S(2)}) %collective-permute-start.12) | collective-permute-done | bytes 524320 | tf_op jit(solution)/shard_map/ppermute | solution.py:510
  51.8 10.0 %early_rows.2.state_in = f32[4,512,384]{2,1,0:T(8,128)} custom-call(s32[4]{0:T(128)} %copy-done.1, bf16[512,512]{1,0:T(8,128)(2,1)} %q_ref.7, bf16[1024,256]{1,0:T(8,128)(2,1)} %copy-done.7, bf16[1024,256]{1,0:T(8,128)(2,1)} %copy-done.8, f32[4,512,384]{2,1,0:T(8,128)} %own_row.1.state_in), custom_call_target="tpu_custom_call" | custom-call | flops 4294967296 | bytes 8388608 | tf_op jit(solution)/shard_map/early_rows/pallas_call | solution.py:414
  61.8 11.5 %collective-permute-done.15.above_ref = bf16[1024,256]{1,0:T(8,128)(2,1)S(1)} collective-permute-done((bf16[1024,256]{1,0:T(8,128)(2,1)}, bf16[1024,256]{1,0:T(8,128)(2,1)S(1)}, u32[]{:S(2)}, u32[]{:S(2)}) %collective-permute-start.15) | collective-permute-done | bytes 524320 | tf_op jit(solution)/shard_map/ppermute | solution.py:510
  73.4 1.9 %collective-permute-start.18 = (bf16[1024,256]{1,0:T(8,128)(2,1)}, bf16[1024,256]{1,0:T(8,128)(2,1)S(1)}, u32[]{:S(2)}, u32[]{:S(2)}) collective-permute-start(bf16[1024,256]{1,0:T(8,128)(2,1)} %copy-done.8), channel_id=1, source_target_pairs={{0,192},{8,200},{16,208},{24,216},{32,224},{40,232},{48,240},{56,2... | collective-permute-start | bytes 1572872 | tf_op jit(solution)/shard_map/ppermute | solution.py:510
  76.6 9.3 %collective-permute-start.16 = (bf16[272,256]{1,0:T(8,128)(2,1)S(1)}, bf16[272,256]{1,0:T(8,128)(2,1)S(1)}, u32[]{:S(2)}, u32[]{:S(2)}) collective-permute-start(bf16[272,256]{1,0:T(8,128)(2,1)S(1)} %add.24), channel_id=1, source_target_pairs={{0,8},{64,72},{128,136},{192,200},{16,24},{80,88},{144,152},{208,2... | collective-permute-start | bytes 417800 | tf_op jit(solution)/shard_map/ppermute | solution.py:510
  85.9 22.5 %early_rows.3 = (f32[4,512,384]{2,1,0:T(8,128)}, bf16[256,256]{1,0:T(8,128)(2,1)}) custom-call(s32[4]{0:T(128)} %copy-done.1, bf16[512,512]{1,0:T(8,128)(2,1)} %q_ref.7, bf16[1024,256]{1,0:T(8,128)(2,1)} %copy-done.9, bf16[1024,256]{1,0:T(8,128)(2,1)} %copy-done.10, bf16[1024,256]{1,0:T(8,128)(2,1)} %copy-done.4, bf16[1024,256]{1,0:T(8,128)(2,1)} %copy-done.7, ...), custom_call_target="tpu_custom_call" | custom-call | flops 4294967296 | bytes 8388608 | tf_op jit(solution)/shard_map/early_rows/pallas_call | solution.py:414
  109.4 27.5 %rest_rows.1 = (bf16[4,512,512]{2,1,0:T(8,128)(2,1)S(1)}, bf16[512,512]{1,0:T(8,128)(2,1)S(1)}, bf16[3,512,512]{2,1,0:T(8,128)(2,1)S(1)}) custom-call(s32[4]{0:T(128)S(1)} %copy-done.2, bf16[512,512]{1,0:T(8,128)(2,1)S(1)} %copy-done.3, bf16[272,256]{1,0:T(8,128)(2,1)S(1)} %add.25.rest_ref, bf16[256,256]{1,0:T(8,128)(2,1)S(1)} %copy-done.6, ...), custom_call_target="tpu_custom_call" | custom-call | flops 5368709120 | bytes 8388608 | tf_op jit(solution)/shard_map/rest_rows/pallas_call | solution.py:433
  137.0 1.9 %collective-permute-done.19.other_ref = bf16[512,512]{1,0:T(8,128)(2,1)S(1)} collective-permute-done((bf16[512,512]{1,0:T(8,128)(2,1)S(1)}, bf16[512,512]{1,0:T(8,128)(2,1)S(1)}, u32[]{:S(2)}, u32[]{:S(2)}) %collective-permute-start.19) | collective-permute-done | bytes 524320 | tf_op jit(solution)/shard_map/ppermute | solution.py:554
  143.4 2.4 %collective-permute-start.22 = (bf16[256,512]{1,0:T(8,128)(2,1)S(1)}, bf16[256,512]{1,0:T(8,128)(2,1)S(1)}, u32[]{:S(2)}, u32[]{:S(2)}) collective-permute-start(bf16[256,512]{1,0:T(8,128)(2,1)S(1)} %get-tuple-element.77), channel_id=1, source_target_pairs={{0,2},{1,3},{2,4},{3,5},{4,6},{5,7},{6,0},{7,1},{8,10},{9,11},{10,... | collective-permute-start | bytes 786440 | tf_op jit(solution)/shard_map/ppermute | solution.py:563
  145.8 2.6 %collective-permute-done.23.refs_2_ = bf16[256,512]{1,0:T(8,128)(2,1)S(1)} collective-permute-done((bf16[256,512]{1,0:T(8,128)(2,1)S(1)}, bf16[256,512]{1,0:T(8,128)(2,1)S(1)}, u32[]{:S(2)}, u32[]{:S(2)}) %collective-permute-start.23) | collective-permute-done | bytes 262176 | tf_op jit(solution)/shard_map/ppermute | solution.py:559
  148.4 1.7 %collective-permute-done.24.refs_5_ = bf16[256,512]{1,0:T(8,128)(2,1)S(1)} collective-permute-done((bf16[256,512]{1,0:T(8,128)(2,1)S(1)}, bf16[256,512]{1,0:T(8,128)(2,1)S(1)}, u32[]{:S(2)}, u32[]{:S(2)}) %collective-permute-start.24) | collective-permute-done | bytes 262176 | tf_op jit(solution)/shard_map/ppermute | solution.py:559
  150.7 1.7 %collective-permute-start.26 = (bf16[256,512]{1,0:T(8,128)(2,1)S(1)}, bf16[256,512]{1,0:T(8,128)(2,1)S(1)}, u32[]{:S(2)}, u32[]{:S(2)}) collective-permute-start(bf16[256,512]{1,0:T(8,128)(2,1)S(1)} %get-tuple-element.84), channel_id=1, source_target_pairs={{0,6},{1,7},{2,0},{3,1},{4,2},{5,3},{6,4},{7,5},{8,14},{9,15},{10,... | collective-permute-start | bytes 786440 | tf_op jit(solution)/shard_map/ppermute | solution.py:566
  152.4 3.3 %collective-permute-done.21.refs_2_ = bf16[256,512]{1,0:T(8,128)(2,1)S(1)} collective-permute-done((bf16[256,512]{1,0:T(8,128)(2,1)S(1)}, bf16[256,512]{1,0:T(8,128)(2,1)S(1)}, u32[]{:S(2)}, u32[]{:S(2)}) %collective-permute-start.21) | collective-permute-done | bytes 262176 | tf_op jit(solution)/shard_map/ppermute | solution.py:563
  156.0 3.1 %collective-permute-done.25.refs_1_ = bf16[256,512]{1,0:T(8,128)(2,1)S(1)} collective-permute-done((bf16[256,512]{1,0:T(8,128)(2,1)S(1)}, bf16[256,512]{1,0:T(8,128)(2,1)S(1)}, u32[]{:S(2)}, u32[]{:S(2)}) %collective-permute-start.25) | collective-permute-done | bytes 262176 | tf_op jit(solution)/shard_map/ppermute | solution.py:566
  (72 shorter events, 23.6 us)
Async XLA Ops:
  3.8 5.5 %collective-permute-start.1 = (bf16[256,256]{1,0:T(8,128)(2,1)}, bf16[256,256]{1,0:T(8,128)(2,1)S(1)}, u32[]{:S(2)}, u32[]{:S(2)}) collective-permute-start(bf16[256,256]{1,0:T(8,128)(2,1)} %get-tuple-element.45.refs_8_), channel_id=1, source_target_pairs={{0,56},{8,0},{16,8},{24,16},{32,24},{40,32},{48,40},{56,48},{64,12... | collective-permute-start | bytes 393224 | tf_op jit(solution)/shard_map/ppermute | solution.py:510
  4.9 5.2 %collective-permute-start = (bf16[256,256]{1,0:T(8,128)(2,1)}, bf16[256,256]{1,0:T(8,128)(2,1)S(1)}, u32[]{:S(2)}, u32[]{:S(2)}) collective-permute-start(bf16[256,256]{1,0:T(8,128)(2,1)} %get-tuple-element.45.refs_8_), channel_id=1, source_target_pairs={{0,8},{8,16},{16,24},{24,32},{32,40},{40,48},{48,56},{56,0},{64,72... | collective-permute-start | bytes 393224 | tf_op jit(solution)/shard_map/ppermute | solution.py:510
  10.7 5.0 %collective-permute-start.3 = (bf16[256,256]{1,0:T(8,128)(2,1)S(1)}, bf16[256,256]{1,0:T(8,128)(2,1)S(1)}, u32[]{:S(2)}, u32[]{:S(2)}) collective-permute-start(bf16[256,256]{1,0:T(8,128)(2,1)S(1)} %collective-permute-done.refs_7_), channel_id=1, source_target_pairs={{0,8},{8,16},{16,24},{24,32},{32,40},{40,48},{48,56},{56,0},{64,72... | collective-permute-start | bytes 393224 | tf_op jit(solution)/shard_map/ppermute | solution.py:510
  12.3 6.5 %collective-permute-start.4 = (bf16[256,256]{1,0:T(8,128)(2,1)S(1)}, bf16[256,256]{1,0:T(8,128)(2,1)S(1)}, u32[]{:S(2)}, u32[]{:S(2)}) collective-permute-start(bf16[256,256]{1,0:T(8,128)(2,1)S(1)} %collective-permute-done.1.refs_0_), channel_id=1, source_target_pairs={{0,56},{8,0},{16,8},{24,16},{32,24},{40,32},{48,40},{56,48},{64,12... | collective-permute-start | bytes 393224 | tf_op jit(solution)/shard_map/ppermute | solution.py:510
  18.8 6.2 %collective-permute-start.6 = (bf16[256,256]{1,0:T(8,128)(2,1)S(1)}, bf16[256,256]{1,0:T(8,128)(2,1)S(1)}, u32[]{:S(2)}, u32[]{:S(2)}) collective-permute-start(bf16[256,256]{1,0:T(8,128)(2,1)S(1)} %collective-permute-done.4.refs_1_), channel_id=1, source_target_pairs={{0,56},{8,0},{16,8},{24,16},{32,24},{40,32},{48,40},{56,48},{64,12... | collective-permute-start | bytes 393224 | tf_op jit(solution)/shard_map/ppermute | solution.py:510
  18.8 6.2 %collective-permute-start.7 = (bf16[256,256]{1,0:T(8,128)(2,1)S(1)}, bf16[256,256]{1,0:T(8,128)(2,1)S(1)}, u32[]{:S(2)}, u32[]{:S(2)}) collective-permute-start(bf16[256,256]{1,0:T(8,128)(2,1)S(1)} %collective-permute-done.3.refs_6_), channel_id=1, source_target_pairs={{0,8},{8,16},{16,24},{24,32},{32,40},{40,48},{48,56},{56,0},{64,72... | collective-permute-start | bytes 393224 | tf_op jit(solution)/shard_map/ppermute | solution.py:510
  25.1 5.8 %collective-permute-start.9 = (bf16[128,256]{1,0:T(8,128)(2,1)S(1)}, bf16[128,256]{1,0:T(8,128)(2,1)S(1)}, u32[]{:S(2)}, u32[]{:S(2)}) collective-permute-start(bf16[128,256]{1,0:T(8,128)(2,1)S(1)} %slice.9), channel_id=1, source_target_pairs={{0,56},{8,0},{16,8},{24,16},{32,24},{40,32},{48,40},{56,48},{64,12... | collective-permute-start | bytes 196616 | tf_op jit(solution)/shard_map/ppermute | solution.py:510
  25.1 5.8 %collective-permute-start.8 = (bf16[128,256]{1,0:T(8,128)(2,1)S(1)}, bf16[128,256]{1,0:T(8,128)(2,1)S(1)}, u32[]{:S(2)}, u32[]{:S(2)}) collective-permute-start(bf16[128,256]{1,0:T(8,128)(2,1)S(1)} %slice.8), channel_id=1, source_target_pairs={{0,8},{8,16},{16,24},{24,32},{32,40},{40,48},{48,56},{56,0},{64,72... | collective-permute-start | bytes 196616 | tf_op jit(solution)/shard_map/ppermute | solution.py:510
  32.5 12.1 %collective-permute-start.11 = (bf16[1024,256]{1,0:T(8,128)(2,1)S(1)}, bf16[1024,256]{1,0:T(8,128)(2,1)S(1)}, u32[]{:S(2)}, u32[]{:S(2)}) collective-permute-start(bf16[1024,256]{1,0:T(8,128)(2,1)S(1)} %get-tuple-element.62.row_a), channel_id=1, source_target_pairs={{0,64},{8,72},{16,80},{24,88},{32,96},{40,104},{48,112},{56,120},{... | collective-permute-start | bytes 1572872 | tf_op jit(solution)/shard_map/ppermute | solution.py:510
  33.8 14.0 %collective-permute-start.12 = (bf16[1024,256]{1,0:T(8,128)(2,1)S(1)}, bf16[1024,256]{1,0:T(8,128)(2,1)S(1)}, u32[]{:S(2)}, u32[]{:S(2)}) collective-permute-start(bf16[1024,256]{1,0:T(8,128)(2,1)S(1)} %get-tuple-element.61.row_b), channel_id=1, source_target_pairs={{0,192},{8,200},{16,208},{24,216},{32,224},{40,232},{48,240},{56,2... | collective-permute-start | bytes 1572872 | tf_op jit(solution)/shard_map/ppermute | solution.py:510
  35.1 9.4 %collective-permute-start.10 = (bf16[272,256]{1,0:T(8,128)(2,1)S(1)}, bf16[272,256]{1,0:T(8,128)(2,1)S(1)}, u32[]{:S(2)}, u32[]{:S(2)}) collective-permute-start(bf16[272,256]{1,0:T(8,128)(2,1)S(1)} %add.22), channel_id=1, source_target_pairs={{0,32},{64,96},{128,160},{192,224},{1,33},{65,97},{129,161},{193,2... | collective-permute-start | bytes 417800 | tf_op jit(solution)/shard_map/ppermute | solution.py:510
  47.8 14.0 %collective-permute-start.14 = (bf16[1024,256]{1,0:T(8,128)(2,1)}, bf16[1024,256]{1,0:T(8,128)(2,1)S(1)}, u32[]{:S(2)}, u32[]{:S(2)}) collective-permute-start(bf16[1024,256]{1,0:T(8,128)(2,1)} %copy-done.5), channel_id=1, source_target_pairs={{0,64},{8,72},{16,80},{24,88},{32,96},{40,104},{48,112},{56,120},{... | collective-permute-start | bytes 1572872 | tf_op jit(solution)/shard_map/ppermute | solution.py:510
  49.1 24.2 %collective-permute-start.15 = (bf16[1024,256]{1,0:T(8,128)(2,1)}, bf16[1024,256]{1,0:T(8,128)(2,1)S(1)}, u32[]{:S(2)}, u32[]{:S(2)}) collective-permute-start(bf16[1024,256]{1,0:T(8,128)(2,1)} %copy-done.4), channel_id=1, source_target_pairs={{0,192},{8,200},{16,208},{24,216},{32,224},{40,232},{48,240},{56,2... | collective-permute-start | bytes 1572872 | tf_op jit(solution)/shard_map/ppermute | solution.py:510
  50.4 11.3 %collective-permute-start.13 = (bf16[272,256]{1,0:T(8,128)(2,1)S(1)}, bf16[272,256]{1,0:T(8,128)(2,1)S(1)}, u32[]{:S(2)}, u32[]{:S(2)}) collective-permute-start(bf16[272,256]{1,0:T(8,128)(2,1)S(1)} %add.23), channel_id=1, source_target_pairs={{0,16},{64,80},{128,144},{192,208},{32,48},{96,112},{160,176},{224... | collective-permute-start | bytes 417800 | tf_op jit(solution)/shard_map/ppermute | solution.py:510
  73.4 35.1 %collective-permute-start.18 = (bf16[1024,256]{1,0:T(8,128)(2,1)}, bf16[1024,256]{1,0:T(8,128)(2,1)S(1)}, u32[]{:S(2)}, u32[]{:S(2)}) collective-permute-start(bf16[1024,256]{1,0:T(8,128)(2,1)} %copy-done.8), channel_id=1, source_target_pairs={{0,192},{8,200},{16,208},{24,216},{32,224},{40,232},{48,240},{56,2... | collective-permute-start | bytes 1572872 | tf_op jit(solution)/shard_map/ppermute | solution.py:510
  75.3 33.2 %collective-permute-start.17 = (bf16[1024,256]{1,0:T(8,128)(2,1)}, bf16[1024,256]{1,0:T(8,128)(2,1)S(1)}, u32[]{:S(2)}, u32[]{:S(2)}) collective-permute-start(bf16[1024,256]{1,0:T(8,128)(2,1)} %copy-done.7), channel_id=1, source_target_pairs={{64,128},{72,136},{80,144},{88,152},{96,160},{104,168},{112,176},{... | collective-permute-start | bytes 1572872 | tf_op jit(solution)/shard_map/ppermute | solution.py:510
  76.6 31.8 %collective-permute-start.16 = (bf16[272,256]{1,0:T(8,128)(2,1)S(1)}, bf16[272,256]{1,0:T(8,128)(2,1)S(1)}, u32[]{:S(2)}, u32[]{:S(2)}) collective-permute-start(bf16[272,256]{1,0:T(8,128)(2,1)S(1)} %add.24), channel_id=1, source_target_pairs={{0,8},{64,72},{128,136},{192,200},{16,24},{80,88},{144,152},{208,2... | collective-permute-start | bytes 417800 | tf_op jit(solution)/shard_map/ppermute | solution.py:510
  138.9 3.4 %collective-permute-start.20 = (bf16[3,512,512]{2,1,0:T(8,128)(2,1)S(1)}, bf16[3,512,512]{2,1,0:T(8,128)(2,1)S(1)}, u32[]{:S(2)}, u32[]{:S(2)}) collective-permute-start(bf16[3,512,512]{2,1,0:T(8,128)(2,1)S(1)} %get-tuple-element.75), channel_id=1, source_target_pairs={{0,1},{1,0},{2,3},{3,2},{4,5},{5,4},{6,7},{7,6},{8,9},{9,8},{10,11... | collective-permute-start | bytes 4718600 | tf_op jit(solution)/shard_map/ppermute | solution.py:555
  139.2 9.2 %collective-permute-start.23 = (bf16[256,512]{1,0:T(8,128)(2,1)S(1)}, bf16[256,512]{1,0:T(8,128)(2,1)S(1)}, u32[]{:S(2)}, u32[]{:S(2)}) collective-permute-start(bf16[256,512]{1,0:T(8,128)(2,1)S(1)} %get-tuple-element.79), channel_id=1, source_target_pairs={{0,2},{1,3},{2,4},{3,5},{4,6},{5,7},{6,0},{7,1},{8,10},{9,11},{10,... | collective-permute-start | bytes 786440 | tf_op jit(solution)/shard_map/ppermute | solution.py:559
  139.8 10.4 %collective-permute-start.24 = (bf16[256,512]{1,0:T(8,128)(2,1)S(1)}, bf16[256,512]{1,0:T(8,128)(2,1)S(1)}, u32[]{:S(2)}, u32[]{:S(2)}) collective-permute-start(bf16[256,512]{1,0:T(8,128)(2,1)S(1)} %get-tuple-element.80), channel_id=1, source_target_pairs={{0,6},{1,7},{2,0},{3,1},{4,2},{5,3},{6,4},{7,5},{8,14},{9,15},{10,... | collective-permute-start | bytes 786440 | tf_op jit(solution)/shard_map/ppermute | solution.py:559
  142.5 13.3 %collective-permute-start.21 = (bf16[256,512]{1,0:T(8,128)(2,1)S(1)}, bf16[256,512]{1,0:T(8,128)(2,1)S(1)}, u32[]{:S(2)}, u32[]{:S(2)}) collective-permute-start(bf16[256,512]{1,0:T(8,128)(2,1)S(1)} %get-tuple-element.76), channel_id=1, source_target_pairs={{0,6},{1,7},{2,0},{3,1},{4,2},{5,3},{6,4},{7,5},{8,14},{9,15},{10,... | collective-permute-start | bytes 786440 | tf_op jit(solution)/shard_map/ppermute | solution.py:563
  143.4 12.4 %collective-permute-start.22 = (bf16[256,512]{1,0:T(8,128)(2,1)S(1)}, bf16[256,512]{1,0:T(8,128)(2,1)S(1)}, u32[]{:S(2)}, u32[]{:S(2)}) collective-permute-start(bf16[256,512]{1,0:T(8,128)(2,1)S(1)} %get-tuple-element.77), channel_id=1, source_target_pairs={{0,2},{1,3},{2,4},{3,5},{4,6},{5,7},{6,0},{7,1},{8,10},{9,11},{10,... | collective-permute-start | bytes 786440 | tf_op jit(solution)/shard_map/ppermute | solution.py:563
  150.3 8.7 %collective-permute-start.25 = (bf16[256,512]{1,0:T(8,128)(2,1)S(1)}, bf16[256,512]{1,0:T(8,128)(2,1)S(1)}, u32[]{:S(2)}, u32[]{:S(2)}) collective-permute-start(bf16[256,512]{1,0:T(8,128)(2,1)S(1)} %get-tuple-element.83), channel_id=1, source_target_pairs={{0,2},{1,3},{2,4},{3,5},{4,6},{5,7},{6,0},{7,1},{8,10},{9,11},{10,... | collective-permute-start | bytes 786440 | tf_op jit(solution)/shard_map/ppermute | solution.py:566
  150.7 9.8 %collective-permute-start.26 = (bf16[256,512]{1,0:T(8,128)(2,1)S(1)}, bf16[256,512]{1,0:T(8,128)(2,1)S(1)}, u32[]{:S(2)}, u32[]{:S(2)}) collective-permute-start(bf16[256,512]{1,0:T(8,128)(2,1)S(1)} %get-tuple-element.84), channel_id=1, source_target_pairs={{0,6},{1,7},{2,0},{3,1},{4,2},{5,3},{6,4},{7,5},{8,14},{9,15},{10,... | collective-permute-start | bytes 786440 | tf_op jit(solution)/shard_map/ppermute | solution.py:566
  (14 other events, 164.0 us)

commit v8 on v7

--- a/solution.py
+++ b/solution.py
@@ -183,46 +183,76 @@
 
 
 def own_row_kernel(
-    place_ref, q_ref, k_ref, v_ref, row_a, row_b, state_ref, row_ref, bias_ref, sems
+    place_ref, q_ref, k_ref, v_ref, row_a, row_b, below_a, above_b, state_ref, first_ref,
+    bank_ref, bias_ref, sems,
 ):
+    y, z = place_ref[0] // WIDE, place_ref[0] % WIDE
     acc_ref, peak_ref = sums(state_ref)
-    keys = place_ref[0] % WIDE * KEEP
-    tiles, part = keys // TILE, jnp.where(keys % TILE > 0, 1, 0)
-    half = row_a.shape[0]
+    keys, half = z * KEEP, row_a.shape[0]
+    row_steps = keys // STEP
+    masked = (keys - row_steps * STEP + TILE - 1) // TILE
     copies = [
-        pltpu.make_async_copy(ref, row_ref.at[pl.ds(at * half, half)], sems.at[at])
-        for at, ref in enumerate((row_a, row_b))
+        (row_a, bank_ref.at[pl.ds(0, half)], z >= 0),
+        (row_b, bank_ref.at[pl.ds(half, half)], z >= 0),
+        (below_a, bank_ref.at[pl.ds(2 * half, half)], y > 0),
+        (above_b, bank_ref.at[pl.ds(3 * half, half)], y == 3),
+        (row_a.at[pl.ds(0, KEEP)], first_ref, y == 0),
+        (below_a.at[pl.ds(0, KEEP)], first_ref, y == 1),
     ]
-    for copy in copies:
-        copy.start()
+    copies = [
+        (pltpu.make_async_copy(source, target, sems.at[at]), on)
+        for at, (source, target, on) in enumerate(copies)
+    ]
+    for one, on in copies:
+        pl.when(on)(one.start)
     view, heads = head_view(q_ref, acc_ref, peak_ref), acc_ref.shape[0]
 
     def start(h):
         query, acc, peak = view(h)
         local(query, k_ref[...], v_ref[...], acc, peak)
 
+    def read_masked(tile):
+        at = row_steps * STEP + tile * TILE
+        bias_ref[...] = bias_where(count_along(bias_ref.shape, 1) + at < keys)
+        return *tile_of(bank_ref, at, TILE), bias_ref[...]
+
+    def step_start(step):
+        return jnp.where(step < row_steps, step, step - row_steps + 2 * half // STEP) * STEP
+
+    def read_fast(step, with_bias):
+        if with_bias:
+            return read_masked(step)
+        for at, (one, on) in enumerate(copies[2:4]):
+            pl.when(on & (step == row_steps + at))(one.wait)
+        return *tile_of(bank_ref, step_start(step), STEP), None
+
     def read(tile):
-        bias_ref[...] = bias_where(count_along(bias_ref.shape, 1) + tile * TILE < keys)
-        return *tile_of(row_ref, tile * TILE, TILE), bias_ref[...]
-
-    def read_fast(step, masked):
-        return read(tiles) if masked else (*tile_of(row_ref, step * TILE, TILE), None)
+        after = jnp.maximum(tile - masked, 0)
+        plain = step_start(after // 2) + after % 2 * TILE
+        at = jnp.where(tile < masked, row_steps * STEP + tile * TILE, plain)
+        limit = jnp.where(tile < masked, keys, bank_ref.shape[0])
+        bias_ref[...] = bias_where(count_along(bias_ref.shape, 1) + at < limit)
+        return *tile_of(bank_ref, at, TILE), bias_ref[...]
 
     for h in range(heads):
         start(h)
-    for copy in copies:
-        copy.wait()
-    absorb(heads, view, part, tiles, read_fast)
-    absorb_again(acc_ref, view, start, tiles + part, read)
-
-
-def more_keys(q_ref, rest_ref, state_in, refs, used, firsts, pieces, steps):
-    acc_ref, peak_ref, bank_ref, carried_ref, bias_ref, sems = refs
+    for one, on in copies[:2]:
+        pl.when(on)(one.wait)
+    steps = row_steps + jnp.where(y == 3, 2, jnp.minimum(y, 1))
+    absorb(heads, view, masked, steps, read_fast)
+    absorb_again(acc_ref, view, start, masked + STEP // TILE * steps, read)
+    for one, on in copies[4:]:
+        pl.when(on)(one.wait)
+
+
+def more_keys(queries, rest_ref, state_in, refs, used, firsts, pieces, steps, then):
+    acc_ref, peak_ref, q_ref, bank_ref, carried_ref, bias_ref, sems = refs
     acc_in, peak_in = sums(state_in)
-    copies = [(peak_in, peak_ref, True), (acc_in, carried_ref, True)]
+    copies = [(queries, q_ref, True), (peak_in, peak_ref, True)]
     copies += [(ref.at[pl.ds(0, KEEP)], bank_ref.at[pl.ds(0, KEEP)], on) for ref, on in firsts]
     for at, (ref, on) in enumerate(pieces):
         copies.append((ref, bank_ref.at[pl.ds(TILE + at * STEP, STEP)], on))
+    copies.append((acc_in, carried_ref, True))
     copies = [
         (pltpu.make_async_copy(source, target, sems.at[at]), on)
         for at, (source, target, on) in enumerate(copies)
@@ -236,6 +266,7 @@
 
     for one, on in copies:
         under(on, one.start)
+    then()
     acc_ref[...] = jnp.zeros(acc_ref.shape, jnp.float32)
     view, masked = head_view(q_ref, acc_ref, peak_ref), None
     if firsts:
@@ -256,7 +287,7 @@
         tile = jnp.where(masked > 0, step, step + 1)
         return *tile_of(bank_ref, tile * TILE, TILE), bias_ref[jnp.minimum(tile, 1)]
 
-    here, later = copies[2 : 2 + len(firsts)], copies[2 + len(firsts) :]
+    here, later = copies[2 : 2 + len(firsts)], copies[2 + len(firsts) : -1]
 
     def read_fast(step, with_bias):
         if with_bias:
@@ -267,47 +298,28 @@
             pl.when(on & (step == at))(one.wait)
         return *tile_of(bank_ref, TILE + step * STEP, STEP), None
 
-    copies[0][0].wait()
+    for one, _ in copies[:2]:
+        one.wait()
     absorb(acc_ref.shape[0], view, masked, steps, read_fast)
-    copies[1][0].wait()
+    copies[-1][0].wait()
     acc_ref[...] += carried_ref[...]
     tiles = STEP // TILE * steps + (0 if masked is None else masked)
     absorb_again(acc_ref, view, start, tiles, read)
 
 
-def early_kernel(place_ref, q_ref, below_ref, above_ref, state_in, state_ref, *refs):
-    y = place_ref[0] // WIDE
-    pieces = (below_ref, y > 0), (above_ref, y == 3)
-    steps = jnp.where(y == 3, 2, jnp.minimum(y, 1))
-    refs = *sums(state_ref), *refs
-    more_keys(q_ref, None, state_in, refs, None, (), pieces, steps)
-
-
-def hand_on_kernel(place_ref, q_ref, below_ref, above_ref, row_a, below_a, state_in, *refs):
-    y = place_ref[0] // WIDE
-    state_ref, first_ref, *refs, first_sem = refs
-    copies = [
-        (y == row, pltpu.make_async_copy(ref.at[pl.ds(0, KEEP)], first_ref, first_sem))
-        for row, ref in ((0, row_a), (1, below_a), (3, above_ref))
-    ]
-    for on, copy in copies:
-        pl.when(on)(copy.start)
-    early_kernel(place_ref, q_ref, below_ref, above_ref, state_in, state_ref, *refs)
-    for on, copy in copies:
-        pl.when(on)(copy.wait)
-
-
 def rest_kernel(
-    place_ref, q_ref, rest_ref, first_ref, below2_ref, above2_ref, weight_ref, state_in,
+    place_ref, rest_ref, queries, first_ref, below_b, above_a, below2_ref, above2_ref, weight_ref, state_in,
     own_out, far_out, near_out, own_ref, send_ref, w_ref, att_ref, out_sems, *refs,
 ):
     mine, used = place_ref[0], place_ref[1]
     y = mine // WIDE
+    pieces = (below_b, y > 0), (below2_ref, y > 1), (above2_ref, y > 1), (above_a, y == 3)
+    firsts = (first_ref, (mine > 0) & (y < 2)), (below2_ref, y == 2), (above_a, y == 3)
+    steps = jnp.where(y == 3, 4, jnp.where(y == 2, 3, y))
     weight_copy = pltpu.make_async_copy(weight_ref, w_ref, out_sems.at[3])
-    weight_copy.start()
-    pieces = (below2_ref, y > 1), (above2_ref, y > 1)
-    firsts = (first_ref, (mine > 0) & (y != 2)), (below2_ref, y == 2)
-    more_keys(q_ref, rest_ref, state_in, refs, used, firsts, pieces, jnp.where(y > 1, 2, 0))
+    more_keys(
+        queries, rest_ref, state_in, refs, used, firsts, pieces, steps, weight_copy.start
+    )
     acc_ref = refs[0]
     for h in range(acc_ref.shape[0]):
         att_ref[:, h * HEAD : (h + 1) * HEAD] = (
@@ -375,58 +387,31 @@
     return jax.ShapeDtypeStruct((heads, length, 3 * HEAD), jnp.float32)
 
 
-def work_of(length, heads, steps):
-    return [
-        pltpu.VMEM((TILE + steps * STEP, 2 * HEAD), jnp.bfloat16),
-        pltpu.VMEM((heads, length, 2 * HEAD), jnp.float32),
-        pltpu.VMEM((2, 8, TILE), jnp.float32),
-        pltpu.SemaphoreType.DMA((9,)),
-    ]
-
-
-def own_row(place, queries, keys, values, row_a, row_b):
+def own_row(place, queries, keys, values, *pieces):
     length, width = queries.shape
-    whole = lambda x: pl.BlockSpec(x.shape, lambda i: (0,) * x.ndim)
+    whole = lambda x: pl.BlockSpec(x.shape, lambda i: (0,) * len(x.shape))
     state = state_of(length, width // HEAD)
+    first = jax.ShapeDtypeStruct((KEEP, 2 * HEAD), jnp.bfloat16)
     return pl.pallas_call(
         own_row_kernel,
         grid=(1,),
-        out_shape=state,
-        in_specs=[SMEM, *[whole(x) for x in (queries, keys, values)], ANY, ANY],
-        out_specs=whole(state),
+        out_shape=[state, first],
+        in_specs=[SMEM, *[whole(x) for x in (queries, keys, values)], *[ANY] * len(pieces)],
+        out_specs=[whole(state), ANY],
         scratch_shapes=[
-            pltpu.VMEM((WIDE * KEEP, 2 * HEAD), jnp.bfloat16),
+            pltpu.VMEM((4 * STEP, 2 * HEAD), jnp.bfloat16),
             pltpu.VMEM((8, TILE), jnp.float32),
-            pltpu.SemaphoreType.DMA((2,)),
+            pltpu.SemaphoreType.DMA((6,)),
         ],
         compiler_params=PARAMS,
-        cost_estimate=cost(length * width // HEAD, length + WIDE * KEEP),
+        cost_estimate=cost(length * width // HEAD, length + 4 * STEP),
         name="own_row",
-    )(place, queries, keys, values, row_a, row_b)
-
-
-def early_rows(place, queries, pieces, state, hand_on):
-    length, width = queries.shape
-    heads = width // HEAD
-    whole = lambda x: pl.BlockSpec(x.shape, lambda i: (0,) * len(x.shape))
-    sources = hand_on or ()
-    first = jax.ShapeDtypeStruct((KEEP, 2 * HEAD), jnp.bfloat16)
-    return pl.pallas_call(
-        hand_on_kernel if hand_on else early_kernel,
-        grid=(1,),
-        out_shape=[state_of(length, heads)] + [first] * bool(hand_on),
-        in_specs=[SMEM, whole(queries), *[ANY] * (len(pieces) + len(sources) + 1)],
-        out_specs=[whole(state)] + [ANY] * bool(hand_on),
-        scratch_shapes=work_of(length, heads, 2) + [pltpu.SemaphoreType.DMA] * bool(hand_on),
-        compiler_params=PARAMS,
-        cost_estimate=cost(length * heads, 2 * STEP),
-        name="early_rows",
-    )(place, queries, *pieces, *sources, state)
+    )(place, queries, keys, values, *pieces)
 
 
 def rest_rows(place, queries, rest, banks, weight, state, chips):
     length, width = queries.shape
-    heads, keys = width // HEAD, TILE + 2 * STEP
+    heads, keys = width // HEAD, TILE + 4 * STEP
     whole = lambda x: pl.BlockSpec(x.shape, lambda i: (0,) * len(x.shape))
     one = (length, weight.shape[1] // chips // 2)
     shapes = (chips, *one), one, (chips - 1, *one)
@@ -434,7 +419,7 @@
         rest_kernel,
         grid=(1,),
         out_shape=[jax.ShapeDtypeStruct(shape, jnp.bfloat16) for shape in shapes],
-        in_specs=[SMEM, whole(queries), whole(rest), *[ANY] * (len(banks) + 2)],
+        in_specs=[SMEM, whole(rest), *[ANY] * (len(banks) + 3)],
         out_specs=[ANY] * 3,
         scratch_shapes=[
             *[pltpu.VMEM((chips, *one), jnp.bfloat16)] * 2,
@@ -443,12 +428,16 @@
             pltpu.SemaphoreType.DMA((4,)),
             pltpu.VMEM((heads, length, 2 * HEAD), jnp.float32),
             pltpu.VMEM((heads, length, HEAD), jnp.float32),
-            *work_of(length, heads, 2),
+            pltpu.VMEM((length, width), jnp.bfloat16),
+            pltpu.VMEM((keys, 2 * HEAD), jnp.bfloat16),
+            pltpu.VMEM((heads, length, 2 * HEAD), jnp.float32),
+            pltpu.VMEM((2, 8, TILE), jnp.float32),
+            pltpu.SemaphoreType.DMA((10,)),
         ],
         compiler_params=pltpu.CompilerParams(vmem_limit_bytes=47 * 2**20),
         cost_estimate=cost(length * heads, keys),
         name="rest_rows",
-    )(place, queries, rest, *banks, weight, state)
+    )(place, rest, queries, *banks, weight, state)
 
 
 def summed(*refs):
@@ -532,24 +521,16 @@
     above_b = permute(ends[1], across([(0, 3), (1, 0)]))
     rest, ends = lax.optimization_barrier((rest, ends))
     rest = rest + permute(rest, spread([(0, 4)]))
-    state = own_row(place, queries, key_rows, value_rows, *ends)
-    rest, below_a, above_b, state, ends = lax.optimization_barrier(
-        (rest, below_a, above_b, state, ends)
-    )
+    rest = rest + permute(rest, spread([(0, 2), (4, 6)]))
+    rest, below_a, above_b, ends = lax.optimization_barrier((rest, below_a, above_b, ends))
     below_b = permute(ends[1], across([(0, 1), (1, 2), (2, 3)]))
     above_a = permute(ends[0], across([(0, 3)]))
-    rest = rest + permute(rest, spread([(0, 2), (4, 6)]))
-    (state,) = early_rows(place, queries, (below_a, above_b), state, None)
-    rest, below_a, above_b, below_b, above_a, state = lax.optimization_barrier(
-        (rest, below_a, above_b, below_b, above_a, state)
-    )
     below2 = permute(below_a, across([(1, 2), (2, 3)]))
     above2 = permute(above_b, across([(0, 3), (3, 2)]))
     rest = rest + permute(rest, spread([(0, 1), (2, 3), (4, 5), (6, 7)]))
-    state, first = early_rows(place, queries, (below_b, above_a), state, (ends[0], below_a))
-    own, far, near = rest_rows(
-        place, queries, rest, (first, below2, above2), output_weight, state, chips
-    )
+    state, first = own_row(place, queries, key_rows, value_rows, *ends, below_a, above_b)
+    banks = (first, below_b, above_a, below2, above2)
+    own, far, near = rest_rows(place, queries, rest, banks, output_weight, state, chips)
 
     far, near = lax.optimization_barrier((lax.ppermute(far, "head", swap), near))
     near = lax.ppermute(near, "head", swap)

time: 162 us -> 150 us (0.926)
  the two profiles are of different devices: /device:TPU:222 before, /device:TPU:30 now
where the time goes in v8:
time: 150 us
  Pallas kernels  58.7 us (39%)
  waiting for transfers between devices  46 us (31%)
  starting transfers between devices  41.6 us (28%)
  local copies, waits for them, and re-layouts  2.5 us (2%)
    pallas_call x1, Pallas kernels, rest_rows(): pl.pallas_call(rest_kernel, grid=(1,), out_shape=[jax.ShapeDtypeStruct(sh...  44.2 us
    ppermute x19, starting transfers between devices, on_device(): permute = lambda x, pairs: lax.ppermute(x, 'ctx', pairs)  33.8 us
    ppermute x19, waiting for transfers between devices, on_device(): permute = lambda x, pairs: lax.ppermute(x, 'ctx', pairs)  30.8 us
    pallas_call x1, Pallas kernels, own_row(): pl.pallas_call(own_row_kernel, grid=(1,), out_shape=[state, first], in_sp...  9.71 us
    ppermute x1, waiting for transfers between devices, on_device(): lax.ppermute(upper_down, 'head', down)  3.3 us
    ppermute x1, waiting for transfers between devices, on_device(): lax.ppermute(upper_up, 'head', up)  3.11 us
  transfers between devices with their start and end apart: 27, of which 18 were waited for; matrix products, arithmetic and copies ran while one was open for 0% of the time, Pallas kernels for 7%

profile of v8, /device:TPU:30, one launch (start us, length us, event | category | flops | bytes accessed | tf_op | source)
XLA Modules:
  0.0 150.0 jit_solution(12432768974514713786)
XLA Ops:
  0.7 2.4 %select_kept.1 = (bf16[256,256]{1,0:T(8,128)(2,1)}, bf16[272,256]{1,0:T(8,128)(2,1)}) custom-call(s32[1]{0:T(128)S(6)} %copy.7.used_ref, s32[1,256]{1,0:T(1,128)} %refs_0_.1, bf16[512,128]{1,0:T(8,128)(2,1)} %k_ref.1, bf16[512,128]{1,0:T(8,128)(2,1)} %v_ref.1), custom_call_target="tpu_custom_call" | custom-call | tf_op jit(solution)/shard_map/select_kept/pallas_call | solution.py:77
  3.8 5.9 %collective-permute-start.1 = (bf16[256,256]{1,0:T(8,128)(2,1)}, bf16[256,256]{1,0:T(8,128)(2,1)S(1)}, u32[]{:S(2)}, u32[]{:S(2)}) collective-permute-start(bf16[256,256]{1,0:T(8,128)(2,1)} %get-tuple-element.38.refs_8_), channel_id=1, source_target_pairs={{0,56},{8,0},{16,8},{24,16},{32,24},{40,32},{48,40},{56,48},{64,12... | collective-permute-start | bytes 393224 | tf_op jit(solution)/shard_map/ppermute | solution.py:499
  9.8 3.0 %collective-permute-done.1.refs_0_ = bf16[256,256]{1,0:T(8,128)(2,1)S(1)} collective-permute-done((bf16[256,256]{1,0:T(8,128)(2,1)}, bf16[256,256]{1,0:T(8,128)(2,1)S(1)}, u32[]{:S(2)}, u32[]{:S(2)}) %collective-permute-start.1) | collective-permute-done | bytes 131104 | tf_op jit(solution)/shard_map/ppermute | solution.py:499
  12.8 3.3 %collective-permute-done.refs_7_ = bf16[256,256]{1,0:T(8,128)(2,1)S(1)} collective-permute-done((bf16[256,256]{1,0:T(8,128)(2,1)}, bf16[256,256]{1,0:T(8,128)(2,1)S(1)}, u32[]{:S(2)}, u32[]{:S(2)}) %collective-permute-start) | collective-permute-done | bytes 131104 | tf_op jit(solution)/shard_map/ppermute | solution.py:499
  17.5 3.2 %collective-permute-start.4 = (bf16[256,256]{1,0:T(8,128)(2,1)S(1)}, bf16[256,256]{1,0:T(8,128)(2,1)S(1)}, u32[]{:S(2)}, u32[]{:S(2)}) collective-permute-start(bf16[256,256]{1,0:T(8,128)(2,1)S(1)} %collective-permute-done.1.refs_0_), channel_id=1, source_target_pairs={{0,56},{8,0},{16,8},{24,16},{32,24},{40,32},{48,40},{56,48},{64,12... | collective-permute-start | bytes 393224 | tf_op jit(solution)/shard_map/ppermute | solution.py:499
  20.7 3.5 %collective-permute-done.5 = bf16[272,256]{1,0:T(8,128)(2,1)S(1)} collective-permute-done((bf16[272,256]{1,0:T(8,128)(2,1)S(1)}, bf16[272,256]{1,0:T(8,128)(2,1)S(1)}, u32[]{:S(2)}, u32[]{:S(2)}) %collective-permute-start.5) | collective-permute-done | bytes 139296 | tf_op jit(solution)/shard_map/ppermute | solution.py:499
  24.3 2.6 %collective-permute-start.6 = (bf16[256,256]{1,0:T(8,128)(2,1)S(1)}, bf16[256,256]{1,0:T(8,128)(2,1)S(1)}, u32[]{:S(2)}, u32[]{:S(2)}) collective-permute-start(bf16[256,256]{1,0:T(8,128)(2,1)S(1)} %collective-permute-done.4.refs_1_), channel_id=1, source_target_pairs={{0,56},{8,0},{16,8},{24,16},{32,24},{40,32},{48,40},{56,48},{64,12... | collective-permute-start | bytes 393224 | tf_op jit(solution)/shard_map/ppermute | solution.py:499
  26.9 3.2 %collective-permute-done.6.refs_2_ = bf16[256,256]{1,0:T(8,128)(2,1)S(1)} collective-permute-done((bf16[256,256]{1,0:T(8,128)(2,1)S(1)}, bf16[256,256]{1,0:T(8,128)(2,1)S(1)}, u32[]{:S(2)}, u32[]{:S(2)}) %collective-permute-start.6) | collective-permute-done | bytes 131104 | tf_op jit(solution)/shard_map/ppermute | solution.py:499
  30.1 3.4 %collective-permute-start.9 = (bf16[128,256]{1,0:T(8,128)(2,1)S(1)}, bf16[128,256]{1,0:T(8,128)(2,1)S(1)}, u32[]{:S(2)}, u32[]{:S(2)}) collective-permute-start(bf16[128,256]{1,0:T(8,128)(2,1)S(1)} %slice.9), channel_id=1, source_target_pairs={{0,56},{8,0},{16,8},{24,16},{32,24},{40,32},{48,40},{56,48},{64,12... | collective-permute-start | bytes 196616 | tf_op jit(solution)/shard_map/ppermute | solution.py:499
  35.4 3.8 %collective-permute-done.8.refs_3_ = bf16[128,256]{1,0:T(8,128)(2,1)S(1)} collective-permute-done((bf16[128,256]{1,0:T(8,128)(2,1)S(1)}, bf16[128,256]{1,0:T(8,128)(2,1)S(1)}, u32[]{:S(2)}, u32[]{:S(2)}) %collective-permute-start.8) | collective-permute-done | bytes 65568 | tf_op jit(solution)/shard_map/ppermute | solution.py:499
  43.4 2.5 %collective-permute-start.10 = (bf16[272,256]{1,0:T(8,128)(2,1)S(1)}, bf16[272,256]{1,0:T(8,128)(2,1)S(1)}, u32[]{:S(2)}, u32[]{:S(2)}) collective-permute-start(bf16[272,256]{1,0:T(8,128)(2,1)S(1)} %add.22), channel_id=1, source_target_pairs={{0,32},{64,96},{128,160},{192,224},{1,33},{65,97},{129,161},{193,2... | collective-permute-start | bytes 417800 | tf_op jit(solution)/shard_map/ppermute | solution.py:499
  45.9 2.6 %collective-permute-done.10 = bf16[272,256]{1,0:T(8,128)(2,1)S(1)} collective-permute-done((bf16[272,256]{1,0:T(8,128)(2,1)S(1)}, bf16[272,256]{1,0:T(8,128)(2,1)S(1)}, u32[]{:S(2)}, u32[]{:S(2)}) %collective-permute-start.10) | collective-permute-done | bytes 139296 | tf_op jit(solution)/shard_map/ppermute | solution.py:499
  49.8 3.2 %collective-permute-done.11 = bf16[272,256]{1,0:T(8,128)(2,1)S(1)} collective-permute-done((bf16[272,256]{1,0:T(8,128)(2,1)S(1)}, bf16[272,256]{1,0:T(8,128)(2,1)S(1)}, u32[]{:S(2)}, u32[]{:S(2)}) %collective-permute-start.11) | collective-permute-done | bytes 139296 | tf_op jit(solution)/shard_map/ppermute | solution.py:499
  53.1 3.8 %collective-permute-done.13.above_b = bf16[1024,256]{1,0:T(8,128)(2,1)} collective-permute-done((bf16[1024,256]{1,0:T(8,128)(2,1)S(1)}, bf16[1024,256]{1,0:T(8,128)(2,1)}, u32[]{:S(2)}, u32[]{:S(2)}) %collective-permute-start.13) | collective-permute-done | bytes 524320 | tf_op jit(solution)/shard_map/ppermute | solution.py:499
  62.1 5.2 %collective-permute-start.18 = (bf16[1024,256]{1,0:T(8,128)(2,1)}, bf16[1024,256]{1,0:T(8,128)(2,1)S(1)}, u32[]{:S(2)}, u32[]{:S(2)}) collective-permute-start(bf16[1024,256]{1,0:T(8,128)(2,1)} %collective-permute-done.13.above_b), channel_id=1, source_target_pairs={{0,192},{8,200},{16,208},{24,216},{32,224},{40,232},{48,240},{56,2... | collective-permute-start | bytes 1572872 | tf_op jit(solution)/shard_map/ppermute | solution.py:499
  67.3 9.7 %own_row.1 = (f32[4,512,384]{2,1,0:T(8,128)}, bf16[256,256]{1,0:T(8,128)(2,1)}) custom-call(s32[4]{0:T(128)} %copy-done.1, bf16[512,512]{1,0:T(8,128)(2,1)} %queries.1, bf16[512,128]{1,0:T(8,128)(2,1)} %k_ref.1, bf16[512,128]{1,0:T(8,128)(2,1)} %v_ref.1, bf16[1024,256]{1,0:T(8,128)(2,1)} %copy-done.5, bf16[1024,256]{1,0:T(8,128)(2,1)} %copy-done.4, ...), custom_call_target="tpu_custom_call" | custom-call | flops 9663676416 | bytes 8388608 | tf_op jit(solution)/shard_map/own_row/pallas_call | solution.py:395
  77.1 2.6 %collective-permute-done.17.below2_ref = bf16[1024,256]{1,0:T(8,128)(2,1)S(1)} collective-permute-done((bf16[1024,256]{1,0:T(8,128)(2,1)}, bf16[1024,256]{1,0:T(8,128)(2,1)S(1)}, u32[]{:S(2)}, u32[]{:S(2)}) %collective-permute-start.17) | collective-permute-done | bytes 524320 | tf_op jit(solution)/shard_map/ppermute | solution.py:499
  81.2 44.2 %rest_rows.1 = (bf16[4,512,512]{2,1,0:T(8,128)(2,1)S(1)}, bf16[512,512]{1,0:T(8,128)(2,1)S(1)}, bf16[3,512,512]{2,1,0:T(8,128)(2,1)S(1)}) custom-call(s32[4]{0:T(128)S(1)} %copy-done.2, bf16[272,256]{1,0:T(8,128)(2,1)S(1)} %add.25.rest_ref, bf16[512,512]{1,0:T(8,128)(2,1)S(1)} %copy-done.3, bf16[256,256]{1,0:T(8,128)(2,1)S(1)} %copy-done.6, ...), custom_call_target="tpu_custom_call" | custom-call | flops 9663676416 | bytes 8388608 | tf_op jit(solution)/shard_map/rest_rows/pallas_call | solution.py:418
  125.5 1.9 %collective-permute-done.19.other_ref = bf16[512,512]{1,0:T(8,128)(2,1)S(1)} collective-permute-done((bf16[512,512]{1,0:T(8,128)(2,1)S(1)}, bf16[512,512]{1,0:T(8,128)(2,1)S(1)}, u32[]{:S(2)}, u32[]{:S(2)}) %collective-permute-start.19) | collective-permute-done | bytes 524320 | tf_op jit(solution)/shard_map/ppermute | solution.py:535
  131.9 2.4 %collective-permute-start.22 = (bf16[256,512]{1,0:T(8,128)(2,1)S(1)}, bf16[256,512]{1,0:T(8,128)(2,1)S(1)}, u32[]{:S(2)}, u32[]{:S(2)}) collective-permute-start(bf16[256,512]{1,0:T(8,128)(2,1)S(1)} %get-tuple-element.63), channel_id=1, source_target_pairs={{0,2},{1,3},{2,4},{3,5},{4,6},{5,7},{6,0},{7,1},{8,10},{9,11},{10,... | collective-permute-start | bytes 786440 | tf_op jit(solution)/shard_map/ppermute | solution.py:544
  134.3 2.6 %collective-permute-done.23.refs_2_ = bf16[256,512]{1,0:T(8,128)(2,1)S(1)} collective-permute-done((bf16[256,512]{1,0:T(8,128)(2,1)S(1)}, bf16[256,512]{1,0:T(8,128)(2,1)S(1)}, u32[]{:S(2)}, u32[]{:S(2)}) %collective-permute-start.23) | collective-permute-done | bytes 262176 | tf_op jit(solution)/shard_map/ppermute | solution.py:540
  139.2 1.7 %collective-permute-start.26 = (bf16[256,512]{1,0:T(8,128)(2,1)S(1)}, bf16[256,512]{1,0:T(8,128)(2,1)S(1)}, u32[]{:S(2)}, u32[]{:S(2)}) collective-permute-start(bf16[256,512]{1,0:T(8,128)(2,1)S(1)} %get-tuple-element.70), channel_id=1, source_target_pairs={{0,6},{1,7},{2,0},{3,1},{4,2},{5,3},{6,4},{7,5},{8,14},{9,15},{10,... | collective-permute-start | bytes 786440 | tf_op jit(solution)/shard_map/ppermute | solution.py:547
  141.0 3.3 %collective-permute-done.21.refs_2_ = bf16[256,512]{1,0:T(8,128)(2,1)S(1)} collective-permute-done((bf16[256,512]{1,0:T(8,128)(2,1)S(1)}, bf16[256,512]{1,0:T(8,128)(2,1)S(1)}, u32[]{:S(2)}, u32[]{:S(2)}) %collective-permute-start.21) | collective-permute-done | bytes 262176 | tf_op jit(solution)/shard_map/ppermute | solution.py:544
  144.5 3.1 %collective-permute-done.25.refs_1_ = bf16[256,512]{1,0:T(8,128)(2,1)S(1)} collective-permute-done((bf16[256,512]{1,0:T(8,128)(2,1)S(1)}, bf16[256,512]{1,0:T(8,128)(2,1)S(1)}, u32[]{:S(2)}, u32[]{:S(2)}) %collective-permute-start.25) | collective-permute-done | bytes 262176 | tf_op jit(solution)/shard_map/ppermute | solution.py:547
  (62 shorter events, 25.9 us)
Async XLA Ops:
  3.1 6.6 %collective-permute-start.2 = (bf16[272,256]{1,0:T(8,128)(2,1)S(1)}, bf16[272,256]{1,0:T(8,128)(2,1)S(1)}, u32[]{:S(2)}, u32[]{:S(2)}) collective-permute-start(bf16[272,256]{1,0:T(8,128)(2,1)S(1)} %broadcast_select_fusion), channel_id=1, source_target_pairs={{0,64},{1,65},{2,66},{3,67},{4,68},{5,69},{6,70},{7,71}} | collective-permute-start | bytes 417800 | tf_op jit(solution)/shard_map/ppermute | solution.py:499
  3.8 9.0 %collective-permute-start.1 = (bf16[256,256]{1,0:T(8,128)(2,1)}, bf16[256,256]{1,0:T(8,128)(2,1)S(1)}, u32[]{:S(2)}, u32[]{:S(2)}) collective-permute-start(bf16[256,256]{1,0:T(8,128)(2,1)} %get-tuple-element.38.refs_8_), channel_id=1, source_target_pairs={{0,56},{8,0},{16,8},{24,16},{32,24},{40,32},{48,40},{56,48},{64,12... | collective-permute-start | bytes 393224 | tf_op jit(solution)/shard_map/ppermute | solution.py:499
  9.7 6.4 %collective-permute-start = (bf16[256,256]{1,0:T(8,128)(2,1)}, bf16[256,256]{1,0:T(8,128)(2,1)S(1)}, u32[]{:S(2)}, u32[]{:S(2)}) collective-permute-start(bf16[256,256]{1,0:T(8,128)(2,1)} %get-tuple-element.38.refs_8_), channel_id=1, source_target_pairs={{0,8},{8,16},{16,24},{24,32},{32,40},{40,48},{48,56},{56,0},{64,72... | collective-permute-start | bytes 393224 | tf_op jit(solution)/shard_map/ppermute | solution.py:499
  16.1 8.1 %collective-permute-start.5 = (bf16[272,256]{1,0:T(8,128)(2,1)S(1)}, bf16[272,256]{1,0:T(8,128)(2,1)S(1)}, u32[]{:S(2)}, u32[]{:S(2)}) collective-permute-start(bf16[272,256]{1,0:T(8,128)(2,1)S(1)} %fusion), channel_id=1, source_target_pairs={{0,192},{64,128},{1,193},{65,129},{2,194},{66,130},{3,195},{67,131... | collective-permute-start | bytes 417800 | tf_op jit(solution)/shard_map/ppermute | solution.py:499
  17.4 6.9 %collective-permute-start.3 = (bf16[256,256]{1,0:T(8,128)(2,1)S(1)}, bf16[256,256]{1,0:T(8,128)(2,1)S(1)}, u32[]{:S(2)}, u32[]{:S(2)}) collective-permute-start(bf16[256,256]{1,0:T(8,128)(2,1)S(1)} %collective-permute-done.refs_7_), channel_id=1, source_target_pairs={{0,8},{8,16},{16,24},{24,32},{32,40},{40,48},{48,56},{56,0},{64,72... | collective-permute-start | bytes 393224 | tf_op jit(solution)/shard_map/ppermute | solution.py:499
  17.5 6.8 %collective-permute-start.4 = (bf16[256,256]{1,0:T(8,128)(2,1)S(1)}, bf16[256,256]{1,0:T(8,128)(2,1)S(1)}, u32[]{:S(2)}, u32[]{:S(2)}) collective-permute-start(bf16[256,256]{1,0:T(8,128)(2,1)S(1)} %collective-permute-done.1.refs_0_), channel_id=1, source_target_pairs={{0,56},{8,0},{16,8},{24,16},{32,24},{40,32},{48,40},{56,48},{64,12... | collective-permute-start | bytes 393224 | tf_op jit(solution)/shard_map/ppermute | solution.py:499
  24.3 5.7 %collective-permute-start.6 = (bf16[256,256]{1,0:T(8,128)(2,1)S(1)}, bf16[256,256]{1,0:T(8,128)(2,1)S(1)}, u32[]{:S(2)}, u32[]{:S(2)}) collective-permute-start(bf16[256,256]{1,0:T(8,128)(2,1)S(1)} %collective-permute-done.4.refs_1_), channel_id=1, source_target_pairs={{0,56},{8,0},{16,8},{24,16},{32,24},{40,32},{48,40},{56,48},{64,12... | collective-permute-start | bytes 393224 | tf_op jit(solution)/shard_map/ppermute | solution.py:499
  26.9 6.8 %collective-permute-start.7 = (bf16[256,256]{1,0:T(8,128)(2,1)S(1)}, bf16[256,256]{1,0:T(8,128)(2,1)S(1)}, u32[]{:S(2)}, u32[]{:S(2)}) collective-permute-start(bf16[256,256]{1,0:T(8,128)(2,1)S(1)} %collective-permute-done.3.refs_6_), channel_id=1, source_target_pairs={{0,8},{8,16},{16,24},{24,32},{32,40},{40,48},{48,56},{56,0},{64,72... | collective-permute-start | bytes 393224 | tf_op jit(solution)/shard_map/ppermute | solution.py:499
  30.1 5.3 %collective-permute-start.9 = (bf16[128,256]{1,0:T(8,128)(2,1)S(1)}, bf16[128,256]{1,0:T(8,128)(2,1)S(1)}, u32[]{:S(2)}, u32[]{:S(2)}) collective-permute-start(bf16[128,256]{1,0:T(8,128)(2,1)S(1)} %slice.9), channel_id=1, source_target_pairs={{0,56},{8,0},{16,8},{24,16},{32,24},{40,32},{48,40},{56,48},{64,12... | collective-permute-start | bytes 196616 | tf_op jit(solution)/shard_map/ppermute | solution.py:499
  33.7 5.5 %collective-permute-start.8 = (bf16[128,256]{1,0:T(8,128)(2,1)S(1)}, bf16[128,256]{1,0:T(8,128)(2,1)S(1)}, u32[]{:S(2)}, u32[]{:S(2)}) collective-permute-start(bf16[128,256]{1,0:T(8,128)(2,1)S(1)} %slice.8), channel_id=1, source_target_pairs={{0,8},{8,16},{16,24},{24,32},{32,40},{40,48},{48,56},{56,0},{64,72... | collective-permute-start | bytes 196616 | tf_op jit(solution)/shard_map/ppermute | solution.py:499
  40.8 12.3 %collective-permute-start.12 = (bf16[1024,256]{1,0:T(8,128)(2,1)S(1)}, bf16[1024,256]{1,0:T(8,128)(2,1)}, u32[]{:S(2)}, u32[]{:S(2)}) collective-permute-start(bf16[1024,256]{1,0:T(8,128)(2,1)S(1)} %get-tuple-element.52.row_a), channel_id=1, source_target_pairs={{0,64},{8,72},{16,80},{24,88},{32,96},{40,104},{48,112},{56,120},{... | collective-permute-start | bytes 1572872 | tf_op jit(solution)/shard_map/ppermute | solution.py:499
  42.1 14.8 %collective-permute-start.13 = (bf16[1024,256]{1,0:T(8,128)(2,1)S(1)}, bf16[1024,256]{1,0:T(8,128)(2,1)}, u32[]{:S(2)}, u32[]{:S(2)}) collective-permute-start(bf16[1024,256]{1,0:T(8,128)(2,1)S(1)} %get-tuple-element.53.row_b), channel_id=1, source_target_pairs={{0,192},{8,200},{16,208},{24,216},{32,224},{40,232},{48,240},{56,2... | collective-permute-start | bytes 1572872 | tf_op jit(solution)/shard_map/ppermute | solution.py:499
  43.4 5.1 %collective-permute-start.10 = (bf16[272,256]{1,0:T(8,128)(2,1)S(1)}, bf16[272,256]{1,0:T(8,128)(2,1)S(1)}, u32[]{:S(2)}, u32[]{:S(2)}) collective-permute-start(bf16[272,256]{1,0:T(8,128)(2,1)S(1)} %add.22), channel_id=1, source_target_pairs={{0,32},{64,96},{128,160},{192,224},{1,33},{65,97},{129,161},{193,2... | collective-permute-start | bytes 417800 | tf_op jit(solution)/shard_map/ppermute | solution.py:499
  56.9 20.1 %collective-permute-start.14 = (bf16[272,256]{1,0:T(8,128)(2,1)S(1)}, bf16[272,256]{1,0:T(8,128)(2,1)S(1)}, u32[]{:S(2)}, u32[]{:S(2)}) collective-permute-start(bf16[272,256]{1,0:T(8,128)(2,1)S(1)} %add.24), channel_id=1, source_target_pairs={{0,8},{64,72},{128,136},{192,200},{16,24},{80,88},{144,152},{208,2... | collective-permute-start | bytes 417800 | tf_op jit(solution)/shard_map/ppermute | solution.py:499
  58.2 18.9 %collective-permute-start.16 = (bf16[1024,256]{1,0:T(8,128)(2,1)S(1)}, bf16[1024,256]{1,0:T(8,128)(2,1)S(1)}, u32[]{:S(2)}, u32[]{:S(2)}) collective-permute-start(bf16[1024,256]{1,0:T(8,128)(2,1)S(1)} %get-tuple-element.52.row_a), channel_id=1, source_target_pairs={{0,192},{8,200},{16,208},{24,216},{32,224},{40,232},{48,240},{56,2... | collective-permute-start | bytes 1572872 | tf_op jit(solution)/shard_map/ppermute | solution.py:499
  59.5 17.6 %collective-permute-start.15 = (bf16[1024,256]{1,0:T(8,128)(2,1)S(1)}, bf16[1024,256]{1,0:T(8,128)(2,1)S(1)}, u32[]{:S(2)}, u32[]{:S(2)}) collective-permute-start(bf16[1024,256]{1,0:T(8,128)(2,1)S(1)} %get-tuple-element.53.row_b), channel_id=1, source_target_pairs={{0,64},{8,72},{16,80},{24,88},{32,96},{40,104},{48,112},{56,120},{... | collective-permute-start | bytes 1572872 | tf_op jit(solution)/shard_map/ppermute | solution.py:499
  60.8 18.9 %collective-permute-start.17 = (bf16[1024,256]{1,0:T(8,128)(2,1)}, bf16[1024,256]{1,0:T(8,128)(2,1)S(1)}, u32[]{:S(2)}, u32[]{:S(2)}) collective-permute-start(bf16[1024,256]{1,0:T(8,128)(2,1)} %collective-permute-done.12.below_a), channel_id=1, source_target_pairs={{64,128},{72,136},{80,144},{88,152},{96,160},{104,168},{112,176},{... | collective-permute-start | bytes 1572872 | tf_op jit(solution)/shard_map/ppermute | solution.py:499
  62.1 17.6 %collective-permute-start.18 = (bf16[1024,256]{1,0:T(8,128)(2,1)}, bf16[1024,256]{1,0:T(8,128)(2,1)S(1)}, u32[]{:S(2)}, u32[]{:S(2)}) collective-permute-start(bf16[1024,256]{1,0:T(8,128)(2,1)} %collective-permute-done.13.above_b), channel_id=1, source_target_pairs={{0,192},{8,200},{16,208},{24,216},{32,224},{40,232},{48,240},{56,2... | collective-permute-start | bytes 1572872 | tf_op jit(solution)/shard_map/ppermute | solution.py:499
  127.7 9.2 %collective-permute-start.23 = (bf16[256,512]{1,0:T(8,128)(2,1)S(1)}, bf16[256,512]{1,0:T(8,128)(2,1)S(1)}, u32[]{:S(2)}, u32[]{:S(2)}) collective-permute-start(bf16[256,512]{1,0:T(8,128)(2,1)S(1)} %get-tuple-element.65), channel_id=1, source_target_pairs={{0,2},{1,3},{2,4},{3,5},{4,6},{5,7},{6,0},{7,1},{8,10},{9,11},{10,... | collective-permute-start | bytes 786440 | tf_op jit(solution)/shard_map/ppermute | solution.py:540
  128.3 10.4 %collective-permute-start.24 = (bf16[256,512]{1,0:T(8,128)(2,1)S(1)}, bf16[256,512]{1,0:T(8,128)(2,1)S(1)}, u32[]{:S(2)}, u32[]{:S(2)}) collective-permute-start(bf16[256,512]{1,0:T(8,128)(2,1)S(1)} %get-tuple-element.66), channel_id=1, source_target_pairs={{0,6},{1,7},{2,0},{3,1},{4,2},{5,3},{6,4},{7,5},{8,14},{9,15},{10,... | collective-permute-start | bytes 786440 | tf_op jit(solution)/shard_map/ppermute | solution.py:540
  131.0 13.3 %collective-permute-start.21 = (bf16[256,512]{1,0:T(8,128)(2,1)S(1)}, bf16[256,512]{1,0:T(8,128)(2,1)S(1)}, u32[]{:S(2)}, u32[]{:S(2)}) collective-permute-start(bf16[256,512]{1,0:T(8,128)(2,1)S(1)} %get-tuple-element.62), channel_id=1, source_target_pairs={{0,6},{1,7},{2,0},{3,1},{4,2},{5,3},{6,4},{7,5},{8,14},{9,15},{10,... | collective-permute-start | bytes 786440 | tf_op jit(solution)/shard_map/ppermute | solution.py:544
  131.9 12.4 %collective-permute-start.22 = (bf16[256,512]{1,0:T(8,128)(2,1)S(1)}, bf16[256,512]{1,0:T(8,128)(2,1)S(1)}, u32[]{:S(2)}, u32[]{:S(2)}) collective-permute-start(bf16[256,512]{1,0:T(8,128)(2,1)S(1)} %get-tuple-element.63), channel_id=1, source_target_pairs={{0,2},{1,3},{2,4},{3,5},{4,6},{5,7},{6,0},{7,1},{8,10},{9,11},{10,... | collective-permute-start | bytes 786440 | tf_op jit(solution)/shard_map/ppermute | solution.py:544
  138.9 8.8 %collective-permute-start.25 = (bf16[256,512]{1,0:T(8,128)(2,1)S(1)}, bf16[256,512]{1,0:T(8,128)(2,1)S(1)}, u32[]{:S(2)}, u32[]{:S(2)}) collective-permute-start(bf16[256,512]{1,0:T(8,128)(2,1)S(1)} %get-tuple-element.69), channel_id=1, source_target_pairs={{0,2},{1,3},{2,4},{3,5},{4,6},{5,7},{6,0},{7,1},{8,10},{9,11},{10,... | collective-permute-start | bytes 786440 | tf_op jit(solution)/shard_map/ppermute | solution.py:547
  139.2 9.9 %collective-permute-start.26 = (bf16[256,512]{1,0:T(8,128)(2,1)S(1)}, bf16[256,512]{1,0:T(8,128)(2,1)S(1)}, u32[]{:S(2)}, u32[]{:S(2)}) collective-permute-start(bf16[256,512]{1,0:T(8,128)(2,1)S(1)} %get-tuple-element.70), channel_id=1, source_target_pairs={{0,6},{1,7},{2,0},{3,1},{4,2},{5,3},{6,4},{7,5},{8,14},{9,15},{10,... | collective-permute-start | bytes 786440 | tf_op jit(solution)/shard_map/ppermute | solution.py:547
  (10 other events, 125.4 us)

commit v9 on v8

--- a/solution.py
+++ b/solution.py
@@ -183,8 +183,8 @@
 
 
 def own_row_kernel(
-    place_ref, q_ref, k_ref, v_ref, row_a, row_b, below_a, above_b, state_ref, first_ref,
-    bank_ref, bias_ref, sems,
+    place_ref, q_ref, k_ref, v_ref, row_a, row_b, below_a, above_b, state_ref, bank_ref, bias_ref,
+    sems,
 ):
     y, z = place_ref[0] // WIDE, place_ref[0] % WIDE
     acc_ref, peak_ref = sums(state_ref)
@@ -196,8 +196,6 @@
         (row_b, bank_ref.at[pl.ds(half, half)], z >= 0),
         (below_a, bank_ref.at[pl.ds(2 * half, half)], y > 0),
         (above_b, bank_ref.at[pl.ds(3 * half, half)], y == 3),
-        (row_a.at[pl.ds(0, KEEP)], first_ref, y == 0),
-        (below_a.at[pl.ds(0, KEEP)], first_ref, y == 1),
     ]
     copies = [
         (pltpu.make_async_copy(source, target, sems.at[at]), on)
@@ -222,7 +220,7 @@
     def read_fast(step, with_bias):
         if with_bias:
             return read_masked(step)
-        for at, (one, on) in enumerate(copies[2:4]):
+        for at, (one, on) in enumerate(copies[2:]):
             pl.when(on & (step == row_steps + at))(one.wait)
         return *tile_of(bank_ref, step_start(step), STEP), None
 
@@ -241,8 +239,6 @@
     steps = row_steps + jnp.where(y == 3, 2, jnp.minimum(y, 1))
     absorb(heads, view, masked, steps, read_fast)
     absorb_again(acc_ref, view, start, masked + STEP // TILE * steps, read)
-    for one, on in copies[4:]:
-        pl.when(on)(one.wait)
 
 
 def more_keys(queries, rest_ref, state_in, refs, used, firsts, pieces, steps, then):
@@ -391,17 +387,16 @@
     length, width = queries.shape
     whole = lambda x: pl.BlockSpec(x.shape, lambda i: (0,) * len(x.shape))
     state = state_of(length, width // HEAD)
-    first = jax.ShapeDtypeStruct((KEEP, 2 * HEAD), jnp.bfloat16)
     return pl.pallas_call(
         own_row_kernel,
         grid=(1,),
-        out_shape=[state, first],
+        out_shape=state,
         in_specs=[SMEM, *[whole(x) for x in (queries, keys, values)], *[ANY] * len(pieces)],
-        out_specs=[whole(state), ANY],
+        out_specs=whole(state),
         scratch_shapes=[
             pltpu.VMEM((4 * STEP, 2 * HEAD), jnp.bfloat16),
             pltpu.VMEM((8, TILE), jnp.float32),
-            pltpu.SemaphoreType.DMA((6,)),
+            pltpu.SemaphoreType.DMA((4,)),
         ],
         compiler_params=PARAMS,
         cost_estimate=cost(length * width // HEAD, length + 4 * STEP),
@@ -513,7 +508,6 @@
         right.append(permute(right[-1], minus))
         if step < len(upward):
             rest = rest + permute(rest, upward[step])
-            left[-1], right[-1], rest = lax.optimization_barrier((left[-1], right[-1], rest))
     opposite = [permute(left[-1][:half], plus), permute(right[-1][half:], minus)]
     ends = pack_row(place, right[1:] + opposite + left[:0:-1] + [kept])
 
@@ -522,13 +516,16 @@
     rest, ends = lax.optimization_barrier((rest, ends))
     rest = rest + permute(rest, spread([(0, 4)]))
     rest = rest + permute(rest, spread([(0, 2), (4, 6)]))
-    rest, below_a, above_b, ends = lax.optimization_barrier((rest, below_a, above_b, ends))
+    rest = rest + permute(rest, spread([(0, 1), (2, 3), (4, 5), (6, 7)]))
+    first = jnp.where(mine // WIDE == 1, below_a[:KEEP], ends[0][:KEEP])
+    rest, first, below_a, above_b, ends = lax.optimization_barrier(
+        (rest, first, below_a, above_b, ends)
+    )
     below_b = permute(ends[1], across([(0, 1), (1, 2), (2, 3)]))
     above_a = permute(ends[0], across([(0, 3)]))
     below2 = permute(below_a, across([(1, 2), (2, 3)]))
     above2 = permute(above_b, across([(0, 3), (3, 2)]))
-    rest = rest + permute(rest, spread([(0, 1), (2, 3), (4, 5), (6, 7)]))
-    state, first = own_row(place, queries, key_rows, value_rows, *ends, below_a, above_b)
+    state = own_row(place, queries, key_rows, value_rows, *ends, below_a, above_b)
     banks = (first, below_b, above_a, below2, above2)
     own, far, near = rest_rows(place, queries, rest, banks, output_weight, state, chips)
 

time: 150 us -> 148 us (0.987); the launches traced: 150 us -> 146 us
  waiting for transfers between devices: 46 us -> 37.3 us
  starting transfers between devices: 41.6 us -> 45.7 us
    ppermute x19, waiting for transfers between devices: 30.8 us -> 22.3 us  [on_device(): permute = lambda x, pairs: lax.ppermute(x, 'ctx', pairs)]
    ppermute x19, starting transfers between devices: 33.8 us -> 37.7 us  [on_device(): permute = lambda x, pairs: lax.ppermute(x, 'ctx', pairs)]
    unnamed x14 -> x16, local copies, waits for them, and re-layouts: 2.49 us -> 3.12 us
  transfers between devices with their start and end apart: 27 -> 27, of which waited for: 18 -> 17; matrix products, arithmetic and copies ran while one was open for 0% -> 0% of each run, Pallas kernels for 7% -> 8%
where the time goes in v9:
time: 148 us; the launch traced here: 146 us
  Pallas kernels  58.5 us (40%)
  starting transfers between devices  45.7 us (31%)
  waiting for transfers between devices  37.3 us (25%)
  local copies, waits for them, and re-layouts  3.13 us (2%)
    pallas_call x1, Pallas kernels, rest_rows(): pl.pallas_call(rest_kernel, grid=(1,), out_shape=[jax.ShapeDtypeStruct(sh...  44.2 us
    ppermute x19, starting transfers between devices, on_device(): permute = lambda x, pairs: lax.ppermute(x, 'ctx', pairs)  37.7 us
    ppermute x19, waiting for transfers between devices, on_device(): permute = lambda x, pairs: lax.ppermute(x, 'ctx', pairs)  22.3 us
    pallas_call x1, Pallas kernels, own_row(): pl.pallas_call(own_row_kernel, grid=(1,), out_shape=state, in_specs=[SMEM...  9.67 us
    ppermute x1, waiting for transfers between devices, on_device(): lax.ppermute(upper_down, 'head', down)  3.32 us
    ppermute x1, waiting for transfers between devices, on_device(): lax.ppermute(upper_up, 'head', up)  3.16 us
    unnamed x16, local copies, waits for them, and re-layouts  3.12 us
  transfers between devices with their start and end apart: 27, of which 17 were waited for; matrix products, arithmetic and copies ran while one was open for 0% of the time, Pallas kernels for 8%

profile of v9, /device:TPU:30, one launch (start us, length us, event | category | flops | bytes accessed | tf_op | source)
XLA Modules:
  0.0 145.8 jit_solution(9424365710760434839)
XLA Ops:
  0.7 2.4 %select_kept.1 = (bf16[256,256]{1,0:T(8,128)(2,1)}, bf16[272,256]{1,0:T(8,128)(2,1)}) custom-call(s32[1]{0:T(128)S(6)} %copy.7.used_ref, s32[1,256]{1,0:T(1,128)} %refs_0_.1, bf16[512,128]{1,0:T(8,128)(2,1)} %k_ref.1, bf16[512,128]{1,0:T(8,128)(2,1)} %v_ref.1), custom_call_target="tpu_custom_call" | custom-call | tf_op jit(solution)/shard_map/select_kept/pallas_call | solution.py:77
  3.1 2.0 %collective-permute-start.5 = (bf16[256,256]{1,0:T(8,128)(2,1)}, bf16[256,256]{1,0:T(8,128)(2,1)S(1)}, u32[]{:S(2)}, u32[]{:S(2)}) collective-permute-start(bf16[256,256]{1,0:T(8,128)(2,1)} %get-tuple-element.32.refs_8_), channel_id=1, source_target_pairs={{0,8},{8,16},{16,24},{24,32},{32,40},{40,48},{48,56},{56,0},{64,72... | collective-permute-start | bytes 393224 | tf_op jit(solution)/shard_map/ppermute | solution.py:494
  5.1 4.0 %collective-permute-start.2 = (bf16[256,256]{1,0:T(8,128)(2,1)}, bf16[256,256]{1,0:T(8,128)(2,1)S(1)}, u32[]{:S(2)}, u32[]{:S(2)}) collective-permute-start(bf16[256,256]{1,0:T(8,128)(2,1)} %get-tuple-element.32.refs_8_), channel_id=1, source_target_pairs={{0,56},{8,0},{16,8},{24,16},{32,24},{40,32},{48,40},{56,48},{64,12... | collective-permute-start | bytes 393224 | tf_op jit(solution)/shard_map/ppermute | solution.py:494
  9.8 2.9 %collective-permute-done.5.refs_7_ = bf16[256,256]{1,0:T(8,128)(2,1)S(1)} collective-permute-done((bf16[256,256]{1,0:T(8,128)(2,1)}, bf16[256,256]{1,0:T(8,128)(2,1)S(1)}, u32[]{:S(2)}, u32[]{:S(2)}) %collective-permute-start.5) | collective-permute-done | bytes 131104 | tf_op jit(solution)/shard_map/ppermute | solution.py:494
  12.7 3.2 %collective-permute-start.3 = (bf16[256,256]{1,0:T(8,128)(2,1)S(1)}, bf16[256,256]{1,0:T(8,128)(2,1)S(1)}, u32[]{:S(2)}, u32[]{:S(2)}) collective-permute-start(bf16[256,256]{1,0:T(8,128)(2,1)S(1)} %collective-permute-done.2.refs_0_), channel_id=1, source_target_pairs={{0,56},{8,0},{16,8},{24,16},{32,24},{40,32},{48,40},{56,48},{64,12... | collective-permute-start | bytes 393224 | tf_op jit(solution)/shard_map/ppermute | solution.py:494
  16.0 2.9 %collective-permute-done.6.refs_6_ = bf16[256,256]{1,0:T(8,128)(2,1)S(1)} collective-permute-done((bf16[256,256]{1,0:T(8,128)(2,1)S(1)}, bf16[256,256]{1,0:T(8,128)(2,1)S(1)}, u32[]{:S(2)}, u32[]{:S(2)}) %collective-permute-start.6) | collective-permute-done | bytes 131104 | tf_op jit(solution)/shard_map/ppermute | solution.py:494
  18.9 3.2 %collective-permute-start.4 = (bf16[256,256]{1,0:T(8,128)(2,1)S(1)}, bf16[256,256]{1,0:T(8,128)(2,1)S(1)}, u32[]{:S(2)}, u32[]{:S(2)}) collective-permute-start(bf16[256,256]{1,0:T(8,128)(2,1)S(1)} %collective-permute-done.3.refs_1_), channel_id=1, source_target_pairs={{0,56},{8,0},{16,8},{24,16},{32,24},{40,32},{48,40},{56,48},{64,12... | collective-permute-start | bytes 393224 | tf_op jit(solution)/shard_map/ppermute | solution.py:494
  25.1 3.3 %collective-permute-start.9 = (bf16[128,256]{1,0:T(8,128)(2,1)S(1)}, bf16[128,256]{1,0:T(8,128)(2,1)S(1)}, u32[]{:S(2)}, u32[]{:S(2)}) collective-permute-start(bf16[128,256]{1,0:T(8,128)(2,1)S(1)} %slice.17), channel_id=1, source_target_pairs={{0,56},{8,0},{16,8},{24,16},{32,24},{40,32},{48,40},{56,48},{64,12... | collective-permute-start | bytes 196616 | tf_op jit(solution)/shard_map/ppermute | solution.py:494
  28.5 2.1 %collective-permute-done.8.refs_3_ = bf16[128,256]{1,0:T(8,128)(2,1)S(1)} collective-permute-done((bf16[128,256]{1,0:T(8,128)(2,1)S(1)}, bf16[128,256]{1,0:T(8,128)(2,1)S(1)}, u32[]{:S(2)}, u32[]{:S(2)}) %collective-permute-start.8) | collective-permute-done | bytes 65568 | tf_op jit(solution)/shard_map/ppermute | solution.py:494
  33.6 6.2 %collective-permute-start.10 = (bf16[272,256]{1,0:T(8,128)(2,1)S(1)}, bf16[272,256]{1,0:T(8,128)(2,1)S(1)}, u32[]{:S(2)}, u32[]{:S(2)}) collective-permute-start(bf16[272,256]{1,0:T(8,128)(2,1)S(1)} %add.23), channel_id=1, source_target_pairs={{0,32},{64,96},{128,160},{192,224},{1,33},{65,97},{129,161},{193,2... | collective-permute-start | bytes 417800 | tf_op jit(solution)/shard_map/ppermute | solution.py:494
  43.9 2.6 %collective-permute-done.11 = bf16[272,256]{1,0:T(8,128)(2,1)S(1)} collective-permute-done((bf16[272,256]{1,0:T(8,128)(2,1)S(1)}, bf16[272,256]{1,0:T(8,128)(2,1)S(1)}, u32[]{:S(2)}, u32[]{:S(2)}) %collective-permute-start.11) | collective-permute-done | bytes 139296 | tf_op jit(solution)/shard_map/ppermute | solution.py:494
  47.8 2.6 %collective-permute-done.12 = bf16[272,256]{1,0:T(8,128)(2,1)S(1)} collective-permute-done((bf16[272,256]{1,0:T(8,128)(2,1)S(1)}, bf16[272,256]{1,0:T(8,128)(2,1)S(1)}, u32[]{:S(2)}, u32[]{:S(2)}) %collective-permute-start.12) | collective-permute-done | bytes 139296 | tf_op jit(solution)/shard_map/ppermute | solution.py:494
  56.8 4.7 %collective-permute-start.18 = (bf16[1024,256]{1,0:T(8,128)(2,1)}, bf16[1024,256]{1,0:T(8,128)(2,1)}, u32[]{:S(2)}, u32[]{:S(2)}) collective-permute-start(bf16[1024,256]{1,0:T(8,128)(2,1)} %copy-done.7), channel_id=1, source_target_pairs={{0,192},{8,200},{16,208},{24,216},{32,224},{40,232},{48,240},{56,2... | collective-permute-start | bytes 1572872 | tf_op jit(solution)/shard_map/ppermute | solution.py:494
  61.5 9.7 %own_row.1.state_in = f32[4,512,384]{2,1,0:T(8,128)} custom-call(s32[4]{0:T(128)} %copy-done.2, bf16[512,512]{1,0:T(8,128)(2,1)} %queries.1, bf16[512,128]{1,0:T(8,128)(2,1)} %k_ref.1, bf16[512,128]{1,0:T(8,128)(2,1)} %v_ref.1, bf16[1024,256]{1,0:T(8,128)(2,1)} %copy-done.1, bf16[1024,256]{1,0:T(8,128)(2,1)} %copy-done.5, bf16[1024,256]{1,0:T(8,128)(2,1)} %copy-done.6, ...), custom_call_target="tpu_custom_call" | custom-call | flops 9663676416 | bytes 8388608 | tf_op jit(solution)/shard_map/own_row/pallas_call | solution.py:390
  71.2 2.7 %collective-permute-done.17.below2_ref = bf16[1024,256]{1,0:T(8,128)(2,1)S(1)} collective-permute-done((bf16[1024,256]{1,0:T(8,128)(2,1)}, bf16[1024,256]{1,0:T(8,128)(2,1)S(1)}, u32[]{:S(2)}, u32[]{:S(2)}) %collective-permute-start.17) | collective-permute-done | bytes 524320 | tf_op jit(solution)/shard_map/ppermute | solution.py:494
  73.9 2.6 %collective-permute-done.18.above2_ref = bf16[1024,256]{1,0:T(8,128)(2,1)} collective-permute-done((bf16[1024,256]{1,0:T(8,128)(2,1)}, bf16[1024,256]{1,0:T(8,128)(2,1)}, u32[]{:S(2)}, u32[]{:S(2)}) %collective-permute-start.18) | collective-permute-done | bytes 524320 | tf_op jit(solution)/shard_map/ppermute | solution.py:494
  77.2 44.2 %rest_rows.1 = (bf16[4,512,512]{2,1,0:T(8,128)(2,1)S(1)}, bf16[512,512]{1,0:T(8,128)(2,1)S(1)}, bf16[3,512,512]{2,1,0:T(8,128)(2,1)S(1)}) custom-call(s32[4]{0:T(128)S(1)} %copy-done.3, bf16[272,256]{1,0:T(8,128)(2,1)S(1)} %add.26.rest_ref, bf16[512,512]{1,0:T(8,128)(2,1)S(1)} %copy-done.4, bf16[256,256]{1,0:T(8,128)(2,1)S(1)} %slice_select_fusion.first_ref, ...), custom_call_target="tpu_custom_call" | custom-call | flops 9663676416 | bytes 8388608 | tf_op jit(solution)/shard_map/rest_rows/pallas_call | solution.py:413
  121.5 1.9 %collective-permute-done.19.other_ref = bf16[512,512]{1,0:T(8,128)(2,1)S(1)} collective-permute-done((bf16[512,512]{1,0:T(8,128)(2,1)S(1)}, bf16[512,512]{1,0:T(8,128)(2,1)S(1)}, u32[]{:S(2)}, u32[]{:S(2)}) %collective-permute-start.19) | collective-permute-done | bytes 524320 | tf_op jit(solution)/shard_map/ppermute | solution.py:532
  128.0 2.4 %collective-permute-start.22 = (bf16[256,512]{1,0:T(8,128)(2,1)S(1)}, bf16[256,512]{1,0:T(8,128)(2,1)S(1)}, u32[]{:S(2)}, u32[]{:S(2)}) collective-permute-start(bf16[256,512]{1,0:T(8,128)(2,1)S(1)} %get-tuple-element.49), channel_id=1, source_target_pairs={{0,2},{1,3},{2,4},{3,5},{4,6},{5,7},{6,0},{7,1},{8,10},{9,11},{10,... | collective-permute-start | bytes 786440 | tf_op jit(solution)/shard_map/ppermute | solution.py:541
  130.5 2.4 %collective-permute-done.23.refs_2_ = bf16[256,512]{1,0:T(8,128)(2,1)S(1)} collective-permute-done((bf16[256,512]{1,0:T(8,128)(2,1)S(1)}, bf16[256,512]{1,0:T(8,128)(2,1)S(1)}, u32[]{:S(2)}, u32[]{:S(2)}) %collective-permute-start.23) | collective-permute-done | bytes 262176 | tf_op jit(solution)/shard_map/ppermute | solution.py:537
  132.9 1.7 %collective-permute-done.24.refs_5_ = bf16[256,512]{1,0:T(8,128)(2,1)S(1)} collective-permute-done((bf16[256,512]{1,0:T(8,128)(2,1)S(1)}, bf16[256,512]{1,0:T(8,128)(2,1)S(1)}, u32[]{:S(2)}, u32[]{:S(2)}) %collective-permute-start.24) | collective-permute-done | bytes 262176 | tf_op jit(solution)/shard_map/ppermute | solution.py:537
  135.1 1.8 %collective-permute-start.26 = (bf16[256,512]{1,0:T(8,128)(2,1)S(1)}, bf16[256,512]{1,0:T(8,128)(2,1)S(1)}, u32[]{:S(2)}, u32[]{:S(2)}) collective-permute-start(bf16[256,512]{1,0:T(8,128)(2,1)S(1)} %get-tuple-element.56), channel_id=1, source_target_pairs={{0,6},{1,7},{2,0},{3,1},{4,2},{5,3},{6,4},{7,5},{8,14},{9,15},{10,... | collective-permute-start | bytes 786440 | tf_op jit(solution)/shard_map/ppermute | solution.py:544
  136.9 3.3 %collective-permute-done.21.refs_2_ = bf16[256,512]{1,0:T(8,128)(2,1)S(1)} collective-permute-done((bf16[256,512]{1,0:T(8,128)(2,1)S(1)}, bf16[256,512]{1,0:T(8,128)(2,1)S(1)}, u32[]{:S(2)}, u32[]{:S(2)}) %collective-permute-start.21) | collective-permute-done | bytes 262176 | tf_op jit(solution)/shard_map/ppermute | solution.py:541
  140.4 3.2 %collective-permute-done.25.refs_1_ = bf16[256,512]{1,0:T(8,128)(2,1)S(1)} collective-permute-done((bf16[256,512]{1,0:T(8,128)(2,1)S(1)}, bf16[256,512]{1,0:T(8,128)(2,1)S(1)}, u32[]{:S(2)}, u32[]{:S(2)}) %collective-permute-start.25) | collective-permute-done | bytes 262176 | tf_op jit(solution)/shard_map/ppermute | solution.py:544
  (65 shorter events, 26.8 us)
Async XLA Ops:
  3.1 9.6 %collective-permute-start.5 = (bf16[256,256]{1,0:T(8,128)(2,1)}, bf16[256,256]{1,0:T(8,128)(2,1)S(1)}, u32[]{:S(2)}, u32[]{:S(2)}) collective-permute-start(bf16[256,256]{1,0:T(8,128)(2,1)} %get-tuple-element.32.refs_8_), channel_id=1, source_target_pairs={{0,8},{8,16},{16,24},{24,32},{32,40},{40,48},{48,56},{56,0},{64,72... | collective-permute-start | bytes 393224 | tf_op jit(solution)/shard_map/ppermute | solution.py:494
  5.1 7.7 %collective-permute-start.2 = (bf16[256,256]{1,0:T(8,128)(2,1)}, bf16[256,256]{1,0:T(8,128)(2,1)S(1)}, u32[]{:S(2)}, u32[]{:S(2)}) collective-permute-start(bf16[256,256]{1,0:T(8,128)(2,1)} %get-tuple-element.32.refs_8_), channel_id=1, source_target_pairs={{0,56},{8,0},{16,8},{24,16},{32,24},{40,32},{48,40},{56,48},{64,12... | collective-permute-start | bytes 393224 | tf_op jit(solution)/shard_map/ppermute | solution.py:494
  9.1 13.0 %collective-permute-start = (bf16[272,256]{1,0:T(8,128)(2,1)S(1)}, bf16[272,256]{1,0:T(8,128)(2,1)S(1)}, u32[]{:S(2)}, u32[]{:S(2)}) collective-permute-start(bf16[272,256]{1,0:T(8,128)(2,1)S(1)} %broadcast_select_fusion), channel_id=1, source_target_pairs={{0,64},{1,65},{2,66},{3,67},{4,68},{5,69},{6,70},{7,71}} | collective-permute-start | bytes 417800 | tf_op jit(solution)/shard_map/ppermute | solution.py:494
  12.7 6.2 %collective-permute-start.6 = (bf16[256,256]{1,0:T(8,128)(2,1)S(1)}, bf16[256,256]{1,0:T(8,128)(2,1)S(1)}, u32[]{:S(2)}, u32[]{:S(2)}) collective-permute-start(bf16[256,256]{1,0:T(8,128)(2,1)S(1)} %collective-permute-done.5.refs_7_), channel_id=1, source_target_pairs={{0,8},{8,16},{16,24},{24,32},{32,40},{40,48},{48,56},{56,0},{64,72... | collective-permute-start | bytes 393224 | tf_op jit(solution)/shard_map/ppermute | solution.py:494
  12.7 6.2 %collective-permute-start.3 = (bf16[256,256]{1,0:T(8,128)(2,1)S(1)}, bf16[256,256]{1,0:T(8,128)(2,1)S(1)}, u32[]{:S(2)}, u32[]{:S(2)}) collective-permute-start(bf16[256,256]{1,0:T(8,128)(2,1)S(1)} %collective-permute-done.2.refs_0_), channel_id=1, source_target_pairs={{0,56},{8,0},{16,8},{24,16},{32,24},{40,32},{48,40},{56,48},{64,12... | collective-permute-start | bytes 393224 | tf_op jit(solution)/shard_map/ppermute | solution.py:494
  18.9 6.2 %collective-permute-start.7 = (bf16[256,256]{1,0:T(8,128)(2,1)S(1)}, bf16[256,256]{1,0:T(8,128)(2,1)S(1)}, u32[]{:S(2)}, u32[]{:S(2)}) collective-permute-start(bf16[256,256]{1,0:T(8,128)(2,1)S(1)} %collective-permute-done.6.refs_6_), channel_id=1, source_target_pairs={{0,8},{8,16},{16,24},{24,32},{32,40},{40,48},{48,56},{56,0},{64,72... | collective-permute-start | bytes 393224 | tf_op jit(solution)/shard_map/ppermute | solution.py:494
  18.9 6.2 %collective-permute-start.4 = (bf16[256,256]{1,0:T(8,128)(2,1)S(1)}, bf16[256,256]{1,0:T(8,128)(2,1)S(1)}, u32[]{:S(2)}, u32[]{:S(2)}) collective-permute-start(bf16[256,256]{1,0:T(8,128)(2,1)S(1)} %collective-permute-done.3.refs_1_), channel_id=1, source_target_pairs={{0,56},{8,0},{16,8},{24,16},{32,24},{40,32},{48,40},{56,48},{64,12... | collective-permute-start | bytes 393224 | tf_op jit(solution)/shard_map/ppermute | solution.py:494
  22.2 11.4 %collective-permute-start.1 = (bf16[272,256]{1,0:T(8,128)(2,1)S(1)}, bf16[272,256]{1,0:T(8,128)(2,1)S(1)}, u32[]{:S(2)}, u32[]{:S(2)}) collective-permute-start(bf16[272,256]{1,0:T(8,128)(2,1)S(1)} %fusion), channel_id=1, source_target_pairs={{0,192},{64,128},{1,193},{65,129},{2,194},{66,130},{3,195},{67,131... | collective-permute-start | bytes 417800 | tf_op jit(solution)/shard_map/ppermute | solution.py:494
  25.1 5.5 %collective-permute-start.8 = (bf16[128,256]{1,0:T(8,128)(2,1)S(1)}, bf16[128,256]{1,0:T(8,128)(2,1)S(1)}, u32[]{:S(2)}, u32[]{:S(2)}) collective-permute-start(bf16[128,256]{1,0:T(8,128)(2,1)S(1)} %slice.16), channel_id=1, source_target_pairs={{0,8},{8,16},{16,24},{24,32},{32,40},{40,48},{48,56},{56,0},{64,72... | collective-permute-start | bytes 196616 | tf_op jit(solution)/shard_map/ppermute | solution.py:494
  25.1 5.4 %collective-permute-start.9 = (bf16[128,256]{1,0:T(8,128)(2,1)S(1)}, bf16[128,256]{1,0:T(8,128)(2,1)S(1)}, u32[]{:S(2)}, u32[]{:S(2)}) collective-permute-start(bf16[128,256]{1,0:T(8,128)(2,1)S(1)} %slice.17), channel_id=1, source_target_pairs={{0,56},{8,0},{16,8},{24,16},{32,24},{40,32},{48,40},{56,48},{64,12... | collective-permute-start | bytes 196616 | tf_op jit(solution)/shard_map/ppermute | solution.py:494
  32.2 18.2 %collective-permute-start.13 = (bf16[1024,256]{1,0:T(8,128)(2,1)S(1)}, bf16[1024,256]{1,0:T(8,128)(2,1)S(1)}, u32[]{:S(2)}, u32[]{:S(2)}) collective-permute-start(bf16[1024,256]{1,0:T(8,128)(2,1)S(1)} %get-tuple-element.41.row_a), channel_id=1, source_target_pairs={{0,64},{8,72},{16,80},{24,88},{32,96},{40,104},{48,112},{56,120},{... | collective-permute-start | bytes 1572872 | tf_op jit(solution)/shard_map/ppermute | solution.py:494
  33.6 9.0 %collective-permute-start.10 = (bf16[272,256]{1,0:T(8,128)(2,1)S(1)}, bf16[272,256]{1,0:T(8,128)(2,1)S(1)}, u32[]{:S(2)}, u32[]{:S(2)}) collective-permute-start(bf16[272,256]{1,0:T(8,128)(2,1)S(1)} %add.23), channel_id=1, source_target_pairs={{0,32},{64,96},{128,160},{192,224},{1,33},{65,97},{129,161},{193,2... | collective-permute-start | bytes 417800 | tf_op jit(solution)/shard_map/ppermute | solution.py:494
  39.8 12.3 %collective-permute-start.14 = (bf16[1024,256]{1,0:T(8,128)(2,1)S(1)}, bf16[1024,256]{1,0:T(8,128)(2,1)S(1)}, u32[]{:S(2)}, u32[]{:S(2)}) collective-permute-start(bf16[1024,256]{1,0:T(8,128)(2,1)S(1)} %get-tuple-element.40.row_b), channel_id=1, source_target_pairs={{0,192},{8,200},{16,208},{24,216},{32,224},{40,232},{48,240},{56,2... | collective-permute-start | bytes 1572872 | tf_op jit(solution)/shard_map/ppermute | solution.py:494
  42.6 3.9 %collective-permute-start.11 = (bf16[272,256]{1,0:T(8,128)(2,1)S(1)}, bf16[272,256]{1,0:T(8,128)(2,1)S(1)}, u32[]{:S(2)}, u32[]{:S(2)}) collective-permute-start(bf16[272,256]{1,0:T(8,128)(2,1)S(1)} %add.24), channel_id=1, source_target_pairs={{0,16},{64,80},{128,144},{192,208},{32,48},{96,112},{160,176},{224... | collective-permute-start | bytes 417800 | tf_op jit(solution)/shard_map/ppermute | solution.py:494
  52.9 18.3 %collective-permute-start.15 = (bf16[1024,256]{1,0:T(8,128)(2,1)S(1)}, bf16[1024,256]{1,0:T(8,128)(2,1)S(1)}, u32[]{:S(2)}, u32[]{:S(2)}) collective-permute-start(bf16[1024,256]{1,0:T(8,128)(2,1)S(1)} %get-tuple-element.40.row_b), channel_id=1, source_target_pairs={{0,64},{8,72},{16,80},{24,88},{32,96},{40,104},{48,112},{56,120},{... | collective-permute-start | bytes 1572872 | tf_op jit(solution)/shard_map/ppermute | solution.py:494
  54.2 17.0 %collective-permute-start.16 = (bf16[1024,256]{1,0:T(8,128)(2,1)S(1)}, bf16[1024,256]{1,0:T(8,128)(2,1)S(1)}, u32[]{:S(2)}, u32[]{:S(2)}) collective-permute-start(bf16[1024,256]{1,0:T(8,128)(2,1)S(1)} %get-tuple-element.41.row_a), channel_id=1, source_target_pairs={{0,192},{8,200},{16,208},{24,216},{32,224},{40,232},{48,240},{56,2... | collective-permute-start | bytes 1572872 | tf_op jit(solution)/shard_map/ppermute | solution.py:494
  55.5 18.4 %collective-permute-start.17 = (bf16[1024,256]{1,0:T(8,128)(2,1)}, bf16[1024,256]{1,0:T(8,128)(2,1)S(1)}, u32[]{:S(2)}, u32[]{:S(2)}) collective-permute-start(bf16[1024,256]{1,0:T(8,128)(2,1)} %copy-done.6), channel_id=1, source_target_pairs={{64,128},{72,136},{80,144},{88,152},{96,160},{104,168},{112,176},{... | collective-permute-start | bytes 1572872 | tf_op jit(solution)/shard_map/ppermute | solution.py:494
  56.8 19.8 %collective-permute-start.18 = (bf16[1024,256]{1,0:T(8,128)(2,1)}, bf16[1024,256]{1,0:T(8,128)(2,1)}, u32[]{:S(2)}, u32[]{:S(2)}) collective-permute-start(bf16[1024,256]{1,0:T(8,128)(2,1)} %copy-done.7), channel_id=1, source_target_pairs={{0,192},{8,200},{16,208},{24,216},{32,224},{40,232},{48,240},{56,2... | collective-permute-start | bytes 1572872 | tf_op jit(solution)/shard_map/ppermute | solution.py:494
  123.6 9.2 %collective-permute-start.23 = (bf16[256,512]{1,0:T(8,128)(2,1)S(1)}, bf16[256,512]{1,0:T(8,128)(2,1)S(1)}, u32[]{:S(2)}, u32[]{:S(2)}) collective-permute-start(bf16[256,512]{1,0:T(8,128)(2,1)S(1)} %get-tuple-element.51), channel_id=1, source_target_pairs={{0,2},{1,3},{2,4},{3,5},{4,6},{5,7},{6,0},{7,1},{8,10},{9,11},{10,... | collective-permute-start | bytes 786440 | tf_op jit(solution)/shard_map/ppermute | solution.py:537
  124.2 10.4 %collective-permute-start.24 = (bf16[256,512]{1,0:T(8,128)(2,1)S(1)}, bf16[256,512]{1,0:T(8,128)(2,1)S(1)}, u32[]{:S(2)}, u32[]{:S(2)}) collective-permute-start(bf16[256,512]{1,0:T(8,128)(2,1)S(1)} %get-tuple-element.52), channel_id=1, source_target_pairs={{0,6},{1,7},{2,0},{3,1},{4,2},{5,3},{6,4},{7,5},{8,14},{9,15},{10,... | collective-permute-start | bytes 786440 | tf_op jit(solution)/shard_map/ppermute | solution.py:537
  126.9 13.3 %collective-permute-start.21 = (bf16[256,512]{1,0:T(8,128)(2,1)S(1)}, bf16[256,512]{1,0:T(8,128)(2,1)S(1)}, u32[]{:S(2)}, u32[]{:S(2)}) collective-permute-start(bf16[256,512]{1,0:T(8,128)(2,1)S(1)} %get-tuple-element.48), channel_id=1, source_target_pairs={{0,6},{1,7},{2,0},{3,1},{4,2},{5,3},{6,4},{7,5},{8,14},{9,15},{10,... | collective-permute-start | bytes 786440 | tf_op jit(solution)/shard_map/ppermute | solution.py:541
  128.0 12.2 %collective-permute-start.22 = (bf16[256,512]{1,0:T(8,128)(2,1)S(1)}, bf16[256,512]{1,0:T(8,128)(2,1)S(1)}, u32[]{:S(2)}, u32[]{:S(2)}) collective-permute-start(bf16[256,512]{1,0:T(8,128)(2,1)S(1)} %get-tuple-element.49), channel_id=1, source_target_pairs={{0,2},{1,3},{2,4},{3,5},{4,6},{5,7},{6,0},{7,1},{8,10},{9,11},{10,... | collective-permute-start | bytes 786440 | tf_op jit(solution)/shard_map/ppermute | solution.py:541
  134.8 8.8 %collective-permute-start.25 = (bf16[256,512]{1,0:T(8,128)(2,1)S(1)}, bf16[256,512]{1,0:T(8,128)(2,1)S(1)}, u32[]{:S(2)}, u32[]{:S(2)}) collective-permute-start(bf16[256,512]{1,0:T(8,128)(2,1)S(1)} %get-tuple-element.55), channel_id=1, source_target_pairs={{0,2},{1,3},{2,4},{3,5},{4,6},{5,7},{6,0},{7,1},{8,10},{9,11},{10,... | collective-permute-start | bytes 786440 | tf_op jit(solution)/shard_map/ppermute | solution.py:544
  135.1 9.8 %collective-permute-start.26 = (bf16[256,512]{1,0:T(8,128)(2,1)S(1)}, bf16[256,512]{1,0:T(8,128)(2,1)S(1)}, u32[]{:S(2)}, u32[]{:S(2)}) collective-permute-start(bf16[256,512]{1,0:T(8,128)(2,1)S(1)} %get-tuple-element.56), channel_id=1, source_target_pairs={{0,6},{1,7},{2,0},{3,1},{4,2},{5,3},{6,4},{7,5},{8,14},{9,15},{10,... | collective-permute-start | bytes 786440 | tf_op jit(solution)/shard_map/ppermute | solution.py:544
  (11 other events, 129.4 us)

commit v10 on v9

--- a/solution.py
+++ b/solution.py
@@ -508,24 +508,24 @@
         right.append(permute(right[-1], minus))
         if step < len(upward):
             rest = rest + permute(rest, upward[step])
+        else:
+            left[-1], right[-1], rest = lax.optimization_barrier((left[-1], right[-1], rest))
     opposite = [permute(left[-1][:half], plus), permute(right[-1][half:], minus)]
     ends = pack_row(place, right[1:] + opposite + left[:0:-1] + [kept])
 
     below_a = permute(ends[0], across([(0, 1), (1, 2), (2, 3)]))
     above_b = permute(ends[1], across([(0, 3), (1, 0)]))
     rest, ends = lax.optimization_barrier((rest, ends))
-    rest = rest + permute(rest, spread([(0, 4)]))
-    rest = rest + permute(rest, spread([(0, 2), (4, 6)]))
-    rest = rest + permute(rest, spread([(0, 1), (2, 3), (4, 5), (6, 7)]))
-    first = jnp.where(mine // WIDE == 1, below_a[:KEEP], ends[0][:KEEP])
-    rest, first, below_a, above_b, ends = lax.optimization_barrier(
-        (rest, first, below_a, above_b, ends)
-    )
+    rest = rest + permute(rest, spread([(0, 2)]))
+    rest = rest + permute(rest, spread([(0, 6), (2, 4)]))
+    rest, below_a, above_b, ends = lax.optimization_barrier((rest, below_a, above_b, ends))
     below_b = permute(ends[1], across([(0, 1), (1, 2), (2, 3)]))
     above_a = permute(ends[0], across([(0, 3)]))
     below2 = permute(below_a, across([(1, 2), (2, 3)]))
     above2 = permute(above_b, across([(0, 3), (3, 2)]))
+    rest = rest + permute(rest, spread([(0, 1), (2, 3), (4, 5), (6, 7)]))
     state = own_row(place, queries, key_rows, value_rows, *ends, below_a, above_b)
+    first = jnp.where(mine // WIDE == 1, below_a[:KEEP], ends[0][:KEEP])
     banks = (first, below_b, above_a, below2, above2)
     own, far, near = rest_rows(place, queries, rest, banks, output_weight, state, chips)
 

time: 148 us -> 145 us (0.980)
  starting transfers between devices: 45.7 us -> 41.2 us
  waiting for transfers between devices: 37.3 us -> 40.6 us
  local copies, waits for them, and re-layouts: 3.13 us -> 1.62 us
    ppermute x19, starting transfers between devices: 37.7 us -> 33.5 us  [on_device(): permute = lambda x, pairs: lax.ppermute(x, 'ctx', pairs)]
    ppermute x19, waiting for transfers between devices: 22.3 us -> 25.3 us  [on_device(): permute = lambda x, pairs: lax.ppermute(x, 'ctx', pairs)]
    unnamed x16 -> x12, local copies, waits for them, and re-layouts: 3.12 us -> 1.61 us
  transfers between devices with their start and end apart: 27 -> 27, of which waited for: 17 -> 19; matrix products, arithmetic and copies ran while one was open for 0% -> 1% of each run, Pallas kernels for 8% -> 7%
where the time goes in v10:
time: 145 us; the launch traced here: 144 us
  Pallas kernels  58.5 us (40%)
  starting transfers between devices  41.2 us (28%)
  waiting for transfers between devices  40.6 us (28%)
  local copies, waits for them, and re-layouts  1.62 us (1%)
    pallas_call x1, Pallas kernels, rest_rows(): pl.pallas_call(rest_kernel, grid=(1,), out_shape=[jax.ShapeDtypeStruct(sh...  44.2 us
    ppermute x19, starting transfers between devices, on_device(): permute = lambda x, pairs: lax.ppermute(x, 'ctx', pairs)  33.5 us
    ppermute x19, waiting for transfers between devices, on_device(): permute = lambda x, pairs: lax.ppermute(x, 'ctx', pairs)  25.3 us
    pallas_call x1, Pallas kernels, own_row(): pl.pallas_call(own_row_kernel, grid=(1,), out_shape=state, in_specs=[SMEM...  9.67 us
    ppermute x1, waiting for transfers between devices, on_device(): lax.ppermute(upper_down, 'head', down)  3.32 us
    ppermute x1, waiting for transfers between devices, on_device(): lax.ppermute(upper_up, 'head', up)  3.17 us
  transfers between devices with their start and end apart: 27, of which 19 were waited for; matrix products, arithmetic and copies ran while one was open for 1% of the time, Pallas kernels for 7%

profile of v10, /device:TPU:30, one launch (start us, length us, event | category | flops | bytes accessed | tf_op | source)
XLA Modules:
  0.0 144.2 jit_solution(4763612872026497755)
XLA Ops:
  0.7 2.4 %select_kept.1 = (bf16[256,256]{1,0:T(8,128)(2,1)}, bf16[272,256]{1,0:T(8,128)(2,1)}) custom-call(s32[1]{0:T(128)S(6)} %copy.7.used_ref, s32[1,256]{1,0:T(1,128)} %refs_0_.1, bf16[512,128]{1,0:T(8,128)(2,1)} %k_ref.1, bf16[512,128]{1,0:T(8,128)(2,1)} %v_ref.1), custom_call_target="tpu_custom_call" | custom-call | tf_op jit(solution)/shard_map/select_kept/pallas_call | solution.py:77
  3.8 5.9 %collective-permute-start.3 = (bf16[256,256]{1,0:T(8,128)(2,1)}, bf16[256,256]{1,0:T(8,128)(2,1)S(1)}, u32[]{:S(2)}, u32[]{:S(2)}) collective-permute-start(bf16[256,256]{1,0:T(8,128)(2,1)} %get-tuple-element.33.refs_8_), channel_id=1, source_target_pairs={{0,56},{8,0},{16,8},{24,16},{32,24},{40,32},{48,40},{56,48},{64,12... | collective-permute-start | bytes 393224 | tf_op jit(solution)/shard_map/ppermute | solution.py:494
  9.7 3.1 %collective-permute-done.3.refs_0_ = bf16[256,256]{1,0:T(8,128)(2,1)S(1)} collective-permute-done((bf16[256,256]{1,0:T(8,128)(2,1)}, bf16[256,256]{1,0:T(8,128)(2,1)S(1)}, u32[]{:S(2)}, u32[]{:S(2)}) %collective-permute-start.3) | collective-permute-done | bytes 131104 | tf_op jit(solution)/shard_map/ppermute | solution.py:494
  12.8 3.6 %collective-permute-start.4 = (bf16[256,256]{1,0:T(8,128)(2,1)S(1)}, bf16[256,256]{1,0:T(8,128)(2,1)S(1)}, u32[]{:S(2)}, u32[]{:S(2)}) collective-permute-start(bf16[256,256]{1,0:T(8,128)(2,1)S(1)} %collective-permute-done.3.refs_0_), channel_id=1, source_target_pairs={{0,56},{8,0},{16,8},{24,16},{32,24},{40,32},{48,40},{56,48},{64,12... | collective-permute-start | bytes 393224 | tf_op jit(solution)/shard_map/ppermute | solution.py:494
  18.9 3.7 %collective-permute-start.5 = (bf16[256,256]{1,0:T(8,128)(2,1)S(1)}, bf16[256,256]{1,0:T(8,128)(2,1)S(1)}, u32[]{:S(2)}, u32[]{:S(2)}) collective-permute-start(bf16[256,256]{1,0:T(8,128)(2,1)S(1)} %collective-permute-done.4.refs_1_), channel_id=1, source_target_pairs={{0,56},{8,0},{16,8},{24,16},{32,24},{40,32},{48,40},{56,48},{64,12... | collective-permute-start | bytes 393224 | tf_op jit(solution)/shard_map/ppermute | solution.py:494
  22.6 2.0 %collective-permute-done.7 = bf16[272,256]{1,0:T(8,128)(2,1)S(1)} collective-permute-done((bf16[272,256]{1,0:T(8,128)(2,1)S(1)}, bf16[272,256]{1,0:T(8,128)(2,1)S(1)}, u32[]{:S(2)}, u32[]{:S(2)}) %collective-permute-start.7) | collective-permute-done | bytes 139296 | tf_op jit(solution)/shard_map/ppermute | solution.py:494
  25.1 3.7 %collective-permute-done.2.refs_5_ = bf16[256,256]{1,0:T(8,128)(2,1)S(1)} collective-permute-done((bf16[256,256]{1,0:T(8,128)(2,1)S(1)}, bf16[256,256]{1,0:T(8,128)(2,1)S(1)}, u32[]{:S(2)}, u32[]{:S(2)}) %collective-permute-start.2) | collective-permute-done | bytes 131104 | tf_op jit(solution)/shard_map/ppermute | solution.py:494
  28.9 3.2 %collective-permute-start.9 = (bf16[128,256]{1,0:T(8,128)(2,1)S(1)}, bf16[128,256]{1,0:T(8,128)(2,1)S(1)}, u32[]{:S(2)}, u32[]{:S(2)}) collective-permute-start(bf16[128,256]{1,0:T(8,128)(2,1)S(1)} %slice.13), channel_id=1, source_target_pairs={{0,56},{8,0},{16,8},{24,16},{32,24},{40,32},{48,40},{56,48},{64,12... | collective-permute-start | bytes 196616 | tf_op jit(solution)/shard_map/ppermute | solution.py:494
  32.2 2.2 %collective-permute-done.8.refs_3_ = bf16[128,256]{1,0:T(8,128)(2,1)S(1)} collective-permute-done((bf16[128,256]{1,0:T(8,128)(2,1)S(1)}, bf16[128,256]{1,0:T(8,128)(2,1)S(1)}, u32[]{:S(2)}, u32[]{:S(2)}) %collective-permute-start.8) | collective-permute-done | bytes 65568 | tf_op jit(solution)/shard_map/ppermute | solution.py:494
  40.0 2.6 %collective-permute-done.10 = bf16[272,256]{1,0:T(8,128)(2,1)S(1)} collective-permute-done((bf16[272,256]{1,0:T(8,128)(2,1)S(1)}, bf16[272,256]{1,0:T(8,128)(2,1)S(1)}, u32[]{:S(2)}, u32[]{:S(2)}) %collective-permute-start.10) | collective-permute-done | bytes 139296 | tf_op jit(solution)/shard_map/ppermute | solution.py:494
  43.9 2.6 %collective-permute-done.11 = bf16[272,256]{1,0:T(8,128)(2,1)S(1)} collective-permute-done((bf16[272,256]{1,0:T(8,128)(2,1)S(1)}, bf16[272,256]{1,0:T(8,128)(2,1)S(1)}, u32[]{:S(2)}, u32[]{:S(2)}) %collective-permute-start.11) | collective-permute-done | bytes 139296 | tf_op jit(solution)/shard_map/ppermute | solution.py:494
  47.2 2.5 %collective-permute-done.13.above_b = bf16[1024,256]{1,0:T(8,128)(2,1)} collective-permute-done((bf16[1024,256]{1,0:T(8,128)(2,1)S(1)}, bf16[1024,256]{1,0:T(8,128)(2,1)}, u32[]{:S(2)}, u32[]{:S(2)}) %collective-permute-start.13) | collective-permute-done | bytes 524320 | tf_op jit(solution)/shard_map/ppermute | solution.py:494
  52.3 4.5 %collective-permute-start.18 = (bf16[1024,256]{1,0:T(8,128)(2,1)}, bf16[1024,256]{1,0:T(8,128)(2,1)S(1)}, u32[]{:S(2)}, u32[]{:S(2)}) collective-permute-start(bf16[1024,256]{1,0:T(8,128)(2,1)} %collective-permute-done.13.above_b), channel_id=1, source_target_pairs={{0,192},{8,200},{16,208},{24,216},{32,224},{40,232},{48,240},{56,2... | collective-permute-start | bytes 1572872 | tf_op jit(solution)/shard_map/ppermute | solution.py:494
  59.5 9.7 %own_row.1.state_in = f32[4,512,384]{2,1,0:T(8,128)} custom-call(s32[4]{0:T(128)} %copy-done.2, bf16[512,512]{1,0:T(8,128)(2,1)} %queries.1, bf16[512,128]{1,0:T(8,128)(2,1)} %k_ref.1, bf16[512,128]{1,0:T(8,128)(2,1)} %v_ref.1, bf16[1024,256]{1,0:T(8,128)(2,1)} %copy-done.1, bf16[1024,256]{1,0:T(8,128)(2,1)} %copy-done.5, ...), custom_call_target="tpu_custom_call" | custom-call | flops 9663676416 | bytes 8388608 | tf_op jit(solution)/shard_map/own_row/pallas_call | solution.py:390
  70.2 1.8 %collective-permute-done.17.below2_ref = bf16[1024,256]{1,0:T(8,128)(2,1)S(1)} collective-permute-done((bf16[1024,256]{1,0:T(8,128)(2,1)}, bf16[1024,256]{1,0:T(8,128)(2,1)S(1)}, u32[]{:S(2)}, u32[]{:S(2)}) %collective-permute-start.17) | collective-permute-done | bytes 524320 | tf_op jit(solution)/shard_map/ppermute | solution.py:494
  72.0 2.7 %collective-permute-done.16.above_a = bf16[1024,256]{1,0:T(8,128)(2,1)S(1)} collective-permute-done((bf16[1024,256]{1,0:T(8,128)(2,1)S(1)}, bf16[1024,256]{1,0:T(8,128)(2,1)S(1)}, u32[]{:S(2)}, u32[]{:S(2)}) %collective-permute-start.16) | collective-permute-done | bytes 524320 | tf_op jit(solution)/shard_map/ppermute | solution.py:494
  75.4 44.2 %rest_rows.1 = (bf16[4,512,512]{2,1,0:T(8,128)(2,1)S(1)}, bf16[512,512]{1,0:T(8,128)(2,1)S(1)}, bf16[3,512,512]{2,1,0:T(8,128)(2,1)S(1)}) custom-call(s32[4]{0:T(128)S(1)} %copy-done.3, bf16[272,256]{1,0:T(8,128)(2,1)S(1)} %add.26.rest_ref, bf16[512,512]{1,0:T(8,128)(2,1)S(1)} %copy-done.4, bf16[256,256]{1,0:T(8,128)(2,1)S(1)} %slice_select_fusion.first_ref, ...), custom_call_target="tpu_custom_call" | custom-call | flops 9663676416 | bytes 8388608 | tf_op jit(solution)/shard_map/rest_rows/pallas_call | solution.py:413
  119.7 1.9 %collective-permute-done.19.other_ref = bf16[512,512]{1,0:T(8,128)(2,1)S(1)} collective-permute-done((bf16[512,512]{1,0:T(8,128)(2,1)S(1)}, bf16[512,512]{1,0:T(8,128)(2,1)S(1)}, u32[]{:S(2)}, u32[]{:S(2)}) %collective-permute-start.19) | collective-permute-done | bytes 524320 | tf_op jit(solution)/shard_map/ppermute | solution.py:532
  126.1 2.4 %collective-permute-start.22 = (bf16[256,512]{1,0:T(8,128)(2,1)S(1)}, bf16[256,512]{1,0:T(8,128)(2,1)S(1)}, u32[]{:S(2)}, u32[]{:S(2)}) collective-permute-start(bf16[256,512]{1,0:T(8,128)(2,1)S(1)} %get-tuple-element.53), channel_id=1, source_target_pairs={{0,2},{1,3},{2,4},{3,5},{4,6},{5,7},{6,0},{7,1},{8,10},{9,11},{10,... | collective-permute-start | bytes 786440 | tf_op jit(solution)/shard_map/ppermute | solution.py:541
  128.5 2.6 %collective-permute-done.23.refs_2_ = bf16[256,512]{1,0:T(8,128)(2,1)S(1)} collective-permute-done((bf16[256,512]{1,0:T(8,128)(2,1)S(1)}, bf16[256,512]{1,0:T(8,128)(2,1)S(1)}, u32[]{:S(2)}, u32[]{:S(2)}) %collective-permute-start.23) | collective-permute-done | bytes 262176 | tf_op jit(solution)/shard_map/ppermute | solution.py:537
  131.1 1.7 %collective-permute-done.24.refs_5_ = bf16[256,512]{1,0:T(8,128)(2,1)S(1)} collective-permute-done((bf16[256,512]{1,0:T(8,128)(2,1)S(1)}, bf16[256,512]{1,0:T(8,128)(2,1)S(1)}, u32[]{:S(2)}, u32[]{:S(2)}) %collective-permute-start.24) | collective-permute-done | bytes 262176 | tf_op jit(solution)/shard_map/ppermute | solution.py:537
  133.4 1.7 %collective-permute-start.26 = (bf16[256,512]{1,0:T(8,128)(2,1)S(1)}, bf16[256,512]{1,0:T(8,128)(2,1)S(1)}, u32[]{:S(2)}, u32[]{:S(2)}) collective-permute-start(bf16[256,512]{1,0:T(8,128)(2,1)S(1)} %get-tuple-element.60), channel_id=1, source_target_pairs={{0,6},{1,7},{2,0},{3,1},{4,2},{5,3},{6,4},{7,5},{8,14},{9,15},{10,... | collective-permute-start | bytes 786440 | tf_op jit(solution)/shard_map/ppermute | solution.py:544
  135.1 3.3 %collective-permute-done.21.refs_2_ = bf16[256,512]{1,0:T(8,128)(2,1)S(1)} collective-permute-done((bf16[256,512]{1,0:T(8,128)(2,1)S(1)}, bf16[256,512]{1,0:T(8,128)(2,1)S(1)}, u32[]{:S(2)}, u32[]{:S(2)}) %collective-permute-start.21) | collective-permute-done | bytes 262176 | tf_op jit(solution)/shard_map/ppermute | solution.py:541
  138.6 3.2 %collective-permute-done.25.refs_1_ = bf16[256,512]{1,0:T(8,128)(2,1)S(1)} collective-permute-done((bf16[256,512]{1,0:T(8,128)(2,1)S(1)}, bf16[256,512]{1,0:T(8,128)(2,1)S(1)}, u32[]{:S(2)}, u32[]{:S(2)}) %collective-permute-start.25) | collective-permute-done | bytes 262176 | tf_op jit(solution)/shard_map/ppermute | solution.py:544
  (61 shorter events, 26.0 us)
Async XLA Ops:
  3.1 13.3 %collective-permute-start.6 = (bf16[272,256]{1,0:T(8,128)(2,1)S(1)}, bf16[272,256]{1,0:T(8,128)(2,1)S(1)}, u32[]{:S(2)}, u32[]{:S(2)}) collective-permute-start(bf16[272,256]{1,0:T(8,128)(2,1)S(1)} %broadcast_select_fusion), channel_id=1, source_target_pairs={{0,64},{1,65},{2,66},{3,67},{4,68},{5,69},{6,70},{7,71}} | collective-permute-start | bytes 417800 | tf_op jit(solution)/shard_map/ppermute | solution.py:494
  3.8 9.0 %collective-permute-start.3 = (bf16[256,256]{1,0:T(8,128)(2,1)}, bf16[256,256]{1,0:T(8,128)(2,1)S(1)}, u32[]{:S(2)}, u32[]{:S(2)}) collective-permute-start(bf16[256,256]{1,0:T(8,128)(2,1)} %get-tuple-element.33.refs_8_), channel_id=1, source_target_pairs={{0,56},{8,0},{16,8},{24,16},{32,24},{40,32},{48,40},{56,48},{64,12... | collective-permute-start | bytes 393224 | tf_op jit(solution)/shard_map/ppermute | solution.py:494
  9.7 6.7 %collective-permute-start = (bf16[256,256]{1,0:T(8,128)(2,1)}, bf16[256,256]{1,0:T(8,128)(2,1)S(1)}, u32[]{:S(2)}, u32[]{:S(2)}) collective-permute-start(bf16[256,256]{1,0:T(8,128)(2,1)} %get-tuple-element.33.refs_8_), channel_id=1, source_target_pairs={{0,8},{8,16},{16,24},{24,32},{32,40},{40,48},{48,56},{56,0},{64,72... | collective-permute-start | bytes 393224 | tf_op jit(solution)/shard_map/ppermute | solution.py:494
  12.8 6.1 %collective-permute-start.4 = (bf16[256,256]{1,0:T(8,128)(2,1)S(1)}, bf16[256,256]{1,0:T(8,128)(2,1)S(1)}, u32[]{:S(2)}, u32[]{:S(2)}) collective-permute-start(bf16[256,256]{1,0:T(8,128)(2,1)S(1)} %collective-permute-done.3.refs_0_), channel_id=1, source_target_pairs={{0,56},{8,0},{16,8},{24,16},{32,24},{40,32},{48,40},{56,48},{64,12... | collective-permute-start | bytes 393224 | tf_op jit(solution)/shard_map/ppermute | solution.py:494
  16.4 6.2 %collective-permute-start.1 = (bf16[256,256]{1,0:T(8,128)(2,1)S(1)}, bf16[256,256]{1,0:T(8,128)(2,1)S(1)}, u32[]{:S(2)}, u32[]{:S(2)}) collective-permute-start(bf16[256,256]{1,0:T(8,128)(2,1)S(1)} %collective-permute-done.refs_7_), channel_id=1, source_target_pairs={{0,8},{8,16},{16,24},{24,32},{32,40},{40,48},{48,56},{56,0},{64,72... | collective-permute-start | bytes 393224 | tf_op jit(solution)/shard_map/ppermute | solution.py:494
  16.4 8.2 %collective-permute-start.7 = (bf16[272,256]{1,0:T(8,128)(2,1)S(1)}, bf16[272,256]{1,0:T(8,128)(2,1)S(1)}, u32[]{:S(2)}, u32[]{:S(2)}) collective-permute-start(bf16[272,256]{1,0:T(8,128)(2,1)S(1)} %fusion), channel_id=1, source_target_pairs={{0,192},{64,128},{1,193},{65,129},{2,194},{66,130},{3,195},{67,131... | collective-permute-start | bytes 417800 | tf_op jit(solution)/shard_map/ppermute | solution.py:494
  18.9 6.2 %collective-permute-start.5 = (bf16[256,256]{1,0:T(8,128)(2,1)S(1)}, bf16[256,256]{1,0:T(8,128)(2,1)S(1)}, u32[]{:S(2)}, u32[]{:S(2)}) collective-permute-start(bf16[256,256]{1,0:T(8,128)(2,1)S(1)} %collective-permute-done.4.refs_1_), channel_id=1, source_target_pairs={{0,56},{8,0},{16,8},{24,16},{32,24},{40,32},{48,40},{56,48},{64,12... | collective-permute-start | bytes 393224 | tf_op jit(solution)/shard_map/ppermute | solution.py:494
  22.6 6.2 %collective-permute-start.2 = (bf16[256,256]{1,0:T(8,128)(2,1)S(1)}, bf16[256,256]{1,0:T(8,128)(2,1)S(1)}, u32[]{:S(2)}, u32[]{:S(2)}) collective-permute-start(bf16[256,256]{1,0:T(8,128)(2,1)S(1)} %collective-permute-done.1.refs_6_), channel_id=1, source_target_pairs={{0,8},{8,16},{16,24},{24,32},{32,40},{40,48},{48,56},{56,0},{64,72... | collective-permute-start | bytes 393224 | tf_op jit(solution)/shard_map/ppermute | solution.py:494
  28.8 5.6 %collective-permute-start.8 = (bf16[128,256]{1,0:T(8,128)(2,1)S(1)}, bf16[128,256]{1,0:T(8,128)(2,1)S(1)}, u32[]{:S(2)}, u32[]{:S(2)}) collective-permute-start(bf16[128,256]{1,0:T(8,128)(2,1)S(1)} %slice.12), channel_id=1, source_target_pairs={{0,8},{8,16},{16,24},{24,32},{32,40},{40,48},{48,56},{56,0},{64,72... | collective-permute-start | bytes 196616 | tf_op jit(solution)/shard_map/ppermute | solution.py:494
  28.9 5.5 %collective-permute-start.9 = (bf16[128,256]{1,0:T(8,128)(2,1)S(1)}, bf16[128,256]{1,0:T(8,128)(2,1)S(1)}, u32[]{:S(2)}, u32[]{:S(2)}) collective-permute-start(bf16[128,256]{1,0:T(8,128)(2,1)S(1)} %slice.13), channel_id=1, source_target_pairs={{0,56},{8,0},{16,8},{24,16},{32,24},{40,32},{48,40},{56,48},{64,12... | collective-permute-start | bytes 196616 | tf_op jit(solution)/shard_map/ppermute | solution.py:494
  36.0 11.2 %collective-permute-start.12 = (bf16[1024,256]{1,0:T(8,128)(2,1)S(1)}, bf16[1024,256]{1,0:T(8,128)(2,1)}, u32[]{:S(2)}, u32[]{:S(2)}) collective-permute-start(bf16[1024,256]{1,0:T(8,128)(2,1)S(1)} %get-tuple-element.45.row_a), channel_id=1, source_target_pairs={{0,64},{8,72},{16,80},{24,88},{32,96},{40,104},{48,112},{56,120},{... | collective-permute-start | bytes 1572872 | tf_op jit(solution)/shard_map/ppermute | solution.py:494
  37.3 12.4 %collective-permute-start.13 = (bf16[1024,256]{1,0:T(8,128)(2,1)S(1)}, bf16[1024,256]{1,0:T(8,128)(2,1)}, u32[]{:S(2)}, u32[]{:S(2)}) collective-permute-start(bf16[1024,256]{1,0:T(8,128)(2,1)S(1)} %get-tuple-element.46.row_b), channel_id=1, source_target_pairs={{0,192},{8,200},{16,208},{24,216},{32,224},{40,232},{48,240},{56,2... | collective-permute-start | bytes 1572872 | tf_op jit(solution)/shard_map/ppermute | solution.py:494
  38.6 4.0 %collective-permute-start.10 = (bf16[272,256]{1,0:T(8,128)(2,1)S(1)}, bf16[272,256]{1,0:T(8,128)(2,1)S(1)}, u32[]{:S(2)}, u32[]{:S(2)}) collective-permute-start(bf16[272,256]{1,0:T(8,128)(2,1)S(1)} %add.23), channel_id=1, source_target_pairs={{0,16},{64,80},{128,144},{192,208},{1,17},{65,81},{129,145},{193,2... | collective-permute-start | bytes 417800 | tf_op jit(solution)/shard_map/ppermute | solution.py:494
  49.7 20.5 %collective-permute-start.14 = (bf16[272,256]{1,0:T(8,128)(2,1)S(1)}, bf16[272,256]{1,0:T(8,128)(2,1)S(1)}, u32[]{:S(2)}, u32[]{:S(2)}) collective-permute-start(bf16[272,256]{1,0:T(8,128)(2,1)S(1)} %add.25), channel_id=1, source_target_pairs={{0,8},{64,72},{128,136},{192,200},{16,24},{80,88},{144,152},{208,2... | collective-permute-start | bytes 417800 | tf_op jit(solution)/shard_map/ppermute | solution.py:494
  51.0 19.2 %collective-permute-start.15 = (bf16[1024,256]{1,0:T(8,128)(2,1)S(1)}, bf16[1024,256]{1,0:T(8,128)(2,1)S(1)}, u32[]{:S(2)}, u32[]{:S(2)}) collective-permute-start(bf16[1024,256]{1,0:T(8,128)(2,1)S(1)} %get-tuple-element.46.row_b), channel_id=1, source_target_pairs={{0,64},{8,72},{16,80},{24,88},{32,96},{40,104},{48,112},{56,120},{... | collective-permute-start | bytes 1572872 | tf_op jit(solution)/shard_map/ppermute | solution.py:494
  52.3 17.9 %collective-permute-start.18 = (bf16[1024,256]{1,0:T(8,128)(2,1)}, bf16[1024,256]{1,0:T(8,128)(2,1)S(1)}, u32[]{:S(2)}, u32[]{:S(2)}) collective-permute-start(bf16[1024,256]{1,0:T(8,128)(2,1)} %collective-permute-done.13.above_b), channel_id=1, source_target_pairs={{0,192},{8,200},{16,208},{24,216},{32,224},{40,232},{48,240},{56,2... | collective-permute-start | bytes 1572872 | tf_op jit(solution)/shard_map/ppermute | solution.py:494
  56.8 15.2 %collective-permute-start.17 = (bf16[1024,256]{1,0:T(8,128)(2,1)}, bf16[1024,256]{1,0:T(8,128)(2,1)S(1)}, u32[]{:S(2)}, u32[]{:S(2)}) collective-permute-start(bf16[1024,256]{1,0:T(8,128)(2,1)} %collective-permute-done.12.below_a), channel_id=1, source_target_pairs={{64,128},{72,136},{80,144},{88,152},{96,160},{104,168},{112,176},{... | collective-permute-start | bytes 1572872 | tf_op jit(solution)/shard_map/ppermute | solution.py:494
  58.1 16.6 %collective-permute-start.16 = (bf16[1024,256]{1,0:T(8,128)(2,1)S(1)}, bf16[1024,256]{1,0:T(8,128)(2,1)S(1)}, u32[]{:S(2)}, u32[]{:S(2)}) collective-permute-start(bf16[1024,256]{1,0:T(8,128)(2,1)S(1)} %get-tuple-element.45.row_a), channel_id=1, source_target_pairs={{0,192},{8,200},{16,208},{24,216},{32,224},{40,232},{48,240},{56,2... | collective-permute-start | bytes 1572872 | tf_op jit(solution)/shard_map/ppermute | solution.py:494
  121.9 9.2 %collective-permute-start.23 = (bf16[256,512]{1,0:T(8,128)(2,1)S(1)}, bf16[256,512]{1,0:T(8,128)(2,1)S(1)}, u32[]{:S(2)}, u32[]{:S(2)}) collective-permute-start(bf16[256,512]{1,0:T(8,128)(2,1)S(1)} %get-tuple-element.55), channel_id=1, source_target_pairs={{0,2},{1,3},{2,4},{3,5},{4,6},{5,7},{6,0},{7,1},{8,10},{9,11},{10,... | collective-permute-start | bytes 786440 | tf_op jit(solution)/shard_map/ppermute | solution.py:537
  122.5 10.4 %collective-permute-start.24 = (bf16[256,512]{1,0:T(8,128)(2,1)S(1)}, bf16[256,512]{1,0:T(8,128)(2,1)S(1)}, u32[]{:S(2)}, u32[]{:S(2)}) collective-permute-start(bf16[256,512]{1,0:T(8,128)(2,1)S(1)} %get-tuple-element.56), channel_id=1, source_target_pairs={{0,6},{1,7},{2,0},{3,1},{4,2},{5,3},{6,4},{7,5},{8,14},{9,15},{10,... | collective-permute-start | bytes 786440 | tf_op jit(solution)/shard_map/ppermute | solution.py:537
  125.2 13.3 %collective-permute-start.21 = (bf16[256,512]{1,0:T(8,128)(2,1)S(1)}, bf16[256,512]{1,0:T(8,128)(2,1)S(1)}, u32[]{:S(2)}, u32[]{:S(2)}) collective-permute-start(bf16[256,512]{1,0:T(8,128)(2,1)S(1)} %get-tuple-element.52), channel_id=1, source_target_pairs={{0,6},{1,7},{2,0},{3,1},{4,2},{5,3},{6,4},{7,5},{8,14},{9,15},{10,... | collective-permute-start | bytes 786440 | tf_op jit(solution)/shard_map/ppermute | solution.py:541
  126.1 12.4 %collective-permute-start.22 = (bf16[256,512]{1,0:T(8,128)(2,1)S(1)}, bf16[256,512]{1,0:T(8,128)(2,1)S(1)}, u32[]{:S(2)}, u32[]{:S(2)}) collective-permute-start(bf16[256,512]{1,0:T(8,128)(2,1)S(1)} %get-tuple-element.53), channel_id=1, source_target_pairs={{0,2},{1,3},{2,4},{3,5},{4,6},{5,7},{6,0},{7,1},{8,10},{9,11},{10,... | collective-permute-start | bytes 786440 | tf_op jit(solution)/shard_map/ppermute | solution.py:541
  133.0 8.8 %collective-permute-start.25 = (bf16[256,512]{1,0:T(8,128)(2,1)S(1)}, bf16[256,512]{1,0:T(8,128)(2,1)S(1)}, u32[]{:S(2)}, u32[]{:S(2)}) collective-permute-start(bf16[256,512]{1,0:T(8,128)(2,1)S(1)} %get-tuple-element.59), channel_id=1, source_target_pairs={{0,2},{1,3},{2,4},{3,5},{4,6},{5,7},{6,0},{7,1},{8,10},{9,11},{10,... | collective-permute-start | bytes 786440 | tf_op jit(solution)/shard_map/ppermute | solution.py:544
  133.4 9.9 %collective-permute-start.26 = (bf16[256,512]{1,0:T(8,128)(2,1)S(1)}, bf16[256,512]{1,0:T(8,128)(2,1)S(1)}, u32[]{:S(2)}, u32[]{:S(2)}) collective-permute-start(bf16[256,512]{1,0:T(8,128)(2,1)S(1)} %get-tuple-element.60), channel_id=1, source_target_pairs={{0,6},{1,7},{2,0},{3,1},{4,2},{5,3},{6,4},{7,5},{8,14},{9,15},{10,... | collective-permute-start | bytes 786440 | tf_op jit(solution)/shard_map/ppermute | solution.py:544
  (9 other events, 113.3 us)

commit v11 on v10

--- a/solution.py
+++ b/solution.py
@@ -183,10 +183,10 @@
 
 
 def own_row_kernel(
-    place_ref, q_ref, k_ref, v_ref, row_a, row_b, below_a, above_b, state_ref, bank_ref, bias_ref,
+    place_ref, q_ref, k_ref, v_ref, row_a, row_b, one_a, other_b, state_ref, bank_ref, bias_ref,
     sems,
 ):
-    y, z = place_ref[0] // WIDE, place_ref[0] % WIDE
+    y, z, core = place_ref[0] // WIDE, place_ref[0] % WIDE, place_ref[3]
     acc_ref, peak_ref = sums(state_ref)
     keys, half = z * KEEP, row_a.shape[0]
     row_steps = keys // STEP
@@ -194,8 +194,10 @@
     copies = [
         (row_a, bank_ref.at[pl.ds(0, half)], z >= 0),
         (row_b, bank_ref.at[pl.ds(half, half)], z >= 0),
-        (below_a, bank_ref.at[pl.ds(2 * half, half)], y > 0),
-        (above_b, bank_ref.at[pl.ds(3 * half, half)], y == 3),
+        (one_a, bank_ref.at[pl.ds(2 * half, half)], (core == 0) & (y > 0)),
+        (other_b, bank_ref.at[pl.ds(2 * half, half)], (core == 1) & (y > 0)),
+        (one_a, bank_ref.at[pl.ds(3 * half, half)], (core == 1) & (y == 3)),
+        (other_b, bank_ref.at[pl.ds(3 * half, half)], (core == 0) & (y == 3)),
     ]
     copies = [
         (pltpu.make_async_copy(source, target, sems.at[at]), on)
@@ -221,7 +223,7 @@
         if with_bias:
             return read_masked(step)
         for at, (one, on) in enumerate(copies[2:]):
-            pl.when(on & (step == row_steps + at))(one.wait)
+            pl.when(on & (step == row_steps + at // 2))(one.wait)
         return *tile_of(bank_ref, step_start(step), STEP), None
 
     def read(tile):
@@ -246,7 +248,7 @@
     acc_in, peak_in = sums(state_in)
     copies = [(queries, q_ref, True), (peak_in, peak_ref, True)]
     copies += [(ref.at[pl.ds(0, KEEP)], bank_ref.at[pl.ds(0, KEEP)], on) for ref, on in firsts]
-    for at, (ref, on) in enumerate(pieces):
+    for ref, on, at in pieces:
         copies.append((ref, bank_ref.at[pl.ds(TILE + at * STEP, STEP)], on))
     copies.append((acc_in, carried_ref, True))
     copies = [
@@ -290,7 +292,7 @@
             for one, on in here:
                 under(on, one.wait)
             return *tile_of(bank_ref, 0, TILE), bias_ref[0]
-        for at, (one, on) in enumerate(later):
+        for (one, on), (_, _, at) in zip(later, pieces):
             pl.when(on & (step == at))(one.wait)
         return *tile_of(bank_ref, TILE + step * STEP, STEP), None
 
@@ -304,13 +306,22 @@
 
 
 def rest_kernel(
-    place_ref, rest_ref, queries, first_ref, below_b, above_a, below2_ref, above2_ref, weight_ref, state_in,
+    place_ref, rest_ref, queries, first_ref, one_b, other_a, two_a, two_b, weight_ref, state_in,
     own_out, far_out, near_out, own_ref, send_ref, w_ref, att_ref, out_sems, *refs,
 ):
     mine, used = place_ref[0], place_ref[1]
     y = mine // WIDE
-    pieces = (below_b, y > 0), (below2_ref, y > 1), (above2_ref, y > 1), (above_a, y == 3)
-    firsts = (first_ref, (mine > 0) & (y < 2)), (below2_ref, y == 2), (above_a, y == 3)
+    core = place_ref[3]
+    last = (core == 1) & (y == 1) | (core == 0) & (y == 3)
+    pieces = (
+        (one_b, (core == 0) & (y > 0), 0),
+        (other_a, (core == 1) & (y > 0), 0),
+        (two_a, y > 1, 1),
+        (two_b, y > 1, 2),
+        (one_b, (core == 1) & (y == 3), 3),
+        (other_a, (core == 0) & (y == 3), 3),
+    )
+    firsts = (first_ref, (mine > 0) & (y != 2) & ~last), (two_a, y == 2), (other_a, last)
     steps = jnp.where(y == 3, 4, jnp.where(y == 2, 3, y))
     weight_copy = pltpu.make_async_copy(weight_ref, w_ref, out_sems.at[3])
     more_keys(
@@ -348,23 +359,22 @@
     pltpu.make_async_copy(send_ref.at[pl.ds(1, chips - 1)], near_out, out_sems.at[2]).wait()
 
 
-def pack_row_kernel(place_ref, *refs):
-    z = place_ref[0] % WIDE
-    at, middle = KEEP, WIDE * KEEP // 2
-    for ref in refs[:-2]:
-        rows = ref.shape[0]
-        start = pl.multiple_of(lax.rem(z * KEEP + at, WIDE * KEEP), KEEP // 2)
-        at += rows
+def pack_row_kernel(moves, place_ref, *refs):
+    z, way = place_ref[0] % WIDE, 1 - 2 * place_ref[3]
+    middle = WIDE * KEEP // 2
+    for ref, (blocks, row) in zip(refs[:-2], moves):
+        start = lax.rem(z + way * blocks + WIDE, WIDE) * KEEP + row
         for out_ref, first in zip(refs[-2:], (0, middle)):
 
             @pl.when((start >= first) & (start < first + middle))
             def _():
-                out_ref[pl.ds(pl.multiple_of(start - first, KEEP // 2), rows)] = ref[...]
-
-
-def pack_row(place, pieces):
+                at = pl.multiple_of(start - first, KEEP // 2)
+                out_ref[pl.ds(at, ref.shape[0])] = ref[...]
+
+
+def pack_row(place, pieces, moves):
     return pl.pallas_call(
-        pack_row_kernel,
+        functools.partial(pack_row_kernel, moves),
         out_shape=[jax.ShapeDtypeStruct((WIDE * KEEP // 2, 2 * HEAD), jnp.bfloat16)] * 2,
         in_specs=[SMEM] + [VMEM] * len(pieces),
         out_specs=[VMEM] * 2,
@@ -396,7 +406,7 @@
         scratch_shapes=[
             pltpu.VMEM((4 * STEP, 2 * HEAD), jnp.bfloat16),
             pltpu.VMEM((8, TILE), jnp.float32),
-            pltpu.SemaphoreType.DMA((4,)),
+            pltpu.SemaphoreType.DMA((6,)),
         ],
         compiler_params=PARAMS,
         cost_estimate=cost(length * width // HEAD, length + 4 * STEP),
@@ -427,7 +437,7 @@
             pltpu.VMEM((keys, 2 * HEAD), jnp.bfloat16),
             pltpu.VMEM((heads, length, 2 * HEAD), jnp.float32),
             pltpu.VMEM((2, 8, TILE), jnp.float32),
-            pltpu.SemaphoreType.DMA((10,)),
+            pltpu.SemaphoreType.DMA((12,)),
         ],
         compiler_params=pltpu.CompilerParams(vmem_limit_bytes=47 * 2**20),
         cost_estimate=cost(length * heads, keys),
@@ -493,6 +503,15 @@
     across = lambda hops: [(a * WIDE + c, b * WIDE + c) for a, b in hops for c in range(WIDE)]
     permute = lambda x, pairs: lax.ppermute(x, "ctx", pairs)
 
+    def both(x, *ways):
+        pairs = [
+            (a * devices + h, b * devices + h)
+            for one, way in enumerate(ways)
+            for a, b in way
+            for h in range(one, devices, 2)
+        ]
+        return lax.ppermute(x, ("ctx", "head"), pairs)
+
     spots = jnp.stack([chip, core]).astype(jnp.int32)
     place = jnp.concatenate([mine.astype(jnp.int32)[None], anchor_length, spots])
     kept, rest = select(anchor_length, kept_positions, key_rows, value_rows)
@@ -504,29 +523,35 @@
     spread = lambda hops: [(r * WIDE + a, r * WIDE + b) for a, b in hops for r in range(tall)]
     upward = [(0, WIDE)], [(0, 3 * WIDE), (WIDE, 2 * WIDE)]
     for step in range(WIDE // 2 - 1):
-        left.append(permute(left[-1], plus))
-        right.append(permute(right[-1], minus))
+        left.append(both(left[-1], plus, minus))
+        right.append(both(right[-1], minus, plus))
         if step < len(upward):
             rest = rest + permute(rest, upward[step])
         else:
             left[-1], right[-1], rest = lax.optimization_barrier((left[-1], right[-1], rest))
-    opposite = [permute(left[-1][:half], plus), permute(right[-1][half:], minus)]
-    ends = pack_row(place, right[1:] + opposite + left[:0:-1] + [kept])
-
-    below_a = permute(ends[0], across([(0, 1), (1, 2), (2, 3)]))
-    above_b = permute(ends[1], across([(0, 3), (1, 0)]))
+    left.append(both(left[-1][:half], plus, minus))
+    right.append(both(right[-1][half:], minus, plus))
+    moves = [(-at, 0) for at in range(5)] + [(1, 0), (2, 0), (3, 0), (4, half)]
+    ends = pack_row(place, left + right[1:], moves)
+
+    to_above, to_below = across([(0, 1), (1, 2), (2, 3)]), across([(0, 3), (1, 0)])
+    one_a = both(ends[0], to_above, to_below)
+    other_b = both(ends[1], to_below, to_above)
     rest, ends = lax.optimization_barrier((rest, ends))
     rest = rest + permute(rest, spread([(0, 2)]))
     rest = rest + permute(rest, spread([(0, 6), (2, 4)]))
-    rest, below_a, above_b, ends = lax.optimization_barrier((rest, below_a, above_b, ends))
-    below_b = permute(ends[1], across([(0, 1), (1, 2), (2, 3)]))
-    above_a = permute(ends[0], across([(0, 3)]))
-    below2 = permute(below_a, across([(1, 2), (2, 3)]))
-    above2 = permute(above_b, across([(0, 3), (3, 2)]))
+    rest, one_a, other_b, ends = lax.optimization_barrier((rest, one_a, other_b, ends))
+    one_b = both(ends[1], to_above, across([(0, 3)]))
+    other_a = both(ends[0], across([(0, 3)]), to_above)
+    on_above, on_below = across([(1, 2), (2, 3)]), across([(0, 3), (3, 2)])
+    two_a = both(one_a, on_above, on_below)
+    two_b = both(other_b, on_below, on_above)
     rest = rest + permute(rest, spread([(0, 1), (2, 3), (4, 5), (6, 7)]))
-    state = own_row(place, queries, key_rows, value_rows, *ends, below_a, above_b)
-    first = jnp.where(mine // WIDE == 1, below_a[:KEEP], ends[0][:KEEP])
-    banks = (first, below_b, above_a, below2, above2)
+    state = own_row(place, queries, key_rows, value_rows, *ends, one_a, other_b)
+    y = mine // WIDE
+    came = (y == 1) & (core == 0) | (y == 3) & (core == 1)
+    first = jnp.where(came, one_a[:KEEP], ends[0][:KEEP])
+    banks = (first, one_b, other_a, two_a, two_b)
     own, far, near = rest_rows(place, queries, rest, banks, output_weight, state, chips)
 
     far, near = lax.optimization_barrier((lax.ppermute(far, "head", swap), near))

time: 145 us -> 166 us (1.14)
  the two profiles are of different devices: /device:TPU:30 before, /device:TPU:254 now
where the time goes in v11:
time: 166 us
  Pallas kernels  63.6 us (38%)
  starting transfers between devices  60.8 us (37%)
  waiting for transfers between devices  37.8 us (23%)
    pallas_call x1, Pallas kernels, rest_rows(): pl.pallas_call(rest_kernel, grid=(1,), out_shape=[jax.ShapeDtypeStruct(sh...  44.2 us
    ppermute x14, starting transfers between devices, both(): return lax.ppermute(x, ('ctx', 'head'), pairs)  25.6 us
    ppermute x1, starting transfers between devices, on_device(): lax.ppermute(far, 'head', swap)  23.4 us
    ppermute x14, waiting for transfers between devices, both(): return lax.ppermute(x, ('ctx', 'head'), pairs)  23.1 us
    pallas_call x1, Pallas kernels, own_row(): pl.pallas_call(own_row_kernel, grid=(1,), out_shape=state, in_specs=[SMEM...  14.7 us
    ppermute x5, starting transfers between devices, on_device(): permute = lambda x, pairs: lax.ppermute(x, 'ctx', pairs)  3.96 us
    ppermute x1, waiting for transfers between devices, on_device(): lax.ppermute(upper_down, 'head', down)  3.32 us
  transfers between devices with their start and end apart: 27, of which 16 were waited for; matrix products, arithmetic and copies ran while one was open for 1% of the time, Pallas kernels for 9%

profile of v11, /device:TPU:254, one launch (start us, length us, event | category | flops | bytes accessed | tf_op | source)
XLA Modules:
  0.0 166.1 jit_solution(3141800250497369836)
XLA Ops:
  0.7 2.4 %select_kept.1 = (bf16[256,256]{1,0:T(8,128)(2,1)}, bf16[272,256]{1,0:T(8,128)(2,1)}) custom-call(s32[1]{0:T(128)S(6)} %copy.7.used_ref, s32[1,256]{1,0:T(1,128)} %refs_0_.1, bf16[512,128]{1,0:T(8,128)(2,1)} %k_ref.1, bf16[512,128]{1,0:T(8,128)(2,1)} %v_ref.1), custom_call_target="tpu_custom_call" | custom-call | tf_op jit(solution)/shard_map/select_kept/pallas_call | solution.py:77
  4.9 2.2 %collective-permute-start = (bf16[256,256]{1,0:T(8,128)(2,1)}, bf16[256,256]{1,0:T(8,128)(2,1)S(1)}, u32[]{:S(2)}, u32[]{:S(2)}) collective-permute-start(bf16[256,256]{1,0:T(8,128)(2,1)} %get-tuple-element.33.refs_0_), channel_id=1, source_target_pairs={{0,8},{2,10},{4,12},{6,14},{8,16},{10,18},{12,20},{14,22},{16,24},... | collective-permute-start | bytes 393224 | tf_op jit(solution)/shard_map/ppermute | solution.py:513
  7.1 3.5 %collective-permute-done.3.refs_5_ = bf16[256,256]{1,0:T(8,128)(2,1)S(1)} collective-permute-done((bf16[256,256]{1,0:T(8,128)(2,1)}, bf16[256,256]{1,0:T(8,128)(2,1)S(1)}, u32[]{:S(2)}, u32[]{:S(2)}) %collective-permute-start.3) | collective-permute-done | bytes 131104 | tf_op jit(solution)/shard_map/ppermute | solution.py:513
  11.1 2.9 %collective-permute-start.1 = (bf16[256,256]{1,0:T(8,128)(2,1)S(1)}, bf16[256,256]{1,0:T(8,128)(2,1)S(1)}, u32[]{:S(2)}, u32[]{:S(2)}) collective-permute-start(bf16[256,256]{1,0:T(8,128)(2,1)S(1)} %collective-permute-done.refs_1_), channel_id=1, source_target_pairs={{0,8},{2,10},{4,12},{6,14},{8,16},{10,18},{12,20},{14,22},{16,24},... | collective-permute-start | bytes 393224 | tf_op jit(solution)/shard_map/ppermute | solution.py:513
  14.7 2.1 %collective-permute-done.4.refs_6_ = bf16[256,256]{1,0:T(8,128)(2,1)S(1)} collective-permute-done((bf16[256,256]{1,0:T(8,128)(2,1)S(1)}, bf16[256,256]{1,0:T(8,128)(2,1)S(1)}, u32[]{:S(2)}, u32[]{:S(2)}) %collective-permute-start.4) | collective-permute-done | bytes 131104 | tf_op jit(solution)/shard_map/ppermute | solution.py:513
  17.6 3.7 %collective-permute-start.2 = (bf16[256,256]{1,0:T(8,128)(2,1)S(1)}, bf16[256,256]{1,0:T(8,128)(2,1)S(1)}, u32[]{:S(2)}, u32[]{:S(2)}) collective-permute-start(bf16[256,256]{1,0:T(8,128)(2,1)S(1)} %collective-permute-done.1.refs_2_), channel_id=1, source_target_pairs={{0,8},{2,10},{4,12},{6,14},{8,16},{10,18},{12,20},{14,22},{16,24},... | collective-permute-start | bytes 393224 | tf_op jit(solution)/shard_map/ppermute | solution.py:513
  21.4 1.6 collective-permute-done.5.refs_7_
  24.0 3.7 %collective-permute-start.8 = (bf16[128,256]{1,0:T(8,128)(2,1)S(1)}, bf16[128,256]{1,0:T(8,128)(2,1)S(1)}, u32[]{:S(2)}, u32[]{:S(2)}) collective-permute-start(bf16[128,256]{1,0:T(8,128)(2,1)S(1)} %slice.12), channel_id=1, source_target_pairs={{0,8},{2,10},{4,12},{6,14},{8,16},{10,18},{12,20},{14,22},{16,24},... | collective-permute-start | bytes 196616 | tf_op jit(solution)/shard_map/ppermute | solution.py:513
  27.8 2.1 %collective-permute-done.9.refs_8_ = bf16[128,256]{1,0:T(8,128)(2,1)S(1)} collective-permute-done((bf16[128,256]{1,0:T(8,128)(2,1)S(1)}, bf16[128,256]{1,0:T(8,128)(2,1)S(1)}, u32[]{:S(2)}, u32[]{:S(2)}) %collective-permute-start.9) | collective-permute-done | bytes 65568 | tf_op jit(solution)/shard_map/ppermute | solution.py:513
  35.6 8.6 %collective-permute-done.12.one_a = bf16[1024,256]{1,0:T(8,128)(2,1)} collective-permute-done((bf16[1024,256]{1,0:T(8,128)(2,1)S(1)}, bf16[1024,256]{1,0:T(8,128)(2,1)}, u32[]{:S(2)}, u32[]{:S(2)}) %collective-permute-start.12) | collective-permute-done | bytes 524320 | tf_op jit(solution)/shard_map/ppermute | solution.py:513
  47.8 4.9 %collective-permute-start.18 = (bf16[1024,256]{1,0:T(8,128)(2,1)}, bf16[1024,256]{1,0:T(8,128)(2,1)S(1)}, u32[]{:S(2)}, u32[]{:S(2)}) collective-permute-start(bf16[1024,256]{1,0:T(8,128)(2,1)} %collective-permute-done.13.other_b), channel_id=1, source_target_pairs={{0,192},{2,194},{4,196},{6,198},{8,200},{10,202},{12,204},{14,206}... | collective-permute-start | bytes 1572872 | tf_op jit(solution)/shard_map/ppermute | solution.py:513
  55.4 14.7 %own_row.1.state_in = f32[4,512,384]{2,1,0:T(8,128)} custom-call(s32[4]{0:T(128)} %copy-done.2, bf16[512,512]{1,0:T(8,128)(2,1)} %queries.1, bf16[512,128]{1,0:T(8,128)(2,1)} %k_ref.1, bf16[512,128]{1,0:T(8,128)(2,1)} %v_ref.1, bf16[1024,256]{1,0:T(8,128)(2,1)} %copy-done.1, bf16[1024,256]{1,0:T(8,128)(2,1)} %copy-done.5, ...), custom_call_target="tpu_custom_call" | custom-call | flops 9663676416 | bytes 8388608 | tf_op jit(solution)/shard_map/own_row/pallas_call | solution.py:400
  71.1 2.5 %collective-permute-done.17.two_a = bf16[1024,256]{1,0:T(8,128)(2,1)S(1)} collective-permute-done((bf16[1024,256]{1,0:T(8,128)(2,1)}, bf16[1024,256]{1,0:T(8,128)(2,1)S(1)}, u32[]{:S(2)}, u32[]{:S(2)}) %collective-permute-start.17) | collective-permute-done | bytes 524320 | tf_op jit(solution)/shard_map/ppermute | solution.py:513
  74.3 44.2 %rest_rows.1 = (bf16[4,512,512]{2,1,0:T(8,128)(2,1)S(1)}, bf16[512,512]{1,0:T(8,128)(2,1)S(1)}, bf16[3,512,512]{2,1,0:T(8,128)(2,1)S(1)}) custom-call(s32[4]{0:T(128)S(1)} %copy-done.3, bf16[272,256]{1,0:T(8,128)(2,1)S(1)} %add.26.rest_ref, bf16[512,512]{1,0:T(8,128)(2,1)S(1)} %copy-done.4, bf16[256,256]{1,0:T(8,128)(2,1)S(1)} %slice_select_fusion.first_ref, ...), custom_call_target="tpu_custom_call" | custom-call | flops 9663676416 | bytes 8388608 | tf_op jit(solution)/shard_map/rest_rows/pallas_call | solution.py:423
  118.6 23.4 %collective-permute-start.19 = (bf16[512,512]{1,0:T(8,128)(2,1)S(1)}, bf16[512,512]{1,0:T(8,128)(2,1)S(1)}, u32[]{:S(2)}, u32[]{:S(2)}) collective-permute-start(bf16[512,512]{1,0:T(8,128)(2,1)S(1)} %get-tuple-element.49), channel_id=1, source_target_pairs={{0,1},{1,0},{2,3},{3,2},{4,5},{5,4},{6,7},{7,6},{8,9},{9,8},{10,11... | collective-permute-start | bytes 1572872 | tf_op jit(solution)/shard_map/ppermute | solution.py:557
  142.0 1.5 collective-permute-done.19.other_ref
  144.6 1.5 collective-permute-start.24
  148.0 2.4 %collective-permute-start.22 = (bf16[256,512]{1,0:T(8,128)(2,1)S(1)}, bf16[256,512]{1,0:T(8,128)(2,1)S(1)}, u32[]{:S(2)}, u32[]{:S(2)}) collective-permute-start(bf16[256,512]{1,0:T(8,128)(2,1)S(1)} %get-tuple-element.53), channel_id=1, source_target_pairs={{0,2},{1,3},{2,4},{3,5},{4,6},{5,7},{6,0},{7,1},{8,10},{9,11},{10,... | collective-permute-start | bytes 786440 | tf_op jit(solution)/shard_map/ppermute | solution.py:566
  150.4 2.9 %collective-permute-done.23.refs_2_ = bf16[256,512]{1,0:T(8,128)(2,1)S(1)} collective-permute-done((bf16[256,512]{1,0:T(8,128)(2,1)S(1)}, bf16[256,512]{1,0:T(8,128)(2,1)S(1)}, u32[]{:S(2)}, u32[]{:S(2)}) %collective-permute-start.23) | collective-permute-done | bytes 262176 | tf_op jit(solution)/shard_map/ppermute | solution.py:562
  153.2 1.7 %collective-permute-done.24.refs_5_ = bf16[256,512]{1,0:T(8,128)(2,1)S(1)} collective-permute-done((bf16[256,512]{1,0:T(8,128)(2,1)S(1)}, bf16[256,512]{1,0:T(8,128)(2,1)S(1)}, u32[]{:S(2)}, u32[]{:S(2)}) %collective-permute-start.24) | collective-permute-done | bytes 262176 | tf_op jit(solution)/shard_map/ppermute | solution.py:562
  155.5 1.7 %collective-permute-start.26 = (bf16[256,512]{1,0:T(8,128)(2,1)S(1)}, bf16[256,512]{1,0:T(8,128)(2,1)S(1)}, u32[]{:S(2)}, u32[]{:S(2)}) collective-permute-start(bf16[256,512]{1,0:T(8,128)(2,1)S(1)} %get-tuple-element.60), channel_id=1, source_target_pairs={{0,6},{1,7},{2,0},{3,1},{4,2},{5,3},{6,4},{7,5},{8,14},{9,15},{10,... | collective-permute-start | bytes 786440 | tf_op jit(solution)/shard_map/ppermute | solution.py:569
  157.3 3.3 %collective-permute-done.21.refs_2_ = bf16[256,512]{1,0:T(8,128)(2,1)S(1)} collective-permute-done((bf16[256,512]{1,0:T(8,128)(2,1)S(1)}, bf16[256,512]{1,0:T(8,128)(2,1)S(1)}, u32[]{:S(2)}, u32[]{:S(2)}) %collective-permute-start.21) | collective-permute-done | bytes 262176 | tf_op jit(solution)/shard_map/ppermute | solution.py:566
  160.8 2.9 %collective-permute-done.25.refs_1_ = bf16[256,512]{1,0:T(8,128)(2,1)S(1)} collective-permute-done((bf16[256,512]{1,0:T(8,128)(2,1)S(1)}, bf16[256,512]{1,0:T(8,128)(2,1)S(1)}, u32[]{:S(2)}, u32[]{:S(2)}) %collective-permute-start.25) | collective-permute-done | bytes 262176 | tf_op jit(solution)/shard_map/ppermute | solution.py:569
  163.7 1.5 collective-permute-done.26.refs_2_
  (61 shorter events, 23.0 us)
Async XLA Ops:
  3.1 10.9 %collective-permute-start.6 = (bf16[272,256]{1,0:T(8,128)(2,1)S(1)}, bf16[272,256]{1,0:T(8,128)(2,1)S(1)}, u32[]{:S(2)}, u32[]{:S(2)}) collective-permute-start(bf16[272,256]{1,0:T(8,128)(2,1)S(1)} %broadcast_select_fusion), channel_id=1, source_target_pairs={{0,64},{1,65},{2,66},{3,67},{4,68},{5,69},{6,70},{7,71}} | collective-permute-start | bytes 417800 | tf_op jit(solution)/shard_map/ppermute | solution.py:504
  3.8 6.8 %collective-permute-start.3 = (bf16[256,256]{1,0:T(8,128)(2,1)}, bf16[256,256]{1,0:T(8,128)(2,1)S(1)}, u32[]{:S(2)}, u32[]{:S(2)}) collective-permute-start(bf16[256,256]{1,0:T(8,128)(2,1)} %get-tuple-element.33.refs_0_), channel_id=1, source_target_pairs={{0,56},{2,58},{4,60},{6,62},{8,0},{10,2},{12,4},{14,6},{16,8},{18,... | collective-permute-start | bytes 393224 | tf_op jit(solution)/shard_map/ppermute | solution.py:513
  4.9 6.2 %collective-permute-start = (bf16[256,256]{1,0:T(8,128)(2,1)}, bf16[256,256]{1,0:T(8,128)(2,1)S(1)}, u32[]{:S(2)}, u32[]{:S(2)}) collective-permute-start(bf16[256,256]{1,0:T(8,128)(2,1)} %get-tuple-element.33.refs_0_), channel_id=1, source_target_pairs={{0,8},{2,10},{4,12},{6,14},{8,16},{10,18},{12,20},{14,22},{16,24},... | collective-permute-start | bytes 393224 | tf_op jit(solution)/shard_map/ppermute | solution.py:513
  10.6 6.2 %collective-permute-start.4 = (bf16[256,256]{1,0:T(8,128)(2,1)S(1)}, bf16[256,256]{1,0:T(8,128)(2,1)S(1)}, u32[]{:S(2)}, u32[]{:S(2)}) collective-permute-start(bf16[256,256]{1,0:T(8,128)(2,1)S(1)} %collective-permute-done.3.refs_5_), channel_id=1, source_target_pairs={{0,56},{2,58},{4,60},{6,62},{8,0},{10,2},{12,4},{14,6},{16,8},{18,... | collective-permute-start | bytes 393224 | tf_op jit(solution)/shard_map/ppermute | solution.py:513
  11.1 6.6 %collective-permute-start.1 = (bf16[256,256]{1,0:T(8,128)(2,1)S(1)}, bf16[256,256]{1,0:T(8,128)(2,1)S(1)}, u32[]{:S(2)}, u32[]{:S(2)}) collective-permute-start(bf16[256,256]{1,0:T(8,128)(2,1)S(1)} %collective-permute-done.refs_1_), channel_id=1, source_target_pairs={{0,8},{2,10},{4,12},{6,14},{8,16},{10,18},{12,20},{14,22},{16,24},... | collective-permute-start | bytes 393224 | tf_op jit(solution)/shard_map/ppermute | solution.py:513
  14.0 7.3 %collective-permute-start.7 = (bf16[272,256]{1,0:T(8,128)(2,1)S(1)}, bf16[272,256]{1,0:T(8,128)(2,1)S(1)}, u32[]{:S(2)}, u32[]{:S(2)}) collective-permute-start(bf16[272,256]{1,0:T(8,128)(2,1)S(1)} %fusion), channel_id=1, source_target_pairs={{0,192},{64,128},{1,193},{65,129},{2,194},{66,130},{3,195},{67,131... | collective-permute-start | bytes 417800 | tf_op jit(solution)/shard_map/ppermute | solution.py:504
  16.8 6.2 %collective-permute-start.5 = (bf16[256,256]{1,0:T(8,128)(2,1)S(1)}, bf16[256,256]{1,0:T(8,128)(2,1)S(1)}, u32[]{:S(2)}, u32[]{:S(2)}) collective-permute-start(bf16[256,256]{1,0:T(8,128)(2,1)S(1)} %collective-permute-done.4.refs_6_), channel_id=1, source_target_pairs={{0,56},{2,58},{4,60},{6,62},{8,0},{10,2},{12,4},{14,6},{16,8},{18,... | collective-permute-start | bytes 393224 | tf_op jit(solution)/shard_map/ppermute | solution.py:513
  17.6 6.2 %collective-permute-start.2 = (bf16[256,256]{1,0:T(8,128)(2,1)S(1)}, bf16[256,256]{1,0:T(8,128)(2,1)S(1)}, u32[]{:S(2)}, u32[]{:S(2)}) collective-permute-start(bf16[256,256]{1,0:T(8,128)(2,1)S(1)} %collective-permute-done.1.refs_2_), channel_id=1, source_target_pairs={{0,8},{2,10},{4,12},{6,14},{8,16},{10,18},{12,20},{14,22},{16,24},... | collective-permute-start | bytes 393224 | tf_op jit(solution)/shard_map/ppermute | solution.py:513
  23.9 6.0 %collective-permute-start.9 = (bf16[128,256]{1,0:T(8,128)(2,1)S(1)}, bf16[128,256]{1,0:T(8,128)(2,1)S(1)}, u32[]{:S(2)}, u32[]{:S(2)}) collective-permute-start(bf16[128,256]{1,0:T(8,128)(2,1)S(1)} %slice.13), channel_id=1, source_target_pairs={{0,56},{2,58},{4,60},{6,62},{8,0},{10,2},{12,4},{14,6},{16,8},{18,... | collective-permute-start | bytes 196616 | tf_op jit(solution)/shard_map/ppermute | solution.py:513
  24.0 5.9 %collective-permute-start.8 = (bf16[128,256]{1,0:T(8,128)(2,1)S(1)}, bf16[128,256]{1,0:T(8,128)(2,1)S(1)}, u32[]{:S(2)}, u32[]{:S(2)}) collective-permute-start(bf16[128,256]{1,0:T(8,128)(2,1)S(1)} %slice.12), channel_id=1, source_target_pairs={{0,8},{2,10},{4,12},{6,14},{8,16},{10,18},{12,20},{14,22},{16,24},... | collective-permute-start | bytes 196616 | tf_op jit(solution)/shard_map/ppermute | solution.py:513
  31.5 12.7 %collective-permute-start.12 = (bf16[1024,256]{1,0:T(8,128)(2,1)S(1)}, bf16[1024,256]{1,0:T(8,128)(2,1)}, u32[]{:S(2)}, u32[]{:S(2)}) collective-permute-start(bf16[1024,256]{1,0:T(8,128)(2,1)S(1)} %get-tuple-element.45.row_a), channel_id=1, source_target_pairs={{0,64},{2,66},{4,68},{6,70},{8,72},{10,74},{12,76},{14,78},{16,80}... | collective-permute-start | bytes 1572872 | tf_op jit(solution)/shard_map/ppermute | solution.py:513
  32.8 12.4 %collective-permute-start.13 = (bf16[1024,256]{1,0:T(8,128)(2,1)S(1)}, bf16[1024,256]{1,0:T(8,128)(2,1)}, u32[]{:S(2)}, u32[]{:S(2)}) collective-permute-start(bf16[1024,256]{1,0:T(8,128)(2,1)S(1)} %get-tuple-element.46.row_b), channel_id=1, source_target_pairs={{0,192},{2,194},{4,196},{6,198},{8,200},{10,202},{12,204},{14,206}... | collective-permute-start | bytes 1572872 | tf_op jit(solution)/shard_map/ppermute | solution.py:513
  45.2 25.8 %collective-permute-start.14 = (bf16[272,256]{1,0:T(8,128)(2,1)S(1)}, bf16[272,256]{1,0:T(8,128)(2,1)S(1)}, u32[]{:S(2)}, u32[]{:S(2)}) collective-permute-start(bf16[272,256]{1,0:T(8,128)(2,1)S(1)} %add.25), channel_id=1, source_target_pairs={{0,8},{64,72},{128,136},{192,200},{16,24},{80,88},{144,152},{208,2... | collective-permute-start | bytes 417800 | tf_op jit(solution)/shard_map/ppermute | solution.py:504
  46.5 24.6 %collective-permute-start.15 = (bf16[1024,256]{1,0:T(8,128)(2,1)S(1)}, bf16[1024,256]{1,0:T(8,128)(2,1)S(1)}, u32[]{:S(2)}, u32[]{:S(2)}) collective-permute-start(bf16[1024,256]{1,0:T(8,128)(2,1)S(1)} %get-tuple-element.46.row_b), channel_id=1, source_target_pairs={{0,64},{2,66},{4,68},{6,70},{8,72},{10,74},{12,76},{14,78},{16,80}... | collective-permute-start | bytes 1572872 | tf_op jit(solution)/shard_map/ppermute | solution.py:513
  47.8 23.3 %collective-permute-start.18 = (bf16[1024,256]{1,0:T(8,128)(2,1)}, bf16[1024,256]{1,0:T(8,128)(2,1)S(1)}, u32[]{:S(2)}, u32[]{:S(2)}) collective-permute-start(bf16[1024,256]{1,0:T(8,128)(2,1)} %collective-permute-done.13.other_b), channel_id=1, source_target_pairs={{0,192},{2,194},{4,196},{6,198},{8,200},{10,202},{12,204},{14,206}... | collective-permute-start | bytes 1572872 | tf_op jit(solution)/shard_map/ppermute | solution.py:513
  52.7 20.9 %collective-permute-start.17 = (bf16[1024,256]{1,0:T(8,128)(2,1)}, bf16[1024,256]{1,0:T(8,128)(2,1)S(1)}, u32[]{:S(2)}, u32[]{:S(2)}) collective-permute-start(bf16[1024,256]{1,0:T(8,128)(2,1)} %collective-permute-done.12.one_a), channel_id=1, source_target_pairs={{64,128},{66,130},{68,132},{70,134},{72,136},{74,138},{76,140},{78... | collective-permute-start | bytes 1572872 | tf_op jit(solution)/shard_map/ppermute | solution.py:513
  54.0 19.6 %collective-permute-start.16 = (bf16[1024,256]{1,0:T(8,128)(2,1)S(1)}, bf16[1024,256]{1,0:T(8,128)(2,1)S(1)}, u32[]{:S(2)}, u32[]{:S(2)}) collective-permute-start(bf16[1024,256]{1,0:T(8,128)(2,1)S(1)} %get-tuple-element.45.row_a), channel_id=1, source_target_pairs={{0,192},{2,194},{4,196},{6,198},{8,200},{10,202},{12,204},{14,206}... | collective-permute-start | bytes 1572872 | tf_op jit(solution)/shard_map/ppermute | solution.py:513
  118.6 24.9 %collective-permute-start.19 = (bf16[512,512]{1,0:T(8,128)(2,1)S(1)}, bf16[512,512]{1,0:T(8,128)(2,1)S(1)}, u32[]{:S(2)}, u32[]{:S(2)}) collective-permute-start(bf16[512,512]{1,0:T(8,128)(2,1)S(1)} %get-tuple-element.49), channel_id=1, source_target_pairs={{0,1},{1,0},{2,3},{3,2},{4,5},{5,4},{6,7},{7,6},{8,9},{9,8},{10,11... | collective-permute-start | bytes 1572872 | tf_op jit(solution)/shard_map/ppermute | solution.py:557
  144.0 9.2 %collective-permute-start.23 = (bf16[256,512]{1,0:T(8,128)(2,1)S(1)}, bf16[256,512]{1,0:T(8,128)(2,1)S(1)}, u32[]{:S(2)}, u32[]{:S(2)}) collective-permute-start(bf16[256,512]{1,0:T(8,128)(2,1)S(1)} %get-tuple-element.55), channel_id=1, source_target_pairs={{0,2},{1,3},{2,4},{3,5},{4,6},{5,7},{6,0},{7,1},{8,10},{9,11},{10,... | collective-permute-start | bytes 786440 | tf_op jit(solution)/shard_map/ppermute | solution.py:562
  144.6 10.4 %collective-permute-start.24 = (bf16[256,512]{1,0:T(8,128)(2,1)S(1)}, bf16[256,512]{1,0:T(8,128)(2,1)S(1)}, u32[]{:S(2)}, u32[]{:S(2)}) collective-permute-start(bf16[256,512]{1,0:T(8,128)(2,1)S(1)} %get-tuple-element.56), channel_id=1, source_target_pairs={{0,6},{1,7},{2,0},{3,1},{4,2},{5,3},{6,4},{7,5},{8,14},{9,15},{10,... | collective-permute-start | bytes 786440 | tf_op jit(solution)/shard_map/ppermute | solution.py:562
  147.0 13.5 %collective-permute-start.21 = (bf16[256,512]{1,0:T(8,128)(2,1)S(1)}, bf16[256,512]{1,0:T(8,128)(2,1)S(1)}, u32[]{:S(2)}, u32[]{:S(2)}) collective-permute-start(bf16[256,512]{1,0:T(8,128)(2,1)S(1)} %get-tuple-element.52), channel_id=1, source_target_pairs={{0,6},{1,7},{2,0},{3,1},{4,2},{5,3},{6,4},{7,5},{8,14},{9,15},{10,... | collective-permute-start | bytes 786440 | tf_op jit(solution)/shard_map/ppermute | solution.py:566
  148.0 12.6 %collective-permute-start.22 = (bf16[256,512]{1,0:T(8,128)(2,1)S(1)}, bf16[256,512]{1,0:T(8,128)(2,1)S(1)}, u32[]{:S(2)}, u32[]{:S(2)}) collective-permute-start(bf16[256,512]{1,0:T(8,128)(2,1)S(1)} %get-tuple-element.53), channel_id=1, source_target_pairs={{0,2},{1,3},{2,4},{3,5},{4,6},{5,7},{6,0},{7,1},{8,10},{9,11},{10,... | collective-permute-start | bytes 786440 | tf_op jit(solution)/shard_map/ppermute | solution.py:566
  155.2 8.5 %collective-permute-start.25 = (bf16[256,512]{1,0:T(8,128)(2,1)S(1)}, bf16[256,512]{1,0:T(8,128)(2,1)S(1)}, u32[]{:S(2)}, u32[]{:S(2)}) collective-permute-start(bf16[256,512]{1,0:T(8,128)(2,1)S(1)} %get-tuple-element.59), channel_id=1, source_target_pairs={{0,2},{1,3},{2,4},{3,5},{4,6},{5,7},{6,0},{7,1},{8,10},{9,11},{10,... | collective-permute-start | bytes 786440 | tf_op jit(solution)/shard_map/ppermute | solution.py:569
  155.5 9.7 %collective-permute-start.26 = (bf16[256,512]{1,0:T(8,128)(2,1)S(1)}, bf16[256,512]{1,0:T(8,128)(2,1)S(1)}, u32[]{:S(2)}, u32[]{:S(2)}) collective-permute-start(bf16[256,512]{1,0:T(8,128)(2,1)S(1)} %get-tuple-element.60), channel_id=1, source_target_pairs={{0,6},{1,7},{2,0},{3,1},{4,2},{5,3},{6,4},{7,5},{8,14},{9,15},{10,... | collective-permute-start | bytes 786440 | tf_op jit(solution)/shard_map/ppermute | solution.py:569
  (9 other events, 119.7 us)

commit v12 on v10

--- a/solution.py
+++ b/solution.py
@@ -508,14 +508,12 @@
         right.append(permute(right[-1], minus))
         if step < len(upward):
             rest = rest + permute(rest, upward[step])
-        else:
-            left[-1], right[-1], rest = lax.optimization_barrier((left[-1], right[-1], rest))
     opposite = [permute(left[-1][:half], plus), permute(right[-1][half:], minus)]
     ends = pack_row(place, right[1:] + opposite + left[:0:-1] + [kept])
 
+    rest, ends = lax.optimization_barrier((rest, ends))
     below_a = permute(ends[0], across([(0, 1), (1, 2), (2, 3)]))
     above_b = permute(ends[1], across([(0, 3), (1, 0)]))
-    rest, ends = lax.optimization_barrier((rest, ends))
     rest = rest + permute(rest, spread([(0, 2)]))
     rest = rest + permute(rest, spread([(0, 6), (2, 4)]))
     rest, below_a, above_b, ends = lax.optimization_barrier((rest, below_a, above_b, ends))

time: 145 us -> 144 us (level)
  waiting for transfers between devices: 40.6 us -> 37.5 us
  starting transfers between devices: 41.2 us -> 43.3 us
    ppermute x19, waiting for transfers between devices: 25.3 us -> 22.2 us  [on_device(): permute = lambda x, pairs: lax.ppermute(x, 'ctx', pairs)]
    ppermute x19, starting transfers between devices: 33.5 us -> 35.5 us  [on_device(): permute = lambda x, pairs: lax.ppermute(x, 'ctx', pairs)]
  transfers between devices with their start and end apart: 27 -> 27, of which waited for: 19 -> 18; matrix products, arithmetic and copies ran while one was open for 1% -> 1% of each run, Pallas kernels for 7% -> 7%
where the time goes in v12:
time: 144 us; the launch traced here: 143 us
  Pallas kernels  58.5 us (41%)
  starting transfers between devices  43.3 us (30%)
  waiting for transfers between devices  37.5 us (26%)
  local copies, waits for them, and re-layouts  1.62 us (1%)
    pallas_call x1, Pallas kernels, rest_rows(): pl.pallas_call(rest_kernel, grid=(1,), out_shape=[jax.ShapeDtypeStruct(sh...  44.2 us
    ppermute x19, starting transfers between devices, on_device(): permute = lambda x, pairs: lax.ppermute(x, 'ctx', pairs)  35.5 us
    ppermute x19, waiting for transfers between devices, on_device(): permute = lambda x, pairs: lax.ppermute(x, 'ctx', pairs)  22.2 us
    pallas_call x1, Pallas kernels, own_row(): pl.pallas_call(own_row_kernel, grid=(1,), out_shape=state, in_specs=[SMEM...  9.67 us
    ppermute x1, waiting for transfers between devices, on_device(): lax.ppermute(upper_down, 'head', down)  3.32 us
    ppermute x1, waiting for transfers between devices, on_device(): lax.ppermute(upper_up, 'head', up)  3.18 us
  transfers between devices with their start and end apart: 27, of which 18 were waited for; matrix products, arithmetic and copies ran while one was open for 1% of the time, Pallas kernels for 7%

profile of v12, /device:TPU:30, one launch (start us, length us, event | category | flops | bytes accessed | tf_op | source)
XLA Modules:
  0.0 143.1 jit_solution(3795086405142890206)
XLA Ops:
  0.7 2.4 %select_kept.1 = (bf16[256,256]{1,0:T(8,128)(2,1)}, bf16[272,256]{1,0:T(8,128)(2,1)}) custom-call(s32[1]{0:T(128)S(6)} %copy.7.used_ref, s32[1,256]{1,0:T(1,128)} %refs_0_.1, bf16[512,128]{1,0:T(8,128)(2,1)} %k_ref.1, bf16[512,128]{1,0:T(8,128)(2,1)} %v_ref.1), custom_call_target="tpu_custom_call" | custom-call | tf_op jit(solution)/shard_map/select_kept/pallas_call | solution.py:77
  3.1 2.0 %collective-permute-start.5 = (bf16[256,256]{1,0:T(8,128)(2,1)}, bf16[256,256]{1,0:T(8,128)(2,1)S(1)}, u32[]{:S(2)}, u32[]{:S(2)}) collective-permute-start(bf16[256,256]{1,0:T(8,128)(2,1)} %get-tuple-element.31.refs_8_), channel_id=1, source_target_pairs={{0,8},{8,16},{16,24},{24,32},{32,40},{40,48},{48,56},{56,0},{64,72... | collective-permute-start | bytes 393224 | tf_op jit(solution)/shard_map/ppermute | solution.py:494
  5.1 4.0 %collective-permute-start.2 = (bf16[256,256]{1,0:T(8,128)(2,1)}, bf16[256,256]{1,0:T(8,128)(2,1)S(1)}, u32[]{:S(2)}, u32[]{:S(2)}) collective-permute-start(bf16[256,256]{1,0:T(8,128)(2,1)} %get-tuple-element.31.refs_8_), channel_id=1, source_target_pairs={{0,56},{8,0},{16,8},{24,16},{32,24},{40,32},{48,40},{56,48},{64,12... | collective-permute-start | bytes 393224 | tf_op jit(solution)/shard_map/ppermute | solution.py:494
  9.8 2.9 %collective-permute-done.5.refs_7_ = bf16[256,256]{1,0:T(8,128)(2,1)S(1)} collective-permute-done((bf16[256,256]{1,0:T(8,128)(2,1)}, bf16[256,256]{1,0:T(8,128)(2,1)S(1)}, u32[]{:S(2)}, u32[]{:S(2)}) %collective-permute-start.5) | collective-permute-done | bytes 131104 | tf_op jit(solution)/shard_map/ppermute | solution.py:494
  12.7 3.2 %collective-permute-start.3 = (bf16[256,256]{1,0:T(8,128)(2,1)S(1)}, bf16[256,256]{1,0:T(8,128)(2,1)S(1)}, u32[]{:S(2)}, u32[]{:S(2)}) collective-permute-start(bf16[256,256]{1,0:T(8,128)(2,1)S(1)} %collective-permute-done.2.refs_0_), channel_id=1, source_target_pairs={{0,56},{8,0},{16,8},{24,16},{32,24},{40,32},{48,40},{56,48},{64,12... | collective-permute-start | bytes 393224 | tf_op jit(solution)/shard_map/ppermute | solution.py:494
  16.0 2.9 %collective-permute-done.6.refs_6_ = bf16[256,256]{1,0:T(8,128)(2,1)S(1)} collective-permute-done((bf16[256,256]{1,0:T(8,128)(2,1)S(1)}, bf16[256,256]{1,0:T(8,128)(2,1)S(1)}, u32[]{:S(2)}, u32[]{:S(2)}) %collective-permute-start.6) | collective-permute-done | bytes 131104 | tf_op jit(solution)/shard_map/ppermute | solution.py:494
  18.9 3.2 %collective-permute-start.4 = (bf16[256,256]{1,0:T(8,128)(2,1)S(1)}, bf16[256,256]{1,0:T(8,128)(2,1)S(1)}, u32[]{:S(2)}, u32[]{:S(2)}) collective-permute-start(bf16[256,256]{1,0:T(8,128)(2,1)S(1)} %collective-permute-done.3.refs_1_), channel_id=1, source_target_pairs={{0,56},{8,0},{16,8},{24,16},{32,24},{40,32},{48,40},{56,48},{64,12... | collective-permute-start | bytes 393224 | tf_op jit(solution)/shard_map/ppermute | solution.py:494
  25.1 3.3 %collective-permute-start.9 = (bf16[128,256]{1,0:T(8,128)(2,1)S(1)}, bf16[128,256]{1,0:T(8,128)(2,1)S(1)}, u32[]{:S(2)}, u32[]{:S(2)}) collective-permute-start(bf16[128,256]{1,0:T(8,128)(2,1)S(1)} %slice.17), channel_id=1, source_target_pairs={{0,56},{8,0},{16,8},{24,16},{32,24},{40,32},{48,40},{56,48},{64,12... | collective-permute-start | bytes 196616 | tf_op jit(solution)/shard_map/ppermute | solution.py:494
  28.5 1.8 %collective-permute-done.1 = bf16[272,256]{1,0:T(8,128)(2,1)S(1)} collective-permute-done((bf16[272,256]{1,0:T(8,128)(2,1)S(1)}, bf16[272,256]{1,0:T(8,128)(2,1)S(1)}, u32[]{:S(2)}, u32[]{:S(2)}) %collective-permute-start.1) | collective-permute-done | bytes 139296 | tf_op jit(solution)/shard_map/ppermute | solution.py:494
  34.8 4.2 %collective-permute-start.10 = (bf16[272,256]{1,0:T(8,128)(2,1)S(1)}, bf16[272,256]{1,0:T(8,128)(2,1)S(1)}, u32[]{:S(2)}, u32[]{:S(2)}) collective-permute-start(bf16[272,256]{1,0:T(8,128)(2,1)S(1)} %add.23), channel_id=1, source_target_pairs={{0,16},{64,80},{128,144},{192,208},{1,17},{65,81},{129,145},{193,2... | collective-permute-start | bytes 417800 | tf_op jit(solution)/shard_map/ppermute | solution.py:494
  39.0 2.6 %collective-permute-done.10 = bf16[272,256]{1,0:T(8,128)(2,1)S(1)} collective-permute-done((bf16[272,256]{1,0:T(8,128)(2,1)S(1)}, bf16[272,256]{1,0:T(8,128)(2,1)S(1)}, u32[]{:S(2)}, u32[]{:S(2)}) %collective-permute-start.10) | collective-permute-done | bytes 139296 | tf_op jit(solution)/shard_map/ppermute | solution.py:494
  43.0 2.6 %collective-permute-done.11 = bf16[272,256]{1,0:T(8,128)(2,1)S(1)} collective-permute-done((bf16[272,256]{1,0:T(8,128)(2,1)S(1)}, bf16[272,256]{1,0:T(8,128)(2,1)S(1)}, u32[]{:S(2)}, u32[]{:S(2)}) %collective-permute-start.11) | collective-permute-done | bytes 139296 | tf_op jit(solution)/shard_map/ppermute | solution.py:494
  45.6 1.8 %collective-permute-done.13.above_b = bf16[1024,256]{1,0:T(8,128)(2,1)} collective-permute-done((bf16[1024,256]{1,0:T(8,128)(2,1)S(1)}, bf16[1024,256]{1,0:T(8,128)(2,1)}, u32[]{:S(2)}, u32[]{:S(2)}) %collective-permute-start.13) | collective-permute-done | bytes 524320 | tf_op jit(solution)/shard_map/ppermute | solution.py:494
  50.0 4.5 %collective-permute-start.18 = (bf16[1024,256]{1,0:T(8,128)(2,1)}, bf16[1024,256]{1,0:T(8,128)(2,1)S(1)}, u32[]{:S(2)}, u32[]{:S(2)}) collective-permute-start(bf16[1024,256]{1,0:T(8,128)(2,1)} %collective-permute-done.13.above_b), channel_id=1, source_target_pairs={{0,192},{8,200},{16,208},{24,216},{32,224},{40,232},{48,240},{56,2... | collective-permute-start | bytes 1572872 | tf_op jit(solution)/shard_map/ppermute | solution.py:494
  57.2 9.7 %own_row.1.state_in = f32[4,512,384]{2,1,0:T(8,128)} custom-call(s32[4]{0:T(128)} %copy-done.2, bf16[512,512]{1,0:T(8,128)(2,1)} %queries.1, bf16[512,128]{1,0:T(8,128)(2,1)} %k_ref.1, bf16[512,128]{1,0:T(8,128)(2,1)} %v_ref.1, bf16[1024,256]{1,0:T(8,128)(2,1)} %copy-done.1, bf16[1024,256]{1,0:T(8,128)(2,1)} %copy-done.5, ...), custom_call_target="tpu_custom_call" | custom-call | flops 9663676416 | bytes 8388608 | tf_op jit(solution)/shard_map/own_row/pallas_call | solution.py:390
  68.0 2.8 %collective-permute-done.17.below2_ref = bf16[1024,256]{1,0:T(8,128)(2,1)S(1)} collective-permute-done((bf16[1024,256]{1,0:T(8,128)(2,1)}, bf16[1024,256]{1,0:T(8,128)(2,1)S(1)}, u32[]{:S(2)}, u32[]{:S(2)}) %collective-permute-start.17) | collective-permute-done | bytes 524320 | tf_op jit(solution)/shard_map/ppermute | solution.py:494
  70.9 2.8 %collective-permute-done.16.above_a = bf16[1024,256]{1,0:T(8,128)(2,1)S(1)} collective-permute-done((bf16[1024,256]{1,0:T(8,128)(2,1)S(1)}, bf16[1024,256]{1,0:T(8,128)(2,1)S(1)}, u32[]{:S(2)}, u32[]{:S(2)}) %collective-permute-start.16) | collective-permute-done | bytes 524320 | tf_op jit(solution)/shard_map/ppermute | solution.py:494
  74.3 44.2 %rest_rows.1 = (bf16[4,512,512]{2,1,0:T(8,128)(2,1)S(1)}, bf16[512,512]{1,0:T(8,128)(2,1)S(1)}, bf16[3,512,512]{2,1,0:T(8,128)(2,1)S(1)}) custom-call(s32[4]{0:T(128)S(1)} %copy-done.3, bf16[272,256]{1,0:T(8,128)(2,1)S(1)} %add.26.rest_ref, bf16[512,512]{1,0:T(8,128)(2,1)S(1)} %copy-done.4, bf16[256,256]{1,0:T(8,128)(2,1)S(1)} %slice_select_fusion.first_ref, ...), custom_call_target="tpu_custom_call" | custom-call | flops 9663676416 | bytes 8388608 | tf_op jit(solution)/shard_map/rest_rows/pallas_call | solution.py:413
  118.6 1.9 %collective-permute-done.19.other_ref = bf16[512,512]{1,0:T(8,128)(2,1)S(1)} collective-permute-done((bf16[512,512]{1,0:T(8,128)(2,1)S(1)}, bf16[512,512]{1,0:T(8,128)(2,1)S(1)}, u32[]{:S(2)}, u32[]{:S(2)}) %collective-permute-start.19) | collective-permute-done | bytes 524320 | tf_op jit(solution)/shard_map/ppermute | solution.py:530
  125.0 2.4 %collective-permute-start.22 = (bf16[256,512]{1,0:T(8,128)(2,1)S(1)}, bf16[256,512]{1,0:T(8,128)(2,1)S(1)}, u32[]{:S(2)}, u32[]{:S(2)}) collective-permute-start(bf16[256,512]{1,0:T(8,128)(2,1)S(1)} %get-tuple-element.47), channel_id=1, source_target_pairs={{0,2},{1,3},{2,4},{3,5},{4,6},{5,7},{6,0},{7,1},{8,10},{9,11},{10,... | collective-permute-start | bytes 786440 | tf_op jit(solution)/shard_map/ppermute | solution.py:539
  127.4 2.6 %collective-permute-done.23.refs_2_ = bf16[256,512]{1,0:T(8,128)(2,1)S(1)} collective-permute-done((bf16[256,512]{1,0:T(8,128)(2,1)S(1)}, bf16[256,512]{1,0:T(8,128)(2,1)S(1)}, u32[]{:S(2)}, u32[]{:S(2)}) %collective-permute-start.23) | collective-permute-done | bytes 262176 | tf_op jit(solution)/shard_map/ppermute | solution.py:535
  132.3 1.7 %collective-permute-start.26 = (bf16[256,512]{1,0:T(8,128)(2,1)S(1)}, bf16[256,512]{1,0:T(8,128)(2,1)S(1)}, u32[]{:S(2)}, u32[]{:S(2)}) collective-permute-start(bf16[256,512]{1,0:T(8,128)(2,1)S(1)} %get-tuple-element.54), channel_id=1, source_target_pairs={{0,6},{1,7},{2,0},{3,1},{4,2},{5,3},{6,4},{7,5},{8,14},{9,15},{10,... | collective-permute-start | bytes 786440 | tf_op jit(solution)/shard_map/ppermute | solution.py:542
  134.0 3.3 %collective-permute-done.21.refs_2_ = bf16[256,512]{1,0:T(8,128)(2,1)S(1)} collective-permute-done((bf16[256,512]{1,0:T(8,128)(2,1)S(1)}, bf16[256,512]{1,0:T(8,128)(2,1)S(1)}, u32[]{:S(2)}, u32[]{:S(2)}) %collective-permute-start.21) | collective-permute-done | bytes 262176 | tf_op jit(solution)/shard_map/ppermute | solution.py:539
  137.5 3.2 %collective-permute-done.25.refs_1_ = bf16[256,512]{1,0:T(8,128)(2,1)S(1)} collective-permute-done((bf16[256,512]{1,0:T(8,128)(2,1)S(1)}, bf16[256,512]{1,0:T(8,128)(2,1)S(1)}, u32[]{:S(2)}, u32[]{:S(2)}) %collective-permute-start.25) | collective-permute-done | bytes 262176 | tf_op jit(solution)/shard_map/ppermute | solution.py:542
  (61 shorter events, 25.9 us)
Async XLA Ops:
  3.1 9.6 %collective-permute-start.5 = (bf16[256,256]{1,0:T(8,128)(2,1)}, bf16[256,256]{1,0:T(8,128)(2,1)S(1)}, u32[]{:S(2)}, u32[]{:S(2)}) collective-permute-start(bf16[256,256]{1,0:T(8,128)(2,1)} %get-tuple-element.31.refs_8_), channel_id=1, source_target_pairs={{0,8},{8,16},{16,24},{24,32},{32,40},{40,48},{48,56},{56,0},{64,72... | collective-permute-start | bytes 393224 | tf_op jit(solution)/shard_map/ppermute | solution.py:494
  5.1 7.7 %collective-permute-start.2 = (bf16[256,256]{1,0:T(8,128)(2,1)}, bf16[256,256]{1,0:T(8,128)(2,1)S(1)}, u32[]{:S(2)}, u32[]{:S(2)}) collective-permute-start(bf16[256,256]{1,0:T(8,128)(2,1)} %get-tuple-element.31.refs_8_), channel_id=1, source_target_pairs={{0,56},{8,0},{16,8},{24,16},{32,24},{40,32},{48,40},{56,48},{64,12... | collective-permute-start | bytes 393224 | tf_op jit(solution)/shard_map/ppermute | solution.py:494
  9.1 13.0 %collective-permute-start = (bf16[272,256]{1,0:T(8,128)(2,1)S(1)}, bf16[272,256]{1,0:T(8,128)(2,1)S(1)}, u32[]{:S(2)}, u32[]{:S(2)}) collective-permute-start(bf16[272,256]{1,0:T(8,128)(2,1)S(1)} %broadcast_select_fusion), channel_id=1, source_target_pairs={{0,64},{1,65},{2,66},{3,67},{4,68},{5,69},{6,70},{7,71}} | collective-permute-start | bytes 417800 | tf_op jit(solution)/shard_map/ppermute | solution.py:494
  12.7 6.2 %collective-permute-start.6 = (bf16[256,256]{1,0:T(8,128)(2,1)S(1)}, bf16[256,256]{1,0:T(8,128)(2,1)S(1)}, u32[]{:S(2)}, u32[]{:S(2)}) collective-permute-start(bf16[256,256]{1,0:T(8,128)(2,1)S(1)} %collective-permute-done.5.refs_7_), channel_id=1, source_target_pairs={{0,8},{8,16},{16,24},{24,32},{32,40},{40,48},{48,56},{56,0},{64,72... | collective-permute-start | bytes 393224 | tf_op jit(solution)/shard_map/ppermute | solution.py:494
  12.7 6.2 %collective-permute-start.3 = (bf16[256,256]{1,0:T(8,128)(2,1)S(1)}, bf16[256,256]{1,0:T(8,128)(2,1)S(1)}, u32[]{:S(2)}, u32[]{:S(2)}) collective-permute-start(bf16[256,256]{1,0:T(8,128)(2,1)S(1)} %collective-permute-done.2.refs_0_), channel_id=1, source_target_pairs={{0,56},{8,0},{16,8},{24,16},{32,24},{40,32},{48,40},{56,48},{64,12... | collective-permute-start | bytes 393224 | tf_op jit(solution)/shard_map/ppermute | solution.py:494
  18.9 6.2 %collective-permute-start.7 = (bf16[256,256]{1,0:T(8,128)(2,1)S(1)}, bf16[256,256]{1,0:T(8,128)(2,1)S(1)}, u32[]{:S(2)}, u32[]{:S(2)}) collective-permute-start(bf16[256,256]{1,0:T(8,128)(2,1)S(1)} %collective-permute-done.6.refs_6_), channel_id=1, source_target_pairs={{0,8},{8,16},{16,24},{24,32},{32,40},{40,48},{48,56},{56,0},{64,72... | collective-permute-start | bytes 393224 | tf_op jit(solution)/shard_map/ppermute | solution.py:494
  18.9 6.2 %collective-permute-start.4 = (bf16[256,256]{1,0:T(8,128)(2,1)S(1)}, bf16[256,256]{1,0:T(8,128)(2,1)S(1)}, u32[]{:S(2)}, u32[]{:S(2)}) collective-permute-start(bf16[256,256]{1,0:T(8,128)(2,1)S(1)} %collective-permute-done.3.refs_1_), channel_id=1, source_target_pairs={{0,56},{8,0},{16,8},{24,16},{32,24},{40,32},{48,40},{56,48},{64,12... | collective-permute-start | bytes 393224 | tf_op jit(solution)/shard_map/ppermute | solution.py:494
  22.2 8.2 %collective-permute-start.1 = (bf16[272,256]{1,0:T(8,128)(2,1)S(1)}, bf16[272,256]{1,0:T(8,128)(2,1)S(1)}, u32[]{:S(2)}, u32[]{:S(2)}) collective-permute-start(bf16[272,256]{1,0:T(8,128)(2,1)S(1)} %fusion), channel_id=1, source_target_pairs={{0,192},{64,128},{1,193},{65,129},{2,194},{66,130},{3,195},{67,131... | collective-permute-start | bytes 417800 | tf_op jit(solution)/shard_map/ppermute | solution.py:494
  25.1 5.5 %collective-permute-start.8 = (bf16[128,256]{1,0:T(8,128)(2,1)S(1)}, bf16[128,256]{1,0:T(8,128)(2,1)S(1)}, u32[]{:S(2)}, u32[]{:S(2)}) collective-permute-start(bf16[128,256]{1,0:T(8,128)(2,1)S(1)} %slice.16), channel_id=1, source_target_pairs={{0,8},{8,16},{16,24},{24,32},{32,40},{40,48},{48,56},{56,0},{64,72... | collective-permute-start | bytes 196616 | tf_op jit(solution)/shard_map/ppermute | solution.py:494
  25.1 5.4 %collective-permute-start.9 = (bf16[128,256]{1,0:T(8,128)(2,1)S(1)}, bf16[128,256]{1,0:T(8,128)(2,1)S(1)}, u32[]{:S(2)}, u32[]{:S(2)}) collective-permute-start(bf16[128,256]{1,0:T(8,128)(2,1)S(1)} %slice.17), channel_id=1, source_target_pairs={{0,56},{8,0},{16,8},{24,16},{32,24},{40,32},{48,40},{56,48},{64,12... | collective-permute-start | bytes 196616 | tf_op jit(solution)/shard_map/ppermute | solution.py:494
  32.2 13.3 %collective-permute-start.12 = (bf16[1024,256]{1,0:T(8,128)(2,1)S(1)}, bf16[1024,256]{1,0:T(8,128)(2,1)}, u32[]{:S(2)}, u32[]{:S(2)}) collective-permute-start(bf16[1024,256]{1,0:T(8,128)(2,1)S(1)} %get-tuple-element.39.row_a), channel_id=1, source_target_pairs={{0,64},{8,72},{16,80},{24,88},{32,96},{40,104},{48,112},{56,120},{... | collective-permute-start | bytes 1572872 | tf_op jit(solution)/shard_map/ppermute | solution.py:494
  33.5 13.9 %collective-permute-start.13 = (bf16[1024,256]{1,0:T(8,128)(2,1)S(1)}, bf16[1024,256]{1,0:T(8,128)(2,1)}, u32[]{:S(2)}, u32[]{:S(2)}) collective-permute-start(bf16[1024,256]{1,0:T(8,128)(2,1)S(1)} %get-tuple-element.40.row_b), channel_id=1, source_target_pairs={{0,192},{8,200},{16,208},{24,216},{32,224},{40,232},{48,240},{56,2... | collective-permute-start | bytes 1572872 | tf_op jit(solution)/shard_map/ppermute | solution.py:494
  34.8 6.8 %collective-permute-start.10 = (bf16[272,256]{1,0:T(8,128)(2,1)S(1)}, bf16[272,256]{1,0:T(8,128)(2,1)S(1)}, u32[]{:S(2)}, u32[]{:S(2)}) collective-permute-start(bf16[272,256]{1,0:T(8,128)(2,1)S(1)} %add.23), channel_id=1, source_target_pairs={{0,16},{64,80},{128,144},{192,208},{1,17},{65,81},{129,145},{193,2... | collective-permute-start | bytes 417800 | tf_op jit(solution)/shard_map/ppermute | solution.py:494
  47.4 20.5 %collective-permute-start.14 = (bf16[272,256]{1,0:T(8,128)(2,1)S(1)}, bf16[272,256]{1,0:T(8,128)(2,1)S(1)}, u32[]{:S(2)}, u32[]{:S(2)}) collective-permute-start(bf16[272,256]{1,0:T(8,128)(2,1)S(1)} %add.25), channel_id=1, source_target_pairs={{0,8},{64,72},{128,136},{192,200},{16,24},{80,88},{144,152},{208,2... | collective-permute-start | bytes 417800 | tf_op jit(solution)/shard_map/ppermute | solution.py:494
  48.7 19.2 %collective-permute-start.15 = (bf16[1024,256]{1,0:T(8,128)(2,1)S(1)}, bf16[1024,256]{1,0:T(8,128)(2,1)S(1)}, u32[]{:S(2)}, u32[]{:S(2)}) collective-permute-start(bf16[1024,256]{1,0:T(8,128)(2,1)S(1)} %get-tuple-element.40.row_b), channel_id=1, source_target_pairs={{0,64},{8,72},{16,80},{24,88},{32,96},{40,104},{48,112},{56,120},{... | collective-permute-start | bytes 1572872 | tf_op jit(solution)/shard_map/ppermute | solution.py:494
  50.0 18.0 %collective-permute-start.18 = (bf16[1024,256]{1,0:T(8,128)(2,1)}, bf16[1024,256]{1,0:T(8,128)(2,1)S(1)}, u32[]{:S(2)}, u32[]{:S(2)}) collective-permute-start(bf16[1024,256]{1,0:T(8,128)(2,1)} %collective-permute-done.13.above_b), channel_id=1, source_target_pairs={{0,192},{8,200},{16,208},{24,216},{32,224},{40,232},{48,240},{56,2... | collective-permute-start | bytes 1572872 | tf_op jit(solution)/shard_map/ppermute | solution.py:494
  54.5 16.3 %collective-permute-start.17 = (bf16[1024,256]{1,0:T(8,128)(2,1)}, bf16[1024,256]{1,0:T(8,128)(2,1)S(1)}, u32[]{:S(2)}, u32[]{:S(2)}) collective-permute-start(bf16[1024,256]{1,0:T(8,128)(2,1)} %collective-permute-done.12.below_a), channel_id=1, source_target_pairs={{64,128},{72,136},{80,144},{88,152},{96,160},{104,168},{112,176},{... | collective-permute-start | bytes 1572872 | tf_op jit(solution)/shard_map/ppermute | solution.py:494
  55.8 17.8 %collective-permute-start.16 = (bf16[1024,256]{1,0:T(8,128)(2,1)S(1)}, bf16[1024,256]{1,0:T(8,128)(2,1)S(1)}, u32[]{:S(2)}, u32[]{:S(2)}) collective-permute-start(bf16[1024,256]{1,0:T(8,128)(2,1)S(1)} %get-tuple-element.39.row_a), channel_id=1, source_target_pairs={{0,192},{8,200},{16,208},{24,216},{32,224},{40,232},{48,240},{56,2... | collective-permute-start | bytes 1572872 | tf_op jit(solution)/shard_map/ppermute | solution.py:494
  120.8 9.2 %collective-permute-start.23 = (bf16[256,512]{1,0:T(8,128)(2,1)S(1)}, bf16[256,512]{1,0:T(8,128)(2,1)S(1)}, u32[]{:S(2)}, u32[]{:S(2)}) collective-permute-start(bf16[256,512]{1,0:T(8,128)(2,1)S(1)} %get-tuple-element.49), channel_id=1, source_target_pairs={{0,2},{1,3},{2,4},{3,5},{4,6},{5,7},{6,0},{7,1},{8,10},{9,11},{10,... | collective-permute-start | bytes 786440 | tf_op jit(solution)/shard_map/ppermute | solution.py:535
  121.4 10.4 %collective-permute-start.24 = (bf16[256,512]{1,0:T(8,128)(2,1)S(1)}, bf16[256,512]{1,0:T(8,128)(2,1)S(1)}, u32[]{:S(2)}, u32[]{:S(2)}) collective-permute-start(bf16[256,512]{1,0:T(8,128)(2,1)S(1)} %get-tuple-element.50), channel_id=1, source_target_pairs={{0,6},{1,7},{2,0},{3,1},{4,2},{5,3},{6,4},{7,5},{8,14},{9,15},{10,... | collective-permute-start | bytes 786440 | tf_op jit(solution)/shard_map/ppermute | solution.py:535
  124.1 13.3 %collective-permute-start.21 = (bf16[256,512]{1,0:T(8,128)(2,1)S(1)}, bf16[256,512]{1,0:T(8,128)(2,1)S(1)}, u32[]{:S(2)}, u32[]{:S(2)}) collective-permute-start(bf16[256,512]{1,0:T(8,128)(2,1)S(1)} %get-tuple-element.46), channel_id=1, source_target_pairs={{0,6},{1,7},{2,0},{3,1},{4,2},{5,3},{6,4},{7,5},{8,14},{9,15},{10,... | collective-permute-start | bytes 786440 | tf_op jit(solution)/shard_map/ppermute | solution.py:539
  125.0 12.4 %collective-permute-start.22 = (bf16[256,512]{1,0:T(8,128)(2,1)S(1)}, bf16[256,512]{1,0:T(8,128)(2,1)S(1)}, u32[]{:S(2)}, u32[]{:S(2)}) collective-permute-start(bf16[256,512]{1,0:T(8,128)(2,1)S(1)} %get-tuple-element.47), channel_id=1, source_target_pairs={{0,2},{1,3},{2,4},{3,5},{4,6},{5,7},{6,0},{7,1},{8,10},{9,11},{10,... | collective-permute-start | bytes 786440 | tf_op jit(solution)/shard_map/ppermute | solution.py:539
  131.9 8.8 %collective-permute-start.25 = (bf16[256,512]{1,0:T(8,128)(2,1)S(1)}, bf16[256,512]{1,0:T(8,128)(2,1)S(1)}, u32[]{:S(2)}, u32[]{:S(2)}) collective-permute-start(bf16[256,512]{1,0:T(8,128)(2,1)S(1)} %get-tuple-element.53), channel_id=1, source_target_pairs={{0,2},{1,3},{2,4},{3,5},{4,6},{5,7},{6,0},{7,1},{8,10},{9,11},{10,... | collective-permute-start | bytes 786440 | tf_op jit(solution)/shard_map/ppermute | solution.py:542
  132.3 9.9 %collective-permute-start.26 = (bf16[256,512]{1,0:T(8,128)(2,1)S(1)}, bf16[256,512]{1,0:T(8,128)(2,1)S(1)}, u32[]{:S(2)}, u32[]{:S(2)}) collective-permute-start(bf16[256,512]{1,0:T(8,128)(2,1)S(1)} %get-tuple-element.54), channel_id=1, source_target_pairs={{0,6},{1,7},{2,0},{3,1},{4,2},{5,3},{6,4},{7,5},{8,14},{9,15},{10,... | collective-permute-start | bytes 786440 | tf_op jit(solution)/shard_map/ppermute | solution.py:542
  (9 other events, 117.5 us)

commit v13 on v12

--- a/solution.py
+++ b/solution.py
@@ -511,10 +511,10 @@
     opposite = [permute(left[-1][:half], plus), permute(right[-1][half:], minus)]
     ends = pack_row(place, right[1:] + opposite + left[:0:-1] + [kept])
 
+    rest = rest + permute(rest, spread([(0, 2)]))
     rest, ends = lax.optimization_barrier((rest, ends))
     below_a = permute(ends[0], across([(0, 1), (1, 2), (2, 3)]))
     above_b = permute(ends[1], across([(0, 3), (1, 0)]))
-    rest = rest + permute(rest, spread([(0, 2)]))
     rest = rest + permute(rest, spread([(0, 6), (2, 4)]))
     rest, below_a, above_b, ends = lax.optimization_barrier((rest, below_a, above_b, ends))
     below_b = permute(ends[1], across([(0, 1), (1, 2), (2, 3)]))

time: 144 us -> 146 us (1.014)
  waiting for transfers between devices: 37.5 us -> 39.1 us
    ppermute x19, waiting for transfers between devices: 22.2 us -> 23.9 us  [on_device(): permute = lambda x, pairs: lax.ppermute(x, 'ctx', pairs)]
  transfers between devices with their start and end apart: 27 -> 27, of which waited for: 18 -> 17; matrix products, arithmetic and copies ran while one was open for 1% -> 1% of each run, Pallas kernels for 7% -> 7%
where the time goes in v13:
time: 146 us; the launch traced here: 145 us
  Pallas kernels  58.5 us (40%)
  starting transfers between devices  43.7 us (30%)
  waiting for transfers between devices  39.1 us (27%)
  local copies, waits for them, and re-layouts  1.62 us (1%)
    pallas_call x1, Pallas kernels, rest_rows(): pl.pallas_call(rest_kernel, grid=(1,), out_shape=[jax.ShapeDtypeStruct(sh...  44.2 us
    ppermute x19, starting transfers between devices, on_device(): permute = lambda x, pairs: lax.ppermute(x, 'ctx', pairs)  35.9 us
    ppermute x19, waiting for transfers between devices, on_device(): permute = lambda x, pairs: lax.ppermute(x, 'ctx', pairs)  23.9 us
    pallas_call x1, Pallas kernels, own_row(): pl.pallas_call(own_row_kernel, grid=(1,), out_shape=state, in_specs=[SMEM...  9.67 us
    ppermute x1, waiting for transfers between devices, on_device(): lax.ppermute(upper_down, 'head', down)  3.32 us
    ppermute x1, waiting for transfers between devices, on_device(): lax.ppermute(upper_up, 'head', up)  3.18 us
  transfers between devices with their start and end apart: 27, of which 17 were waited for; matrix products, arithmetic and copies ran while one was open for 1% of the time, Pallas kernels for 7%

profile of v13, /device:TPU:30, one launch (start us, length us, event | category | flops | bytes accessed | tf_op | source)
XLA Modules:
  0.0 145.2 jit_solution(13387880861260665817)
XLA Ops:
  0.7 2.4 %select_kept.1 = (bf16[256,256]{1,0:T(8,128)(2,1)}, bf16[272,256]{1,0:T(8,128)(2,1)}) custom-call(s32[1]{0:T(128)S(6)} %copy.7.used_ref, s32[1,256]{1,0:T(1,128)} %refs_0_.1, bf16[512,128]{1,0:T(8,128)(2,1)} %k_ref.1, bf16[512,128]{1,0:T(8,128)(2,1)} %v_ref.1), custom_call_target="tpu_custom_call" | custom-call | tf_op jit(solution)/shard_map/select_kept/pallas_call | solution.py:77
  3.8 2.0 %collective-permute-start.6 = (bf16[256,256]{1,0:T(8,128)(2,1)}, bf16[256,256]{1,0:T(8,128)(2,1)S(1)}, u32[]{:S(2)}, u32[]{:S(2)}) collective-permute-start(bf16[256,256]{1,0:T(8,128)(2,1)} %get-tuple-element.31.refs_8_), channel_id=1, source_target_pairs={{0,8},{8,16},{16,24},{24,32},{32,40},{40,48},{48,56},{56,0},{64,72... | collective-permute-start | bytes 393224 | tf_op jit(solution)/shard_map/ppermute | solution.py:494
  5.8 4.0 %collective-permute-start.3 = (bf16[256,256]{1,0:T(8,128)(2,1)}, bf16[256,256]{1,0:T(8,128)(2,1)S(1)}, u32[]{:S(2)}, u32[]{:S(2)}) collective-permute-start(bf16[256,256]{1,0:T(8,128)(2,1)} %get-tuple-element.31.refs_8_), channel_id=1, source_target_pairs={{0,56},{8,0},{16,8},{24,16},{32,24},{40,32},{48,40},{56,48},{64,12... | collective-permute-start | bytes 393224 | tf_op jit(solution)/shard_map/ppermute | solution.py:494
  9.8 3.6 %collective-permute-done.6.refs_7_ = bf16[256,256]{1,0:T(8,128)(2,1)S(1)} collective-permute-done((bf16[256,256]{1,0:T(8,128)(2,1)}, bf16[256,256]{1,0:T(8,128)(2,1)S(1)}, u32[]{:S(2)}, u32[]{:S(2)}) %collective-permute-start.6) | collective-permute-done | bytes 131104 | tf_op jit(solution)/shard_map/ppermute | solution.py:494
  13.4 3.2 %collective-permute-start.4 = (bf16[256,256]{1,0:T(8,128)(2,1)S(1)}, bf16[256,256]{1,0:T(8,128)(2,1)S(1)}, u32[]{:S(2)}, u32[]{:S(2)}) collective-permute-start(bf16[256,256]{1,0:T(8,128)(2,1)S(1)} %collective-permute-done.3.refs_0_), channel_id=1, source_target_pairs={{0,56},{8,0},{16,8},{24,16},{32,24},{40,32},{48,40},{56,48},{64,12... | collective-permute-start | bytes 393224 | tf_op jit(solution)/shard_map/ppermute | solution.py:494
  19.6 3.2 %collective-permute-start.5 = (bf16[256,256]{1,0:T(8,128)(2,1)S(1)}, bf16[256,256]{1,0:T(8,128)(2,1)S(1)}, u32[]{:S(2)}, u32[]{:S(2)}) collective-permute-start(bf16[256,256]{1,0:T(8,128)(2,1)S(1)} %collective-permute-done.4.refs_1_), channel_id=1, source_target_pairs={{0,56},{8,0},{16,8},{24,16},{32,24},{40,32},{48,40},{56,48},{64,12... | collective-permute-start | bytes 393224 | tf_op jit(solution)/shard_map/ppermute | solution.py:494
  22.9 2.0 %collective-permute-done.1 = bf16[272,256]{1,0:T(8,128)(2,1)S(1)} collective-permute-done((bf16[272,256]{1,0:T(8,128)(2,1)S(1)}, bf16[272,256]{1,0:T(8,128)(2,1)S(1)}, u32[]{:S(2)}, u32[]{:S(2)}) %collective-permute-start.1) | collective-permute-done | bytes 139296 | tf_op jit(solution)/shard_map/ppermute | solution.py:494
  26.4 3.3 %collective-permute-start.10 = (bf16[128,256]{1,0:T(8,128)(2,1)S(1)}, bf16[128,256]{1,0:T(8,128)(2,1)S(1)}, u32[]{:S(2)}, u32[]{:S(2)}) collective-permute-start(bf16[128,256]{1,0:T(8,128)(2,1)S(1)} %slice.17), channel_id=1, source_target_pairs={{0,56},{8,0},{16,8},{24,16},{32,24},{40,32},{48,40},{56,48},{64,12... | collective-permute-start | bytes 196616 | tf_op jit(solution)/shard_map/ppermute | solution.py:494
  29.8 2.0 %collective-permute-done.9.refs_3_ = bf16[128,256]{1,0:T(8,128)(2,1)S(1)} collective-permute-done((bf16[128,256]{1,0:T(8,128)(2,1)S(1)}, bf16[128,256]{1,0:T(8,128)(2,1)S(1)}, u32[]{:S(2)}, u32[]{:S(2)}) %collective-permute-start.9) | collective-permute-done | bytes 65568 | tf_op jit(solution)/shard_map/ppermute | solution.py:494
  36.1 3.5 %collective-permute-start.11 = (bf16[272,256]{1,0:T(8,128)(2,1)S(1)}, bf16[272,256]{1,0:T(8,128)(2,1)S(1)}, u32[]{:S(2)}, u32[]{:S(2)}) collective-permute-start(bf16[272,256]{1,0:T(8,128)(2,1)S(1)} %add.24), channel_id=1, source_target_pairs={{0,48},{64,112},{128,176},{192,240},{16,32},{80,96},{144,160},{208... | collective-permute-start | bytes 417800 | tf_op jit(solution)/shard_map/ppermute | solution.py:494
  39.6 2.6 %collective-permute-done.11 = bf16[272,256]{1,0:T(8,128)(2,1)S(1)} collective-permute-done((bf16[272,256]{1,0:T(8,128)(2,1)S(1)}, bf16[272,256]{1,0:T(8,128)(2,1)S(1)}, u32[]{:S(2)}, u32[]{:S(2)}) %collective-permute-start.11) | collective-permute-done | bytes 139296 | tf_op jit(solution)/shard_map/ppermute | solution.py:494
  42.2 3.6 %collective-permute-done.12.below_a = bf16[1024,256]{1,0:T(8,128)(2,1)} collective-permute-done((bf16[1024,256]{1,0:T(8,128)(2,1)S(1)}, bf16[1024,256]{1,0:T(8,128)(2,1)}, u32[]{:S(2)}, u32[]{:S(2)}) %collective-permute-start.12) | collective-permute-done | bytes 524320 | tf_op jit(solution)/shard_map/ppermute | solution.py:494
  45.7 2.5 %collective-permute-done.13.above_b = bf16[1024,256]{1,0:T(8,128)(2,1)} collective-permute-done((bf16[1024,256]{1,0:T(8,128)(2,1)S(1)}, bf16[1024,256]{1,0:T(8,128)(2,1)}, u32[]{:S(2)}, u32[]{:S(2)}) %collective-permute-start.13) | collective-permute-done | bytes 524320 | tf_op jit(solution)/shard_map/ppermute | solution.py:494
  48.2 2.3 %collective-permute-start.14 = (bf16[272,256]{1,0:T(8,128)(2,1)S(1)}, bf16[272,256]{1,0:T(8,128)(2,1)S(1)}, u32[]{:S(2)}, u32[]{:S(2)}) collective-permute-start(bf16[272,256]{1,0:T(8,128)(2,1)S(1)} %add.25), channel_id=1, source_target_pairs={{0,8},{64,72},{128,136},{192,200},{16,24},{80,88},{144,152},{208,2... | collective-permute-start | bytes 417800 | tf_op jit(solution)/shard_map/ppermute | solution.py:494
  51.9 4.5 %collective-permute-start.18 = (bf16[1024,256]{1,0:T(8,128)(2,1)}, bf16[1024,256]{1,0:T(8,128)(2,1)S(1)}, u32[]{:S(2)}, u32[]{:S(2)}) collective-permute-start(bf16[1024,256]{1,0:T(8,128)(2,1)} %collective-permute-done.13.above_b), channel_id=1, source_target_pairs={{0,192},{8,200},{16,208},{24,216},{32,224},{40,232},{48,240},{56,2... | collective-permute-start | bytes 1572872 | tf_op jit(solution)/shard_map/ppermute | solution.py:494
  59.0 9.7 %own_row.1.state_in = f32[4,512,384]{2,1,0:T(8,128)} custom-call(s32[4]{0:T(128)} %copy-done.2, bf16[512,512]{1,0:T(8,128)(2,1)} %queries.1, bf16[512,128]{1,0:T(8,128)(2,1)} %k_ref.1, bf16[512,128]{1,0:T(8,128)(2,1)} %v_ref.1, bf16[1024,256]{1,0:T(8,128)(2,1)} %copy-done.1, bf16[1024,256]{1,0:T(8,128)(2,1)} %copy-done.5, ...), custom_call_target="tpu_custom_call" | custom-call | flops 9663676416 | bytes 8388608 | tf_op jit(solution)/shard_map/own_row/pallas_call | solution.py:390
  70.0 3.0 %collective-permute-done.17.below2_ref = bf16[1024,256]{1,0:T(8,128)(2,1)S(1)} collective-permute-done((bf16[1024,256]{1,0:T(8,128)(2,1)}, bf16[1024,256]{1,0:T(8,128)(2,1)S(1)}, u32[]{:S(2)}, u32[]{:S(2)}) %collective-permute-start.17) | collective-permute-done | bytes 524320 | tf_op jit(solution)/shard_map/ppermute | solution.py:494
  73.0 2.7 %collective-permute-done.16.above_a = bf16[1024,256]{1,0:T(8,128)(2,1)S(1)} collective-permute-done((bf16[1024,256]{1,0:T(8,128)(2,1)S(1)}, bf16[1024,256]{1,0:T(8,128)(2,1)S(1)}, u32[]{:S(2)}, u32[]{:S(2)}) %collective-permute-start.16) | collective-permute-done | bytes 524320 | tf_op jit(solution)/shard_map/ppermute | solution.py:494
  76.4 44.2 %rest_rows.1 = (bf16[4,512,512]{2,1,0:T(8,128)(2,1)S(1)}, bf16[512,512]{1,0:T(8,128)(2,1)S(1)}, bf16[3,512,512]{2,1,0:T(8,128)(2,1)S(1)}) custom-call(s32[4]{0:T(128)S(1)} %copy-done.3, bf16[272,256]{1,0:T(8,128)(2,1)S(1)} %add.26.rest_ref, bf16[512,512]{1,0:T(8,128)(2,1)S(1)} %copy-done.4, bf16[256,256]{1,0:T(8,128)(2,1)S(1)} %slice_select_fusion.first_ref, ...), custom_call_target="tpu_custom_call" | custom-call | flops 9663676416 | bytes 8388608 | tf_op jit(solution)/shard_map/rest_rows/pallas_call | solution.py:413
  120.7 1.9 %collective-permute-done.19.other_ref = bf16[512,512]{1,0:T(8,128)(2,1)S(1)} collective-permute-done((bf16[512,512]{1,0:T(8,128)(2,1)S(1)}, bf16[512,512]{1,0:T(8,128)(2,1)S(1)}, u32[]{:S(2)}, u32[]{:S(2)}) %collective-permute-start.19) | collective-permute-done | bytes 524320 | tf_op jit(solution)/shard_map/ppermute | solution.py:530
  127.1 2.4 %collective-permute-start.22 = (bf16[256,512]{1,0:T(8,128)(2,1)S(1)}, bf16[256,512]{1,0:T(8,128)(2,1)S(1)}, u32[]{:S(2)}, u32[]{:S(2)}) collective-permute-start(bf16[256,512]{1,0:T(8,128)(2,1)S(1)} %get-tuple-element.47), channel_id=1, source_target_pairs={{0,2},{1,3},{2,4},{3,5},{4,6},{5,7},{6,0},{7,1},{8,10},{9,11},{10,... | collective-permute-start | bytes 786440 | tf_op jit(solution)/shard_map/ppermute | solution.py:539
  129.5 2.6 %collective-permute-done.23.refs_2_ = bf16[256,512]{1,0:T(8,128)(2,1)S(1)} collective-permute-done((bf16[256,512]{1,0:T(8,128)(2,1)S(1)}, bf16[256,512]{1,0:T(8,128)(2,1)S(1)}, u32[]{:S(2)}, u32[]{:S(2)}) %collective-permute-start.23) | collective-permute-done | bytes 262176 | tf_op jit(solution)/shard_map/ppermute | solution.py:535
  136.1 3.3 %collective-permute-done.21.refs_2_ = bf16[256,512]{1,0:T(8,128)(2,1)S(1)} collective-permute-done((bf16[256,512]{1,0:T(8,128)(2,1)S(1)}, bf16[256,512]{1,0:T(8,128)(2,1)S(1)}, u32[]{:S(2)}, u32[]{:S(2)}) %collective-permute-start.21) | collective-permute-done | bytes 262176 | tf_op jit(solution)/shard_map/ppermute | solution.py:539
  139.6 3.2 %collective-permute-done.25.refs_1_ = bf16[256,512]{1,0:T(8,128)(2,1)S(1)} collective-permute-done((bf16[256,512]{1,0:T(8,128)(2,1)S(1)}, bf16[256,512]{1,0:T(8,128)(2,1)S(1)}, u32[]{:S(2)}, u32[]{:S(2)}) %collective-permute-start.25) | collective-permute-done | bytes 262176 | tf_op jit(solution)/shard_map/ppermute | solution.py:542
  (61 shorter events, 26.4 us)
Async XLA Ops:
  3.1 13.6 %collective-permute-start = (bf16[272,256]{1,0:T(8,128)(2,1)S(1)}, bf16[272,256]{1,0:T(8,128)(2,1)S(1)}, u32[]{:S(2)}, u32[]{:S(2)}) collective-permute-start(bf16[272,256]{1,0:T(8,128)(2,1)S(1)} %broadcast_select_fusion), channel_id=1, source_target_pairs={{0,64},{1,65},{2,66},{3,67},{4,68},{5,69},{6,70},{7,71}} | collective-permute-start | bytes 417800 | tf_op jit(solution)/shard_map/ppermute | solution.py:494
  3.8 9.6 %collective-permute-start.6 = (bf16[256,256]{1,0:T(8,128)(2,1)}, bf16[256,256]{1,0:T(8,128)(2,1)S(1)}, u32[]{:S(2)}, u32[]{:S(2)}) collective-permute-start(bf16[256,256]{1,0:T(8,128)(2,1)} %get-tuple-element.31.refs_8_), channel_id=1, source_target_pairs={{0,8},{8,16},{16,24},{24,32},{32,40},{40,48},{48,56},{56,0},{64,72... | collective-permute-start | bytes 393224 | tf_op jit(solution)/shard_map/ppermute | solution.py:494
  5.8 7.6 %collective-permute-start.3 = (bf16[256,256]{1,0:T(8,128)(2,1)}, bf16[256,256]{1,0:T(8,128)(2,1)S(1)}, u32[]{:S(2)}, u32[]{:S(2)}) collective-permute-start(bf16[256,256]{1,0:T(8,128)(2,1)} %get-tuple-element.31.refs_8_), channel_id=1, source_target_pairs={{0,56},{8,0},{16,8},{24,16},{32,24},{40,32},{48,40},{56,48},{64,12... | collective-permute-start | bytes 393224 | tf_op jit(solution)/shard_map/ppermute | solution.py:494
  13.4 6.2 %collective-permute-start.7 = (bf16[256,256]{1,0:T(8,128)(2,1)S(1)}, bf16[256,256]{1,0:T(8,128)(2,1)S(1)}, u32[]{:S(2)}, u32[]{:S(2)}) collective-permute-start(bf16[256,256]{1,0:T(8,128)(2,1)S(1)} %collective-permute-done.6.refs_7_), channel_id=1, source_target_pairs={{0,8},{8,16},{16,24},{24,32},{32,40},{40,48},{48,56},{56,0},{64,72... | collective-permute-start | bytes 393224 | tf_op jit(solution)/shard_map/ppermute | solution.py:494
  13.4 6.2 %collective-permute-start.4 = (bf16[256,256]{1,0:T(8,128)(2,1)S(1)}, bf16[256,256]{1,0:T(8,128)(2,1)S(1)}, u32[]{:S(2)}, u32[]{:S(2)}) collective-permute-start(bf16[256,256]{1,0:T(8,128)(2,1)S(1)} %collective-permute-done.3.refs_0_), channel_id=1, source_target_pairs={{0,56},{8,0},{16,8},{24,16},{32,24},{40,32},{48,40},{56,48},{64,12... | collective-permute-start | bytes 393224 | tf_op jit(solution)/shard_map/ppermute | solution.py:494
  16.7 8.2 %collective-permute-start.1 = (bf16[272,256]{1,0:T(8,128)(2,1)S(1)}, bf16[272,256]{1,0:T(8,128)(2,1)S(1)}, u32[]{:S(2)}, u32[]{:S(2)}) collective-permute-start(bf16[272,256]{1,0:T(8,128)(2,1)S(1)} %fusion), channel_id=1, source_target_pairs={{0,192},{64,128},{1,193},{65,129},{2,194},{66,130},{3,195},{67,131... | collective-permute-start | bytes 417800 | tf_op jit(solution)/shard_map/ppermute | solution.py:494
  19.6 6.6 %collective-permute-start.8 = (bf16[256,256]{1,0:T(8,128)(2,1)S(1)}, bf16[256,256]{1,0:T(8,128)(2,1)S(1)}, u32[]{:S(2)}, u32[]{:S(2)}) collective-permute-start(bf16[256,256]{1,0:T(8,128)(2,1)S(1)} %collective-permute-done.7.refs_6_), channel_id=1, source_target_pairs={{0,8},{8,16},{16,24},{24,32},{32,40},{40,48},{48,56},{56,0},{64,72... | collective-permute-start | bytes 393224 | tf_op jit(solution)/shard_map/ppermute | solution.py:494
  19.6 6.7 %collective-permute-start.5 = (bf16[256,256]{1,0:T(8,128)(2,1)S(1)}, bf16[256,256]{1,0:T(8,128)(2,1)S(1)}, u32[]{:S(2)}, u32[]{:S(2)}) collective-permute-start(bf16[256,256]{1,0:T(8,128)(2,1)S(1)} %collective-permute-done.4.refs_1_), channel_id=1, source_target_pairs={{0,56},{8,0},{16,8},{24,16},{32,24},{40,32},{48,40},{56,48},{64,12... | collective-permute-start | bytes 393224 | tf_op jit(solution)/shard_map/ppermute | solution.py:494
  26.3 5.6 %collective-permute-start.9 = (bf16[128,256]{1,0:T(8,128)(2,1)S(1)}, bf16[128,256]{1,0:T(8,128)(2,1)S(1)}, u32[]{:S(2)}, u32[]{:S(2)}) collective-permute-start(bf16[128,256]{1,0:T(8,128)(2,1)S(1)} %slice.16), channel_id=1, source_target_pairs={{0,8},{8,16},{16,24},{24,32},{32,40},{40,48},{48,56},{56,0},{64,72... | collective-permute-start | bytes 196616 | tf_op jit(solution)/shard_map/ppermute | solution.py:494
  26.4 5.4 %collective-permute-start.10 = (bf16[128,256]{1,0:T(8,128)(2,1)S(1)}, bf16[128,256]{1,0:T(8,128)(2,1)S(1)}, u32[]{:S(2)}, u32[]{:S(2)}) collective-permute-start(bf16[128,256]{1,0:T(8,128)(2,1)S(1)} %slice.17), channel_id=1, source_target_pairs={{0,56},{8,0},{16,8},{24,16},{32,24},{40,32},{48,40},{56,48},{64,12... | collective-permute-start | bytes 196616 | tf_op jit(solution)/shard_map/ppermute | solution.py:494
  33.5 12.3 %collective-permute-start.12 = (bf16[1024,256]{1,0:T(8,128)(2,1)S(1)}, bf16[1024,256]{1,0:T(8,128)(2,1)}, u32[]{:S(2)}, u32[]{:S(2)}) collective-permute-start(bf16[1024,256]{1,0:T(8,128)(2,1)S(1)} %get-tuple-element.39.row_a), channel_id=1, source_target_pairs={{0,64},{8,72},{16,80},{24,88},{32,96},{40,104},{48,112},{56,120},{... | collective-permute-start | bytes 1572872 | tf_op jit(solution)/shard_map/ppermute | solution.py:494
  34.8 13.5 %collective-permute-start.13 = (bf16[1024,256]{1,0:T(8,128)(2,1)S(1)}, bf16[1024,256]{1,0:T(8,128)(2,1)}, u32[]{:S(2)}, u32[]{:S(2)}) collective-permute-start(bf16[1024,256]{1,0:T(8,128)(2,1)S(1)} %get-tuple-element.40.row_b), channel_id=1, source_target_pairs={{0,192},{8,200},{16,208},{24,216},{32,224},{40,232},{48,240},{56,2... | collective-permute-start | bytes 1572872 | tf_op jit(solution)/shard_map/ppermute | solution.py:494
  36.1 6.0 %collective-permute-start.11 = (bf16[272,256]{1,0:T(8,128)(2,1)S(1)}, bf16[272,256]{1,0:T(8,128)(2,1)S(1)}, u32[]{:S(2)}, u32[]{:S(2)}) collective-permute-start(bf16[272,256]{1,0:T(8,128)(2,1)S(1)} %add.24), channel_id=1, source_target_pairs={{0,48},{64,112},{128,176},{192,240},{16,32},{80,96},{144,160},{208... | collective-permute-start | bytes 417800 | tf_op jit(solution)/shard_map/ppermute | solution.py:494
  48.2 21.5 %collective-permute-start.14 = (bf16[272,256]{1,0:T(8,128)(2,1)S(1)}, bf16[272,256]{1,0:T(8,128)(2,1)S(1)}, u32[]{:S(2)}, u32[]{:S(2)}) collective-permute-start(bf16[272,256]{1,0:T(8,128)(2,1)S(1)} %add.25), channel_id=1, source_target_pairs={{0,8},{64,72},{128,136},{192,200},{16,24},{80,88},{144,152},{208,2... | collective-permute-start | bytes 417800 | tf_op jit(solution)/shard_map/ppermute | solution.py:494
  50.6 19.2 %collective-permute-start.15 = (bf16[1024,256]{1,0:T(8,128)(2,1)S(1)}, bf16[1024,256]{1,0:T(8,128)(2,1)S(1)}, u32[]{:S(2)}, u32[]{:S(2)}) collective-permute-start(bf16[1024,256]{1,0:T(8,128)(2,1)S(1)} %get-tuple-element.40.row_b), channel_id=1, source_target_pairs={{0,64},{8,72},{16,80},{24,88},{32,96},{40,104},{48,112},{56,120},{... | collective-permute-start | bytes 1572872 | tf_op jit(solution)/shard_map/ppermute | solution.py:494
  51.9 18.2 %collective-permute-start.18 = (bf16[1024,256]{1,0:T(8,128)(2,1)}, bf16[1024,256]{1,0:T(8,128)(2,1)S(1)}, u32[]{:S(2)}, u32[]{:S(2)}) collective-permute-start(bf16[1024,256]{1,0:T(8,128)(2,1)} %collective-permute-done.13.above_b), channel_id=1, source_target_pairs={{0,192},{8,200},{16,208},{24,216},{32,224},{40,232},{48,240},{56,2... | collective-permute-start | bytes 1572872 | tf_op jit(solution)/shard_map/ppermute | solution.py:494
  56.4 16.6 %collective-permute-start.17 = (bf16[1024,256]{1,0:T(8,128)(2,1)}, bf16[1024,256]{1,0:T(8,128)(2,1)S(1)}, u32[]{:S(2)}, u32[]{:S(2)}) collective-permute-start(bf16[1024,256]{1,0:T(8,128)(2,1)} %collective-permute-done.12.below_a), channel_id=1, source_target_pairs={{64,128},{72,136},{80,144},{88,152},{96,160},{104,168},{112,176},{... | collective-permute-start | bytes 1572872 | tf_op jit(solution)/shard_map/ppermute | solution.py:494
  57.7 18.0 %collective-permute-start.16 = (bf16[1024,256]{1,0:T(8,128)(2,1)S(1)}, bf16[1024,256]{1,0:T(8,128)(2,1)S(1)}, u32[]{:S(2)}, u32[]{:S(2)}) collective-permute-start(bf16[1024,256]{1,0:T(8,128)(2,1)S(1)} %get-tuple-element.39.row_a), channel_id=1, source_target_pairs={{0,192},{8,200},{16,208},{24,216},{32,224},{40,232},{48,240},{56,2... | collective-permute-start | bytes 1572872 | tf_op jit(solution)/shard_map/ppermute | solution.py:494
  122.9 9.2 %collective-permute-start.23 = (bf16[256,512]{1,0:T(8,128)(2,1)S(1)}, bf16[256,512]{1,0:T(8,128)(2,1)S(1)}, u32[]{:S(2)}, u32[]{:S(2)}) collective-permute-start(bf16[256,512]{1,0:T(8,128)(2,1)S(1)} %get-tuple-element.49), channel_id=1, source_target_pairs={{0,2},{1,3},{2,4},{3,5},{4,6},{5,7},{6,0},{7,1},{8,10},{9,11},{10,... | collective-permute-start | bytes 786440 | tf_op jit(solution)/shard_map/ppermute | solution.py:535
  123.5 10.4 %collective-permute-start.24 = (bf16[256,512]{1,0:T(8,128)(2,1)S(1)}, bf16[256,512]{1,0:T(8,128)(2,1)S(1)}, u32[]{:S(2)}, u32[]{:S(2)}) collective-permute-start(bf16[256,512]{1,0:T(8,128)(2,1)S(1)} %get-tuple-element.50), channel_id=1, source_target_pairs={{0,6},{1,7},{2,0},{3,1},{4,2},{5,3},{6,4},{7,5},{8,14},{9,15},{10,... | collective-permute-start | bytes 786440 | tf_op jit(solution)/shard_map/ppermute | solution.py:535
  126.2 13.3 %collective-permute-start.21 = (bf16[256,512]{1,0:T(8,128)(2,1)S(1)}, bf16[256,512]{1,0:T(8,128)(2,1)S(1)}, u32[]{:S(2)}, u32[]{:S(2)}) collective-permute-start(bf16[256,512]{1,0:T(8,128)(2,1)S(1)} %get-tuple-element.46), channel_id=1, source_target_pairs={{0,6},{1,7},{2,0},{3,1},{4,2},{5,3},{6,4},{7,5},{8,14},{9,15},{10,... | collective-permute-start | bytes 786440 | tf_op jit(solution)/shard_map/ppermute | solution.py:539
  127.1 12.4 %collective-permute-start.22 = (bf16[256,512]{1,0:T(8,128)(2,1)S(1)}, bf16[256,512]{1,0:T(8,128)(2,1)S(1)}, u32[]{:S(2)}, u32[]{:S(2)}) collective-permute-start(bf16[256,512]{1,0:T(8,128)(2,1)S(1)} %get-tuple-element.47), channel_id=1, source_target_pairs={{0,2},{1,3},{2,4},{3,5},{4,6},{5,7},{6,0},{7,1},{8,10},{9,11},{10,... | collective-permute-start | bytes 786440 | tf_op jit(solution)/shard_map/ppermute | solution.py:539
  134.0 8.8 %collective-permute-start.25 = (bf16[256,512]{1,0:T(8,128)(2,1)S(1)}, bf16[256,512]{1,0:T(8,128)(2,1)S(1)}, u32[]{:S(2)}, u32[]{:S(2)}) collective-permute-start(bf16[256,512]{1,0:T(8,128)(2,1)S(1)} %get-tuple-element.53), channel_id=1, source_target_pairs={{0,2},{1,3},{2,4},{3,5},{4,6},{5,7},{6,0},{7,1},{8,10},{9,11},{10,... | collective-permute-start | bytes 786440 | tf_op jit(solution)/shard_map/ppermute | solution.py:542
  134.4 9.9 %collective-permute-start.26 = (bf16[256,512]{1,0:T(8,128)(2,1)S(1)}, bf16[256,512]{1,0:T(8,128)(2,1)S(1)}, u32[]{:S(2)}, u32[]{:S(2)}) collective-permute-start(bf16[256,512]{1,0:T(8,128)(2,1)S(1)} %get-tuple-element.54), channel_id=1, source_target_pairs={{0,6},{1,7},{2,0},{3,1},{4,2},{5,3},{6,4},{7,5},{8,14},{9,15},{10,... | collective-permute-start | bytes 786440 | tf_op jit(solution)/shard_map/ppermute | solution.py:542
  (9 other events, 125.8 us)
